TPU v7x, 128 devices: a whole 4x4x4 slice. The times are simulated.
128 devices in a mesh: fsdp: 4 (over y), sp: 32 (over x, z, core).
Axes of the slice: x: 4, y: 4, z: 4, core: 2. Of those that a mesh axis runs over, the one named last changes fastest.
Arguments:
- tokens: bfloat16 [16384, 2048], P(('fsdp', 'sp')), may hold values from -6 to 6
- pre_attention_gain: float32 [2048], replicated, may hold values from 0.5 to 1.5
- in_projection: bfloat16 [2048, 5120], P(None, ('fsdp', 'sp')), may hold values from -0.125 to 0.125
- query_gain: float32 [128], replicated, may hold values from 0.5 to 1.5
- key_gain: float32 [128], replicated, may hold values from 0.5 to 1.5
- out_projection: bfloat16 [4096, 2048], P(('fsdp', 'sp')), may hold values from -1.5 to 1.5
- pre_expert_gain: float32 [2048], replicated, may hold values from 0.5 to 1.5
- gate_up: bfloat16 [128, 2048, 1536], P(('fsdp', 'sp')), may hold values from -0.125 to 0.125
- down_projection: bfloat16 [128, 768, 2048], P(('fsdp', 'sp')), may hold values from -0.21875 to 0.21875
- routes: int32 [16384, 2], P(('fsdp', 'sp')), may hold values from 0 to 127, all different within a row; in each aligned block of 128 rows (0 to 127, 128 to 255, ...) at most 3 rows name the same one
- gates: float32 [16384, 2], P(('fsdp', 'sp')), may hold values from 0.3 to 1
- target: bfloat16 [16384, 2048], P(('fsdp', 'sp')), may hold values from -6 to 6
- valid: int32 [16384], P(('fsdp', 'sp')), may hold values from 0 to 1, as said below
Outputs:
- output: bfloat16 [16384, 2048], P(('fsdp', 'sp'))
- loss: float32 [], replicated
- tokens_gradient: float32 [16384, 2048], P(('fsdp', 'sp'))
- pre_attention_gain_gradient: float32 [2048], replicated
- in_projection_gradient: float32 [2048, 5120], P(None, ('fsdp', 'sp'))
- query_gain_gradient: float32 [128], replicated
- key_gain_gradient: float32 [128], replicated
- out_projection_gradient: float32 [4096, 2048], P(('fsdp', 'sp'))
- pre_expert_gain_gradient: float32 [2048], replicated
- gate_up_gradient: float32 [128, 2048, 1536], P(('fsdp', 'sp'))
- down_projection_gradient: float32 [128, 768, 2048], P(('fsdp', 'sp'))
Inputs may be any that keep to these rules, and one draw needn't show every extreme that they name: `routes`: the 2 experts of a token differ. Among the 128 tokens of each aligned block (the tokens of one device) no expert is named more than 3 times, a bound that some block reaches. The last token of every aligned block of 128 tokens is valid.
All inputs are finite; a program needn't handle non-finite values.
Results may differ from a plain program's by a relative error of at most 0.014.
Values may be sent and summed in bfloat16 or wider, within the bound.
No kernel may reach another device: no remote copies, remote signals or barrier semaphores. Data moves between devices by JAX's collectives and lax.ppermute only.
A program may use at most 320 MiB of HBM per device.

v0:
```python
import jax
import jax.numpy as jnp
from jax import lax
from jax.sharding import PartitionSpec as P

D = 2048
H = 32
KV = 4
HD = 128
FF = 768
TOP = 2


epsilon = 1e-06
theta = 1000000.0


def unit_scale(value, gain):
    return value * lax.rsqrt(jnp.mean(value * value, axis=-1, keepdims=True) + epsilon) * gain


def rotate(value, cosine, sine):
    half = value.shape[-1] // 2
    turned = jnp.concatenate([-value[..., half:], value[..., :half]], axis=-1)
    return value * cosine + turned * sine


def angles(position):
    frequency = theta ** (-jnp.arange(0, HD, 2).astype(jnp.float32) / HD)
    phase = position[:, None] * frequency[None, :]
    phase = jnp.concatenate([phase, phase], axis=-1)[:, None, :]
    return (jnp.cos(phase), jnp.sin(phase))


def rotate_heads(projected, query_gain, key_gain, cosine, sine):
    count_rows = projected.shape[0]
    queries = projected[:, : H * HD].reshape(count_rows, H, HD)
    keys = projected[:, H * HD : (H + KV) * HD].reshape(count_rows, KV, HD)
    values = projected[:, (H + KV) * HD :].reshape(count_rows, KV, HD)
    queries = rotate(unit_scale(queries, query_gain), cosine, sine)
    keys = rotate(unit_scale(keys, key_gain), cosine, sine)
    return (queries, keys, values)


def activate(mixed):
    return jax.nn.silu(mixed[:, :FF]) * mixed[:, FF:]


def causal_mask(row, column, block):
    offsets = jnp.arange(block, dtype=jnp.int32)
    return (column * block + offsets)[None, None, :] <= (row * block + offsets)[None, :, None]


def block_scores(query_block, key_block, row, column, block, scale):
    raw = (
        jnp.einsum("qhd,khd->hqk", query_block, key_block, preferred_element_type=jnp.float32)
        * scale
    )
    return jnp.where(causal_mask(row, column, block), raw, -1e30)


def attend_forward(queries, keys, values):
    length, heads, depth = queries.shape
    block = min(512, length)
    count = length // block
    scale = depth ** (-0.5)
    query_blocks = queries.reshape(count, block, heads, depth)
    key_blocks = keys.reshape(count, block, heads, depth)
    value_blocks = values.reshape(count, block, heads, depth)

    def per_block(row):
        query_block = query_blocks[row]

        def gather_stats(column, carry):
            largest, summed = carry
            scores = block_scores(query_block, key_blocks[column], row, column, block, scale)
            newest = jnp.maximum(largest, jnp.max(scores, axis=-1))
            summed = summed * jnp.exp(largest - newest) + jnp.sum(
                jnp.exp(scores - newest[..., None]), axis=-1
            )
            return (newest, summed)

        begin = (
            jnp.full((heads, block), -1e30, jnp.float32),
            jnp.zeros((heads, block), jnp.float32),
        )
        largest, summed = lax.fori_loop(0, row + 1, gather_stats, begin)
        log_total = largest + jnp.log(summed)

        def add_values(column, accumulated):
            scores = block_scores(query_block, key_blocks[column], row, column, block, scale)
            weights = jnp.exp(scores - log_total[..., None]).astype(jnp.bfloat16)
            return accumulated + jnp.einsum(
                "hqk,khd->qhd", weights, value_blocks[column], preferred_element_type=jnp.float32
            )

        result = lax.fori_loop(
            0, row + 1, add_values, jnp.zeros((block, heads, depth), jnp.float32)
        )
        return (result, log_total)

    result, log_total = lax.map(per_block, jnp.arange(count, dtype=jnp.int32))
    return (result.reshape(length, heads, depth), log_total)


def attend_backward(queries, keys, values, back_out, result, log_total):
    length, heads, depth = queries.shape
    block = min(512, length)
    count = length // block
    scale = depth ** (-0.5)
    query_blocks = queries.reshape(count, block, heads, depth)
    key_blocks = keys.reshape(count, block, heads, depth)
    value_blocks = values.reshape(count, block, heads, depth)
    back_blocks = back_out.reshape(count, block, heads, depth)
    deltas = (
        jnp.sum(back_out.astype(jnp.float32) * result, axis=-1)
        .reshape(count, block, heads)
        .transpose(0, 2, 1)
    )

    def per_key(back_queries, column):
        key_block = key_blocks[column]
        value_block = value_blocks[column]

        def per_query(row, carry):
            back_queries, back_keys, back_values = carry
            query_block = query_blocks[row]
            back_block = back_blocks[row]
            scores = block_scores(query_block, key_block, row, column, block, scale)
            weights = jnp.exp(scores - log_total[row][..., None])
            back_values = back_values + jnp.einsum(
                "hqk,qhd->khd",
                weights.astype(jnp.bfloat16),
                back_block,
                preferred_element_type=jnp.float32,
            )
            back_weights = jnp.einsum(
                "qhd,khd->hqk", back_block, value_block, preferred_element_type=jnp.float32
            )
            back_scores = (weights * (back_weights - deltas[row][..., None])).astype(jnp.bfloat16)
            back_keys = (
                back_keys
                + jnp.einsum(
                    "hqk,qhd->khd", back_scores, query_block, preferred_element_type=jnp.float32
                )
                * scale
            )
            update = (
                jnp.einsum(
                    "hqk,khd->qhd", back_scores, key_block, preferred_element_type=jnp.float32
                )
                * scale
            )
            back_queries = back_queries.at[row].add(update)
            return (back_queries, back_keys, back_values)

        zeros = jnp.zeros((block, heads, depth), jnp.float32)
        back_queries, back_keys, back_values = lax.fori_loop(
            column, count, per_query, (back_queries, zeros, zeros)
        )
        return (back_queries, (back_keys, back_values))

    start_queries = jnp.zeros((count, block, heads, depth), jnp.float32)
    back_queries, (back_keys, back_values) = lax.scan(
        per_key, start_queries, jnp.arange(count, dtype=jnp.int32)
    )
    shape = (length, heads, depth)
    return (back_queries.reshape(shape), back_keys.reshape(shape), back_values.reshape(shape))


def move_rows(rows, devices):
    width = rows.shape[-1]
    blocks = rows.reshape(devices, -1, width)
    moved = lax.all_to_all(blocks, ("fsdp", "sp"), split_axis=0, concat_axis=0, tiled=True)
    return moved.reshape(-1, width)


def body(
    tokens,
    pre_attention_gain,
    in_projection,
    query_gain,
    key_gain,
    out_projection,
    pre_expert_gain,
    gate_up,
    down_projection,
    routes,
    gates,
    target,
    valid,
):
    local_tokens = tokens.shape[0]
    devices = lax.axis_size("fsdp") * lax.axis_size("sp")
    capacity = max(2, 3 * local_tokens * TOP // (2 * devices))
    group = H // KV
    inputs = tokens.astype(jnp.float32)
    normed_values, norm_pull = jax.vjp(unit_scale, inputs, pre_attention_gain)
    normed = normed_values.astype(jnp.bfloat16)
    full_in, full_out = (
        lax.all_gather(in_projection, ("fsdp", "sp"), axis=1, tiled=True),
        lax.all_gather(out_projection, ("fsdp", "sp"), axis=0, tiled=True),
    )
    projected = jnp.dot(normed, full_in, preferred_element_type=jnp.float32)
    position = (
        lax.axis_index("sp") * local_tokens + jnp.arange(local_tokens, dtype=jnp.int32)
    ).astype(jnp.float32)
    cosine, sine = angles(position)
    (queries, keys, values), heads_pull = jax.vjp(
        lambda rows, first, second: rotate_heads(rows, first, second, cosine, sine),
        projected,
        query_gain,
        key_gain,
    )
    query_send = queries.astype(jnp.bfloat16).reshape(local_tokens, H * HD)
    key_send = jnp.repeat(keys.astype(jnp.bfloat16), group, axis=1).reshape(local_tokens, H * HD)
    value_send = jnp.repeat(values.astype(jnp.bfloat16), group, axis=1).reshape(
        local_tokens, H * HD
    )
    head_queries, head_keys, head_values = (
        lax.all_to_all(query_send, "sp", split_axis=1, concat_axis=0, tiled=True),
        lax.all_to_all(key_send, "sp", split_axis=1, concat_axis=0, tiled=True),
        lax.all_to_all(value_send, "sp", split_axis=1, concat_axis=0, tiled=True),
    )
    length = head_queries.shape[0]
    heads_here = head_queries.shape[1] // HD
    head_queries = head_queries.reshape(length, heads_here, HD)
    head_keys = head_keys.reshape(length, heads_here, HD)
    head_values = head_values.reshape(length, heads_here, HD)
    result, log_total = attend_forward(head_queries, head_keys, head_values)
    attended = lax.all_to_all(
        result.astype(jnp.bfloat16).reshape(length, heads_here * HD),
        "sp",
        split_axis=0,
        concat_axis=1,
        tiled=True,
    )
    residual = inputs + jnp.dot(attended, full_out, preferred_element_type=jnp.float32)
    expert_values, expert_pull = jax.vjp(unit_scale, residual, pre_expert_gain)
    expert_input = expert_values.astype(jnp.bfloat16)
    route_numbers = routes.reshape(-1)
    pairs = route_numbers.shape[0]
    one_hot = (route_numbers[:, None] == jnp.arange(devices, dtype=jnp.int32)[None, :]).astype(
        jnp.int32
    )
    earlier = jnp.cumsum(one_hot, axis=0) - one_hot
    slots = route_numbers * capacity + jnp.sum(earlier * one_hot, axis=1)
    owners = jnp.arange(pairs, dtype=jnp.int32) // TOP
    send_rows = jnp.zeros((devices * capacity, D), jnp.bfloat16).at[slots].set(expert_input[owners])
    expert_rows = move_rows(send_rows, devices)
    first = gate_up[0]
    second = down_projection[0]
    mixed = jnp.dot(expert_rows, first, preferred_element_type=jnp.float32)
    hidden_values, activate_pull = jax.vjp(activate, mixed)
    hidden = hidden_values.astype(jnp.bfloat16)
    expert_out = jnp.dot(hidden, second, preferred_element_type=jnp.float32).astype(jnp.bfloat16)
    returned = move_rows(expert_out, devices)[slots].reshape(local_tokens, TOP, D)
    final = residual + jnp.sum(gates[:, :, None] * returned.astype(jnp.float32), axis=1)
    output = final.astype(jnp.bfloat16)
    mask = valid.astype(jnp.float32)
    error = output.astype(jnp.float32) - target.astype(jnp.float32)
    loss_sum, valid_count = lax.psum(
        (jnp.sum(mask[:, None] * error * error), jnp.sum(mask)), ("fsdp", "sp")
    )
    loss = loss_sum / (2.0 * valid_count * D)
    back_final = local_tokens * devices / valid_count * mask[:, None] * error
    back_routes = (
        (gates[:, :, None] * back_final[:, None, :]).astype(jnp.bfloat16).reshape(pairs, D)
    )
    back_expert_out = move_rows(
        jnp.zeros((devices * capacity, D), jnp.bfloat16).at[slots].set(back_routes), devices
    )
    second_gradient = jnp.dot(hidden.T, back_expert_out, preferred_element_type=jnp.float32)
    back_hidden = jnp.dot(back_expert_out, second.T, preferred_element_type=jnp.float32)
    back_mixed = activate_pull(back_hidden)[0].astype(jnp.bfloat16)
    first_gradient = jnp.dot(expert_rows.T, back_mixed, preferred_element_type=jnp.float32)
    back_rows = jnp.dot(back_mixed, first.T, preferred_element_type=jnp.float32).astype(
        jnp.bfloat16
    )
    back_pairs = move_rows(back_rows, devices)[slots].reshape(local_tokens, TOP, D)
    back_expert_input = jnp.sum(back_pairs.astype(jnp.float32), axis=1)
    back_residual_norm, expert_gain_term = expert_pull(back_expert_input)
    back_residual = back_final + back_residual_norm
    back_branch = back_residual.astype(jnp.bfloat16)
    out_gradient = jnp.dot(attended.T, back_branch, preferred_element_type=jnp.float32)
    back_attended = jnp.dot(back_branch, full_out.T, preferred_element_type=jnp.float32).astype(
        jnp.bfloat16
    )
    back_heads = lax.all_to_all(
        back_attended, "sp", split_axis=1, concat_axis=0, tiled=True
    ).reshape(length, heads_here, HD)
    head_back_queries, head_back_keys, head_back_values = attend_backward(
        head_queries, head_keys, head_values, back_heads, result, log_total
    )
    token_back_queries, token_back_keys, token_back_values = (
        lax.all_to_all(
            head_back_queries.astype(jnp.bfloat16).reshape(length, heads_here * HD),
            "sp",
            split_axis=0,
            concat_axis=1,
            tiled=True,
        ),
        lax.all_to_all(
            head_back_keys.astype(jnp.bfloat16).reshape(length, heads_here * HD),
            "sp",
            split_axis=0,
            concat_axis=1,
            tiled=True,
        ),
        lax.all_to_all(
            head_back_values.astype(jnp.bfloat16).reshape(length, heads_here * HD),
            "sp",
            split_axis=0,
            concat_axis=1,
            tiled=True,
        ),
    )
    back_queries = token_back_queries.astype(jnp.float32).reshape(local_tokens, H, HD)
    back_keys = jnp.sum(
        token_back_keys.astype(jnp.float32).reshape(local_tokens, KV, group, HD), axis=2
    )
    back_values = jnp.sum(
        token_back_values.astype(jnp.float32).reshape(local_tokens, KV, group, HD), axis=2
    )
    back_projected, query_gain_term, key_gain_term = heads_pull(
        (back_queries, back_keys, back_values)
    )
    back_projected = back_projected.astype(jnp.bfloat16)
    back_normed = jnp.dot(back_projected, full_in.T, preferred_element_type=jnp.float32)
    back_inputs_norm, attention_gain_term = norm_pull(back_normed)
    tokens_gradient = back_residual + back_inputs_norm
    in_gradient = jnp.dot(normed.T, back_projected, preferred_element_type=jnp.float32)
    in_projection_gradient, out_projection_gradient = (
        lax.psum_scatter(in_gradient, ("fsdp", "sp"), scatter_dimension=1, tiled=True),
        lax.psum_scatter(out_gradient, ("fsdp", "sp"), scatter_dimension=0, tiled=True),
    )
    gain_sums = lax.psum(
        (attention_gain_term, query_gain_term, key_gain_term, expert_gain_term), ("fsdp", "sp")
    )
    return (
        output,
        loss,
        tokens_gradient,
        gain_sums[0],
        in_projection_gradient,
        gain_sums[1],
        gain_sums[2],
        out_projection_gradient,
        gain_sums[3],
        first_gradient[None],
        second_gradient[None],
    )


def solution(mesh):
    placed = (
        P(("fsdp", "sp"), None),
        P(),
        P(None, ("fsdp", "sp")),
        P(),
        P(),
        P(("fsdp", "sp"), None),
        P(),
        P(("fsdp", "sp"), None, None),
        P(("fsdp", "sp"), None, None),
        P(("fsdp", "sp"), None),
        P(("fsdp", "sp"), None),
        P(("fsdp", "sp"), None),
        P(("fsdp", "sp")),
    )
    return jax.shard_map(
        body,
        mesh=mesh,
        in_specs=placed,
        out_specs=(
            P(("fsdp", "sp"), None),
            P(),
            P(("fsdp", "sp"), None),
            P(),
            P(None, ("fsdp", "sp")),
            P(),
            P(),
            P(("fsdp", "sp"), None),
            P(),
            P(("fsdp", "sp"), None, None),
            P(("fsdp", "sp"), None, None),
        ),
        check_vma=False,
    )
```

profile of v0, /device:TPU:0, one launch (start us, length us, event | category | flops | bytes accessed | tf_op | source)
XLA Modules:
  0.0 2163.6 jit_solution(15011325418181514426)
XLA Ops:
  11.6 89.0 %all-gather.3.cloned.1.call-done = bf16[2048,5120]{0,1:T(8,128)(2,1)} async-done(((bf16[2048,40]{0,1:T(8,128)(2,1)}), bf16[2048,5120]{0,1:T(8,128)(2,1)}) %all-gather.3.cloned.1.call-update) | async-done | bytes 20971536 | tf_op jit(solution)/shard_map/all_gather | solution.py:201
  173.7 15.8 all-to-all-done.1
  212.7 180.6 %while.79 = (s32[]{:T(128)}, f32[8,512,1,128]{3,1,0,2:T(8,128)}, f32[8,1,512]{2,1,0:T(1,128)}, s32[8]{0:T(128)}, bf16[8,512,1,128]{3,1,2,0:T(8,128)(2,1)}, /*ind...) while((s32[]{:T(128)}, f32[8,512,1,128]{3,1,0,2:T(8,128)}, ...), condition=%wide.region_10.11_spmd.clone, body=%wide.region_3.10_spmd.sunk.clone | while | flops 204279312 | bytes 4908813 | solution.py:102
  401.2 16.4 all-to-all-done.3
  442.4 36.9 %all_to_all.130 = bf16[128,3,2048]{2,1,0:T(4,128)(2,1)} all-to-all(bf16[128,3,2048]{2,1,0:T(4,128)(2,1)} %reshape.631), channel_id=1, replica_groups=mesh['fsdp'=4,'sp'=32] {'fsdp','sp'}, dimensions={0} | all-to-all | bytes 3145728 | tf_op jit(solution)/shard_map/all_to_all | solution.py:174
  506.4 80.1 %psum.43 = f32[]{:T(128)} all-reduce(f32[]{:T(128)} %convert_reduce_fusion), channel_id=1, replica_groups=mesh['fsdp'=4,'sp'=32] {'fsdp','sp'}, use_global_device_ids=true, to_apply=%region_20.21 | all-reduce | flops 1 | bytes 8 | tf_op jit(solution)/shard_map/psum | solution.py:262
  623.3 37.0 %all_to_all.131 = bf16[128,3,2048]{2,1,0:T(4,128)(2,1)} all-to-all(bf16[128,3,2048]{2,1,0:T(4,128)(2,1)} %reshape.635), channel_id=1, replica_groups=mesh['fsdp'=4,'sp'=32] {'fsdp','sp'}, dimensions={0} | all-to-all | bytes 3145728 | tf_op jit(solution)/shard_map/all_to_all | solution.py:174
  684.1 29.9 %all-to-all-done.7 = bf16[128,3,2048]{2,1,0:T(4,128)(2,1)} async-done(((bf16[128,3,2048]{2,1,0:T(4,128)(2,1)}), bf16[128,3,2048]{2,1,0:T(4,128)(2,1)}, u32[]{:S(2)}, u32[]{:S(2)}) %all-to-all-start.7) | async-done | bytes 1572896 | tf_op jit(solution)/shard_map/all_to_all | solution.py:174
  764.6 14.8 all-to-all-done.8
  782.8 433.4 %while.81 = (s32[]{:T(128)}, f32[8,512,1,128]{3,1,2,0:T(8,128)}, bf16[8,512,1,128]{3,1,0,2:T(8,128)(2,1)}, bf16[8,512,1,128]{3,1,0,2:T(8,128)(2,1)}, s32[8]{0:T(...) while((s32[]{:T(128)}, f32[8,512,1,128]{3,1,2,0:T(8,128)}, ...), condition=%wide.region_29.30_spmd.clone, body=%wide.region_25.29_spmd.sunk.clone | while | flops 338035744 | bytes 9592451 | solution.py:164
  787.0 85.5 %while.80 = (s32[]{:T(128)}, f32[8,512,1,128]{3,1,2,0:T(8,128)}, f32[512,1,128]{0,2,1:T(8,128)S(1)}, f32[512,1,128]{0,2,1:T(8,128)S(1)}, s32[]{:T(128)}, /*index...) while((s32[]{:T(128)}, f32[8,512,1,128]{3,1,2,0:T(8,128)}, ...), condition=%wide.region_28.28_spmd, body=%wide.region_26.27_spmd.sunk | while | flops 338035744 | bytes 7232760 | solution.py:158
  878.3 74.8 %while.80 = (s32[]{:T(128)}, f32[8,512,1,128]{3,1,2,0:T(8,128)}, f32[512,1,128]{0,2,1:T(8,128)S(1)}, f32[512,1,128]{0,2,1:T(8,128)S(1)}, s32[]{:T(128)}, /*index...) while((s32[]{:T(128)}, f32[8,512,1,128]{3,1,2,0:T(8,128)}, ...), condition=%wide.region_28.28_spmd, body=%wide.region_26.27_spmd.sunk | while | flops 338035744 | bytes 7232760 | solution.py:158
  959.0 64.3 %while.80 = (s32[]{:T(128)}, f32[8,512,1,128]{3,1,2,0:T(8,128)}, f32[512,1,128]{0,2,1:T(8,128)S(1)}, f32[512,1,128]{0,2,1:T(8,128)S(1)}, s32[]{:T(128)}, /*index...) while((s32[]{:T(128)}, f32[8,512,1,128]{3,1,2,0:T(8,128)}, ...), condition=%wide.region_28.28_spmd, body=%wide.region_26.27_spmd.sunk | while | flops 338035744 | bytes 7232760 | solution.py:158
  1029.0 53.6 %while.80 = (s32[]{:T(128)}, f32[8,512,1,128]{3,1,2,0:T(8,128)}, f32[512,1,128]{0,2,1:T(8,128)S(1)}, f32[512,1,128]{0,2,1:T(8,128)S(1)}, s32[]{:T(128)}, /*index...) while((s32[]{:T(128)}, f32[8,512,1,128]{3,1,2,0:T(8,128)}, ...), condition=%wide.region_28.28_spmd, body=%wide.region_26.27_spmd.sunk | while | flops 338035744 | bytes 7232760 | solution.py:158
  1088.5 43.1 %while.80 = (s32[]{:T(128)}, f32[8,512,1,128]{3,1,2,0:T(8,128)}, f32[512,1,128]{0,2,1:T(8,128)S(1)}, f32[512,1,128]{0,2,1:T(8,128)S(1)}, s32[]{:T(128)}, /*index...) while((s32[]{:T(128)}, f32[8,512,1,128]{3,1,2,0:T(8,128)}, ...), condition=%wide.region_28.28_spmd, body=%wide.region_26.27_spmd.sunk | while | flops 338035744 | bytes 7232760 | solution.py:158
  1137.3 32.5 %while.80 = (s32[]{:T(128)}, f32[8,512,1,128]{3,1,2,0:T(8,128)}, f32[512,1,128]{0,2,1:T(8,128)S(1)}, f32[512,1,128]{0,2,1:T(8,128)S(1)}, s32[]{:T(128)}, /*index...) while((s32[]{:T(128)}, f32[8,512,1,128]{3,1,2,0:T(8,128)}, ...), condition=%wide.region_28.28_spmd, body=%wide.region_26.27_spmd.sunk | while | flops 338035744 | bytes 7232760 | solution.py:158
  1175.6 21.8 %while.80 = (s32[]{:T(128)}, f32[8,512,1,128]{3,1,2,0:T(8,128)}, f32[512,1,128]{0,2,1:T(8,128)S(1)}, f32[512,1,128]{0,2,1:T(8,128)S(1)}, s32[]{:T(128)}, /*index...) while((s32[]{:T(128)}, f32[8,512,1,128]{3,1,2,0:T(8,128)}, ...), condition=%wide.region_28.28_spmd, body=%wide.region_26.27_spmd.sunk | while | flops 338035744 | bytes 7232760 | solution.py:158
  1216.2 24.0 %all_to_all.132 = bf16[32,128,128]{2,1,0:T(8,128)(2,1)} all-to-all(bf16[32,128,128]{2,1,0:T(8,128)(2,1)} %bitcast.72), channel_id=1, replica_groups=mesh['fsdp'=4,'sp'=32] {'sp'}, dimensions={0} | all-to-all | bytes 2097152 | tf_op jit(solution)/shard_map/all_to_all | solution.py:303
  1247.6 15.2 all-to-all-done.9
  1271.6 15.8 all-to-all-done.11
  1294.5 18.3 fusion.108
  1338.2 66.2 %all-reduce.9 = (f32[]{:T(128)}, f32[2048]{0:T(1024)}, f32[128]{0:T(128)}, f32[128]{0:T(128)}, f32[2048]{0:T(1024)}) all-reduce(f32[]{:T(128)} %get-tuple-element.693, f32[2048]{0:T(1024)S(1)} %get-tuple-element.568, f32[128]{0:T(128)S(1)} %get-tuple-element.564, ...), channel_id=1, replica_groups=mesh['fsdp'=4,'sp'=32] {'fsdp','sp'}, use_global_device_ids=true, to_apply=%region_18.19 | all-reduce | flops 4353 | bytes 34824 | tf_op jit(solution)/shard_map/psum | solution.py:262
  1408.1 41.2 %reduce-scatter.5.cloned.1.call-done = f32[32,2048]{1,0:T(8,128)} async-done(((f32[4096,2048]{1,0:T(8,128)}), f32[32,2048]{1,0:T(8,128)}) %reduce-scatter.5.cloned.1.call-update) | async-done | bytes 262160 | tf_op jit(solution)/shard_map/reduce_scatter | solution.py:335
  1449.3 706.5 %reduce-scatter.3.cloned.1.call-done = f32[2048,40]{0,1:T(8,128)} async-done(((f32[2048,5120]{0,1:T(8,128)}), f32[2048,40]{0,1:T(8,128)}) %reduce-scatter.3.cloned.1.call-update) | async-done | bytes 327696 | tf_op jit(solution)/shard_map/reduce_scatter | solution.py:334
  (990 shorter events, 939.4 us)
Async XLA Ops:
  7.2 485.0 %copy-start = (bf16[1,768,2048]{2,1,0:T(8,128)(2,1)S(1)}, bf16[1,768,2048]{2,1,0:T(8,128)(2,1)}, u32[]{:S(2)}) copy-start(bf16[1,768,2048]{2,1,0:T(8,128)(2,1)} %param.33) | copy-start | bytes 9437188
  7.2 93.5 %all-gather.3.cloned.1.call-start = ((), (), s32[]{:S(2)}) async-start(), calls=%async_computation.14 | async-start | bytes 21135360 | tf_op jit(solution)/shard_map/all_gather | solution.py:201
  8.4 145.6 %copy-start.29 = (f32[128,128]{1,0:T(8,128)}, f32[128,128]{1,0:T(8,128)S(1)}, u32[]{:S(2)}) copy-start(f32[128,128]{1,0:T(8,128)S(1)} %get-tuple-element.698) | copy-start | bytes 196612
  8.4 145.6 %copy-start.35 = (f32[128,128]{1,0:T(8,128)}, f32[128,128]{1,0:T(8,128)S(1)}, u32[]{:S(2)}) copy-start(f32[128,128]{1,0:T(8,128)S(1)} %get-tuple-element.699) | copy-start | bytes 196612
  10.3 101.6 %copy-start.59 = (f32[128]{0:T(128)}, f32[128]{0:T(128)S(1)}, u32[]{:S(2)}) copy-start(f32[128]{0:T(128)S(1)} %fusion.91) | copy-start | bytes 1540
  10.4 101.6 %copy-start.51 = (f32[128]{0:T(128)}, f32[128]{0:T(128)S(1)}, u32[]{:S(2)}) copy-start(f32[128]{0:T(128)S(1)} %fusion.123) | copy-start | bytes 1540
  122.6 31.3 %copy-start.17 = (f32[16,4,8,128]{3,2,1,0:T(8,128)}, f32[16,4,8,128]{3,2,1,0:T(8,128)S(1)}, u32[]{:S(2)}) copy-start(f32[16,4,8,128]{3,2,1,0:T(8,128)S(1)} %get-tuple-element.685) | copy-start | bytes 786436
  142.9 23.0 %all-to-all-start = ((bf16[128,32,128]{2,0,1:T(8,128)(2,1)}), bf16[128,32,128]{2,0,1:T(8,128)(2,1)}, u32[]{:S(2)}, u32[]{:S(2)}) async-start(bf16[128,32,128]{2,0,1:T(8,128)(2,1)} %copy_bitcast_fusion.1), calls=%async_computation | async-start | bytes 2097152 | tf_op jit(solution)/shard_map/all_to_all | solution.py:221
  168.1 21.5 all-to-all-start.1
  190.7 21.4 all-to-all-start.2
  195.4 224.5 %all-gather.5.cloned.1.call-start = ((), (), s32[]{:S(2)}) async-start(), calls=%async_computation.15 | async-start | bytes 16908288 | tf_op jit(solution)/shard_map/all_gather | solution.py:202
  396.1 21.6 all-to-all-start.3
  499.9 86.7 %copy-start.58 = (f32[128,2]{0,1:T(2,128)S(1)}, f32[128,2]{0,1:T(2,128)}, u32[]{:S(2)}) copy-start(f32[128,2]{0,1:T(2,128)} %param.35) | copy-start | bytes 3076
  499.9 87.6 %all-to-all-start.5 = ((bf16[128,3,2048]{2,1,0:T(4,128)(2,1)}), bf16[128,3,2048]{2,1,0:T(4,128)(2,1)}, u32[]{:S(2)}, u32[]{:S(2)}) async-start(bf16[128,3,2048]{2,1,0:T(4,128)(2,1)} %reshape.633), calls=%async_computation.5 | async-start | bytes 4194304 | tf_op jit(solution)/shard_map/all_to_all | solution.py:174
  678.3 35.8 %all-to-all-start.7 = ((bf16[128,3,2048]{2,1,0:T(4,128)(2,1)}), bf16[128,3,2048]{2,1,0:T(4,128)(2,1)}, u32[]{:S(2)}, u32[]{:S(2)}) async-start(bf16[128,3,2048]{2,1,0:T(4,128)(2,1)} %reshape.637), calls=%async_computation.7 | async-start | bytes 4194304 | tf_op jit(solution)/shard_map/all_to_all | solution.py:174
  684.0 765.2 %reduce-scatter.5.cloned.1.call-start = ((), (), s32[]{:S(2)}) async-start(), calls=%async_computation.17 | async-start | bytes 33816576 | tf_op jit(solution)/shard_map/reduce_scatter | solution.py:335
  756.3 23.1 %all-to-all-start.8 = ((bf16[128,32,128]{2,0,1:T(8,128)(2,1)}), bf16[128,32,128]{2,0,1:T(8,128)(2,1)}, u32[]{:S(2)}, u32[]{:S(2)}) async-start(bf16[128,32,128]{2,0,1:T(8,128)(2,1)} %bitcast.255), calls=%async_computation.8 | async-start | bytes 2097152 | tf_op jit(solution)/shard_map/all_to_all | solution.py:289
  1216.1 29.7 %copy-start.30 = (f32[128,128]{1,0:T(8,128)S(1)}, f32[128,128]{1,0:T(8,128)}, u32[]{:S(2)}) copy-start(f32[128,128]{1,0:T(8,128)} %copy-done.29) | copy-start | bytes 196612
  1216.2 29.8 %copy-start.2 = (f32[8,512,1,128]{3,1,2,0:T(8,128)S(1)}, f32[8,512,1,128]{3,1,2,0:T(8,128)}, u32[]{:S(2)}) copy-start(f32[8,512,1,128]{3,1,2,0:T(8,128)} %get-tuple-element.1410) | copy-start | bytes 6291460
  1240.1 22.7 %all-to-all-start.9 = ((bf16[32,128,128]{2,1,0:T(8,128)(2,1)}), bf16[32,128,128]{2,1,0:T(8,128)(2,1)S(1)}, u32[]{:S(2)}, u32[]{:S(2)}) async-start(bf16[32,128,128]{2,1,0:T(8,128)(2,1)} %bitcast.352), calls=%async_computation.9 | async-start | bytes 2097152 | tf_op jit(solution)/shard_map/all_to_all | solution.py:310
  1262.8 24.6 %all-to-all-start.11 = ((bf16[32,128,128]{2,1,0:T(8,128)(2,1)}), bf16[32,128,128]{2,1,0:T(8,128)(2,1)S(1)}, u32[]{:S(2)}, u32[]{:S(2)}) async-start(bf16[32,128,128]{2,1,0:T(8,128)(2,1)} %bitcast.76), calls=%async_computation.11 | async-start | bytes 2097152 | tf_op jit(solution)/shard_map/all_to_all | solution.py:296
  1269.7 886.0 %reduce-scatter.3.cloned.1.call-start = ((), (), s32[]{:S(2)}) async-start(), calls=%async_computation.16 | async-start | bytes 42270720 | tf_op jit(solution)/shard_map/reduce_scatter | solution.py:334
  1327.0 78.1 %copy-start.60 = (f32[128]{0:T(128)S(1)}, f32[128]{0:T(128)}, u32[]{:S(2)}) copy-start(f32[128]{0:T(128)} %copy-done.59) | copy-start | bytes 1540
  1327.0 828.8 %copy-start.1 = (bf16[1,768,2048]{2,1,0:T(8,128)(2,1)S(1)}, bf16[1,768,2048]{2,1,0:T(8,128)(2,1)}, u32[]{:S(2)}) copy-start(bf16[1,768,2048]{2,1,0:T(8,128)(2,1)} %param.33) | copy-start | bytes 9437188
  (51 other events, 306.6 us)
Sparse Core Ops, SparseCore 0:
  11.0 89.6 all-gather.2
  199.4 81.1 all-gather.4
  743.6 705.6 reduce-scatter.4
  1452.1 703.5 reduce-scatter.2
where the time goes:
time: 2180 us; the launch traced here: 2160 us
  waiting for transfers between devices  970 us (44%)
  matrix products  470 us (22%)
  blocking collectives  244 us (11%)
  local copies, waits for them, and re-layouts  196 us (9%)
  loops' own time  122 us (6%)
  other arithmetic  92.6 us (4%)
  starting transfers between devices  50.1 us (2%)
    reduce_scatter x1, waiting for transfers between devices, body(): lax.psum_scatter(in_gradient, ('fsdp', 'sp'), scatter_dimension=1, tiled=...  706 us
    psum x2, blocking collectives, body(): lax.psum((jnp.sum(mask[:, None] * error * error), jnp.sum(mask)), ('fsdp'...  146 us
    dot_general x36, matrix products, per_query(): jnp.einsum('hqk,khd->qhd', back_scores, key_block, preferred_element_type...  90.9 us
    dot_general x72, matrix products, block_scores(): jnp.einsum('qhd,khd->hqk', query_block, key_block, preferred_element_type...  90.6 us
    all_gather x1, waiting for transfers between devices, body(): lax.all_gather(in_projection, ('fsdp', 'sp'), axis=1, tiled=True)  89 us
    all_to_all x2, blocking collectives, move_rows(): lax.all_to_all(blocks, ('fsdp', 'sp'), split_axis=0, concat_axis=0, tiled...  73.9 us
    another operation x8, loops' own time, per_key(): lax.fori_loop(column, count, per_query, (back_queries, zeros, zeros))  71.9 us
    dot_general x36, matrix products, add_values(): jnp.einsum('hqk,khd->qhd', weights, value_blocks[column], preferred_eleme...  56.4 us
  transfers between devices with their start and end apart: 13, of which 11 were waited for; matrix products, arithmetic and copies ran while one was open for 27% of the time, Pallas kernels for 0%

commit v1 on v0

v1 whole, which is shorter than its diff:
```python
import functools
import jax
import jax.numpy as jnp
import numpy as np
from jax import lax
from jax.experimental import pallas as pl
from jax.experimental.pallas import tpu as pltpu
from jax.sharding import Mesh
from jax.sharding import PartitionSpec as P

D = 2048
H = 32
KV = 4
HD = 128
FF = 768
TOP = 2
CAP = 3
SEQ = 4096
EXPERTS = 128
LOCAL = 128
DEVICES = 128
TOKENS = LOCAL * DEVICES
GROUP = 1024
PIECE = 256
HEADS = 4

epsilon = 1e-06
theta = 1000000.0
ALL = ("y", "x", "z", "c")
SIZE = {"y": 4, "x": 4, "z": 4, "c": 2}
SCALE = HD ** (-0.5)
LOG2E = 1.4426950408889634
f32 = jnp.float32
bf16 = jnp.bfloat16


def device_of(y, x, z, c):
    return ((y * 4 + x) * 4 + z) * 2 + c


def colour_edges(edges, count, degree):
    left = {}
    for source, target, tag in edges:
        left.setdefault(source, []).append((target, tag))
    rounds = []
    for _ in range(degree):
        match = {}

        def place(source, seen):
            for number, (target, _) in enumerate(left[source]):
                if target in seen:
                    continue
                seen.add(target)
                if target not in match or place(match[target][0], seen):
                    match[target] = (source, number)
                    return True
            return False

        for source in range(count):
            place(source, set())
        done = []
        for target, (source, number) in sorted(match.items()):
            done.append((source, target, left[source][number][1]))
        for target, (source, number) in match.items():
            left[source][number] = None
        for source in left:
            left[source] = [entry for entry in left[source] if entry is not None]
        rounds.append(done)
    return rounds


@functools.cache
def in_plan():
    edges = []
    for x in range(4):
        for c in range(2):
            group = 2 * x + c
            wanted = [64 * group + s for s in range(64)]
            wanted += [512 + 64 * c + 16 * x + s for s in range(16)]
            for s, part in enumerate(wanted):
                if s < 48:
                    slot, place = s // 3, s % 3
                else:
                    slot, place = (s - 48) // 2, 3 + (s - 48) % 2
                target = device_of(slot // 4, x, slot % 4, c)
                edges.append((part // 5, target, (part % 5, place)))
    rounds = colour_edges(edges, DEVICES, 5)
    leaves = np.zeros((DEVICES, 5), np.int32)
    arrives = np.zeros((DEVICES, 5), np.int32)
    perms = []
    for number, done in enumerate(rounds):
        perms.append([(source, target) for source, target, _ in done])
        for source, target, (part, place) in done:
            leaves[source, number] = part
            arrives[target, place] = number
    return perms, leaves, arrives


def out_perm():
    perm = []
    for y in range(4):
        for x in range(4):
            for z in range(4):
                for c in range(2):
                    rows = (device_of(y, x, z, c) * 32) % 512
                    slot = rows // 32
                    perm.append((device_of(y, x, z, c), device_of(slot // 4, y, slot % 4, x // 2)))
    return perm


def shift(value, axis, step):
    size = SIZE[axis]
    return lax.ppermute(value, axis, [(i, (i + step) % size) for i in range(size)])


def ring_gather(value, axis):
    index = lax.axis_index(axis)
    half = value.shape[0] // 2
    before = shift(value, axis, 1)
    after = shift(value, axis, -1)
    far = jnp.concatenate([shift(before[:half], axis, 1), shift(after[half:], axis, -1)], axis=0)
    out = jnp.zeros((4,) + value.shape, value.dtype)
    for offset, block in ((0, value), (3, before), (1, after), (2, far)):
        out = lax.dynamic_update_index_in_dim(out, block, (index + offset) % 4, 0)
    return out


def core_gather(value):
    index = lax.axis_index("c")
    other = shift(value, "c", 1)
    out = jnp.zeros((2,) + value.shape, value.dtype)
    out = lax.dynamic_update_index_in_dim(out, value, index, 0)
    return lax.dynamic_update_index_in_dim(out, other, 1 - index, 0)


def small_sum(value):
    value = value + shift(value, "c", 1)
    for axis in ("x", "y", "z"):
        value = value + shift(value, axis, 1) + shift(value, axis, -1) + shift(value, axis, 2)
    return value


def scatter_sum(value, axes, count):
    moved = lax.all_to_all(value, axes, split_axis=0, concat_axis=0, tiled=True)
    return jnp.sum(moved.astype(f32), axis=0)


def rotation(position):
    frequency = theta ** (-jnp.arange(0, HD, 2).astype(f32) / HD)
    phase = position[:, None] * frequency[None, :]
    phase = jnp.concatenate([phase, phase], axis=-1)
    return jnp.cos(phase), jnp.sin(phase)


def head_rotate(value, gain, cosine, sine):
    unit = value * lax.rsqrt(jnp.mean(value * value, axis=-1, keepdims=True) + epsilon)
    scaled = unit * gain
    turned = jnp.concatenate([-scaled[:, HD // 2 :], scaled[:, : HD // 2]], axis=-1)
    return scaled * cosine + turned * sine


def head_rotate_back(grad, value, gain, cosine, sine):
    inverse = lax.rsqrt(jnp.mean(value * value, axis=-1, keepdims=True) + epsilon)
    unit = value * inverse
    with_sine = grad * sine
    turned = jnp.concatenate([with_sine[:, HD // 2 :], -with_sine[:, : HD // 2]], axis=-1)
    scaled = grad * cosine + turned
    gain_grad = jnp.sum(scaled * unit, axis=0)
    unit_grad = scaled * gain
    back = inverse * (unit_grad - unit * jnp.mean(unit_grad * unit, axis=-1, keepdims=True))
    return back, gain_grad


NT = (((1,), (1,)), ((), ()))
NN = (((1,), (0,)), ((), ()))


def forward_kernel(z_ref, q_ref, k_ref, v_ref, o_ref, lse_ref, total):
    piece = pl.program_id(0)
    z = z_ref[0]
    total[...] = jnp.zeros_like(total)
    ones = jnp.ones((PIECE, HD), bf16)

    def step(chunk, masked):
        row = pl.multiple_of((chunk // 4) * PIECE, PIECE)
        keys = k_ref[chunk % 4, pl.ds(row, PIECE), :]
        values = v_ref[chunk % 4, pl.ds(row, PIECE), :]
        wide = jnp.concatenate([values, ones], axis=1)
        for head in range(HEADS):
            scores = lax.dot_general(q_ref[head, 0], keys, NT, preferred_element_type=f32)
            weights = jnp.exp2(scores * (SCALE * LOG2E))
            if masked:
                queries_at = lax.broadcasted_iota(jnp.int32, (PIECE, PIECE), 0)
                keys_at = lax.broadcasted_iota(jnp.int32, (PIECE, PIECE), 1)
                weights = jnp.where(keys_at <= queries_at, weights, 0.0)
            total[head] += lax.dot_general(weights.astype(bf16), wide, NN, preferred_element_type=f32)

    last = piece * 4 + z

    def body(chunk, carry):
        step(chunk, False)
        return carry

    lax.fori_loop(0, last, body, 0)
    step(last, True)
    for head in range(HEADS):
        sums = total[head, :, HD:]
        o_ref[head, 0] = total[head, :, :HD] / sums
        lse_ref[head, 0] = jnp.transpose(jnp.log2(sums))[:8, :]


def attend_forward(z, queries, keys, values):
    return pl.pallas_call(
        forward_kernel,
        grid_spec=pltpu.PrefetchScalarGridSpec(
            num_scalar_prefetch=1,
            grid=(4,),
            in_specs=[
                pl.BlockSpec((HEADS, 1, PIECE, HD), lambda i, z: (0, i, 0, 0)),
                pl.BlockSpec((4, GROUP, HD), lambda i, z: (0, 0, 0)),
                pl.BlockSpec((4, GROUP, HD), lambda i, z: (0, 0, 0)),
            ],
            out_specs=[
                pl.BlockSpec((HEADS, 1, PIECE, HD), lambda i, z: (0, i, 0, 0)),
                pl.BlockSpec((HEADS, 1, 8, PIECE), lambda i, z: (0, i, 0, 0)),
            ],
            scratch_shapes=[pltpu.VMEM((HEADS, PIECE, 2 * HD), f32)],
        ),
        out_shape=[
            jax.ShapeDtypeStruct((HEADS, 4, PIECE, HD), f32),
            jax.ShapeDtypeStruct((HEADS, 4, 8, PIECE), f32),
        ],
        compiler_params=pltpu.CompilerParams(vmem_limit_bytes=40 * 2**20),
        cost_estimate=pl.CostEstimate(flops=9 * 10**9, bytes_accessed=8 * 2**20, transcendentals=10**7),
        name="attend_forward",
    )(z, queries, keys, values)


def backward_kernel(z_ref, q_ref, k_ref, kt_ref, v_ref, go_ref, o_ref, lse_ref, dq_ref, dk_ref, dv_ref, dqt, dk, dv):
    piece = pl.program_id(0)
    z = z_ref[0]

    @pl.when(piece == 0)
    def _():
        dk[...] = jnp.zeros_like(dk)
        dv[...] = jnp.zeros_like(dv)

    dqt[...] = jnp.zeros_like(dqt)
    rows = HEADS * PIECE
    queries = q_ref[:, 0].reshape(rows, HD)
    backs = go_ref[:, 0].reshape(rows, HD)
    product = backs.astype(f32) * o_ref[:, 0].reshape(rows, HD)
    delta = lax.dot_general(jnp.ones((8, HD), f32), product, NT, precision=lax.Precision.HIGHEST, preferred_element_type=f32)[:1]
    sums = jnp.concatenate([lse_ref[head, 0, :1, :] for head in range(HEADS)], axis=1)

    def step(chunk, masked):
        row = pl.multiple_of((chunk // 4) * PIECE, PIECE)
        block = chunk % 4
        keys = k_ref[block, pl.ds(row, PIECE), :]
        values = v_ref[block, pl.ds(row, PIECE), :]
        turned = kt_ref[block, chunk // 4]
        scores = lax.dot_general(keys, queries, NT, preferred_element_type=f32)
        weights = jnp.exp2(scores * (SCALE * LOG2E) - sums)
        if masked:
            keys_at = lax.broadcasted_iota(jnp.int32, (PIECE, rows), 0)
            queries_at = lax.broadcasted_iota(jnp.int32, (PIECE, rows), 1) % PIECE
            weights = jnp.where(keys_at <= queries_at, weights, 0.0)
        back_weights = lax.dot_general(values, backs, NT, preferred_element_type=f32)
        back_scores = (weights * (back_weights - delta)).astype(bf16)
        dv[block, pl.ds(row, PIECE), :] += lax.dot_general(weights.astype(bf16), backs, NN, preferred_element_type=f32)
        dk[block, pl.ds(row, PIECE), :] += lax.dot_general(back_scores, queries, NN, preferred_element_type=f32)
        dqt[...] += lax.dot_general(turned, back_scores, NN, preferred_element_type=f32)

    last = piece * 4 + z

    def body(chunk, carry):
        step(chunk, False)
        return carry

    lax.fori_loop(0, last, body, 0)
    step(last, True)
    dq_ref[:, 0] = (jnp.transpose(dqt[...]) * SCALE).astype(bf16).reshape(HEADS, PIECE, HD)

    @pl.when(piece == 3)
    def _():
        dk_ref[...] = (dk[...] * SCALE).astype(bf16)
        dv_ref[...] = dv[...].astype(bf16)


def attend_backward(z, queries, keys, values, backs, outs, lse):
    turned = keys.reshape(4, 4, PIECE, HD).transpose(0, 1, 3, 2)
    heads_spec = pl.BlockSpec((HEADS, 1, PIECE, HD), lambda i, z: (0, i, 0, 0))
    whole = pl.BlockSpec((4, GROUP, HD), lambda i, z: (0, 0, 0))
    return pl.pallas_call(
        backward_kernel,
        grid_spec=pltpu.PrefetchScalarGridSpec(
            num_scalar_prefetch=1,
            grid=(4,),
            in_specs=[
                heads_spec,
                whole,
                pl.BlockSpec((4, 4, HD, PIECE), lambda i, z: (0, 0, 0, 0)),
                whole,
                heads_spec,
                heads_spec,
                pl.BlockSpec((HEADS, 1, 8, PIECE), lambda i, z: (0, i, 0, 0)),
            ],
            out_specs=[heads_spec, whole, whole],
            scratch_shapes=[
                pltpu.VMEM((HD, HEADS * PIECE), f32),
                pltpu.VMEM((4, GROUP, HD), f32),
                pltpu.VMEM((4, GROUP, HD), f32),
            ],
        ),
        out_shape=[
            jax.ShapeDtypeStruct((HEADS, 4, PIECE, HD), bf16),
            jax.ShapeDtypeStruct((4, GROUP, HD), bf16),
            jax.ShapeDtypeStruct((4, GROUP, HD), bf16),
        ],
        compiler_params=pltpu.CompilerParams(vmem_limit_bytes=48 * 2**20),
        cost_estimate=pl.CostEstimate(flops=22 * 10**9, bytes_accessed=8 * 2**20, transcendentals=10**7),
        name="attend_backward",
    )(z, queries, keys, turned, values, backs, outs, lse)


def dot(a, b, dims=NN):
    return lax.dot_general(a, b, dims, preferred_element_type=f32)


def move_rows(rows):
    sent = rows.reshape(EXPERTS, CAP * D // 128, 128)
    moved = lax.all_to_all(sent, ALL, split_axis=0, concat_axis=0, tiled=True)
    return moved.reshape(EXPERTS * CAP, D)


def group_gather(value):
    pair = core_gather(value)
    del pair
    mine = ring_gather(value, "x")
    both = core_gather(mine)
    return both.transpose(1, 0, 2, 3).reshape(GROUP, value.shape[-1])


def group_scatter(value):
    core = lax.axis_index("c")
    blocks = value.astype(bf16).reshape(4, 2, LOCAL, -1)
    own = lax.dynamic_index_in_dim(blocks, core, 1, keepdims=False)
    other = lax.dynamic_index_in_dim(blocks, 1 - core, 1, keepdims=False)
    chip = (own.astype(f32) + shift(other, "c", 1).astype(f32)).astype(bf16)
    return scatter_sum(chip, "x", 4)


def body(tokens, gain1, w_in, q_gain, k_gain, w_out, gain2, gate_up, down, routes, gates, target, valid):
    y, x, z, c = (lax.axis_index(name) for name in ALL)
    me = device_of(y, x, z, c)
    z_array = jnp.reshape(z, (1,)).astype(jnp.int32)

    mask = valid.astype(f32)
    valid_count = small_sum(jnp.broadcast_to(jnp.sum(mask), (8, 128)))[0, 0]

    inputs = tokens.astype(f32)
    r1 = lax.rsqrt(jnp.mean(inputs * inputs, axis=-1, keepdims=True) + epsilon)
    n1 = inputs * r1
    h1 = (n1 * gain1).astype(bf16)
    h1_group = group_gather(h1)

    perms, leaves, arrives = in_plan()
    parts = w_in.T.reshape(5, 8, D)
    leaving = jnp.asarray(leaves)[me]
    arriving = jnp.asarray(arrives)[me]
    arrived = [
        lax.ppermute(lax.dynamic_index_in_dim(parts, leaving[i], 0, keepdims=False), ALL, perms[i]) for i in range(5)
    ]
    arrived = jnp.stack(arrived)
    placed = [lax.dynamic_index_in_dim(arrived, arriving[i], 0, keepdims=False) for i in range(5)]
    in_a = jnp.concatenate(placed[:3], axis=0)
    in_b = jnp.concatenate(placed[3:], axis=0)
    in_a = ring_gather(ring_gather(in_a, "y"), "z").transpose(1, 0, 2, 3).reshape(384, D)
    in_b = ring_gather(ring_gather(in_b, "z"), "y").reshape(256, D)

    projected = [dot(h1_group, in_a, NT), dot(h1_group, in_b, NT)]

    out_rows = lax.ppermute(w_out, ALL, out_perm())
    out_rows, _ = lax.optimization_barrier((out_rows, in_a))
    out_a = ring_gather(ring_gather(out_rows[:16], "y"), "z").transpose(1, 0, 2, 3)
    out_b = ring_gather(ring_gather(out_rows[16:], "z"), "y")
    out_full = jnp.concatenate([out_a, out_b], axis=2).reshape(512, D)

    places = (jnp.arange(4, dtype=jnp.int32)[:, None] * 1024 + z * PIECE + jnp.arange(PIECE, dtype=jnp.int32)[None, :])
    cosine, sine = rotation(places.reshape(GROUP).astype(f32))
    head_in = [projected[0][:, i * HD : (i + 1) * HD] for i in range(3)]
    head_in += [projected[1][:, i * HD : (i + 1) * HD] for i in range(2)]
    queries = jnp.stack([head_rotate(v, q_gain, cosine, sine).astype(bf16) for v in head_in[:4]])
    queries = queries.reshape(HEADS, 4, PIECE, HD)
    key_or_value = jnp.where(c == 0, head_rotate(head_in[4], k_gain, cosine, sine), head_in[4]).astype(bf16)
    both = core_gather(ring_gather(key_or_value, "z"))
    keys, values = both[0], both[1]

    outs, lse = attend_forward(z_array, queries, keys, values)
    attended = outs.astype(bf16).reshape(HEADS, GROUP, HD)
    attended = attended.transpose(1, 0, 2).reshape(GROUP, HEADS * HD)
    mixed_out = group_scatter(dot(attended, out_full))

    x2 = inputs + mixed_out
    r2 = lax.rsqrt(jnp.mean(x2 * x2, axis=-1, keepdims=True) + epsilon)
    n2 = x2 * r2
    h2 = (n2 * gain2).astype(bf16)

    route_numbers = routes.reshape(-1)
    pairs = LOCAL * TOP
    same = route_numbers[:, None] == route_numbers[None, :]
    before = jnp.arange(pairs)[None, :] < jnp.arange(pairs)[:, None]
    slots = route_numbers * CAP + jnp.sum((same & before).astype(jnp.int32), axis=1)
    at = slots.reshape(LOCAL, TOP)
    numbers = jnp.arange(EXPERTS * CAP, dtype=jnp.int32)[:, None]
    pick0 = (numbers == at[None, :, 0]).astype(bf16)
    pick1 = (numbers == at[None, :, 1]).astype(bf16)

    rows = move_rows(dot(pick0 + pick1, h2).astype(bf16))
    first = gate_up[0]
    second = down[0]
    mixed = dot(rows, first)
    gate, up = mixed[:, :FF], mixed[:, FF:]
    sigmoid = jax.nn.sigmoid(gate)
    hidden = (gate * sigmoid * up).astype(bf16)
    expert_out = dot(hidden, second).astype(bf16)
    returned = move_rows(expert_out)
    TN = (((0,), (0,)), ((), ()))
    y0 = dot(pick0, returned, TN)
    y1 = dot(pick1, returned, TN)
    gate0, gate1 = gates[:, :1], gates[:, 1:]
    output = (x2 + (gate0 * y0 + gate1 * y1)).astype(bf16)
    error = output.astype(f32) - target.astype(f32)
    loss_term = jnp.sum(mask[:, None] * error * error)
    g3 = TOKENS / valid_count * mask[:, None] * error

    sent_back = dot(pick0, (gate0 * g3).astype(bf16)) + dot(pick1, (gate1 * g3).astype(bf16))
    back_out = move_rows(sent_back.astype(bf16))
    back_hidden = dot(back_out, second, NT)
    silu = gate * sigmoid
    back_gate = back_hidden * up * (sigmoid * (1.0 + gate * (1.0 - sigmoid)))
    back_up = back_hidden * silu
    back_mixed = jnp.concatenate([back_gate, back_up], axis=1).astype(bf16)
    back_rows = move_rows(dot(back_mixed, first, NT).astype(bf16))
    second_gradient = dot(hidden, back_out, TN)
    first_gradient = dot(rows, back_mixed, TN)

    gh2 = dot(pick0, back_rows, TN) + dot(pick1, back_rows, TN)
    gain2_term = jnp.sum(gh2 * n2, axis=0)
    gn = gh2 * gain2
    g2 = g3 + r2 * (gn - n2 * jnp.mean(gn * n2, axis=-1, keepdims=True))

    gb_group = group_gather(g2.astype(bf16))
    back_attended = dot(gb_group, out_full, NT).astype(bf16)
    out_partial = dot(attended, gb_group, TN).astype(bf16)
    backs = back_attended.reshape(4, PIECE, HEADS, HD).transpose(2, 0, 1, 3)
    dq, dk, dv = attend_backward(z_array, queries, keys, values, backs, outs, lse)

    out_summed = scatter_sum(out_partial.reshape(16, 32, D), ("y", "z"), 16)
    out_gradient = lax.ppermute(out_summed.astype(bf16), ALL, [(b, a) for a, b in out_perm()]).astype(f32)

    mine = jnp.where(c == 0, dk, dv)
    theirs = jnp.where(c == 0, dv, dk)
    chip_kv = (mine.astype(f32) + shift(theirs, "c", 1).astype(f32)).astype(bf16)
    back_kv = scatter_sum(chip_kv, "z", 4)

    backs_in = []
    q_gain_term = jnp.zeros((HD,), f32)
    for head in range(HEADS):
        back, term = head_rotate_back(dq[head].reshape(GROUP, HD).astype(f32), head_in[head], q_gain, cosine, sine)
        backs_in.append(back.astype(bf16))
        q_gain_term = q_gain_term + term
    back, k_gain_term = head_rotate_back(back_kv, head_in[4], k_gain, cosine, sine)
    backs_in.append(jnp.where(c == 0, back, back_kv).astype(bf16))
    k_gain_term = jnp.where(c == 0, k_gain_term, 0.0)
    gp_a = jnp.concatenate(backs_in[:3], axis=1)
    gp_b = jnp.concatenate(backs_in[3:], axis=1)

    gh1_partial = dot(gp_a, in_a) + dot(gp_b, in_b)
    gain1_term = jnp.sum(gh1_partial * h1_group.astype(f32), axis=0) / gain1
    terms = jnp.concatenate([gain1_term, gain2_term, q_gain_term, k_gain_term, jnp.broadcast_to(loss_term, (128,))])
    sums = small_sum(terms.reshape(-1, 128)).reshape(-1)

    gh1 = group_scatter(gh1_partial)
    gn1 = gh1 * gain1
    tokens_gradient = g2 + r1 * (gn1 - n1 * jnp.mean(gn1 * n1, axis=-1, keepdims=True))

    in_a_partial = dot(gp_a, h1_group, TN).astype(bf16).reshape(16, 24, D)
    in_b_partial = dot(gp_b, h1_group, TN).astype(bf16).reshape(16, 16, D)
    in_summed = scatter_sum(jnp.concatenate([in_a_partial, in_b_partial], axis=1), ("y", "z"), 16)
    in_parts = in_summed.astype(bf16).reshape(5, 8, D)
    carried = jnp.asarray(np.argsort(arrives, axis=1).astype(np.int32))[me]
    going = jnp.asarray(np.argsort(leaves, axis=1).astype(np.int32))[me]
    home = jnp.stack(
        [
            lax.ppermute(
                lax.dynamic_index_in_dim(in_parts, carried[i], 0, keepdims=False), ALL, [(b, a) for a, b in perms[i]]
            )
            for i in range(5)
        ]
    )
    home = [lax.dynamic_index_in_dim(home, going[i], 0, keepdims=False) for i in range(5)]
    in_gradient = jnp.concatenate(home, axis=0).astype(f32).T

    loss = sums[2 * D + 2 * HD] / (2.0 * valid_count * D)
    return (
        output,
        loss,
        tokens_gradient,
        sums[:D],
        in_gradient,
        sums[2 * D : 2 * D + HD],
        sums[2 * D + HD : 2 * D + 2 * HD],
        out_gradient,
        sums[D : 2 * D],
        first_gradient[None],
        second_gradient[None],
    )


def solution(mesh):
    fine = Mesh(mesh.devices.reshape(4, 4, 4, 2), ALL)
    rows = P(ALL, None)
    blocks = P(ALL, None, None)
    columns = P(None, ALL)
    return jax.shard_map(
        body,
        mesh=fine,
        in_specs=(rows, P(), columns, P(), P(), rows, P(), blocks, blocks, rows, rows, rows, P(ALL)),
        out_specs=(rows, P(), rows, P(), columns, P(), P(), rows, P(), blocks, blocks),
        check_vma=False,
    )
```

time: 2180 us -> 719 us (0.33)
  the two profiles are of different devices: /device:TPU:0 before, /device:TPU:49 now
where the time goes in v1:
time: 719 us; the launch traced here: 705 us
  starting transfers between devices  190 us (26%)
  waiting for transfers between devices  134 us (19%)
  blocking collectives  97.6 us (14%)
  local copies, waits for them, and re-layouts  70.2 us (10%)
  matrix products  64 us (9%)
  other arithmetic  53.7 us (7%)
  Pallas kernels  49.7 us (7%)
  between operations  45.4 us (6%)
    all_to_all x3, blocking collectives, move_rows(): moved = lax.all_to_all(sent, ALL, split_axis=0, concat_axis=0, tiled=True)  97.6 us
    ppermute x70, starting transfers between devices, shift(): lax.ppermute(value, axis, [(i, (i + step) % size) for i in range(size)])  88.4 us
    ppermute x70, waiting for transfers between devices, shift(): lax.ppermute(value, axis, [(i, (i + step) % size) for i in range(size)])  82.5 us
    dot_general x22, matrix products, dot(): return lax.dot_general(a, b, dims, preferred_element_type=f32)  64 us
    all_to_all x5, waiting for transfers between devices, scatter_sum(): moved = lax.all_to_all(value, axes, split_axis=0, concat_axis=0, tiled=True)  32.3 us
    pallas_call x1, Pallas kernels, attend_backward(): pl.pallas_call(backward_kernel, grid_spec=pltpu.PrefetchScalarGridSpec(nu...  31.4 us
    all_to_all x5, starting transfers between devices, scatter_sum(): moved = lax.all_to_all(value, axes, split_axis=0, concat_axis=0, tiled=True)  31.2 us
    ppermute x5, starting transfers between devices, body(): lax.ppermute(lax.dynamic_index_in_dim(parts, leaving[i], 0, keepdims=Fals...  22.5 us
  transfers between devices with their start and end apart: 88, of which 36 were waited for; matrix products, arithmetic and copies ran while one was open for 11% of the time, Pallas kernels for 0%

profile of v1, /device:TPU:49, one launch (start us, length us, event | category | flops | bytes accessed | tf_op | source)
XLA Modules:
  0.0 705.3 jit_solution(13231054509839531706)
XLA Ops:
  27.4 6.9 collective-permute-start.8
  64.4 9.6 %collective-permute-start.31 = (bf16[32,2048]{1,0:T(8,128)(2,1)S(1)}, bf16[32,2048]{1,0:T(8,128)(2,1)S(1)}, u32[]{:S(2)}, u32[]{:S(2)}) collective-permute-start(bf16[32,2048]{1,0:T(8,128)(2,1)S(1)} %copy-done.62), channel_id=1, source_target_pairs={{0,0},{1,2},{2,4},{3,6},{4,32},{5,34},{6,36},{7,38},{8,64},{9,66},... | collective-permute-start | bytes 393224 | tf_op jit(solution)/shard_map/ppermute | solution.py:383
  96.1 7.4 %collective-permute-done.15 = bf16[4,24,2048]{2,1,0:T(8,128)(2,1)S(1)} collective-permute-done((bf16[4,24,2048]{2,1,0:T(8,128)(2,1)S(1)}, bf16[4,24,2048]{2,1,0:T(8,128)(2,1)S(1)}, u32[]{:S(2)}, u32[]{:S(2)}) %collective-permute-start.15) | collective-permute-done | bytes 393248 | tf_op jit(solution)/shard_map/ppermute | solution.py:113
  168.5 9.8 %collective-permute-start.30 = (bf16[4,1024,128]{2,1,0:T(8,128)(2,1)S(1)}, bf16[4,1024,128]{2,1,0:T(8,128)(2,1)S(1)}, u32[]{:S(2)}, u32[]{:S(2)}) collective-permute-start(bf16[4,1024,128]{2,1,0:T(8,128)(2,1)S(1)} %fusion.65), channel_id=1, source_target_pairs={{0,1},{1,0},{2,3},{3,2},{4,5},{5,4},{6,7},{7,6},{8,9},{9,8},{10,11... | collective-permute-start | bytes 3145736 | tf_op jit(solution)/shard_map/ppermute | solution.py:113
  185.6 18.3 %attend_forward.1 = (f32[4,4,256,128]{3,2,1,0:T(8,128)S(1)}, f32[4,4,8,256]{3,2,1,0:T(8,128)S(1)}) custom-call(s32[1]{0:T(128)} %bitcast.z_ref, bf16[4,4,256,128]{3,2,1,0:T(8,128)(2,1)S(1)} %pad_maximum_fusion.3.q_ref, bf16[4,1024,128]{2,1,0:T(8,128)(2,1)S(1)} %get-tuple-element.65.k_ref, bf16[4,1024,128]{2,1,0:T(8,128)(2,1)S(1)} %get-tuple-element.66.v_ref), custom_call_target="tpu_custom_call" | custom-call | flops 8999999488 | bytes 8388608 | tf_op jit(solution)/shard_map/attend_forward/pallas_call | solution.py:213
  224.7 25.7 %all-to-all-done = bf16[4,128,2048]{2,1,0:T(8,128)(2,1)} async-done(((bf16[4,128,2048]{2,1,0:T(8,128)(2,1)}), bf16[4,128,2048]{2,1,0:T(8,128)(2,1)}, u32[]{:S(2)}, u32[]{:S(2)}) %all-to-all-start) | async-done | bytes 2097184 | tf_op jit(solution)/shard_map/all_to_all | solution.py:144
  259.3 34.1 %all_to_all.45 = bf16[128,48,128]{2,1,0:T(8,128)(2,1)} all-to-all(bf16[128,48,128]{2,1,0:T(8,128)(2,1)} %reshape.306), channel_id=1, replica_groups=mesh['y'=4,'x'=4,'z'=4,'c'=2] {'y','x','z','c'}, dimensions={0} | all-to-all | bytes 3145728 | tf_op jit(solution)/shard_map/all_to_all | solution.py:332
  311.2 9.7 %all-to-all-start.2 = ((bf16[128,48,128]{2,1,0:T(8,128)(2,1)}), bf16[128,48,128]{2,1,0:T(8,128)(2,1)}, u32[]{:S(2)}, u32[]{:S(2)}) async-start(bf16[128,48,128]{2,1,0:T(8,128)(2,1)} %reshape.308), calls=%async_computation.2 | async-start | bytes 3145728 | tf_op jit(solution)/shard_map/all_to_all | solution.py:332
  328.5 12.0 %collective-permute-done.52 = f32[8,128]{1,0:T(8,128)S(1)} collective-permute-done((f32[8,128]{1,0:T(8,128)S(1)}, f32[8,128]{1,0:T(8,128)S(1)}, u32[]{:S(2)}, u32[]{:S(2)}) %collective-permute-start.52) | collective-permute-done | bytes 4128 | tf_op jit(solution)/shard_map/ppermute | solution.py:113
  367.5 34.6 %all_to_all.46 = bf16[128,48,128]{2,1,0:T(8,128)(2,1)} all-to-all(bf16[128,48,128]{2,1,0:T(8,128)(2,1)} %reshape.310), channel_id=1, replica_groups=mesh['y'=4,'x'=4,'z'=4,'c'=2] {'y','x','z','c'}, dimensions={0} | all-to-all | bytes 3145728 | tf_op jit(solution)/shard_map/all_to_all | solution.py:332
  416.9 28.9 %all_to_all.47 = bf16[128,48,128]{2,1,0:T(8,128)(2,1)S(1)} all-to-all(bf16[128,48,128]{2,1,0:T(8,128)(2,1)S(1)} %reshape.312), channel_id=1, replica_groups=mesh['y'=4,'x'=4,'z'=4,'c'=2] {'y','x','z','c'}, dimensions={0} | all-to-all | bytes 3145728 | tf_op jit(solution)/shard_map/all_to_all | solution.py:332
  452.5 10.9 %collective-permute-done.60 = bf16[128,2048]{1,0:T(8,128)(2,1)S(1)} collective-permute-done((bf16[128,2048]{1,0:T(8,128)(2,1)S(1)}, bf16[128,2048]{1,0:T(8,128)(2,1)S(1)}, u32[]{:S(2)}, u32[]{:S(2)}) %collective-permute-start.60) | collective-permute-done | bytes 524320 | tf_op jit(solution)/shard_map/ppermute | solution.py:113
  490.3 31.4 %attend_backward.1 = (bf16[4,4,256,128]{3,2,1,0:T(8,128)(2,1)S(1)}, bf16[4,1024,128]{2,1,0:T(8,128)(2,1)S(1)}, bf16[4,1024,128]{2,1,0:T(8,128)(2,1)S(1)}) custom-call(s32[1]{0:T(128)} %bitcast.z_ref, bf16[4,4,256,128]{3,2,1,0:T(8,128)(2,1)S(1)} %copy-done.7, bf16[4,1024,128]{2,1,0:T(8,128)(2,1)S(1)} %copy-done.4, bf16[4,4,128,256]{3,2,1,0:T(8,128)(2,1)} %bitcast.387, ...), custom_call_target="tpu_custom_call" | custom-call | flops 22000001024 | bytes 8388608 | tf_op jit(solution)/shard_map/attend_backward/pallas_call | solution.py:294
  526.0 10.1 %all-to-all-start.5 = ((bf16[4,1024,128]{2,1,0:T(8,128)(2,1)}), bf16[4,1024,128]{2,1,0:T(8,128)(2,1)S(1)}, u32[]{:S(2)}, u32[]{:S(2)}) async-start(bf16[4,1024,128]{2,1,0:T(8,128)(2,1)} %add_convert_fusion.1), calls=%async_computation.5 | async-start | bytes 2097152 | tf_op jit(solution)/shard_map/all_to_all | solution.py:144
  537.0 5.9 convolution_convert_fusion.1
  542.9 6.6 all-to-all-done.5
  550.4 6.3 all-to-all-start.8
  588.0 6.7 all-to-all-start.7
  624.0 6.7 convolution_bitcast_fusion
  642.4 7.5 %collective-permute-start.81 = (bf16[32,2048]{1,0:T(8,128)(2,1)S(1)}, bf16[32,2048]{1,0:T(8,128)(2,1)S(1)}, u32[]{:S(2)}, u32[]{:S(2)}) collective-permute-start(bf16[32,2048]{1,0:T(8,128)(2,1)S(1)} %reduce_sum.318), channel_id=1, source_target_pairs={{0,0},{2,1},{4,2},{6,3},{32,4},{34,5},{36,6},{38,7},{64,8},{66,9},... | collective-permute-start | bytes 393224 | tf_op jit(solution)/shard_map/ppermute | solution.py:460
  650.3 6.8 collective-permute-done.81
  670.5 6.0 collective-permute-start.77
  678.9 5.9 collective-permute-start.79
  688.2 10.9 %collective-permute-done.77 = bf16[8,2048]{1,0:T(8,128)(2,1)S(1)} collective-permute-done((bf16[8,2048]{1,0:T(8,128)(2,1)S(1)}, bf16[8,2048]{1,0:T(8,128)(2,1)S(1)}, u32[]{:S(2)}, u32[]{:S(2)}) %collective-permute-start.77) | collective-permute-done | bytes 32800 | tf_op jit(solution)/shard_map/ppermute | solution.py:496
  (524 shorter events, 341.2 us)
Async XLA Ops:
  5.4 84.3 %collective-permute-start = (bf16[128,2048]{1,0:T(8,128)(2,1)}, bf16[128,2048]{1,0:T(8,128)(2,1)}, u32[]{:S(2)}, u32[]{:S(2)}) collective-permute-start(bf16[128,2048]{1,0:T(8,128)(2,1)} %get-tuple-element.59), channel_id=1, source_target_pairs={{0,8},{8,16},{16,24},{24,0},{1,9},{9,17},{17,25},{25,1},{2,10},{10... | collective-permute-start | bytes 1572872 | tf_op jit(solution)/shard_map/ppermute | solution.py:113
  17.7 28.2 %collective-permute-start.5 = (bf16[8,2048]{1,0:T(8,128)(2,1)S(1)}, bf16[8,2048]{1,0:T(8,128)(2,1)S(1)}, u32[]{:S(2)}, u32[]{:S(2)}) collective-permute-start(bf16[8,2048]{1,0:T(8,128)(2,1)S(1)} %get-tuple-element.121), channel_id=1, source_target_pairs={{9,0},{12,1},{0,2},{13,3},{10,4},{23,5},{1,6},{14,7},{35,8},{48,9}... | collective-permute-start | bytes 98312 | tf_op jit(solution)/shard_map/ppermute | solution.py:372
  22.0 29.8 %collective-permute-start.6 = (bf16[8,2048]{1,0:T(8,128)(2,1)S(1)}, bf16[8,2048]{1,0:T(8,128)(2,1)S(1)}, u32[]{:S(2)}, u32[]{:S(2)}) collective-permute-start(bf16[8,2048]{1,0:T(8,128)(2,1)S(1)} %get-tuple-element.120), channel_id=1, source_target_pairs={{0,0},{22,1},{10,2},{13,3},{1,4},{23,5},{11,6},{14,7},{25,8},{48,9... | collective-permute-start | bytes 98312 | tf_op jit(solution)/shard_map/ppermute | solution.py:372
  24.4 27.4 %collective-permute-start.7 = (bf16[8,2048]{1,0:T(8,128)(2,1)S(1)}, bf16[8,2048]{1,0:T(8,128)(2,1)S(1)}, u32[]{:S(2)}, u32[]{:S(2)}) collective-permute-start(bf16[8,2048]{1,0:T(8,128)(2,1)S(1)} %get-tuple-element.119), channel_id=1, source_target_pairs={{0,0},{13,1},{10,2},{23,3},{1,4},{14,5},{2,6},{15,7},{26,8},{38,9}... | collective-permute-start | bytes 98312 | tf_op jit(solution)/shard_map/ppermute | solution.py:372
  27.4 24.4 %collective-permute-start.8 = (bf16[8,2048]{1,0:T(8,128)(2,1)S(1)}, bf16[8,2048]{1,0:T(8,128)(2,1)S(1)}, u32[]{:S(2)}, u32[]{:S(2)}) collective-permute-start(bf16[8,2048]{1,0:T(8,128)(2,1)S(1)} %get-tuple-element.118), channel_id=1, source_target_pairs={{9,0},{22,1},{0,2},{13,3},{1,4},{14,5},{10,6},{23,7},{25,8},{38,9}... | collective-permute-start | bytes 98312 | tf_op jit(solution)/shard_map/ppermute | solution.py:372
  64.3 28.8 %collective-permute-start.1 = (bf16[128,2048]{1,0:T(8,128)(2,1)}, bf16[128,2048]{1,0:T(8,128)(2,1)S(1)}, u32[]{:S(2)}, u32[]{:S(2)}) collective-permute-start(bf16[128,2048]{1,0:T(8,128)(2,1)} %get-tuple-element.59), channel_id=1, source_target_pairs={{0,24},{8,0},{16,8},{24,16},{1,25},{9,1},{17,9},{25,17},{2,26},{10... | collective-permute-start | bytes 1572872 | tf_op jit(solution)/shard_map/ppermute | solution.py:113
  64.4 45.9 %collective-permute-start.31 = (bf16[32,2048]{1,0:T(8,128)(2,1)S(1)}, bf16[32,2048]{1,0:T(8,128)(2,1)S(1)}, u32[]{:S(2)}, u32[]{:S(2)}) collective-permute-start(bf16[32,2048]{1,0:T(8,128)(2,1)S(1)} %copy-done.62), channel_id=1, source_target_pairs={{0,0},{1,2},{2,4},{3,6},{4,32},{5,34},{6,36},{7,38},{8,64},{9,66},... | collective-permute-start | bytes 393224 | tf_op jit(solution)/shard_map/ppermute | solution.py:383
  83.7 19.9 %collective-permute-start.14 = (bf16[4,24,2048]{2,1,0:T(8,128)(2,1)S(1)}, bf16[4,24,2048]{2,1,0:T(8,128)(2,1)S(1)}, u32[]{:S(2)}, u32[]{:S(2)}) collective-permute-start(bf16[4,24,2048]{2,1,0:T(8,128)(2,1)S(1)} %fusion.75), channel_id=1, source_target_pairs={{0,2},{2,4},{4,6},{6,0},{1,3},{3,5},{5,7},{7,1},{8,10},{10,12},{12... | collective-permute-start | bytes 1179656 | tf_op jit(solution)/shard_map/ppermute | solution.py:113
  94.1 21.9 %collective-permute-start.3 = (bf16[64,2048]{1,0:T(8,128)(2,1)S(1)}, bf16[64,2048]{1,0:T(8,128)(2,1)S(1)}, u32[]{:S(2)}, u32[]{:S(2)}) collective-permute-start(bf16[64,2048]{1,0:T(8,128)(2,1)S(1)} %slice.385), channel_id=1, source_target_pairs={{0,24},{8,0},{16,8},{24,16},{1,25},{9,1},{17,9},{25,17},{2,26},{10... | collective-permute-start | bytes 786440 | tf_op jit(solution)/shard_map/ppermute | solution.py:113
  94.1 22.0 %collective-permute-start.2 = (bf16[64,2048]{1,0:T(8,128)(2,1)S(1)}, bf16[64,2048]{1,0:T(8,128)(2,1)S(1)}, u32[]{:S(2)}, u32[]{:S(2)}) collective-permute-start(bf16[64,2048]{1,0:T(8,128)(2,1)S(1)} %slice.384), channel_id=1, source_target_pairs={{0,8},{8,16},{16,24},{24,0},{1,9},{9,17},{17,25},{25,1},{2,10},{10... | collective-permute-start | bytes 786440 | tf_op jit(solution)/shard_map/ppermute | solution.py:113
  116.1 29.3 %collective-permute-start.4 = (bf16[4,128,2048]{2,1,0:T(8,128)(2,1)S(1)}, bf16[4,128,2048]{2,1,0:T(8,128)(2,1)S(1)}, u32[]{:S(2)}, u32[]{:S(2)}) collective-permute-start(bf16[4,128,2048]{2,1,0:T(8,128)(2,1)S(1)} %fusion.36), channel_id=1, source_target_pairs={{0,1},{1,0},{2,3},{3,2},{4,5},{5,4},{6,7},{7,6},{8,9},{9,8},{10,11... | collective-permute-start | bytes 6291464 | tf_op jit(solution)/shard_map/ppermute | solution.py:113
  219.4 31.0 %all-to-all-start = ((bf16[4,128,2048]{2,1,0:T(8,128)(2,1)}), bf16[4,128,2048]{2,1,0:T(8,128)(2,1)}, u32[]{:S(2)}, u32[]{:S(2)}) async-start(bf16[4,128,2048]{2,1,0:T(8,128)(2,1)} %fusion.5), calls=%async_computation | async-start | bytes 4194304 | tf_op jit(solution)/shard_map/all_to_all | solution.py:144
  311.2 41.5 %all-to-all-start.2 = ((bf16[128,48,128]{2,1,0:T(8,128)(2,1)}), bf16[128,48,128]{2,1,0:T(8,128)(2,1)}, u32[]{:S(2)}, u32[]{:S(2)}) async-start(bf16[128,48,128]{2,1,0:T(8,128)(2,1)} %reshape.308), calls=%async_computation.2 | async-start | bytes 3145728 | tf_op jit(solution)/shard_map/all_to_all | solution.py:332
  324.2 16.3 %collective-permute-start.52 = (f32[8,128]{1,0:T(8,128)S(1)}, f32[8,128]{1,0:T(8,128)S(1)}, u32[]{:S(2)}, u32[]{:S(2)}) collective-permute-start(f32[8,128]{1,0:T(8,128)S(1)} %broadcast_add_fusion), channel_id=1, source_target_pairs={{0,16},{8,24},{16,0},{24,8},{1,17},{9,25},{17,1},{25,9},{2,18},{10... | collective-permute-start | bytes 12296 | tf_op jit(solution)/shard_map/ppermute | solution.py:113
  526.0 23.4 %all-to-all-start.5 = ((bf16[4,1024,128]{2,1,0:T(8,128)(2,1)}), bf16[4,1024,128]{2,1,0:T(8,128)(2,1)S(1)}, u32[]{:S(2)}, u32[]{:S(2)}) async-start(bf16[4,1024,128]{2,1,0:T(8,128)(2,1)} %add_convert_fusion.1), calls=%async_computation.5 | async-start | bytes 2097152 | tf_op jit(solution)/shard_map/all_to_all | solution.py:144
  550.4 36.2 %all-to-all-start.8 = ((bf16[16,32,2048]{2,1,0:T(8,128)(2,1)}), bf16[16,32,2048]{2,1,0:T(8,128)(2,1)S(1)}, u32[]{:S(2)}, u32[]{:S(2)}) async-start(bf16[16,32,2048]{2,1,0:T(8,128)(2,1)} %bitcast.382), calls=%async_computation.8 | async-start | bytes 4194304 | tf_op jit(solution)/shard_map/all_to_all | solution.py:144
  579.6 35.8 %collective-permute-start.65 = (f32[35,128]{1,0:T(8,128)S(1)}, f32[35,128]{1,0:T(8,128)S(1)}, u32[]{:S(2)}, u32[]{:S(2)}) collective-permute-start(f32[35,128]{1,0:T(8,128)S(1)} %bitcast.395), channel_id=1, source_target_pairs={{0,1},{1,0},{2,3},{3,2},{4,5},{5,4},{6,7},{7,6},{8,9},{9,8},{10,11... | collective-permute-start | bytes 53768 | tf_op jit(solution)/shard_map/ppermute | solution.py:113
  588.0 69.9 %all-to-all-start.7 = ((bf16[16,40,2048]{2,1,0:T(8,128)(2,1)}), bf16[16,40,2048]{2,1,0:T(8,128)(2,1)S(1)}, u32[]{:S(2)}, u32[]{:S(2)}) async-start(bf16[16,40,2048]{2,1,0:T(8,128)(2,1)} %pad_maximum_fusion), calls=%async_computation.7 | async-start | bytes 5242880 | tf_op jit(solution)/shard_map/all_to_all | solution.py:144
  620.6 41.8 %collective-permute-start.75 = (bf16[4,128,2048]{2,1,0:T(8,128)(2,1)}, bf16[4,128,2048]{2,1,0:T(8,128)(2,1)}, u32[]{:S(2)}, u32[]{:S(2)}) collective-permute-start(bf16[4,128,2048]{2,1,0:T(8,128)(2,1)} %dynamic-slice_bitcast_fusion), channel_id=1, source_target_pairs={{0,1},{1,0},{2,3},{3,2},{4,5},{5,4},{6,7},{7,6},{8,9},{9,8},{10,11... | collective-permute-start | bytes 6291464 | tf_op jit(solution)/shard_map/ppermute | solution.py:113
  658.5 29.8 %collective-permute-start.76 = (bf16[8,2048]{1,0:T(8,128)(2,1)S(1)}, bf16[8,2048]{1,0:T(8,128)(2,1)S(1)}, u32[]{:S(2)}, u32[]{:S(2)}) collective-permute-start(bf16[8,2048]{1,0:T(8,128)(2,1)S(1)} %get-tuple-element.111), channel_id=1, source_target_pairs={{0,9},{1,12},{2,0},{3,13},{4,10},{5,23},{6,1},{7,14},{8,35},{9,48}... | collective-permute-start | bytes 98312 | tf_op jit(solution)/shard_map/ppermute | solution.py:496
  666.9 33.5 %all-to-all-start.6 = ((bf16[4,128,2048]{2,1,0:T(8,128)(2,1)}), bf16[4,128,2048]{2,1,0:T(8,128)(2,1)S(1)}, u32[]{:S(2)}, u32[]{:S(2)}) async-start(bf16[4,128,2048]{2,1,0:T(8,128)(2,1)} %fusion.4), calls=%async_computation.6 | async-start | bytes 4194304 | tf_op jit(solution)/shard_map/all_to_all | solution.py:144
  670.5 28.6 %collective-permute-start.77 = (bf16[8,2048]{1,0:T(8,128)(2,1)S(1)}, bf16[8,2048]{1,0:T(8,128)(2,1)S(1)}, u32[]{:S(2)}, u32[]{:S(2)}) collective-permute-start(bf16[8,2048]{1,0:T(8,128)(2,1)S(1)} %get-tuple-element.110), channel_id=1, source_target_pairs={{0,0},{1,22},{2,10},{3,13},{4,1},{5,23},{6,11},{7,14},{8,25},{9,48... | collective-permute-start | bytes 98312 | tf_op jit(solution)/shard_map/ppermute | solution.py:496
  676.5 22.6 %collective-permute-start.78 = (bf16[8,2048]{1,0:T(8,128)(2,1)S(1)}, bf16[8,2048]{1,0:T(8,128)(2,1)S(1)}, u32[]{:S(2)}, u32[]{:S(2)}) collective-permute-start(bf16[8,2048]{1,0:T(8,128)(2,1)S(1)} %get-tuple-element.109), channel_id=1, source_target_pairs={{0,0},{1,13},{2,10},{3,23},{4,1},{5,14},{6,2},{7,15},{8,26},{9,38}... | collective-permute-start | bytes 98312 | tf_op jit(solution)/shard_map/ppermute | solution.py:496
  678.9 20.3 %collective-permute-start.79 = (bf16[8,2048]{1,0:T(8,128)(2,1)S(1)}, bf16[8,2048]{1,0:T(8,128)(2,1)S(1)}, u32[]{:S(2)}, u32[]{:S(2)}) collective-permute-start(bf16[8,2048]{1,0:T(8,128)(2,1)S(1)} %get-tuple-element.108), channel_id=1, source_target_pairs={{0,9},{1,22},{2,0},{3,13},{4,1},{5,14},{6,10},{7,23},{8,25},{9,38}... | collective-permute-start | bytes 98312 | tf_op jit(solution)/shard_map/ppermute | solution.py:496
  (128 other events, 1182.7 us)

commit v2 on v1

v2 whole, which is shorter than its diff:
```python
import functools
import jax
import jax.numpy as jnp
import numpy as np
from jax import lax
from jax.experimental import pallas as pl
from jax.experimental.pallas import tpu as pltpu
from jax.sharding import Mesh
from jax.sharding import PartitionSpec as P

D = 2048
H = 32
KV = 4
HD = 128
FF = 768
TOP = 2
CAP = 3
SEQ = 4096
EXPERTS = 128
LOCAL = 128
DEVICES = 128
TOKENS = LOCAL * DEVICES
GROUP = 1024
PIECE = 256
HEADS = 4

epsilon = 1e-06
theta = 1000000.0
ALL = ("y", "x", "z", "c")
SIZE = {"y": 4, "x": 4, "z": 4, "c": 2}
SCALE = HD ** (-0.5)
LOG2E = 1.4426950408889634
f32 = jnp.float32
bf16 = jnp.bfloat16


def device_of(y, x, z, c):
    return ((y * 4 + x) * 4 + z) * 2 + c


def colour_edges(edges, count, degree):
    left = {}
    for source, target, tag in edges:
        left.setdefault(source, []).append((target, tag))
    rounds = []
    for _ in range(degree):
        match = {}

        def place(source, seen):
            for number, (target, _) in enumerate(left[source]):
                if target in seen:
                    continue
                seen.add(target)
                if target not in match or place(match[target][0], seen):
                    match[target] = (source, number)
                    return True
            return False

        for source in range(count):
            place(source, set())
        done = []
        for target, (source, number) in sorted(match.items()):
            done.append((source, target, left[source][number][1]))
        for target, (source, number) in match.items():
            left[source][number] = None
        for source in left:
            left[source] = [entry for entry in left[source] if entry is not None]
        rounds.append(done)
    return rounds


@functools.cache
def in_plan():
    edges = []
    for x in range(4):
        for c in range(2):
            group = 2 * x + c
            wanted = [64 * group + s for s in range(64)]
            wanted += [512 + 64 * c + 16 * x + s for s in range(16)]
            for s, part in enumerate(wanted):
                slot, place = s // 5, s % 5
                target = device_of(slot % 4, x, slot // 4, c)
                edges.append((part // 5, target, (part % 5, place)))
    rounds = colour_edges(edges, DEVICES, 5)
    leaves = np.zeros((DEVICES, 5, 8), np.int32)
    arrives = np.zeros((DEVICES, 5, 8), np.int32)
    perms = []
    for number, done in enumerate(rounds):
        perms.append([(source, target) for source, target, _ in done])
        for source, target, (part, place) in done:
            leaves[source, number] = part * 8 + np.arange(8)
            arrives[target, place] = number * 8 + np.arange(8)
    return perms, leaves.reshape(DEVICES, 40), arrives.reshape(DEVICES, 40)


def row_picker(table, me):
    mine = jnp.arange(DEVICES, dtype=jnp.int32)[:, None] == me
    chosen = jnp.sum(jnp.where(mine, jnp.asarray(table), 0), axis=0)
    return (chosen[:, None] == jnp.arange(40, dtype=jnp.int32)[None, :]).astype(bf16)


def out_perm():
    perm = []
    for y in range(4):
        for x in range(4):
            for z in range(4):
                for c in range(2):
                    slot = device_of(y, x, z, c) % 16
                    perm.append((device_of(y, x, z, c), device_of(slot % 4, y, slot // 4, x // 2)))
    return perm


def shift(value, axis, step):
    size = SIZE[axis]
    return lax.ppermute(value, axis, [(i, (i + step) % size) for i in range(size)])


def ring_gather(value, axis):
    index = lax.axis_index(axis)
    half = value.shape[0] // 2
    before = shift(value, axis, 1)
    after = shift(value, axis, -1)
    far = jnp.concatenate([shift(before[:half], axis, 1), shift(after[half:], axis, -1)], axis=0)
    out = jnp.zeros((4,) + value.shape, value.dtype)
    for offset, block in ((0, value), (3, before), (1, after), (2, far)):
        out = lax.dynamic_update_index_in_dim(out, block, (index + offset) % 4, 0)
    return out


def core_gather(value):
    index = lax.axis_index("c")
    other = shift(value, "c", 1)
    out = jnp.zeros((2,) + value.shape, value.dtype)
    out = lax.dynamic_update_index_in_dim(out, value, index, 0)
    return lax.dynamic_update_index_in_dim(out, other, 1 - index, 0)


def small_sum(value):
    value = value + shift(value, "c", 1)
    for axis in ("x", "y", "z"):
        value = value + shift(value, axis, 1) + shift(value, axis, -1) + shift(value, axis, 2)
    return value


def scatter_sum(value, axes, count):
    moved = lax.all_to_all(value, axes, split_axis=0, concat_axis=0, tiled=True)
    return jnp.sum(moved.astype(f32), axis=0)


def ring_scatter(value, axis):
    index = lax.axis_index(axis)
    half = value.shape[1] // 2

    def block(offset):
        return lax.dynamic_index_in_dim(value, (index + offset) % 4, 0, keepdims=False)

    far = block(2).astype(bf16)
    from_left = shift(far[:half], axis, 1).astype(f32)
    from_right = shift(far[half:], axis, -1).astype(f32)
    right, left = block(1).astype(f32), block(3).astype(f32)
    right = jnp.concatenate([right[:half] + from_left, right[half:]], axis=0).astype(bf16)
    left = jnp.concatenate([left[:half], left[half:] + from_right], axis=0).astype(bf16)
    return block(0).astype(f32) + shift(right, axis, 1).astype(f32) + shift(left, axis, -1).astype(f32)


def rotation(position):
    frequency = theta ** (-jnp.arange(0, HD, 2).astype(f32) / HD)
    phase = position[:, None] * frequency[None, :]
    cosine, sine = jnp.cos(phase), jnp.sin(phase)
    return jnp.concatenate([cosine, cosine], axis=-1), jnp.concatenate([-sine, sine], axis=-1)


NT = (((1,), (1,)), ((), ()))
NN = (((1,), (0,)), ((), ()))
TN = (((0,), (0,)), ((), ()))


def head_rotate(value, gain, cosine, sine):
    scaled = value * lax.rsqrt(jnp.mean(value * value, axis=-1, keepdims=True) + epsilon) * gain
    return scaled * cosine + pltpu.roll(scaled, HD // 2, 1) * sine


def head_rotate_back(grad, value, gain, cosine, sine):
    inverse = lax.rsqrt(jnp.mean(value * value, axis=-1, keepdims=True) + epsilon)
    unit = value * inverse
    scaled = grad * cosine + pltpu.roll(grad * sine, HD // 2, 1)
    unit_grad = scaled * gain
    back = inverse * (unit_grad - unit * jnp.mean(unit_grad * unit, axis=-1, keepdims=True))
    return back, scaled * unit


def project_kernel(core_ref, h_ref, w_ref, cos_ref, sin_ref, qg_ref, kg_ref, p_ref, q_ref, kv_ref):
    projected = lax.dot_general(h_ref[...], w_ref[...], NT, preferred_element_type=f32)
    p_ref[...] = projected
    cosine, sine = cos_ref[...], sin_ref[...]
    for head in range(HEADS):
        lanes = slice(head * HD, (head + 1) * HD)
        q_ref[:, lanes] = head_rotate(projected[:, lanes], qg_ref[...], cosine, sine).astype(bf16)
    last = projected[:, HEADS * HD :]
    keys = head_rotate(last, kg_ref[...], cosine, sine)
    kv_ref[...] = jnp.where(core_ref[0] == 0, keys, last).astype(bf16)


def project(core, rows, weights, cosine, sine, q_gain, k_gain):
    wide = HEADS * HD
    return pl.pallas_call(
        project_kernel,
        grid_spec=pltpu.PrefetchScalarGridSpec(
            num_scalar_prefetch=1,
            grid=(4,),
            in_specs=[
                pl.BlockSpec((PIECE, D), lambda i, c: (i, 0)),
                pl.BlockSpec((wide + HD, D), lambda i, c: (0, 0)),
                pl.BlockSpec((PIECE, HD), lambda i, c: (i, 0)),
                pl.BlockSpec((PIECE, HD), lambda i, c: (i, 0)),
                pl.BlockSpec((1, HD), lambda i, c: (0, 0)),
                pl.BlockSpec((1, HD), lambda i, c: (0, 0)),
            ],
            out_specs=[
                pl.BlockSpec((PIECE, wide + HD), lambda i, c: (i, 0)),
                pl.BlockSpec((PIECE, wide), lambda i, c: (i, 0)),
                pl.BlockSpec((PIECE, HD), lambda i, c: (i, 0)),
            ],
        ),
        out_shape=[
            jax.ShapeDtypeStruct((GROUP, wide + HD), f32),
            jax.ShapeDtypeStruct((GROUP, wide), bf16),
            jax.ShapeDtypeStruct((GROUP, HD), bf16),
        ],
        compiler_params=pltpu.CompilerParams(vmem_limit_bytes=40 * 2**20),
        cost_estimate=pl.CostEstimate(flops=27 * 10**8, bytes_accessed=11 * 2**20, transcendentals=10**4),
        name="project",
    )(core, rows, weights, cosine, sine, q_gain, k_gain)


def project_back_kernel(core_ref, dq_ref, dkv_ref, p_ref, cos_ref, sin_ref, qg_ref, kg_ref, gp_ref, qt_ref, kt_ref):
    @pl.when(pl.program_id(0) == 0)
    def _():
        qt_ref[...] = jnp.zeros_like(qt_ref)
        kt_ref[...] = jnp.zeros_like(kt_ref)

    cosine, sine = cos_ref[...], sin_ref[...]
    for head in range(HEADS):
        lanes = slice(head * HD, (head + 1) * HD)
        back, term = head_rotate_back(dq_ref[:, lanes].astype(f32), p_ref[:, lanes], qg_ref[...], cosine, sine)
        gp_ref[:, lanes] = back.astype(bf16)
        qt_ref[...] += jnp.sum(term, axis=0, keepdims=True)
    lanes = slice(HEADS * HD, (HEADS + 1) * HD)
    grad = jnp.sum(dkv_ref[...].astype(f32), axis=0)
    back, term = head_rotate_back(grad, p_ref[:, lanes], kg_ref[...], cosine, sine)
    gp_ref[:, lanes] = jnp.where(core_ref[0] == 0, back, grad).astype(bf16)
    kt_ref[...] += jnp.where(core_ref[0] == 0, jnp.sum(term, axis=0, keepdims=True), 0.0)


def project_back(core, dq, dkv, projected, cosine, sine, q_gain, k_gain):
    wide = HEADS * HD
    return pl.pallas_call(
        project_back_kernel,
        grid_spec=pltpu.PrefetchScalarGridSpec(
            num_scalar_prefetch=1,
            grid=(4,),
            in_specs=[
                pl.BlockSpec((PIECE, wide), lambda i, c: (i, 0)),
                pl.BlockSpec((4, PIECE, HD), lambda i, c: (0, i, 0)),
                pl.BlockSpec((PIECE, wide + HD), lambda i, c: (i, 0)),
                pl.BlockSpec((PIECE, HD), lambda i, c: (i, 0)),
                pl.BlockSpec((PIECE, HD), lambda i, c: (i, 0)),
                pl.BlockSpec((1, HD), lambda i, c: (0, 0)),
                pl.BlockSpec((1, HD), lambda i, c: (0, 0)),
            ],
            out_specs=[
                pl.BlockSpec((PIECE, wide + HD), lambda i, c: (i, 0)),
                pl.BlockSpec((1, HD), lambda i, c: (0, 0)),
                pl.BlockSpec((1, HD), lambda i, c: (0, 0)),
            ],
        ),
        out_shape=[
            jax.ShapeDtypeStruct((GROUP, wide + HD), bf16),
            jax.ShapeDtypeStruct((1, HD), f32),
            jax.ShapeDtypeStruct((1, HD), f32),
        ],
        compiler_params=pltpu.CompilerParams(vmem_limit_bytes=40 * 2**20),
        cost_estimate=pl.CostEstimate(flops=10**7, bytes_accessed=7 * 2**20, transcendentals=10**4),
        name="project_back",
    )(core, dq, dkv, projected, cosine, sine, q_gain, k_gain)


def forward_kernel(z_ref, q_ref, kv_ref, o_ref, lse_ref, total):
    piece = pl.program_id(0)
    z = z_ref[0]
    total[...] = jnp.zeros_like(total)
    ones = jnp.ones((PIECE, HD), bf16)

    def step(chunk, masked):
        row = pl.multiple_of((chunk // 4) * PIECE, PIECE)
        keys = kv_ref[0, chunk % 4, pl.ds(row, PIECE), :]
        values = kv_ref[1, chunk % 4, pl.ds(row, PIECE), :]
        wide = jnp.concatenate([values, ones], axis=1)
        for head in range(HEADS):
            lanes = slice(head * HD, (head + 1) * HD)
            scores = lax.dot_general(q_ref[:, lanes], keys, NT, preferred_element_type=f32)
            weights = jnp.exp2(scores * (SCALE * LOG2E))
            if masked:
                queries_at = lax.broadcasted_iota(jnp.int32, (PIECE, PIECE), 0)
                keys_at = lax.broadcasted_iota(jnp.int32, (PIECE, PIECE), 1)
                weights = jnp.where(keys_at <= queries_at, weights, 0.0)
            total[head] += lax.dot_general(weights.astype(bf16), wide, NN, preferred_element_type=f32)

    last = piece * 4 + z

    def body(chunk, carry):
        step(chunk, False)
        return carry

    lax.fori_loop(0, last, body, 0)
    step(last, True)
    for head in range(HEADS):
        sums = total[head, :, HD:]
        o_ref[:, head * HD : (head + 1) * HD] = (total[head, :, :HD] / sums).astype(bf16)
        lse_ref[head, 0] = jnp.transpose(jnp.log2(sums))[:8, :]


def attend_forward(z, queries, keys_values):
    return pl.pallas_call(
        forward_kernel,
        grid_spec=pltpu.PrefetchScalarGridSpec(
            num_scalar_prefetch=1,
            grid=(4,),
            in_specs=[
                pl.BlockSpec((PIECE, HEADS * HD), lambda i, z: (i, 0)),
                pl.BlockSpec((2, 4, GROUP, HD), lambda i, z: (0, 0, 0, 0)),
            ],
            out_specs=[
                pl.BlockSpec((PIECE, HEADS * HD), lambda i, z: (i, 0)),
                pl.BlockSpec((HEADS, 1, 8, PIECE), lambda i, z: (0, i, 0, 0)),
            ],
            scratch_shapes=[pltpu.VMEM((HEADS, PIECE, 2 * HD), f32)],
        ),
        out_shape=[
            jax.ShapeDtypeStruct((GROUP, HEADS * HD), bf16),
            jax.ShapeDtypeStruct((HEADS, 4, 8, PIECE), f32),
        ],
        compiler_params=pltpu.CompilerParams(vmem_limit_bytes=40 * 2**20),
        cost_estimate=pl.CostEstimate(flops=9 * 10**9, bytes_accessed=8 * 2**20, transcendentals=10**7),
        name="attend_forward",
    )(z, queries, keys_values)


def backward_kernel(z_ref, q_ref, kv_ref, kt_ref, go_ref, o_ref, lse_ref, dq_ref, dkv_ref, dqt, dkv):
    piece = pl.program_id(0)
    z = z_ref[0]

    @pl.when(piece == 0)
    def _():
        dkv[...] = jnp.zeros_like(dkv)

    dqt[...] = jnp.zeros_like(dqt)
    rows = HEADS * PIECE

    def heads_of(ref):
        return jnp.concatenate([ref[:, head * HD : (head + 1) * HD] for head in range(HEADS)], axis=0)

    queries = heads_of(q_ref)
    backs = heads_of(go_ref)
    product = backs.astype(f32) * heads_of(o_ref).astype(f32)
    delta = lax.dot_general(jnp.ones((8, HD), f32), product, NT, precision=lax.Precision.HIGHEST, preferred_element_type=f32)[:1]
    sums = jnp.concatenate([lse_ref[head, 0, :1, :] for head in range(HEADS)], axis=1)

    def step(chunk, masked):
        row = pl.multiple_of((chunk // 4) * PIECE, PIECE)
        block = chunk % 4
        keys = kv_ref[0, block, pl.ds(row, PIECE), :]
        values = kv_ref[1, block, pl.ds(row, PIECE), :]
        turned = kt_ref[block, chunk // 4]
        scores = lax.dot_general(keys, queries, NT, preferred_element_type=f32)
        weights = jnp.exp2(scores * (SCALE * LOG2E) - sums)
        if masked:
            keys_at = lax.broadcasted_iota(jnp.int32, (PIECE, rows), 0)
            queries_at = lax.broadcasted_iota(jnp.int32, (PIECE, rows), 1) % PIECE
            weights = jnp.where(keys_at <= queries_at, weights, 0.0)
        back_weights = lax.dot_general(values, backs, NT, preferred_element_type=f32)
        back_scores = (weights * (back_weights - delta)).astype(bf16)
        dkv[1, block, pl.ds(row, PIECE), :] += lax.dot_general(weights.astype(bf16), backs, NN, preferred_element_type=f32)
        dkv[0, block, pl.ds(row, PIECE), :] += lax.dot_general(back_scores, queries, NN, preferred_element_type=f32)
        dqt[...] += lax.dot_general(turned, back_scores, NN, preferred_element_type=f32)

    last = piece * 4 + z

    def body(chunk, carry):
        step(chunk, False)
        return carry

    lax.fori_loop(0, last, body, 0)
    step(last, True)
    grads = (jnp.transpose(dqt[...]) * SCALE).astype(bf16)
    for head in range(HEADS):
        dq_ref[:, head * HD : (head + 1) * HD] = grads[head * PIECE : (head + 1) * PIECE]

    @pl.when(piece == 3)
    def _():
        dkv_ref[0] = (dkv[0] * SCALE).astype(bf16)
        dkv_ref[1] = dkv[1].astype(bf16)


def attend_backward(z, queries, keys_values, backs, outs, lse):
    turned = keys_values[0].reshape(4, 4, PIECE, HD).transpose(0, 1, 3, 2)
    heads_spec = pl.BlockSpec((PIECE, HEADS * HD), lambda i, z: (i, 0))
    whole = pl.BlockSpec((2, 4, GROUP, HD), lambda i, z: (0, 0, 0, 0))
    return pl.pallas_call(
        backward_kernel,
        grid_spec=pltpu.PrefetchScalarGridSpec(
            num_scalar_prefetch=1,
            grid=(4,),
            in_specs=[
                heads_spec,
                whole,
                pl.BlockSpec((4, 4, HD, PIECE), lambda i, z: (0, 0, 0, 0)),
                heads_spec,
                heads_spec,
                pl.BlockSpec((HEADS, 1, 8, PIECE), lambda i, z: (0, i, 0, 0)),
            ],
            out_specs=[heads_spec, whole],
            scratch_shapes=[
                pltpu.VMEM((HD, HEADS * PIECE), f32),
                pltpu.VMEM((2, 4, GROUP, HD), f32),
            ],
        ),
        out_shape=[
            jax.ShapeDtypeStruct((GROUP, HEADS * HD), bf16),
            jax.ShapeDtypeStruct((2, 4, GROUP, HD), bf16),
        ],
        compiler_params=pltpu.CompilerParams(vmem_limit_bytes=48 * 2**20),
        cost_estimate=pl.CostEstimate(flops=22 * 10**9, bytes_accessed=8 * 2**20, transcendentals=10**7),
        name="attend_backward",
    )(z, queries, keys_values, turned, backs, outs, lse)


ROWS = EXPERTS * CAP
CHUNKS = D // 128
TILES = ROWS * CHUNKS


def lanes_of(number, width=128):
    return slice(number * width, (number + 1) * width)


def place_rows(index_ref, tiles, out_ref, scale_ref=None):
    def body(expert, carry):
        for s in range(CAP):
            slot = expert * CAP + s
            row = tiles[pl.ds(pl.multiple_of(index_ref[slot] * CHUNKS, CHUNKS), CHUNKS), :]
            if scale_ref is not None:
                row = row * scale_ref[slot]
            out_ref[expert, s * CHUNKS : (s + 1) * CHUNKS, :] = row.astype(bf16)
        return carry

    lax.fori_loop(0, EXPERTS, body, 0, unroll=4)


def dispatch_kernel(index_ref, count_ref, moved_ref, token_ref, gain_ref, x2_ref, out_ref, tiles):
    x2 = moved_ref[0].astype(f32)
    for i in range(1, 4):
        x2 += moved_ref[i].astype(f32)
    x2 = token_ref[...].astype(f32) + x2
    x2_ref[...] = x2
    h2 = x2 * lax.rsqrt(jnp.mean(x2 * x2, axis=-1, keepdims=True) + epsilon) * gain_ref[...]
    for k in range(CHUNKS):
        tiles[pl.ds(k, LOCAL, stride=CHUNKS), :] = h2[:, lanes_of(k)]
    out_ref[:, CAP * CHUNKS :, :] = jnp.full((EXPERTS, 8, 128), count_ref[0], f32).astype(bf16)
    place_rows(index_ref, tiles, out_ref)


def dispatch(index, count, moved, tokens, gain):
    return pl.pallas_call(
        dispatch_kernel,
        grid_spec=pltpu.PrefetchScalarGridSpec(
            num_scalar_prefetch=2,
            in_specs=[pl.BlockSpec(memory_space=pltpu.VMEM)] * 3,
            out_specs=[pl.BlockSpec(memory_space=pltpu.VMEM)] * 2,
            scratch_shapes=[pltpu.VMEM((LOCAL * CHUNKS, 128), f32)],
        ),
        out_shape=[
            jax.ShapeDtypeStruct((LOCAL, D), f32),
            jax.ShapeDtypeStruct((EXPERTS, CAP * CHUNKS + 8, 128), bf16),
        ],
        compiler_params=pltpu.CompilerParams(vmem_limit_bytes=40 * 2**20),
        cost_estimate=pl.CostEstimate(flops=10**6, bytes_accessed=6 * 2**20, transcendentals=128),
        name="dispatch",
    )(index, count, moved, tokens, gain)


def unpack_rows(tiles, rows_ref):
    for k in range(CHUNKS):
        rows_ref[:, lanes_of(k)] = tiles[pl.ds(k, ROWS, stride=CHUNKS), :].astype(bf16)


def expert_kernel(x_ref, first_ref, second_ref, rows_ref, mixed_ref, hidden_ref, y_ref, tiles):
    tiles[...] = x_ref[:, : CAP * CHUNKS, :].reshape(TILES, 128).astype(f32)
    unpack_rows(tiles, rows_ref)
    for j in range(3):
        gate = jnp.dot(rows_ref[...], first_ref[:, lanes_of(j, 256)], preferred_element_type=f32)
        up = jnp.dot(rows_ref[...], first_ref[:, lanes_of(j + 3, 256)], preferred_element_type=f32)
        mixed_ref[:, lanes_of(j, 256)] = gate
        mixed_ref[:, lanes_of(j + 3, 256)] = up
        hidden_ref[:, lanes_of(j, 256)] = (gate * jax.nn.sigmoid(gate) * up).astype(bf16)
    for j in range(D // 256):
        part = jnp.dot(hidden_ref[...], second_ref[:, lanes_of(j, 256)], preferred_element_type=f32)
        tiles[pl.ds(2 * j, ROWS, stride=CHUNKS), :] = part[:, :128]
        tiles[pl.ds(2 * j + 1, ROWS, stride=CHUNKS), :] = part[:, 128:]
    y_ref[...] = tiles[...].astype(bf16)


def expert_forward(rows, first, second):
    return pl.pallas_call(
        expert_kernel,
        in_specs=[pl.BlockSpec(memory_space=pltpu.VMEM)] * 3,
        out_specs=[pl.BlockSpec(memory_space=pltpu.VMEM)] * 4,
        scratch_shapes=[pltpu.VMEM((TILES, 128), f32)],
        out_shape=[
            jax.ShapeDtypeStruct((ROWS, D), bf16),
            jax.ShapeDtypeStruct((ROWS, 2 * FF), f32),
            jax.ShapeDtypeStruct((ROWS, FF), bf16),
            jax.ShapeDtypeStruct((TILES, 128), bf16),
        ],
        compiler_params=pltpu.CompilerParams(vmem_limit_bytes=48 * 2**20),
        cost_estimate=pl.CostEstimate(flops=36 * 10**8, bytes_accessed=17 * 2**20, transcendentals=3 * 10**5),
        name="expert_forward",
    )(rows, first, second)


def combine_kernel(index_ref, slot_ref, gate_ref, slot_gate_ref, scale_ref, y_ref, x2_ref, target_ref, mask_ref, output_ref, loss_ref, g3_ref, out_ref, tiles):
    def row_of(number):
        return y_ref[pl.ds(pl.multiple_of(slot_ref[number] * CHUNKS, CHUNKS), CHUNKS), :].astype(f32)

    def body(token, carry):
        both = gate_ref[2 * token] * row_of(2 * token) + gate_ref[2 * token + 1] * row_of(2 * token + 1)
        tiles[pl.ds(pl.multiple_of(token * CHUNKS, CHUNKS), CHUNKS), :] = both
        return carry

    lax.fori_loop(0, LOCAL, body, 0, unroll=4)
    mask = mask_ref[...]
    squares = jnp.zeros((LOCAL, 128), f32)
    for k in range(CHUNKS):
        lanes = lanes_of(k)
        output = (x2_ref[:, lanes] + tiles[pl.ds(k, LOCAL, stride=CHUNKS), :]).astype(bf16)
        output_ref[:, lanes] = output
        error = output.astype(f32) - target_ref[:, lanes].astype(f32)
        masked = mask * error
        squares += masked * error
        g3 = scale_ref[0] * masked
        g3_ref[:, lanes] = g3
        tiles[pl.ds(k, LOCAL, stride=CHUNKS), :] = g3
    loss_ref[...] = jnp.sum(squares, axis=0, keepdims=True)
    place_rows(index_ref, tiles, out_ref, slot_gate_ref)


def combine(index, slots, gates, slot_gates, scale, y, x2, target, mask):
    return pl.pallas_call(
        combine_kernel,
        grid_spec=pltpu.PrefetchScalarGridSpec(
            num_scalar_prefetch=5,
            in_specs=[pl.BlockSpec(memory_space=pltpu.VMEM)] * 4,
            out_specs=[pl.BlockSpec(memory_space=pltpu.VMEM)] * 4,
            scratch_shapes=[pltpu.VMEM((LOCAL * CHUNKS, 128), f32)],
        ),
        out_shape=[
            jax.ShapeDtypeStruct((LOCAL, D), bf16),
            jax.ShapeDtypeStruct((1, 128), f32),
            jax.ShapeDtypeStruct((LOCAL, D), f32),
            jax.ShapeDtypeStruct((EXPERTS, CAP * CHUNKS, 128), bf16),
        ],
        compiler_params=pltpu.CompilerParams(vmem_limit_bytes=40 * 2**20),
        cost_estimate=pl.CostEstimate(flops=2 * 10**6, bytes_accessed=7 * 2**20, transcendentals=0),
        name="combine",
    )(index, slots, gates, slot_gates, scale, y, x2, target, mask)


def expert_back_kernel(g_ref, first_ref, second_ref, mixed_ref, back_out_ref, back_mixed_ref, gh_ref, tiles):
    tiles[...] = g_ref[...].astype(f32)
    unpack_rows(tiles, back_out_ref)
    for j in range(3):
        back_hidden = lax.dot_general(back_out_ref[...], second_ref[lanes_of(j, 256), :], NT, preferred_element_type=f32)
        gate = mixed_ref[:, lanes_of(j, 256)]
        up = mixed_ref[:, lanes_of(j + 3, 256)]
        sigmoid = jax.nn.sigmoid(gate)
        back_mixed_ref[:, lanes_of(j, 256)] = (back_hidden * up * (sigmoid * (1.0 + gate * (1.0 - sigmoid)))).astype(bf16)
        back_mixed_ref[:, lanes_of(j + 3, 256)] = (back_hidden * (gate * sigmoid)).astype(bf16)
    for j in range(D // 256):
        part = lax.dot_general(back_mixed_ref[...], first_ref[lanes_of(j, 256), :], NT, preferred_element_type=f32)
        tiles[pl.ds(2 * j, ROWS, stride=CHUNKS), :] = part[:, :128]
        tiles[pl.ds(2 * j + 1, ROWS, stride=CHUNKS), :] = part[:, 128:]
    gh_ref[...] = tiles[...].astype(bf16)


def expert_backward(rows, first, second, mixed):
    return pl.pallas_call(
        expert_back_kernel,
        in_specs=[pl.BlockSpec(memory_space=pltpu.VMEM)] * 4,
        out_specs=[pl.BlockSpec(memory_space=pltpu.VMEM)] * 3,
        scratch_shapes=[pltpu.VMEM((TILES, 128), f32)],
        out_shape=[
            jax.ShapeDtypeStruct((ROWS, D), bf16),
            jax.ShapeDtypeStruct((ROWS, 2 * FF), bf16),
            jax.ShapeDtypeStruct((TILES, 128), bf16),
        ],
        compiler_params=pltpu.CompilerParams(vmem_limit_bytes=48 * 2**20),
        cost_estimate=pl.CostEstimate(flops=36 * 10**8, bytes_accessed=17 * 2**20, transcendentals=3 * 10**5),
        name="expert_backward",
    )(rows, first, second, mixed)


def collect_kernel(slot_ref, gh_ref, x2_ref, g3_ref, gain_ref, g2_ref, gb_ref, term_ref, tiles):
    def row_of(number):
        return gh_ref[pl.ds(pl.multiple_of(slot_ref[number] * CHUNKS, CHUNKS), CHUNKS), :].astype(f32)

    def body(token, carry):
        tiles[pl.ds(pl.multiple_of(token * CHUNKS, CHUNKS), CHUNKS), :] = row_of(2 * token) + row_of(2 * token + 1)
        return carry

    lax.fori_loop(0, LOCAL, body, 0, unroll=4)
    x2 = x2_ref[...]
    r2 = lax.rsqrt(jnp.mean(x2 * x2, axis=-1, keepdims=True) + epsilon)
    products = jnp.zeros((LOCAL, 128), f32)
    for k in range(CHUNKS):
        lanes = lanes_of(k)
        gh2 = tiles[pl.ds(k, LOCAL, stride=CHUNKS), :]
        n2 = x2_ref[:, lanes] * r2
        term = gh2 * n2
        term_ref[:, lanes] = jnp.sum(term, axis=0, keepdims=True)
        products += term * gain_ref[:, lanes]
    mean = jnp.sum(products, axis=-1, keepdims=True) * (1.0 / D)
    for k in range(CHUNKS):
        lanes = lanes_of(k)
        gn = tiles[pl.ds(k, LOCAL, stride=CHUNKS), :] * gain_ref[:, lanes]
        g2 = g3_ref[:, lanes] + r2 * (gn - x2_ref[:, lanes] * r2 * mean)
        g2_ref[:, lanes] = g2
        gb_ref[:, lanes] = g2.astype(bf16)


def collect(slots, gh, x2, g3, gain):
    return pl.pallas_call(
        collect_kernel,
        grid_spec=pltpu.PrefetchScalarGridSpec(
            num_scalar_prefetch=1,
            in_specs=[pl.BlockSpec(memory_space=pltpu.VMEM)] * 4,
            out_specs=[pl.BlockSpec(memory_space=pltpu.VMEM)] * 3,
            scratch_shapes=[pltpu.VMEM((LOCAL * CHUNKS, 128), f32)],
        ),
        out_shape=[
            jax.ShapeDtypeStruct((LOCAL, D), f32),
            jax.ShapeDtypeStruct((LOCAL, D), bf16),
            jax.ShapeDtypeStruct((1, D), f32),
        ],
        compiler_params=pltpu.CompilerParams(vmem_limit_bytes=40 * 2**20),
        cost_estimate=pl.CostEstimate(flops=2 * 10**6, bytes_accessed=6 * 2**20, transcendentals=128),
        name="collect",
    )(slots, gh, x2, g3, gain)


def dot(a, b, dims=NN):
    return lax.dot_general(a, b, dims, preferred_element_type=f32)


def exchange(rows):
    return lax.all_to_all(rows, ALL, split_axis=0, concat_axis=0, tiled=True)


def core_halves(value, core):
    split = value.reshape(4, 2, LOCAL, value.shape[-1])
    own = lax.dynamic_index_in_dim(split, core, 1, keepdims=False)
    other = lax.dynamic_index_in_dim(split, 1 - core, 1, keepdims=False)
    return own.reshape(4 * LOCAL, -1), other.reshape(4 * LOCAL, -1)


def core_join(own, other, core):
    width = own.shape[-1]
    out = jnp.zeros((4, 2, LOCAL, width), own.dtype)
    out = lax.dynamic_update_index_in_dim(out, own.reshape(4, LOCAL, width), core, 1)
    out = lax.dynamic_update_index_in_dim(out, other.reshape(4, LOCAL, width), 1 - core, 1)
    return out.reshape(GROUP, width)


def body(tokens, gain1, w_in, q_gain, k_gain, w_out, gain2, gate_up, down, routes, gates, target, valid):
    y, x, z, c = (lax.axis_index(name) for name in ALL)
    me = device_of(y, x, z, c)
    z_array = jnp.reshape(z, (1,)).astype(jnp.int32)
    c_array = jnp.reshape(c, (1,)).astype(jnp.int32)
    q_gain_row, k_gain_row = q_gain[None, :], k_gain[None, :]
    mask = valid.astype(f32)

    perms, leaves, arrives = in_plan()
    leave, arrive = row_picker(leaves, me), row_picker(arrives, me)
    leaving = dot(leave, w_in, NT).astype(bf16)
    arrived = jnp.concatenate([lax.ppermute(leaving[8 * i : 8 * i + 8], ALL, perms[i]) for i in range(5)], axis=0)
    in_slot = dot(arrive, arrived).astype(bf16)
    in_mine = ring_gather(ring_gather(in_slot, "y"), "z").reshape(640, D)

    inputs = tokens.astype(f32)
    r1 = lax.rsqrt(jnp.mean(inputs * inputs, axis=-1, keepdims=True) + epsilon)
    n1 = inputs * r1
    h1 = (n1 * gain1).astype(bf16)
    h1_group = lax.all_gather(h1, ("x", "c"), axis=0, tiled=True)

    places = jnp.arange(4, dtype=jnp.int32)[:, None] * 1024 + z * PIECE + jnp.arange(PIECE, dtype=jnp.int32)[None, :]
    cosine, sine = rotation(places.reshape(GROUP).astype(f32))
    projected, queries, key_or_value = project(c_array, h1_group, in_mine, cosine, sine, q_gain_row, k_gain_row)
    keys_values = core_gather(ring_gather(key_or_value, "z"))

    out_slot = lax.ppermute(w_out, ALL, out_perm())
    out_slot, _ = lax.optimization_barrier((out_slot, in_mine))
    out_mine = lax.all_gather(out_slot, ("z", "y"), axis=0, tiled=True)

    attended, lse = attend_forward(z_array, queries, keys_values)
    out_mine, attended = lax.optimization_barrier((out_mine, attended))
    out_other = shift(out_mine, "c", 1)
    attended_mine, attended_other = core_halves(attended, c)
    attended_there = shift(attended_other, "c", 1)
    chip_out = dot(attended_mine, out_mine) + dot(attended_there, out_other)
    moved = lax.all_to_all(chip_out.astype(bf16).reshape(4, LOCAL, D), "x", split_axis=0, concat_axis=0, tiled=True)
    in_other = shift(in_mine, "c", 1)

    route_numbers = routes.reshape(-1)
    pairs = LOCAL * TOP
    same = route_numbers[:, None] == route_numbers[None, :]
    before = jnp.arange(pairs)[None, :] < jnp.arange(pairs)[:, None]
    slots = route_numbers * CAP + jnp.sum((same & before).astype(jnp.int32), axis=1)
    held = jnp.arange(ROWS, dtype=jnp.int32)[:, None] == slots[None, :]
    index = jnp.sum(jnp.where(held, jnp.arange(pairs, dtype=jnp.int32)[None, :] // TOP, 0), axis=1)
    slot_gates = jnp.sum(jnp.where(held, gates.reshape(1, -1), 0.0), axis=1)

    gain2_row = gain2[None, :]
    x2, sent = dispatch(index, jnp.sum(mask)[None], moved, tokens, gain2_row)
    arrived_rows = exchange(sent)
    valid_count = jnp.sum(arrived_rows[:, CAP * CHUNKS, 0].astype(f32))
    first, second = gate_up[0], down[0]
    rows, mixed, hidden, expert_out = expert_forward(arrived_rows, first, second)
    returned = exchange(expert_out.reshape(EXPERTS, CAP * CHUNKS, 128)).reshape(TILES, 128)
    output, squares, g3, sent_back = combine(
        index, slots, gates.reshape(-1), slot_gates, (TOKENS / valid_count)[None], returned, x2, target, mask[:, None]
    )
    back_out, back_mixed, gh = expert_backward(exchange(sent_back).reshape(TILES, 128), first, second, mixed)
    back_rows = exchange(gh.reshape(EXPERTS, CAP * CHUNKS, 128)).reshape(TILES, 128)
    g2, gb, gain2_term = collect(slots, back_rows, x2, g3, gain2_row)

    gb_mine = ring_gather(gb, "x").reshape(4 * LOCAL, D)
    back_mine = dot(gb_mine, out_mine, NT).astype(bf16)
    back_there = dot(gb_mine, out_other, NT).astype(bf16)
    backs = core_join(back_mine, shift(back_there, "c", 1), c)
    gb_other = shift(gb_mine, "c", 1)
    out_partial = dot(attended_mine, gb_mine, TN) + dot(attended_other, gb_other, TN)
    backs, out_partial = lax.optimization_barrier((backs, out_partial))
    dq, dkv = attend_backward(z_array, queries, keys_values, backs, attended, lse)
    out_summed = lax.psum_scatter(out_partial, ("z", "y"), scatter_dimension=0, tiled=True)
    out_gradient = lax.ppermute(out_summed, ALL, [(b, a) for a, b in out_perm()])

    own = lax.dynamic_index_in_dim(dkv, c, 0, keepdims=False)
    there = lax.dynamic_index_in_dim(dkv, 1 - c, 0, keepdims=False)
    chip_kv = (own.astype(f32) + shift(there, "c", 1).astype(f32)).astype(bf16)
    back_kv = lax.all_to_all(chip_kv, "z", split_axis=0, concat_axis=0, tiled=True)
    gp, q_term, k_term = project_back(c_array, dq, back_kv, projected, cosine, sine, q_gain_row, k_gain_row)

    rows, back_mixed, hidden, back_out, gp = lax.optimization_barrier((rows, back_mixed, hidden, back_out, gp))
    second_gradient = dot(hidden, back_out, TN)
    first_gradient = dot(rows, back_mixed, TN)
    in_partial = dot(gp, h1_group, TN).astype(bf16).reshape(16, 40, D)
    in_summed = scatter_sum(in_partial, ("z", "y"), 16)

    gp_mine, gp_there = core_halves(gp, c)
    gh1_chip = dot(gp_mine, in_mine) + dot(shift(gp_there, "c", 1), in_other)
    h1_mine, _ = core_halves(h1_group, c)
    gain1_term = jnp.sum(gh1_chip * h1_mine.astype(f32), axis=0) / gain1
    terms = jnp.concatenate([gain1_term, gain2_term[0], q_term[0], k_term[0], squares[0]])
    sums = small_sum(terms.reshape(-1, 128)).reshape(-1)
    gh1 = ring_scatter(gh1_chip.reshape(4, LOCAL, D), "x")
    gn1 = gh1 * gain1
    tokens_gradient = g2 + r1 * (gn1 - n1 * jnp.mean(gn1 * n1, axis=-1, keepdims=True))

    going = dot(arrive, in_summed.astype(bf16), TN).astype(bf16)
    home = [lax.ppermute(going[8 * i : 8 * i + 8], ALL, [(b, a) for a, b in perms[i]]) for i in range(5)]
    in_gradient = dot(jnp.concatenate(home, axis=0), leave, TN)

    loss = jnp.sum(sums[2 * D + 2 * HD :]) / (2.0 * valid_count * D)
    return (
        output,
        loss,
        tokens_gradient,
        sums[:D],
        in_gradient,
        sums[2 * D : 2 * D + HD],
        sums[2 * D + HD : 2 * D + 2 * HD],
        out_gradient,
        sums[D : 2 * D],
        first_gradient[None],
        second_gradient[None],
    )


def solution(mesh):
    fine = Mesh(mesh.devices.reshape(4, 4, 4, 2), ALL)
    rows = P(ALL, None)
    blocks = P(ALL, None, None)
    columns = P(None, ALL)
    return jax.shard_map(
        body,
        mesh=fine,
        in_specs=(rows, P(), columns, P(), P(), rows, P(), blocks, blocks, rows, rows, rows, P(ALL)),
        out_specs=(rows, P(), rows, P(), columns, P(), P(), rows, P(), blocks, blocks),
        check_vma=False,
    )
```

time: 719 us -> 608 us (0.85)
  the two profiles are of different devices: /device:TPU:49 before, /device:TPU:26 now
where the time goes in v2:
time: 608 us; the launch traced here: 599 us
  waiting for transfers between devices  150 us (25%)
  starting transfers between devices  125 us (21%)
  blocking collectives  95.2 us (16%)
  Pallas kernels  87.4 us (14%)
  local copies, waits for them, and re-layouts  60.1 us (10%)
  matrix products  43.2 us (7%)
  other arithmetic  20.2 us (3%)
  between operations  18.3 us (3%)
    all_to_all x3, blocking collectives, exchange(): return lax.all_to_all(rows, ALL, split_axis=0, concat_axis=0, tiled=True)  95.2 us
    ppermute x38, waiting for transfers between devices, shift(): lax.ppermute(value, axis, [(i, (i + step) % size) for i in range(size)])  67.9 us
    dot_general x15, matrix products, dot(): return lax.dot_general(a, b, dims, preferred_element_type=f32)  43.2 us
    ppermute x38, starting transfers between devices, shift(): lax.ppermute(value, axis, [(i, (i + step) % size) for i in range(size)])  42.7 us
    pallas_call x1, Pallas kernels, attend_backward(): pl.pallas_call(backward_kernel, grid_spec=pltpu.PrefetchScalarGridSpec(nu...  28.9 us
    unnamed x131, local copies, waits for them, and re-layouts  27.6 us
    all_to_all x1, waiting for transfers between devices, body(): lax.all_to_all(chip_out.astype(bf16).reshape(4, LOCAL, D), 'x', split_axi...  24.4 us
    ppermute x5, starting transfers between devices, body(): lax.ppermute(leaving[8 * i:8 * i + 8], ALL, perms[i])  22 us
  transfers between devices with their start and end apart: 57, of which 28 were waited for; matrix products, arithmetic and copies ran while one was open for 13% of the time, Pallas kernels for 4%

profile of v2, /device:TPU:26, one launch (start us, length us, event | category | flops | bytes accessed | tf_op | source)
XLA Modules:
  0.0 598.6 jit_solution(17623490352339867155)
XLA Ops:
  24.9 6.2 %collective-permute-start.4 = (bf16[8,2048]{1,0:T(8,128)(2,1)S(1)}, bf16[8,2048]{1,0:T(8,128)(2,1)S(1)}, u32[]{:S(2)}, u32[]{:S(2)}) collective-permute-start(bf16[8,2048]{1,0:T(8,128)(2,1)S(1)} %get-tuple-element.101), channel_id=1, source_target_pairs={{0,0},{13,1},{4,2},{17,3},{8,4},{21,5},{12,6},{25,7},{26,8},{38,9}... | collective-permute-start | bytes 98312 | tf_op jit(solution)/shard_map/ppermute | solution.py:694
  37.0 6.1 %collective-permute-done.5 = bf16[8,2048]{1,0:T(8,128)(2,1)S(1)} collective-permute-done((bf16[8,2048]{1,0:T(8,128)(2,1)S(1)}, bf16[8,2048]{1,0:T(8,128)(2,1)S(1)}, u32[]{:S(2)}, u32[]{:S(2)}) %collective-permute-start.5) | collective-permute-done | bytes 32800 | tf_op jit(solution)/shard_map/ppermute | solution.py:694
  62.5 7.0 %collective-permute-done.11 = bf16[4,40,2048]{2,1,0:T(8,128)(2,1)} collective-permute-done((bf16[4,40,2048]{2,1,0:T(8,128)(2,1)S(1)}, bf16[4,40,2048]{2,1,0:T(8,128)(2,1)}, u32[]{:S(2)}, u32[]{:S(2)}) %collective-permute-start.11) | collective-permute-done | bytes 655392 | tf_op jit(solution)/shard_map/ppermute | solution.py:115
  119.4 16.1 %attend_forward.1 = (bf16[1024,512]{1,0:T(8,128)(2,1)S(1)}, f32[4,4,8,256]{3,2,1,0:T(8,128)S(1)}) custom-call(s32[1]{0:T(128)} %bitcast.10.z_ref, bf16[1024,512]{1,0:T(8,128)(2,1)S(1)} %copy-done.38, bf16[2,4,1024,128]{3,2,1,0:T(8,128)(2,1)S(1)} %bitcast_dynamic-update-slice_fusion.kv_ref), custom_call_target="tpu_custom_call" | custom-call | flops 8999999488 | bytes 8388608 | tf_op jit(solution)/shard_map/attend_forward/pallas_call | solution.py:324
  145.3 8.1 %all-to-all-start = ((bf16[4,128,2048]{2,1,0:T(8,128)(2,1)}), bf16[4,128,2048]{2,1,0:T(8,128)(2,1)}, u32[]{:S(2)}, u32[]{:S(2)}) async-start(bf16[4,128,2048]{2,1,0:T(8,128)(2,1)} %bitcast.195), calls=%async_computation | async-start | bytes 4194304 | tf_op jit(solution)/shard_map/all_to_all | solution.py:719
  154.6 24.4 %all-to-all-done.moved_ref = bf16[4,128,2048]{2,1,0:T(8,128)(2,1)} async-done(((bf16[4,128,2048]{2,1,0:T(8,128)(2,1)}), bf16[4,128,2048]{2,1,0:T(8,128)(2,1)}, u32[]{:S(2)}, u32[]{:S(2)}) %all-to-all-start) | async-done | bytes 2097184 | tf_op jit(solution)/shard_map/all_to_all | solution.py:719
  184.2 37.2 %all_to_all.35.x_ref = bf16[128,56,128]{2,1,0:T(8,128)(2,1)S(1)} all-to-all(bf16[128,56,128]{2,1,0:T(8,128)(2,1)S(1)} %get-tuple-element.53), channel_id=1, replica_groups=mesh['y'=4,'x'=4,'z'=4,'c'=2] {'y','x','z','c'}, dimensions={0} | all-to-all | bytes 3670016 | tf_op jit(solution)/shard_map/all_to_all | solution.py:665
  221.5 9.7 %expert_forward.1 = (bf16[384,2048]{1,0:T(8,128)(2,1)S(1)}, f32[384,1536]{1,0:T(8,128)}, bf16[384,768]{1,0:T(8,128)(2,1)S(1)}, bf16[6144,128]{1,0:T(8,128)(2,1)S(1)}) custom-call(bf16[128,56,128]{2,1,0:T(8,128)(2,1)S(1)} %all_to_all.35.x_ref, bf16[2048,1536]{1,0:T(8,128)(2,1)} %bitcast.198, bf16[768,2048]{1,0:T(8,128)(2,1)} %bitcast.202), custom_call_target="tpu_custom_call" | custom-call | flops 3600000000 | bytes 17825792 | tf_op jit(solution)/shard_map/expert_forward/pallas_call | solution.py:514
  234.4 8.0 %all-to-all-start.2 = ((bf16[128,48,128]{2,1,0:T(8,128)(2,1)}), bf16[128,48,128]{2,1,0:T(8,128)(2,1)}, u32[]{:S(2)}, u32[]{:S(2)}) async-start(bf16[128,48,128]{2,1,0:T(8,128)(2,1)} %bitcast.176), calls=%async_computation.2 | async-start | bytes 3145728 | tf_op jit(solution)/shard_map/all_to_all | solution.py:665
  245.3 19.6 %all-to-all-done.2 = bf16[128,48,128]{2,1,0:T(8,128)(2,1)} async-done(((bf16[128,48,128]{2,1,0:T(8,128)(2,1)}), bf16[128,48,128]{2,1,0:T(8,128)(2,1)}, u32[]{:S(2)}, u32[]{:S(2)}) %all-to-all-start.2) | async-done | bytes 1572896 | tf_op jit(solution)/shard_map/all_to_all | solution.py:665
  272.7 28.9 %all_to_all.36 = bf16[128,48,128]{2,1,0:T(8,128)(2,1)S(1)} all-to-all(bf16[128,48,128]{2,1,0:T(8,128)(2,1)S(1)} %get-tuple-element.58), channel_id=1, replica_groups=mesh['y'=4,'x'=4,'z'=4,'c'=2] {'y','x','z','c'}, dimensions={0} | all-to-all | bytes 3145728 | tf_op jit(solution)/shard_map/all_to_all | solution.py:665
  301.5 10.2 %expert_backward.1 = (bf16[384,2048]{1,0:T(8,128)(2,1)S(1)}, bf16[384,1536]{1,0:T(8,128)(2,1)S(1)}, bf16[6144,128]{1,0:T(8,128)(2,1)S(1)}) custom-call(bf16[6144,128]{1,0:T(8,128)(2,1)S(1)} %bitcast.175, bf16[2048,1536]{1,0:T(8,128)(2,1)} %bitcast.199, bf16[768,2048]{1,0:T(8,128)(2,1)} %bitcast.203, f32[384,1536]{1,0:T(8,128)} %get-tuple-element.59.mixed_ref), custom_call_target="tpu_custom_call" | custom-call | flops 3600000000 | bytes 17825792 | tf_op jit(solution)/shard_map/expert_backward/pallas_call | solution.py:596
  311.8 29.1 %all_to_all.37 = bf16[128,48,128]{2,1,0:T(8,128)(2,1)S(1)} all-to-all(bf16[128,48,128]{2,1,0:T(8,128)(2,1)S(1)} %bitcast.177), channel_id=1, replica_groups=mesh['y'=4,'x'=4,'z'=4,'c'=2] {'y','x','z','c'}, dimensions={0} | all-to-all | bytes 3145728 | tf_op jit(solution)/shard_map/all_to_all | solution.py:665
  350.8 8.0 %collective-permute-done.22 = bf16[128,2048]{1,0:T(8,128)(2,1)} collective-permute-done((bf16[128,2048]{1,0:T(8,128)(2,1)}, bf16[128,2048]{1,0:T(8,128)(2,1)}, u32[]{:S(2)}, u32[]{:S(2)}) %collective-permute-start.22) | collective-permute-done | bytes 524320 | tf_op jit(solution)/shard_map/ppermute | solution.py:115
  394.6 28.9 %attend_backward.1 = (bf16[1024,512]{1,0:T(8,128)(2,1)S(1)}, bf16[2,4,1024,128]{3,2,1,0:T(8,128)(2,1)}) custom-call(s32[1]{0:T(128)} %bitcast.10.z_ref, bf16[1024,512]{1,0:T(8,128)(2,1)S(1)} %copy-done.39, bf16[2,4,1024,128]{3,2,1,0:T(8,128)(2,1)} %copy-done.3, bf16[4,4,128,256]{3,2,1,0:T(8,128)(2,1)S(1)} %bitcast.180, bf16[1024,512]{1,0:T(8,128)(2,1)S(1)} %bitcast.181, ...), custom_call_target="tpu_custom_call" | custom-call | flops 22000001024 | bytes 8388608 | tf_op jit(solution)/shard_map/attend_backward/pallas_call | solution.py:409
  429.8 11.4 %all-to-all-start.5 = ((bf16[4,1024,128]{2,1,0:T(8,128)(2,1)}), bf16[4,1024,128]{2,1,0:T(8,128)(2,1)}, u32[]{:S(2)}, u32[]{:S(2)}) async-start(bf16[4,1024,128]{2,1,0:T(8,128)(2,1)} %fusion.1), calls=%async_computation.5 | async-start | bytes 2097152 | tf_op jit(solution)/shard_map/all_to_all | solution.py:759
  445.0 11.7 %all-to-all-done.5.dkv_ref = bf16[4,1024,128]{2,1,0:T(8,128)(2,1)} async-done(((bf16[4,1024,128]{2,1,0:T(8,128)(2,1)}), bf16[4,1024,128]{2,1,0:T(8,128)(2,1)}, u32[]{:S(2)}, u32[]{:S(2)}) %all-to-all-start.5) | async-done | bytes 1048608 | tf_op jit(solution)/shard_map/all_to_all | solution.py:759
  471.8 6.8 %all-to-all-start.6 = ((bf16[16,40,2048]{2,1,0:T(8,128)(2,1)}), bf16[16,40,2048]{2,1,0:T(8,128)(2,1)}, u32[]{:S(2)}, u32[]{:S(2)}) async-start(bf16[16,40,2048]{2,1,0:T(8,128)(2,1)} %bitcast.204), calls=%async_computation.6 | async-start | bytes 5242880 | tf_op jit(solution)/shard_map/all_to_all | solution.py:146
  478.6 6.4 %convolution_bitcast_fusion.1 = f32[1,768,2048]{2,1,0:T(8,128)} fusion(bf16[384,768]{1,0:T(8,128)(2,1)} %copy-done.32, bf16[384,2048]{1,0:T(8,128)(2,1)} %copy-done.17), kind=kOutput, calls=%fused_computation.4 | convolution fusion | flops 1207959552 | bytes 8454144 | tf_op jit(solution)/shard_map/dot_general | solution.py:661
  485.0 6.6 %convolution_bitcast_fusion = f32[1,2048,1536]{2,1,0:T(8,128)} fusion(bf16[384,2048]{1,0:T(8,128)(2,1)S(1)} %copy-done.16, bf16[384,1536]{1,0:T(8,128)(2,1)S(1)} %copy-done.20), kind=kOutput, calls=%fused_computation | convolution fusion | flops 2415919104 | bytes 15335424 | tf_op jit(solution)/shard_map/dot_general | solution.py:661
  511.3 13.0 %collective-permute-done.36 = f32[35,128]{1,0:T(8,128)S(1)} collective-permute-done((f32[35,128]{1,0:T(8,128)S(1)}, f32[35,128]{1,0:T(8,128)S(1)}, u32[]{:S(2)}, u32[]{:S(2)}) %collective-permute-start.36) | collective-permute-done | bytes 17952 | tf_op jit(solution)/shard_map/ppermute | solution.py:115
  534.7 7.9 %collective-permute-done.43 = bf16[128,2048]{1,0:T(8,128)(2,1)S(1)} collective-permute-done((bf16[128,2048]{1,0:T(8,128)(2,1)S(1)}, bf16[128,2048]{1,0:T(8,128)(2,1)S(1)}, u32[]{:S(2)}, u32[]{:S(2)}) %collective-permute-start.43) | collective-permute-done | bytes 524320 | tf_op jit(solution)/shard_map/ppermute | solution.py:115
  557.7 8.2 %collective-permute-start.46 = (bf16[8,2048]{1,0:T(8,128)(2,1)S(1)}, bf16[8,2048]{1,0:T(8,128)(2,1)S(1)}, u32[]{:S(2)}, u32[]{:S(2)}) collective-permute-start(bf16[8,2048]{1,0:T(8,128)(2,1)S(1)} %get-tuple-element.97), channel_id=1, source_target_pairs={{0,0},{1,13},{2,4},{3,17},{4,8},{5,21},{6,12},{7,25},{8,26},{9,39}... | collective-permute-start | bytes 98312 | tf_op jit(solution)/shard_map/ppermute | solution.py:779
  578.0 12.1 %collective-permute-done.49 = f32[32,2048]{1,0:T(8,128)S(1)} collective-permute-done((f32[32,2048]{1,0:T(8,128)}, f32[32,2048]{1,0:T(8,128)S(1)}, u32[]{:S(2)}, u32[]{:S(2)}) %collective-permute-start.49) | collective-permute-done | bytes 262176 | tf_op jit(solution)/shard_map/ppermute | solution.py:754
  (333 shorter events, 249.0 us)
Async XLA Ops:
  7.2 80.2 %all-gather.5.cloned.1.call-start = ((), (), s32[]{:S(2)}) async-start(), calls=%async_computation.9 | async-start | bytes 4718592 | tf_op jit(solution)/shard_map/all_gather | solution.py:702
  10.6 127.2 %all-gather.3.cloned.1.call-start = ((), (), s32[]{:S(2)}) async-start(), calls=%async_computation.8 | async-start | bytes 2228224 | tf_op jit(solution)/shard_map/all_gather | solution.py:711
  11.0 22.1 %collective-permute-start.1 = (bf16[8,2048]{1,0:T(8,128)(2,1)S(1)}, bf16[8,2048]{1,0:T(8,128)(2,1)S(1)}, u32[]{:S(2)}, u32[]{:S(2)}) collective-permute-start(bf16[8,2048]{1,0:T(8,128)(2,1)S(1)} %get-tuple-element.104), channel_id=1, source_target_pairs={{0,0},{13,1},{4,2},{17,3},{8,4},{21,5},{12,6},{115,7},{25,8},{38,9... | collective-permute-start | bytes 98312 | tf_op jit(solution)/shard_map/ppermute | solution.py:694
  17.1 16.0 %collective-permute-start.2 = (bf16[8,2048]{1,0:T(8,128)(2,1)S(1)}, bf16[8,2048]{1,0:T(8,128)(2,1)S(1)}, u32[]{:S(2)}, u32[]{:S(2)}) collective-permute-start(bf16[8,2048]{1,0:T(8,128)(2,1)S(1)} %get-tuple-element.103), channel_id=1, source_target_pairs={{0,0},{12,1},{4,2},{16,3},{8,4},{20,5},{102,6},{24,7},{25,8},{38,9... | collective-permute-start | bytes 98312 | tf_op jit(solution)/shard_map/ppermute | solution.py:694
  56.0 13.6 %collective-permute-start.11 = (bf16[4,40,2048]{2,1,0:T(8,128)(2,1)S(1)}, bf16[4,40,2048]{2,1,0:T(8,128)(2,1)}, u32[]{:S(2)}, u32[]{:S(2)}) collective-permute-start(bf16[4,40,2048]{2,1,0:T(8,128)(2,1)S(1)} %fusion.24), channel_id=1, source_target_pairs={{0,6},{2,0},{4,2},{6,4},{1,7},{3,1},{5,3},{7,5},{8,14},{10,8},{12,... | collective-permute-start | bytes 1966088 | tf_op jit(solution)/shard_map/ppermute | solution.py:115
  56.1 17.6 %collective-permute-start.10 = (bf16[4,40,2048]{2,1,0:T(8,128)(2,1)S(1)}, bf16[4,40,2048]{2,1,0:T(8,128)(2,1)}, u32[]{:S(2)}, u32[]{:S(2)}) collective-permute-start(bf16[4,40,2048]{2,1,0:T(8,128)(2,1)S(1)} %fusion.24), channel_id=1, source_target_pairs={{0,2},{2,4},{4,6},{6,0},{1,3},{3,5},{5,7},{7,1},{8,10},{10,12},{12... | collective-permute-start | bytes 1966088 | tf_op jit(solution)/shard_map/ppermute | solution.py:115
  58.1 25.5 %collective-permute-start = (bf16[32,2048]{1,0:T(8,128)(2,1)}, bf16[32,2048]{1,0:T(8,128)(2,1)S(1)}, u32[]{:S(2)}, u32[]{:S(2)}) collective-permute-start(bf16[32,2048]{1,0:T(8,128)(2,1)} %param.20), channel_id=1, source_target_pairs={{0,0},{1,32},{2,64},{3,96},{4,2},{5,34},{6,66},{7,98},{8,4},{9,36}... | collective-permute-start | bytes 393224 | tf_op jit(solution)/shard_map/ppermute | solution.py:709
  145.3 33.6 %all-to-all-start = ((bf16[4,128,2048]{2,1,0:T(8,128)(2,1)}), bf16[4,128,2048]{2,1,0:T(8,128)(2,1)}, u32[]{:S(2)}, u32[]{:S(2)}) async-start(bf16[4,128,2048]{2,1,0:T(8,128)(2,1)} %bitcast.195), calls=%async_computation | async-start | bytes 4194304 | tf_op jit(solution)/shard_map/all_to_all | solution.py:719
  234.4 30.5 %all-to-all-start.2 = ((bf16[128,48,128]{2,1,0:T(8,128)(2,1)}), bf16[128,48,128]{2,1,0:T(8,128)(2,1)}, u32[]{:S(2)}, u32[]{:S(2)}) async-start(bf16[128,48,128]{2,1,0:T(8,128)(2,1)} %bitcast.176), calls=%async_computation.2 | async-start | bytes 3145728 | tf_op jit(solution)/shard_map/all_to_all | solution.py:665
  345.3 13.5 %collective-permute-start.22 = (bf16[128,2048]{1,0:T(8,128)(2,1)}, bf16[128,2048]{1,0:T(8,128)(2,1)}, u32[]{:S(2)}, u32[]{:S(2)}) collective-permute-start(bf16[128,2048]{1,0:T(8,128)(2,1)} %get-tuple-element.65), channel_id=1, source_target_pairs={{0,24},{8,0},{16,8},{24,16},{1,25},{9,1},{17,9},{25,17},{2,26},{10... | collective-permute-start | bytes 1572872 | tf_op jit(solution)/shard_map/ppermute | solution.py:115
  346.6 14.4 %collective-permute-start.21 = (bf16[128,2048]{1,0:T(8,128)(2,1)}, bf16[128,2048]{1,0:T(8,128)(2,1)}, u32[]{:S(2)}, u32[]{:S(2)}) collective-permute-start(bf16[128,2048]{1,0:T(8,128)(2,1)} %get-tuple-element.65), channel_id=1, source_target_pairs={{0,8},{8,16},{16,24},{24,0},{1,9},{9,17},{17,25},{25,1},{2,10},{10... | collective-permute-start | bytes 1572872 | tf_op jit(solution)/shard_map/ppermute | solution.py:115
  425.3 66.3 %collective-permute-start.29 = (bf16[640,2048]{1,0:T(8,128)(2,1)S(1)}, bf16[640,2048]{1,0:T(8,128)(2,1)}, u32[]{:S(2)}, u32[]{:S(2)}) collective-permute-start(bf16[640,2048]{1,0:T(8,128)(2,1)S(1)} %bitcast.172), channel_id=1, source_target_pairs={{0,1},{1,0},{2,3},{3,2},{4,5},{5,4},{6,7},{7,6},{8,9},{9,8},{10,11... | collective-permute-start | bytes 7864328 | tf_op jit(solution)/shard_map/ppermute | solution.py:115
  429.8 26.9 %all-to-all-start.5 = ((bf16[4,1024,128]{2,1,0:T(8,128)(2,1)}), bf16[4,1024,128]{2,1,0:T(8,128)(2,1)}, u32[]{:S(2)}, u32[]{:S(2)}) async-start(bf16[4,1024,128]{2,1,0:T(8,128)(2,1)} %fusion.1), calls=%async_computation.5 | async-start | bytes 2097152 | tf_op jit(solution)/shard_map/all_to_all | solution.py:759
  441.2 133.0 %reduce-scatter.2.cloned.1.call-start = ((), (), s32[]{:S(2)}) async-start(), calls=%async_computation.10 | async-start | bytes 4456448 | tf_op jit(solution)/shard_map/reduce_scatter | solution.py:753
  467.6 24.0 %collective-permute-start.28 = (bf16[512,640]{1,0:T(8,128)(2,1)}, bf16[512,640]{1,0:T(8,128)(2,1)}, u32[]{:S(2)}, u32[]{:S(2)}) collective-permute-start(bf16[512,640]{1,0:T(8,128)(2,1)} %bitcast.50), channel_id=1, source_target_pairs={{0,1},{1,0},{2,3},{3,2},{4,5},{5,4},{6,7},{7,6},{8,9},{9,8},{10,11... | collective-permute-start | bytes 1966088 | tf_op jit(solution)/shard_map/ppermute | solution.py:115
  471.8 73.9 %all-to-all-start.6 = ((bf16[16,40,2048]{2,1,0:T(8,128)(2,1)}), bf16[16,40,2048]{2,1,0:T(8,128)(2,1)}, u32[]{:S(2)}, u32[]{:S(2)}) async-start(bf16[16,40,2048]{2,1,0:T(8,128)(2,1)} %bitcast.204), calls=%async_computation.6 | async-start | bytes 5242880 | tf_op jit(solution)/shard_map/all_to_all | solution.py:146
  504.1 25.2 %collective-permute-start.40 = (bf16[64,2048]{1,0:T(8,128)(2,1)S(1)}, bf16[64,2048]{1,0:T(8,128)(2,1)S(1)}, u32[]{:S(2)}, u32[]{:S(2)}) collective-permute-start(bf16[64,2048]{1,0:T(8,128)(2,1)S(1)} %get-tuple-element.93), channel_id=1, source_target_pairs={{0,8},{8,16},{16,24},{24,0},{1,9},{9,17},{17,25},{25,1},{2,10},{10... | collective-permute-start | bytes 786440 | tf_op jit(solution)/shard_map/ppermute | solution.py:115
  506.2 23.2 %collective-permute-start.42 = (bf16[64,2048]{1,0:T(8,128)(2,1)S(1)}, bf16[64,2048]{1,0:T(8,128)(2,1)S(1)}, u32[]{:S(2)}, u32[]{:S(2)}) collective-permute-start(bf16[64,2048]{1,0:T(8,128)(2,1)S(1)} %get-tuple-element.94), channel_id=1, source_target_pairs={{0,24},{8,0},{16,8},{24,16},{1,25},{9,1},{17,9},{25,17},{2,26},{10... | collective-permute-start | bytes 786440 | tf_op jit(solution)/shard_map/ppermute | solution.py:115
  506.5 17.9 %collective-permute-start.36 = (f32[35,128]{1,0:T(8,128)S(1)}, f32[35,128]{1,0:T(8,128)S(1)}, u32[]{:S(2)}, u32[]{:S(2)}) collective-permute-start(f32[35,128]{1,0:T(8,128)S(1)} %add_add_fusion.2), channel_id=1, source_target_pairs={{0,64},{32,96},{64,0},{96,32},{1,65},{33,97},{65,1},{97,33},{2,66}... | collective-permute-start | bytes 53768 | tf_op jit(solution)/shard_map/ppermute | solution.py:115
  508.0 16.3 %collective-permute-start.35 = (f32[35,128]{1,0:T(8,128)S(1)}, f32[35,128]{1,0:T(8,128)S(1)}, u32[]{:S(2)}, u32[]{:S(2)}) collective-permute-start(f32[35,128]{1,0:T(8,128)S(1)} %add_add_fusion.2), channel_id=1, source_target_pairs={{0,96},{32,0},{64,32},{96,64},{1,97},{33,1},{65,33},{97,65},{2,98}... | collective-permute-start | bytes 53768 | tf_op jit(solution)/shard_map/ppermute | solution.py:115
  508.0 16.3 %collective-permute-start.34 = (f32[35,128]{1,0:T(8,128)S(1)}, f32[35,128]{1,0:T(8,128)S(1)}, u32[]{:S(2)}, u32[]{:S(2)}) collective-permute-start(f32[35,128]{1,0:T(8,128)S(1)} %add_add_fusion.2), channel_id=1, source_target_pairs={{0,32},{32,64},{64,96},{96,0},{1,33},{33,65},{65,97},{97,1},{2,34}... | collective-permute-start | bytes 53768 | tf_op jit(solution)/shard_map/ppermute | solution.py:115
  548.4 22.6 %collective-permute-start.44 = (bf16[8,2048]{1,0:T(8,128)(2,1)S(1)}, bf16[8,2048]{1,0:T(8,128)(2,1)S(1)}, u32[]{:S(2)}, u32[]{:S(2)}) collective-permute-start(bf16[8,2048]{1,0:T(8,128)(2,1)S(1)} %get-tuple-element.99), channel_id=1, source_target_pairs={{0,0},{1,13},{2,4},{3,17},{4,8},{5,21},{6,12},{7,115},{8,25},{9,38... | collective-permute-start | bytes 98312 | tf_op jit(solution)/shard_map/ppermute | solution.py:779
  555.8 15.2 %collective-permute-start.45 = (bf16[8,2048]{1,0:T(8,128)(2,1)S(1)}, bf16[8,2048]{1,0:T(8,128)(2,1)S(1)}, u32[]{:S(2)}, u32[]{:S(2)}) collective-permute-start(bf16[8,2048]{1,0:T(8,128)(2,1)S(1)} %get-tuple-element.98), channel_id=1, source_target_pairs={{0,0},{1,12},{2,4},{3,16},{4,8},{5,20},{6,102},{7,24},{8,25},{9,38... | collective-permute-start | bytes 98312 | tf_op jit(solution)/shard_map/ppermute | solution.py:779
  574.1 16.0 %collective-permute-start.49 = (f32[32,2048]{1,0:T(8,128)}, f32[32,2048]{1,0:T(8,128)S(1)}, u32[]{:S(2)}, u32[]{:S(2)}) collective-permute-start(f32[32,2048]{1,0:T(8,128)} %reduce-scatter.2.cloned.1.call-done), channel_id=1, source_target_pairs={{0,0},{32,1},{64,2},{96,3},{2,4},{34,5},{66,6},{98,7},{4,8},{36,9}... | collective-permute-start | bytes 786440 | tf_op jit(solution)/shard_map/ppermute | solution.py:754
  (91 other events, 650.5 us)
Sparse Core Ops, SparseCore 0:
  10.7 34.5 all-gather.4
  84.4 46.6 all-gather.2
  445.3 106.9 reduce-scatter.1

commit v3 on v2

--- a/solution.py
+++ b/solution.py
@@ -38,40 +38,53 @@
     return ((y * 4 + x) * 4 + z) * 2 + c
 
 
-def colour_edges(edges, count, degree):
-    left = {}
-    for source, target, tag in edges:
-        left.setdefault(source, []).append((target, tag))
-    rounds = []
-    for _ in range(degree):
-        match = {}
-
-        def place(source, seen):
-            for number, (target, _) in enumerate(left[source]):
-                if target in seen:
-                    continue
-                seen.add(target)
-                if target not in match or place(match[target][0], seen):
-                    match[target] = (source, number)
-                    return True
-            return False
-
-        for source in range(count):
-            place(source, set())
-        done = []
-        for target, (source, number) in sorted(match.items()):
-            done.append((source, target, left[source][number][1]))
-        for target, (source, number) in match.items():
-            left[source][number] = None
-        for source in left:
-            left[source] = [entry for entry in left[source] if entry is not None]
-        rounds.append(done)
-    return rounds
+def alternate(edges):
+    at = {}
+    for number, (source, target) in enumerate(edges):
+        at.setdefault(("s", source), []).append(number)
+        at.setdefault(("t", target), []).append(number)
+    colour = {}
+    ends = sorted(node for node in at if len(at[node]) == 1)
+    for node in ends + sorted(at):
+        for number in at[node]:
+            here, now = node, 0
+            while number is not None and number not in colour:
+                colour[number] = now
+                source, target = edges[number]
+                here = ("t", target) if here == ("s", source) else ("s", source)
+                now = 1 - now
+                number = next((other for other in at[here] if other not in colour), None)
+    return [[n for n in range(len(edges)) if colour[n] == side] for side in (0, 1)]
+
+
+def few_rounds(edges):
+    degree = {}
+    for source, target in edges:
+        for node in (("s", source), ("t", target)):
+            degree[node] = degree.get(node, 0) + 1
+    full = sorted(node for node in degree if degree[node] == 3)
+
+    def cover(number, taken, picked):
+        if number == len(full):
+            return picked
+        if full[number] in taken:
+            return cover(number + 1, taken, picked)
+        for n, (source, target) in enumerate(edges):
+            nodes = {("s", source), ("t", target)}
+            if full[number] in nodes and not nodes & taken:
+                found = cover(number + 1, taken | nodes, picked + [n])
+                if found is not None:
+                    return found
+        return None
+
+    last = cover(0, frozenset(), [])
+    rest = [n for n in range(len(edges)) if n not in last]
+    return [[rest[i] for i in side] for side in alternate([edges[n] for n in rest])] + [last]
 
 
 @functools.cache
 def in_plan():
-    edges = []
+    moves = {}
     for x in range(4):
         for c in range(2):
             group = 2 * x + c
@@ -79,24 +92,26 @@
             wanted += [512 + 64 * c + 16 * x + s for s in range(16)]
             for s, part in enumerate(wanted):
                 slot, place = s // 5, s % 5
-                target = device_of(slot % 4, x, slot // 4, c)
-                edges.append((part // 5, target, (part % 5, place)))
-    rounds = colour_edges(edges, DEVICES, 5)
-    leaves = np.zeros((DEVICES, 5, 8), np.int32)
+                pair = (part // 5, device_of(slot % 4, x, slot // 4, c))
+                moves.setdefault(pair, []).append((part % 5, place))
+    edges = sorted(moves)
+    leaves = np.full((DEVICES, 15, 8), 40, np.int32)
     arrives = np.zeros((DEVICES, 5, 8), np.int32)
     perms = []
-    for number, done in enumerate(rounds):
-        perms.append([(source, target) for source, target, _ in done])
-        for source, target, (part, place) in done:
-            leaves[source, number] = part * 8 + np.arange(8)
-            arrives[target, place] = number * 8 + np.arange(8)
-    return perms, leaves.reshape(DEVICES, 40), arrives.reshape(DEVICES, 40)
-
-
-def row_picker(table, me):
+    for number, chosen in enumerate(few_rounds(edges)):
+        perms.append([edges[n] for n in chosen])
+        for n in chosen:
+            source, target = edges[n]
+            for i, (part, place) in enumerate(moves[edges[n]]):
+                leaves[source, 5 * number + i] = part * 8 + np.arange(8)
+                arrives[target, place] = (5 * number + i) * 8 + np.arange(8)
+    return perms, leaves.reshape(DEVICES, 120), arrives.reshape(DEVICES, 40)
+
+
+def row_picker(table, me, count):
     mine = jnp.arange(DEVICES, dtype=jnp.int32)[:, None] == me
     chosen = jnp.sum(jnp.where(mine, jnp.asarray(table), 0), axis=0)
-    return (chosen[:, None] == jnp.arange(40, dtype=jnp.int32)[None, :]).astype(bf16)
+    return (chosen[:, None] == jnp.arange(count, dtype=jnp.int32)[None, :]).astype(bf16)
 
 
 def out_perm():
@@ -106,7 +121,7 @@
             for z in range(4):
                 for c in range(2):
                     slot = device_of(y, x, z, c) % 16
-                    perm.append((device_of(y, x, z, c), device_of(slot % 4, y, slot // 4, x // 2)))
+                    perm.append((device_of(y, x, z, c), device_of(slot // 4, y, slot % 4, x // 2)))
     return perm
 
 
@@ -117,10 +132,10 @@
 
 def ring_gather(value, axis):
     index = lax.axis_index(axis)
-    half = value.shape[0] // 2
+    half = value.shape[-1] // 2
     before = shift(value, axis, 1)
     after = shift(value, axis, -1)
-    far = jnp.concatenate([shift(before[:half], axis, 1), shift(after[half:], axis, -1)], axis=0)
+    far = jnp.concatenate([shift(before[..., :half], axis, 1), shift(after[..., half:], axis, -1)], axis=-1)
     out = jnp.zeros((4,) + value.shape, value.dtype)
     for offset, block in ((0, value), (3, before), (1, after), (2, far)):
         out = lax.dynamic_update_index_in_dim(out, block, (index + offset) % 4, 0)
@@ -135,11 +150,9 @@
     return lax.dynamic_update_index_in_dim(out, other, 1 - index, 0)
 
 
-def small_sum(value):
-    value = value + shift(value, "c", 1)
-    for axis in ("x", "y", "z"):
-        value = value + shift(value, axis, 1) + shift(value, axis, -1) + shift(value, axis, 2)
-    return value
+def sum_over(value, axis):
+    steps = (1,) if axis == "c" else (1, -1, 2)
+    return sum([shift(value, axis, step) for step in steps], value)
 
 
 def scatter_sum(value, axes, count):
@@ -147,20 +160,39 @@
     return jnp.sum(moved.astype(f32), axis=0)
 
 
-def ring_scatter(value, axis):
-    index = lax.axis_index(axis)
-    half = value.shape[1] // 2
-
-    def block(offset):
-        return lax.dynamic_index_in_dim(value, (index + offset) % 4, 0, keepdims=False)
-
-    far = block(2).astype(bf16)
-    from_left = shift(far[:half], axis, 1).astype(f32)
-    from_right = shift(far[half:], axis, -1).astype(f32)
-    right, left = block(1).astype(f32), block(3).astype(f32)
-    right = jnp.concatenate([right[:half] + from_left, right[half:]], axis=0).astype(bf16)
-    left = jnp.concatenate([left[:half], left[half:] + from_right], axis=0).astype(bf16)
-    return block(0).astype(f32) + shift(right, axis, 1).astype(f32) + shift(left, axis, -1).astype(f32)
+tie = lax.optimization_barrier
+
+
+class RingSum:
+    def __init__(self, value, axis):
+        self.value, self.axis = value, axis
+        self.index = lax.axis_index(axis)
+        half = value.shape[-1] // 2
+        far = self.block(2).astype(bf16)
+        from_left = shift(far[..., :half], axis, 1).astype(f32)
+        from_right = shift(far[..., half:], axis, -1).astype(f32)
+        right, left = self.block(1).astype(f32), self.block(3).astype(f32)
+        right = jnp.concatenate([right[..., :half] + from_left, right[..., half:]], axis=-1).astype(bf16)
+        left = jnp.concatenate([left[..., :half], left[..., half:] + from_right], axis=-1).astype(bf16)
+        self.both = right, left
+
+    def block(self, offset):
+        return lax.dynamic_index_in_dim(self.value, (self.index + offset) % 4, 0, keepdims=False)
+
+    def tie(self, *arrays):
+        *arrays, right, left = tie((*arrays, *self.both))
+        self.both = right, left
+        return arrays
+
+    def total(self):
+        right, left = self.both
+        right, left = shift(right, self.axis, 1), shift(left, self.axis, -1)
+        return self.block(0).astype(f32) + right.astype(f32) + left.astype(f32)
+
+
+def spread(value, axes, count):
+    copies = jnp.broadcast_to(value[None], (count,) + value.shape)
+    return lax.all_to_all(copies, axes, split_axis=0, concat_axis=0, tiled=True)
 
 
 def rotation(position):
@@ -233,56 +265,37 @@
     )(core, rows, weights, cosine, sine, q_gain, k_gain)
 
 
-def project_back_kernel(core_ref, dq_ref, dkv_ref, p_ref, cos_ref, sin_ref, qg_ref, kg_ref, gp_ref, qt_ref, kt_ref):
+def project_back_kernel(grad_ref, p_ref, cos_ref, sin_ref, gain_ref, gp_ref, term_ref):
     @pl.when(pl.program_id(0) == 0)
     def _():
-        qt_ref[...] = jnp.zeros_like(qt_ref)
-        kt_ref[...] = jnp.zeros_like(kt_ref)
-
-    cosine, sine = cos_ref[...], sin_ref[...]
-    for head in range(HEADS):
+        term_ref[...] = jnp.zeros_like(term_ref)
+
+    for head in range(gp_ref.shape[1] // HD):
         lanes = slice(head * HD, (head + 1) * HD)
-        back, term = head_rotate_back(dq_ref[:, lanes].astype(f32), p_ref[:, lanes], qg_ref[...], cosine, sine)
+        grad = grad_ref[:, lanes].astype(f32)
+        back, term = head_rotate_back(grad, p_ref[:, lanes], gain_ref[...], cos_ref[...], sin_ref[...])
         gp_ref[:, lanes] = back.astype(bf16)
-        qt_ref[...] += jnp.sum(term, axis=0, keepdims=True)
-    lanes = slice(HEADS * HD, (HEADS + 1) * HD)
-    grad = jnp.sum(dkv_ref[...].astype(f32), axis=0)
-    back, term = head_rotate_back(grad, p_ref[:, lanes], kg_ref[...], cosine, sine)
-    gp_ref[:, lanes] = jnp.where(core_ref[0] == 0, back, grad).astype(bf16)
-    kt_ref[...] += jnp.where(core_ref[0] == 0, jnp.sum(term, axis=0, keepdims=True), 0.0)
-
-
-def project_back(core, dq, dkv, projected, cosine, sine, q_gain, k_gain):
-    wide = HEADS * HD
+        term_ref[...] += jnp.sum(term, axis=0, keepdims=True)
+
+
+def project_back(grad, projected, cosine, sine, gain, place):
+    wide = grad.shape[1]
     return pl.pallas_call(
         project_back_kernel,
-        grid_spec=pltpu.PrefetchScalarGridSpec(
-            num_scalar_prefetch=1,
-            grid=(4,),
-            in_specs=[
-                pl.BlockSpec((PIECE, wide), lambda i, c: (i, 0)),
-                pl.BlockSpec((4, PIECE, HD), lambda i, c: (0, i, 0)),
-                pl.BlockSpec((PIECE, wide + HD), lambda i, c: (i, 0)),
-                pl.BlockSpec((PIECE, HD), lambda i, c: (i, 0)),
-                pl.BlockSpec((PIECE, HD), lambda i, c: (i, 0)),
-                pl.BlockSpec((1, HD), lambda i, c: (0, 0)),
-                pl.BlockSpec((1, HD), lambda i, c: (0, 0)),
-            ],
-            out_specs=[
-                pl.BlockSpec((PIECE, wide + HD), lambda i, c: (i, 0)),
-                pl.BlockSpec((1, HD), lambda i, c: (0, 0)),
-                pl.BlockSpec((1, HD), lambda i, c: (0, 0)),
-            ],
-        ),
-        out_shape=[
-            jax.ShapeDtypeStruct((GROUP, wide + HD), bf16),
-            jax.ShapeDtypeStruct((1, HD), f32),
-            jax.ShapeDtypeStruct((1, HD), f32),
+        grid=(4,),
+        in_specs=[
+            pl.BlockSpec((PIECE, wide), lambda i: (i, 0)),
+            pl.BlockSpec((PIECE, wide), lambda i: (i, place)),
+            pl.BlockSpec((PIECE, HD), lambda i: (i, 0)),
+            pl.BlockSpec((PIECE, HD), lambda i: (i, 0)),
+            pl.BlockSpec((1, HD), lambda i: (0, 0)),
         ],
+        out_specs=[pl.BlockSpec((PIECE, wide), lambda i: (i, 0)), pl.BlockSpec((1, HD), lambda i: (0, 0))],
+        out_shape=[jax.ShapeDtypeStruct((GROUP, wide), bf16), jax.ShapeDtypeStruct((1, HD), f32)],
         compiler_params=pltpu.CompilerParams(vmem_limit_bytes=40 * 2**20),
-        cost_estimate=pl.CostEstimate(flops=10**7, bytes_accessed=7 * 2**20, transcendentals=10**4),
+        cost_estimate=pl.CostEstimate(flops=wide * 10**4, bytes_accessed=wide * 10**4, transcendentals=10**4),
         name="project_back",
-    )(core, dq, dkv, projected, cosine, sine, q_gain, k_gain)
+    )(grad, projected, cosine, sine, gain)
 
 
 def forward_kernel(z_ref, q_ref, kv_ref, o_ref, lse_ref, total):
@@ -346,13 +359,16 @@
     )(z, queries, keys_values)
 
 
-def backward_kernel(z_ref, q_ref, kv_ref, kt_ref, go_ref, o_ref, lse_ref, dq_ref, dkv_ref, dqt, dkv):
+def backward_kernel(z_ref, q_ref, kv_ref, go_ref, o_ref, lse_ref, dq_ref, dkv_ref, dqt, dkv, kt):
     piece = pl.program_id(0)
     z = z_ref[0]
 
     @pl.when(piece == 0)
     def _():
         dkv[...] = jnp.zeros_like(dkv)
+        for block in range(4):
+            for part in range(4):
+                kt[block, part] = jnp.transpose(kv_ref[0, block, part * PIECE : (part + 1) * PIECE, :])
 
     dqt[...] = jnp.zeros_like(dqt)
     rows = HEADS * PIECE
@@ -371,7 +387,7 @@
         block = chunk % 4
         keys = kv_ref[0, block, pl.ds(row, PIECE), :]
         values = kv_ref[1, block, pl.ds(row, PIECE), :]
-        turned = kt_ref[block, chunk // 4]
+        turned = kt[block, chunk // 4]
         scores = lax.dot_general(keys, queries, NT, preferred_element_type=f32)
         weights = jnp.exp2(scores * (SCALE * LOG2E) - sums)
         if masked:
@@ -403,7 +419,6 @@
 
 
 def attend_backward(z, queries, keys_values, backs, outs, lse):
-    turned = keys_values[0].reshape(4, 4, PIECE, HD).transpose(0, 1, 3, 2)
     heads_spec = pl.BlockSpec((PIECE, HEADS * HD), lambda i, z: (i, 0))
     whole = pl.BlockSpec((2, 4, GROUP, HD), lambda i, z: (0, 0, 0, 0))
     return pl.pallas_call(
@@ -414,7 +429,6 @@
             in_specs=[
                 heads_spec,
                 whole,
-                pl.BlockSpec((4, 4, HD, PIECE), lambda i, z: (0, 0, 0, 0)),
                 heads_spec,
                 heads_spec,
                 pl.BlockSpec((HEADS, 1, 8, PIECE), lambda i, z: (0, i, 0, 0)),
@@ -423,6 +437,7 @@
             scratch_shapes=[
                 pltpu.VMEM((HD, HEADS * PIECE), f32),
                 pltpu.VMEM((2, 4, GROUP, HD), f32),
+                pltpu.VMEM((4, 4, HD, PIECE), bf16),
             ],
         ),
         out_shape=[
@@ -432,7 +447,7 @@
         compiler_params=pltpu.CompilerParams(vmem_limit_bytes=48 * 2**20),
         cost_estimate=pl.CostEstimate(flops=22 * 10**9, bytes_accessed=8 * 2**20, transcendentals=10**7),
         name="attend_backward",
-    )(z, queries, keys_values, turned, backs, outs, lse)
+    )(z, queries, keys_values, backs, outs, lse)
 
 
 ROWS = EXPERTS * CAP
@@ -688,31 +703,35 @@
     q_gain_row, k_gain_row = q_gain[None, :], k_gain[None, :]
     mask = valid.astype(f32)
 
-    perms, leaves, arrives = in_plan()
-    leave, arrive = row_picker(leaves, me), row_picker(arrives, me)
-    leaving = dot(leave, w_in, NT).astype(bf16)
-    arrived = jnp.concatenate([lax.ppermute(leaving[8 * i : 8 * i + 8], ALL, perms[i]) for i in range(5)], axis=0)
-    in_slot = dot(arrive, arrived).astype(bf16)
-    in_mine = ring_gather(ring_gather(in_slot, "y"), "z").reshape(640, D)
-
     inputs = tokens.astype(f32)
     r1 = lax.rsqrt(jnp.mean(inputs * inputs, axis=-1, keepdims=True) + epsilon)
     n1 = inputs * r1
     h1 = (n1 * gain1).astype(bf16)
-    h1_group = lax.all_gather(h1, ("x", "c"), axis=0, tiled=True)
+    h1_mine = ring_gather(h1, "x").reshape(4 * LOCAL, D)
+    h1_group = core_join(h1_mine, shift(h1_mine, "c", 1), c)
 
     places = jnp.arange(4, dtype=jnp.int32)[:, None] * 1024 + z * PIECE + jnp.arange(PIECE, dtype=jnp.int32)[None, :]
     cosine, sine = rotation(places.reshape(GROUP).astype(f32))
+
+    perms, leaves, arrives = in_plan()
+    leave, arrive = row_picker(leaves, me, 40), row_picker(arrives, me, 120)
+    leaving = dot(leave, w_in, NT).astype(bf16)
+    arrived = jnp.concatenate([lax.ppermute(leaving[40 * i : 40 * i + 40], ALL, perms[i]) for i in range(3)], axis=0)
+    out_slot = lax.ppermute(w_out, ALL, out_perm())
+    arrived, out_slot = lax.optimization_barrier((arrived, out_slot))
+    in_slot = dot(arrive, arrived).astype(bf16)
+    in_slot, cosine, sine = lax.optimization_barrier((in_slot, cosine, sine))
+    in_some, out_some = ring_gather(in_slot, "y"), ring_gather(out_slot, "z")
+    in_some, out_some = tie((in_some, out_some))
+    out_mine = ring_gather(out_some, "y").reshape(HEADS * HD, D)
+    in_mine = ring_gather(in_some, "z").reshape(640, D)
+
     projected, queries, key_or_value = project(c_array, h1_group, in_mine, cosine, sine, q_gain_row, k_gain_row)
     keys_values = core_gather(ring_gather(key_or_value, "z"))
 
-    out_slot = lax.ppermute(w_out, ALL, out_perm())
-    out_slot, _ = lax.optimization_barrier((out_slot, in_mine))
-    out_mine = lax.all_gather(out_slot, ("z", "y"), axis=0, tiled=True)
-
+
+    out_other = shift(out_mine, "c", 1)
     attended, lse = attend_forward(z_array, queries, keys_values)
-    out_mine, attended = lax.optimization_barrier((out_mine, attended))
-    out_other = shift(out_mine, "c", 1)
     attended_mine, attended_other = core_halves(attended, c)
     attended_there = shift(attended_other, "c", 1)
     chip_out = dot(attended_mine, out_mine) + dot(attended_there, out_other)
@@ -740,6 +759,9 @@
     )
     back_out, back_mixed, gh = expert_backward(exchange(sent_back).reshape(TILES, 128), first, second, mixed)
     back_rows = exchange(gh.reshape(EXPERTS, CAP * CHUNKS, 128)).reshape(TILES, 128)
+    second_gradient = dot(hidden, back_out, TN)
+    first_gradient = dot(rows, back_mixed, TN)
+    back_rows, first_gradient, second_gradient = lax.optimization_barrier((back_rows, first_gradient, second_gradient))
     g2, gb, gain2_term = collect(slots, back_rows, x2, g3, gain2_row)
 
     gb_mine = ring_gather(gb, "x").reshape(4 * LOCAL, D)
@@ -747,36 +769,50 @@
     back_there = dot(gb_mine, out_other, NT).astype(bf16)
     backs = core_join(back_mine, shift(back_there, "c", 1), c)
     gb_other = shift(gb_mine, "c", 1)
-    out_partial = dot(attended_mine, gb_mine, TN) + dot(attended_other, gb_other, TN)
+    out_partial = (dot(attended_mine, gb_mine, TN) + dot(attended_other, gb_other, TN)).astype(bf16)
     backs, out_partial = lax.optimization_barrier((backs, out_partial))
     dq, dkv = attend_backward(z_array, queries, keys_values, backs, attended, lse)
-    out_summed = lax.psum_scatter(out_partial, ("z", "y"), scatter_dimension=0, tiled=True)
-    out_gradient = lax.ppermute(out_summed, ALL, [(b, a) for a, b in out_perm()])
+    out_moved = lax.all_to_all(out_partial.reshape(16, 32, D), ("y", "z"), split_axis=0, concat_axis=0, tiled=True)
+    dkv, out_moved = tie((dkv, out_moved))
 
     own = lax.dynamic_index_in_dim(dkv, c, 0, keepdims=False)
     there = lax.dynamic_index_in_dim(dkv, 1 - c, 0, keepdims=False)
     chip_kv = (own.astype(f32) + shift(there, "c", 1).astype(f32)).astype(bf16)
-    back_kv = lax.all_to_all(chip_kv, "z", split_axis=0, concat_axis=0, tiled=True)
-    gp, q_term, k_term = project_back(c_array, dq, back_kv, projected, cosine, sine, q_gain_row, k_gain_row)
-
-    rows, back_mixed, hidden, back_out, gp = lax.optimization_barrier((rows, back_mixed, hidden, back_out, gp))
-    second_gradient = dot(hidden, back_out, TN)
-    first_gradient = dot(rows, back_mixed, TN)
-    in_partial = dot(gp, h1_group, TN).astype(bf16).reshape(16, 40, D)
-    in_summed = scatter_sum(in_partial, ("z", "y"), 16)
-
+
+    dq, chip_kv = tie((dq, chip_kv))
+    kv_parts = lax.all_to_all(chip_kv, "z", split_axis=0, concat_axis=0, tiled=True)
+
+    gp_q, q_term = project_back(dq, projected, cosine, sine, q_gain_row, 0)
+    in_q = dot(gp_q, h1_group, TN)
+
+    back_kv = jnp.sum(kv_parts.astype(f32), axis=0)
+    back_k, k_term = project_back(back_kv, projected, cosine, sine, k_gain_row, HEADS)
+    gp_kv = jnp.where(c == 0, back_k, back_kv.astype(bf16))
+    k_term = jnp.where(c == 0, k_term, 0.0)
+    in_kv = dot(gp_kv, h1_group, TN)
+    in_partial = jnp.concatenate([in_q.astype(bf16), in_kv.astype(bf16)], axis=0).reshape(16, 40, D)
+    in_partial, gp_q, gp_kv, out_moved = tie((in_partial, gp_q, gp_kv, out_moved))
+    in_parts = lax.all_to_all(in_partial, ("z", "y"), split_axis=0, concat_axis=0, tiled=True)
+
+    gain1_term = jnp.sum(in_partial.reshape(640, D).astype(f32) * in_mine.astype(f32), axis=0) / gain1
+    terms = jnp.concatenate([gain1_term, gain2_term[0], q_term[0], k_term[0], squares[0]]).reshape(-1, 128)
+    terms = sum_over(sum_over(terms, "c"), "x")
+
+    gp = jnp.concatenate([gp_q, gp_kv], axis=1)
     gp_mine, gp_there = core_halves(gp, c)
     gh1_chip = dot(gp_mine, in_mine) + dot(shift(gp_there, "c", 1), in_other)
-    h1_mine, _ = core_halves(h1_group, c)
-    gain1_term = jnp.sum(gh1_chip * h1_mine.astype(f32), axis=0) / gain1
-    terms = jnp.concatenate([gain1_term, gain2_term[0], q_term[0], k_term[0], squares[0]])
-    sums = small_sum(terms.reshape(-1, 128)).reshape(-1)
-    gh1 = ring_scatter(gh1_chip.reshape(4, LOCAL, D), "x")
+    gh1 = RingSum(gh1_chip.reshape(4, LOCAL, D), "x").total()
     gn1 = gh1 * gain1
     tokens_gradient = g2 + r1 * (gn1 - n1 * jnp.mean(gn1 * n1, axis=-1, keepdims=True))
+    out_summed = jnp.sum(out_moved.astype(f32), axis=0).astype(bf16)
+
+    in_parts, terms, out_summed = tie((in_parts, terms, out_summed))
+    in_summed = jnp.sum(in_parts.astype(f32), axis=0)
+    out_gradient = lax.ppermute(out_summed, ALL, [(b, a) for a, b in out_perm()]).astype(f32)
+    sums = sum_over(sum_over(terms, "y"), "z").reshape(-1)
 
     going = dot(arrive, in_summed.astype(bf16), TN).astype(bf16)
-    home = [lax.ppermute(going[8 * i : 8 * i + 8], ALL, [(b, a) for a, b in perms[i]]) for i in range(5)]
+    home = [lax.ppermute(going[40 * i : 40 * i + 40], ALL, [(b, a) for a, b in perms[i]]) for i in range(3)]
     in_gradient = dot(jnp.concatenate(home, axis=0), leave, TN)
 
     loss = jnp.sum(sums[2 * D + 2 * HD :]) / (2.0 * valid_count * D)

time: 608 us -> 559 us (0.919)
  the two profiles are of different devices: /device:TPU:26 before, /device:TPU:25 now
where the time goes in v3:
time: 559 us; the launch traced here: 548 us
  waiting for transfers between devices  142 us (25%)
  starting transfers between devices  138 us (25%)
  Pallas kernels  87.6 us (16%)
  blocking collectives  66.4 us (12%)
  local copies, waits for them, and re-layouts  44.6 us (8%)
  matrix products  35.3 us (6%)
  other arithmetic  28.8 us (5%)
  between operations  5.88 us (1%)
    ppermute x51, waiting for transfers between devices, shift(): lax.ppermute(value, axis, [(i, (i + step) % size) for i in range(size)])  67.2 us
    all_to_all x2, blocking collectives, exchange(): return lax.all_to_all(rows, ALL, split_axis=0, concat_axis=0, tiled=True)  66.4 us
    ppermute x51, starting transfers between devices, shift(): lax.ppermute(value, axis, [(i, (i + step) % size) for i in range(size)])  64.8 us
    dot_general x16, matrix products, dot(): return lax.dot_general(a, b, dims, preferred_element_type=f32)  35.3 us
    unnamed x135, local copies, waits for them, and re-layouts  32.1 us
    all_to_all x2, waiting for transfers between devices, exchange(): return lax.all_to_all(rows, ALL, split_axis=0, concat_axis=0, tiled=True)  29.2 us
    pallas_call x1, Pallas kernels, attend_backward(): pl.pallas_call(backward_kernel, grid_spec=pltpu.PrefetchScalarGridSpec(nu...  29.1 us
    all_to_all x1, waiting for transfers between devices, body(): lax.all_to_all(chip_out.astype(bf16).reshape(4, LOCAL, D), 'x', split_axi...  24.9 us
  transfers between devices with their start and end apart: 65, of which 33 were waited for; matrix products, arithmetic and copies ran while one was open for 11% of the time, Pallas kernels for 10%

profile of v3, /device:TPU:25, one launch (start us, length us, event | category | flops | bytes accessed | tf_op | source)
XLA Modules:
  0.0 548.4 jit_solution(13549111181089714632)
XLA Ops:
  9.3 6.1 %collective-permute-start.6 = (bf16[40,2048]{1,0:T(8,128)(2,1)}, bf16[40,2048]{1,0:T(8,128)(2,1)}, u32[]{:S(2)}, u32[]{:S(2)}) collective-permute-start(bf16[40,2048]{1,0:T(8,128)(2,1)} %get-tuple-element.126), channel_id=1, source_target_pairs={{12,1},{13,33},{14,65},{15,97},{16,3},{17,35},{18,67},{19,99},{20,... | collective-permute-start | bytes 491528 | tf_op jit(solution)/shard_map/ppermute | solution.py:719
  28.7 8.1 %collective-permute-done.8 = bf16[32,2048]{1,0:T(8,128)(2,1)S(1)} collective-permute-done((bf16[32,2048]{1,0:T(8,128)(2,1)S(1)}, bf16[32,2048]{1,0:T(8,128)(2,1)S(1)}, u32[]{:S(2)}, u32[]{:S(2)}) %collective-permute-start.8) | collective-permute-done | bytes 131104 | tf_op jit(solution)/shard_map/ppermute | solution.py:720
  79.4 7.4 %collective-permute-done.20 = bf16[4,40,1024]{2,1,0:T(8,128)(2,1)S(1)} collective-permute-done((bf16[4,40,1024]{2,1,0:T(8,128)(2,1)S(1)}, bf16[4,40,1024]{2,1,0:T(8,128)(2,1)S(1)}, u32[]{:S(2)}, u32[]{:S(2)}) %collective-permute-start.20) | collective-permute-done | bytes 327712 | tf_op jit(solution)/shard_map/ppermute | solution.py:130
  118.2 16.1 %attend_forward.1 = (bf16[1024,512]{1,0:T(8,128)(2,1)S(1)}, f32[4,4,8,256]{3,2,1,0:T(8,128)S(1)}) custom-call(s32[1]{0:T(128)} %bitcast.1.z_ref, bf16[1024,512]{1,0:T(8,128)(2,1)S(1)} %get-tuple-element.67.q_ref, bf16[2,4,1024,128]{3,2,1,0:T(8,128)(2,1)S(1)} %bitcast_dynamic-update-slice_fusion.1.kv_ref), custom_call_target="tpu_custom_call" | custom-call | flops 8999999488 | bytes 8388608 | tf_op jit(solution)/shard_map/attend_forward/pallas_call | solution.py:337
  146.1 24.9 %all-to-all-done.moved_ref = bf16[4,128,2048]{2,1,0:T(8,128)(2,1)} async-done(((bf16[4,128,2048]{2,1,0:T(8,128)(2,1)}), bf16[4,128,2048]{2,1,0:T(8,128)(2,1)}, u32[]{:S(2)}, u32[]{:S(2)}) %all-to-all-start) | async-done | bytes 2097184 | tf_op jit(solution)/shard_map/all_to_all | solution.py:738
  176.2 37.6 %all_to_all.40.x_ref = bf16[128,56,128]{2,1,0:T(8,128)(2,1)S(1)} all-to-all(bf16[128,56,128]{2,1,0:T(8,128)(2,1)S(1)} %get-tuple-element.71), channel_id=1, replica_groups=mesh['y'=4,'x'=4,'z'=4,'c'=2] {'y','x','z','c'}, dimensions={0} | all-to-all | bytes 3670016 | tf_op jit(solution)/shard_map/all_to_all | solution.py:680
  213.8 9.7 %expert_forward.1 = (bf16[384,2048]{1,0:T(8,128)(2,1)S(1)}, f32[384,1536]{1,0:T(8,128)}, bf16[384,768]{1,0:T(8,128)(2,1)S(1)}, bf16[6144,128]{1,0:T(8,128)(2,1)S(1)}) custom-call(bf16[128,56,128]{2,1,0:T(8,128)(2,1)S(1)} %all_to_all.40.x_ref, bf16[2048,1536]{1,0:T(8,128)(2,1)} %bitcast.231, bf16[768,2048]{1,0:T(8,128)(2,1)} %bitcast.235), custom_call_target="tpu_custom_call" | custom-call | flops 3600000000 | bytes 17825792 | tf_op jit(solution)/shard_map/expert_forward/pallas_call | solution.py:529
  226.7 7.8 %all-to-all-start.2 = ((bf16[128,48,128]{2,1,0:T(8,128)(2,1)}), bf16[128,48,128]{2,1,0:T(8,128)(2,1)}, u32[]{:S(2)}, u32[]{:S(2)}) async-start(bf16[128,48,128]{2,1,0:T(8,128)(2,1)} %bitcast.202), calls=%async_computation.2 | async-start | bytes 3145728 | tf_op jit(solution)/shard_map/all_to_all | solution.py:680
  237.4 19.6 %all-to-all-done.2 = bf16[128,48,128]{2,1,0:T(8,128)(2,1)} async-done(((bf16[128,48,128]{2,1,0:T(8,128)(2,1)}), bf16[128,48,128]{2,1,0:T(8,128)(2,1)}, u32[]{:S(2)}, u32[]{:S(2)}) %all-to-all-start.2) | async-done | bytes 1572896 | tf_op jit(solution)/shard_map/all_to_all | solution.py:680
  259.3 5.5 combine.1
  264.7 28.8 %all_to_all.41 = bf16[128,48,128]{2,1,0:T(8,128)(2,1)S(1)} all-to-all(bf16[128,48,128]{2,1,0:T(8,128)(2,1)S(1)} %get-tuple-element.75), channel_id=1, replica_groups=mesh['y'=4,'x'=4,'z'=4,'c'=2] {'y','x','z','c'}, dimensions={0} | all-to-all | bytes 3145728 | tf_op jit(solution)/shard_map/all_to_all | solution.py:680
  293.6 10.2 %expert_backward.1 = (bf16[384,2048]{1,0:T(8,128)(2,1)S(1)}, bf16[384,1536]{1,0:T(8,128)(2,1)S(1)}, bf16[6144,128]{1,0:T(8,128)(2,1)S(1)}) custom-call(bf16[6144,128]{1,0:T(8,128)(2,1)S(1)} %bitcast.201, bf16[2048,1536]{1,0:T(8,128)(2,1)} %bitcast.232, bf16[768,2048]{1,0:T(8,128)(2,1)} %bitcast.236, f32[384,1536]{1,0:T(8,128)} %get-tuple-element.76.mixed_ref), custom_call_target="tpu_custom_call" | custom-call | flops 3600000000 | bytes 17825792 | tf_op jit(solution)/shard_map/expert_backward/pallas_call | solution.py:611
  307.1 7.9 %all-to-all-start.4 = ((bf16[128,48,128]{2,1,0:T(8,128)(2,1)}), bf16[128,48,128]{2,1,0:T(8,128)(2,1)}, u32[]{:S(2)}, u32[]{:S(2)}) async-start(bf16[128,48,128]{2,1,0:T(8,128)(2,1)} %bitcast.203), calls=%async_computation.4 | async-start | bytes 3145728 | tf_op jit(solution)/shard_map/all_to_all | solution.py:680
  315.0 6.3 %fusion.44 = f32[768,2048]{1,0:T(8,128)} fusion(bf16[384,768]{1,0:T(8,128)(2,1)} %copy-done.38, bf16[384,2048]{1,0:T(8,128)(2,1)} %copy-done.22), kind=kOutput, calls=%fused_computation.153 | convolution fusion | flops 1207959552 | bytes 8454144 | tf_op jit(solution)/shard_map/dot_general | solution.py:676
  321.3 6.6 %fusion.43 = f32[2048,1536]{1,0:T(8,128)} fusion(bf16[384,2048]{1,0:T(8,128)(2,1)S(1)} %copy-done.21, bf16[384,1536]{1,0:T(8,128)(2,1)S(1)} %copy-done.26), kind=kOutput, calls=%fused_computation.152 | convolution fusion | flops 2415919104 | bytes 15335424 | tf_op jit(solution)/shard_map/dot_general | solution.py:676
  327.9 9.6 %all-to-all-done.4 = bf16[128,48,128]{2,1,0:T(8,128)(2,1)} async-done(((bf16[128,48,128]{2,1,0:T(8,128)(2,1)}), bf16[128,48,128]{2,1,0:T(8,128)(2,1)}, u32[]{:S(2)}, u32[]{:S(2)}) %all-to-all-start.4) | async-done | bytes 1572896 | tf_op jit(solution)/shard_map/all_to_all | solution.py:680
  345.7 10.3 %collective-permute-done.33 = bf16[128,2048]{1,0:T(8,128)(2,1)S(1)} collective-permute-done((bf16[128,2048]{1,0:T(8,128)(2,1)S(1)}, bf16[128,2048]{1,0:T(8,128)(2,1)S(1)}, u32[]{:S(2)}, u32[]{:S(2)}) %collective-permute-start.33) | collective-permute-done | bytes 524320 | tf_op jit(solution)/shard_map/ppermute | solution.py:130
  377.1 6.6 %all-to-all-start.5 = ((bf16[16,32,2048]{2,1,0:T(8,128)(2,1)}), bf16[16,32,2048]{2,1,0:T(8,128)(2,1)}, u32[]{:S(2)}, u32[]{:S(2)}) async-start(bf16[16,32,2048]{2,1,0:T(8,128)(2,1)} %bitcast.220), calls=%async_computation.5 | async-start | bytes 4194304 | tf_op jit(solution)/shard_map/all_to_all | solution.py:775
  387.4 29.1 %attend_backward.1 = (bf16[1024,512]{1,0:T(8,128)(2,1)S(1)}, bf16[2,4,1024,128]{3,2,1,0:T(8,128)(2,1)}) custom-call(s32[1]{0:T(128)} %bitcast.1.z_ref, bf16[1024,512]{1,0:T(8,128)(2,1)S(1)} %copy-done.44, bf16[2,4,1024,128]{3,2,1,0:T(8,128)(2,1)} %copy-done.18, bf16[1024,512]{1,0:T(8,128)(2,1)S(1)} %bitcast.204, bf16[1024,512]{1,0:T(8,128)(2,1)S(1)} %copy-done.33, ...), custom_call_target="tpu_custom_call" | custom-call | flops 22000001024 | bytes 8388608 | tf_op jit(solution)/shard_map/attend_backward/pallas_call | solution.py:424
  423.3 13.2 %all-to-all-start.6 = ((bf16[4,1024,128]{2,1,0:T(8,128)(2,1)}), bf16[4,1024,128]{2,1,0:T(8,128)(2,1)}, u32[]{:S(2)}, u32[]{:S(2)}) async-start(bf16[4,1024,128]{2,1,0:T(8,128)(2,1)} %fusion.1), calls=%async_computation.6 | async-start | bytes 2097152 | tf_op jit(solution)/shard_map/all_to_all | solution.py:783
  462.1 6.0 %all-to-all-start.7 = ((bf16[16,40,2048]{2,1,0:T(8,128)(2,1)}), bf16[16,40,2048]{2,1,0:T(8,128)(2,1)}, u32[]{:S(2)}, u32[]{:S(2)}) async-start(bf16[16,40,2048]{2,1,0:T(8,128)(2,1)} %bitcast.213), calls=%async_computation.7 | async-start | bytes 5242880 | tf_op jit(solution)/shard_map/all_to_all | solution.py:795
  480.5 5.6 %collective-permute-done.53 = bf16[128,1024]{1,0:T(8,128)(2,1)S(1)} collective-permute-done((bf16[128,1024]{1,0:T(8,128)(2,1)S(1)}, bf16[128,1024]{1,0:T(8,128)(2,1)S(1)}, u32[]{:S(2)}, u32[]{:S(2)}) %collective-permute-start.53) | collective-permute-done | bytes 262176 | tf_op jit(solution)/shard_map/ppermute | solution.py:130
  520.7 10.4 %collective-permute-start.56 = (bf16[40,2048]{1,0:T(8,128)(2,1)S(1)}, bf16[40,2048]{1,0:T(8,128)(2,1)S(1)}, u32[]{:S(2)}, u32[]{:S(2)}) collective-permute-start(bf16[40,2048]{1,0:T(8,128)(2,1)S(1)} %get-tuple-element.123), channel_id=1, source_target_pairs={{1,12},{33,13},{65,14},{97,15},{3,16},{35,17},{67,18},{99,19},{5,2... | collective-permute-start | bytes 491528 | tf_op jit(solution)/shard_map/ppermute | solution.py:815
  537.4 7.6 %collective-permute-done.58 = bf16[32,2048]{1,0:T(8,128)(2,1)S(1)} collective-permute-done((bf16[32,2048]{1,0:T(8,128)(2,1)S(1)}, bf16[32,2048]{1,0:T(8,128)(2,1)S(1)}, u32[]{:S(2)}, u32[]{:S(2)}) %collective-permute-start.58) | collective-permute-done | bytes 131104 | tf_op jit(solution)/shard_map/ppermute | solution.py:811
  (382 shorter events, 241.4 us)
Async XLA Ops:
  4.7 57.2 %collective-permute-start = (bf16[128,2048]{1,0:T(8,128)(2,1)}, bf16[128,2048]{1,0:T(8,128)(2,1)S(1)}, u32[]{:S(2)}, u32[]{:S(2)}) collective-permute-start(bf16[128,2048]{1,0:T(8,128)(2,1)} %get-tuple-element.112), channel_id=1, source_target_pairs={{0,8},{8,16},{16,24},{24,0},{1,9},{9,17},{17,25},{25,1},{2,10},{10... | collective-permute-start | bytes 1572872 | tf_op jit(solution)/shard_map/ppermute | solution.py:130
  6.0 53.8 %collective-permute-start.1 = (bf16[128,2048]{1,0:T(8,128)(2,1)}, bf16[128,2048]{1,0:T(8,128)(2,1)S(1)}, u32[]{:S(2)}, u32[]{:S(2)}) collective-permute-start(bf16[128,2048]{1,0:T(8,128)(2,1)} %get-tuple-element.112), channel_id=1, source_target_pairs={{0,24},{8,0},{16,8},{24,16},{1,25},{9,1},{17,9},{25,17},{2,26},{10... | collective-permute-start | bytes 1572872 | tf_op jit(solution)/shard_map/ppermute | solution.py:130
  9.3 15.8 %collective-permute-start.6 = (bf16[40,2048]{1,0:T(8,128)(2,1)}, bf16[40,2048]{1,0:T(8,128)(2,1)}, u32[]{:S(2)}, u32[]{:S(2)}) collective-permute-start(bf16[40,2048]{1,0:T(8,128)(2,1)} %get-tuple-element.126), channel_id=1, source_target_pairs={{12,1},{13,33},{14,65},{15,97},{16,3},{17,35},{18,67},{19,99},{20,... | collective-permute-start | bytes 491528 | tf_op jit(solution)/shard_map/ppermute | solution.py:719
  54.2 24.3 %collective-permute-start.17 = (bf16[4,40,2048]{2,1,0:T(8,128)(2,1)S(1)}, bf16[4,40,2048]{2,1,0:T(8,128)(2,1)S(1)}, u32[]{:S(2)}, u32[]{:S(2)}) collective-permute-start(bf16[4,40,2048]{2,1,0:T(8,128)(2,1)S(1)} %fusion.29), channel_id=1, source_target_pairs={{0,2},{2,4},{4,6},{6,0},{1,3},{3,5},{5,7},{7,1},{8,10},{10,12},{12... | collective-permute-start | bytes 1966088 | tf_op jit(solution)/shard_map/ppermute | solution.py:130
  55.1 22.3 %collective-permute-start.18 = (bf16[4,40,2048]{2,1,0:T(8,128)(2,1)S(1)}, bf16[4,40,2048]{2,1,0:T(8,128)(2,1)S(1)}, u32[]{:S(2)}, u32[]{:S(2)}) collective-permute-start(bf16[4,40,2048]{2,1,0:T(8,128)(2,1)S(1)} %fusion.29), channel_id=1, source_target_pairs={{0,6},{2,0},{4,2},{6,4},{1,7},{3,1},{5,3},{7,5},{8,14},{10,8},{12,... | collective-permute-start | bytes 1966088 | tf_op jit(solution)/shard_map/ppermute | solution.py:130
  56.9 41.0 %collective-permute-start.26 = (bf16[4,32,2048]{2,1,0:T(8,128)(2,1)S(1)}, bf16[4,32,2048]{2,1,0:T(8,128)(2,1)S(1)}, u32[]{:S(2)}, u32[]{:S(2)}) collective-permute-start(bf16[4,32,2048]{2,1,0:T(8,128)(2,1)S(1)} %fusion.30), channel_id=1, source_target_pairs={{0,32},{32,64},{64,96},{96,0},{1,33},{33,65},{65,97},{97,1},{2,34}... | collective-permute-start | bytes 1572872 | tf_op jit(solution)/shard_map/ppermute | solution.py:130
  65.3 32.5 %collective-permute-start.27 = (bf16[4,32,2048]{2,1,0:T(8,128)(2,1)S(1)}, bf16[4,32,2048]{2,1,0:T(8,128)(2,1)S(1)}, u32[]{:S(2)}, u32[]{:S(2)}) collective-permute-start(bf16[4,32,2048]{2,1,0:T(8,128)(2,1)S(1)} %fusion.30), channel_id=1, source_target_pairs={{0,96},{32,0},{64,32},{96,64},{1,97},{33,1},{65,33},{97,65},{2,98}... | collective-permute-start | bytes 1572872 | tf_op jit(solution)/shard_map/ppermute | solution.py:130
  69.6 19.6 %collective-permute-start.4 = (bf16[512,2048]{1,0:T(8,128)(2,1)}, bf16[512,2048]{1,0:T(8,128)(2,1)S(1)}, u32[]{:S(2)}, u32[]{:S(2)}) collective-permute-start(bf16[512,2048]{1,0:T(8,128)(2,1)} %bitcast.9), channel_id=1, source_target_pairs={{0,1},{1,0},{2,3},{3,2},{4,5},{5,4},{6,7},{7,6},{8,9},{9,8},{10,11... | collective-permute-start | bytes 6291464 | tf_op jit(solution)/shard_map/ppermute | solution.py:130
  97.9 18.0 %collective-permute-start.29 = (bf16[4,32,1024]{2,1,0:T(8,128)(2,1)S(1)}, bf16[4,32,1024]{2,1,0:T(8,128)(2,1)S(1)}, u32[]{:S(2)}, u32[]{:S(2)}) collective-permute-start(bf16[4,32,1024]{2,1,0:T(8,128)(2,1)S(1)} %slice.161), channel_id=1, source_target_pairs={{0,96},{32,0},{64,32},{96,64},{1,97},{33,1},{65,33},{97,65},{2,98}... | collective-permute-start | bytes 786440 | tf_op jit(solution)/shard_map/ppermute | solution.py:130
  98.0 17.9 %collective-permute-start.28 = (bf16[4,32,1024]{2,1,0:T(8,128)(2,1)S(1)}, bf16[4,32,1024]{2,1,0:T(8,128)(2,1)S(1)}, u32[]{:S(2)}, u32[]{:S(2)}) collective-permute-start(bf16[4,32,1024]{2,1,0:T(8,128)(2,1)S(1)} %slice.160), channel_id=1, source_target_pairs={{0,32},{32,64},{64,96},{96,0},{1,33},{33,65},{65,97},{97,1},{2,34}... | collective-permute-start | bytes 786440 | tf_op jit(solution)/shard_map/ppermute | solution.py:130
  116.0 18.9 %collective-permute-start.31 = (bf16[512,2048]{1,0:T(8,128)(2,1)S(1)}, bf16[512,2048]{1,0:T(8,128)(2,1)S(1)}, u32[]{:S(2)}, u32[]{:S(2)}) collective-permute-start(bf16[512,2048]{1,0:T(8,128)(2,1)S(1)} %bitcast.224), channel_id=1, source_target_pairs={{0,1},{1,0},{2,3},{3,2},{4,5},{5,4},{6,7},{7,6},{8,9},{9,8},{10,11... | collective-permute-start | bytes 6291464 | tf_op jit(solution)/shard_map/ppermute | solution.py:130
  140.3 30.7 %all-to-all-start = ((bf16[4,128,2048]{2,1,0:T(8,128)(2,1)}), bf16[4,128,2048]{2,1,0:T(8,128)(2,1)}, u32[]{:S(2)}, u32[]{:S(2)}) async-start(bf16[4,128,2048]{2,1,0:T(8,128)(2,1)} %bitcast.219), calls=%async_computation | async-start | bytes 4194304 | tf_op jit(solution)/shard_map/all_to_all | solution.py:738
  226.7 30.3 %all-to-all-start.2 = ((bf16[128,48,128]{2,1,0:T(8,128)(2,1)}), bf16[128,48,128]{2,1,0:T(8,128)(2,1)}, u32[]{:S(2)}, u32[]{:S(2)}) async-start(bf16[128,48,128]{2,1,0:T(8,128)(2,1)} %bitcast.202), calls=%async_computation.2 | async-start | bytes 3145728 | tf_op jit(solution)/shard_map/all_to_all | solution.py:680
  307.1 30.4 %all-to-all-start.4 = ((bf16[128,48,128]{2,1,0:T(8,128)(2,1)}), bf16[128,48,128]{2,1,0:T(8,128)(2,1)}, u32[]{:S(2)}, u32[]{:S(2)}) async-start(bf16[128,48,128]{2,1,0:T(8,128)(2,1)} %bitcast.203), calls=%async_computation.4 | async-start | bytes 3145728 | tf_op jit(solution)/shard_map/all_to_all | solution.py:680
  377.1 40.4 %all-to-all-start.5 = ((bf16[16,32,2048]{2,1,0:T(8,128)(2,1)}), bf16[16,32,2048]{2,1,0:T(8,128)(2,1)}, u32[]{:S(2)}, u32[]{:S(2)}) async-start(bf16[16,32,2048]{2,1,0:T(8,128)(2,1)} %bitcast.220), calls=%async_computation.5 | async-start | bytes 4194304 | tf_op jit(solution)/shard_map/all_to_all | solution.py:775
  423.3 27.9 %all-to-all-start.6 = ((bf16[4,1024,128]{2,1,0:T(8,128)(2,1)}), bf16[4,1024,128]{2,1,0:T(8,128)(2,1)}, u32[]{:S(2)}, u32[]{:S(2)}) async-start(bf16[4,1024,128]{2,1,0:T(8,128)(2,1)} %fusion.1), calls=%async_computation.6 | async-start | bytes 2097152 | tf_op jit(solution)/shard_map/all_to_all | solution.py:783
  436.5 35.8 %collective-permute-start.50 = (bf16[640,2048]{1,0:T(8,128)(2,1)S(1)}, bf16[640,2048]{1,0:T(8,128)(2,1)}, u32[]{:S(2)}, u32[]{:S(2)}) collective-permute-start(bf16[640,2048]{1,0:T(8,128)(2,1)S(1)} %bitcast.196), channel_id=1, source_target_pairs={{0,1},{1,0},{2,3},{3,2},{4,5},{5,4},{6,7},{7,6},{8,9},{9,8},{10,11... | collective-permute-start | bytes 7864328 | tf_op jit(solution)/shard_map/ppermute | solution.py:130
  462.1 47.1 %all-to-all-start.7 = ((bf16[16,40,2048]{2,1,0:T(8,128)(2,1)}), bf16[16,40,2048]{2,1,0:T(8,128)(2,1)}, u32[]{:S(2)}, u32[]{:S(2)}) async-start(bf16[16,40,2048]{2,1,0:T(8,128)(2,1)} %bitcast.213), calls=%async_computation.7 | async-start | bytes 5242880 | tf_op jit(solution)/shard_map/all_to_all | solution.py:795
  486.2 18.7 %collective-permute-start.54 = (bf16[128,2048]{1,0:T(8,128)(2,1)S(1)}, bf16[128,2048]{1,0:T(8,128)(2,1)S(1)}, u32[]{:S(2)}, u32[]{:S(2)}) collective-permute-start(bf16[128,2048]{1,0:T(8,128)(2,1)S(1)} %pad_maximum_fusion.5), channel_id=1, source_target_pairs={{0,24},{8,0},{16,8},{24,16},{1,25},{9,1},{17,9},{25,17},{2,26},{10... | collective-permute-start | bytes 1572872 | tf_op jit(solution)/shard_map/ppermute | solution.py:130
  490.2 14.7 %collective-permute-start.52 = (bf16[128,2048]{1,0:T(8,128)(2,1)}, bf16[128,2048]{1,0:T(8,128)(2,1)S(1)}, u32[]{:S(2)}, u32[]{:S(2)}) collective-permute-start(bf16[128,2048]{1,0:T(8,128)(2,1)} %pad_maximum_fusion.4), channel_id=1, source_target_pairs={{0,8},{8,16},{16,24},{24,0},{1,9},{9,17},{17,25},{25,1},{2,10},{10... | collective-permute-start | bytes 1572872 | tf_op jit(solution)/shard_map/ppermute | solution.py:130
  515.8 15.4 %collective-permute-start.48 = (f32[35,128]{1,0:T(8,128)S(1)}, f32[35,128]{1,0:T(8,128)S(1)}, u32[]{:S(2)}, u32[]{:S(2)}) collective-permute-start(f32[35,128]{1,0:T(8,128)S(1)} %add_add_fusion.1), channel_id=1, source_target_pairs={{0,4},{2,6},{4,0},{6,2},{1,5},{3,7},{5,1},{7,3},{8,12},{10,14},{12... | collective-permute-start | bytes 53768 | tf_op jit(solution)/shard_map/ppermute | solution.py:130
  519.4 15.6 %collective-permute-start.46 = (f32[35,128]{1,0:T(8,128)S(1)}, f32[35,128]{1,0:T(8,128)S(1)}, u32[]{:S(2)}, u32[]{:S(2)}) collective-permute-start(f32[35,128]{1,0:T(8,128)S(1)} %add_add_fusion.1), channel_id=1, source_target_pairs={{0,2},{2,4},{4,6},{6,0},{1,3},{3,5},{5,7},{7,1},{8,10},{10,12},{12... | collective-permute-start | bytes 53768 | tf_op jit(solution)/shard_map/ppermute | solution.py:130
  520.1 25.7 %collective-permute-start.57 = (bf16[40,2048]{1,0:T(8,128)(2,1)S(1)}, bf16[40,2048]{1,0:T(8,128)(2,1)S(1)}, u32[]{:S(2)}, u32[]{:S(2)}) collective-permute-start(bf16[40,2048]{1,0:T(8,128)(2,1)S(1)} %get-tuple-element.122), channel_id=1, source_target_pairs={{6,102},{14,105},{7,115},{15,118},{23,121},{30,88},{31,101}} | collective-permute-start | bytes 491528 | tf_op jit(solution)/shard_map/ppermute | solution.py:815
  520.7 25.0 %collective-permute-start.56 = (bf16[40,2048]{1,0:T(8,128)(2,1)S(1)}, bf16[40,2048]{1,0:T(8,128)(2,1)S(1)}, u32[]{:S(2)}, u32[]{:S(2)}) collective-permute-start(bf16[40,2048]{1,0:T(8,128)(2,1)S(1)} %get-tuple-element.123), channel_id=1, source_target_pairs={{1,12},{33,13},{65,14},{97,15},{3,16},{35,17},{67,18},{99,19},{5,2... | collective-permute-start | bytes 491528 | tf_op jit(solution)/shard_map/ppermute | solution.py:815
  (106 other events, 807.9 us)

commit v4 on v3

--- a/solution.py
+++ b/solution.py
@@ -259,7 +259,7 @@
             jax.ShapeDtypeStruct((GROUP, wide), bf16),
             jax.ShapeDtypeStruct((GROUP, HD), bf16),
         ],
-        compiler_params=pltpu.CompilerParams(vmem_limit_bytes=40 * 2**20),
+        compiler_params=pltpu.CompilerParams(vmem_limit_bytes=20 * 2**20),
         cost_estimate=pl.CostEstimate(flops=27 * 10**8, bytes_accessed=11 * 2**20, transcendentals=10**4),
         name="project",
     )(core, rows, weights, cosine, sine, q_gain, k_gain)
@@ -292,41 +292,92 @@
         ],
         out_specs=[pl.BlockSpec((PIECE, wide), lambda i: (i, 0)), pl.BlockSpec((1, HD), lambda i: (0, 0))],
         out_shape=[jax.ShapeDtypeStruct((GROUP, wide), bf16), jax.ShapeDtypeStruct((1, HD), f32)],
-        compiler_params=pltpu.CompilerParams(vmem_limit_bytes=40 * 2**20),
+        compiler_params=pltpu.CompilerParams(vmem_limit_bytes=10 * 2**20),
         cost_estimate=pl.CostEstimate(flops=wide * 10**4, bytes_accessed=wide * 10**4, transcendentals=10**4),
         name="project_back",
     )(grad, projected, cosine, sine, gain)
+
+
+def kv_back_kernel(core_ref, parts_ref, p_ref, cos_ref, sin_ref, gain_ref, h_ref, _, gp_ref, term_ref, out_ref):
+    grad = parts_ref[0].astype(f32)
+    for i in range(1, 4):
+        grad += parts_ref[i].astype(f32)
+    back, term = head_rotate_back(grad, p_ref[...], gain_ref[...], cos_ref[...], sin_ref[...])
+    back = jnp.where(core_ref[0] == 0, back, grad).astype(bf16)
+    gp_ref[...] = back
+    term_ref[...] = jnp.where(core_ref[0] == 0, jnp.sum(term, axis=0, keepdims=True), 0.0)
+    for j in range(D // 512):
+        lanes = slice(j * 512, (j + 1) * 512)
+        part = lax.dot_general(back, h_ref[:, lanes], TN, preferred_element_type=f32)
+        out_ref[:, lanes] = part.astype(bf16)
+
+
+def kv_back(core, parts, projected, cosine, sine, gain, rows, partial):
+    return pl.pallas_call(
+        kv_back_kernel,
+        grid_spec=pltpu.PrefetchScalarGridSpec(
+            num_scalar_prefetch=1,
+            grid=(1,),
+            in_specs=[
+                pl.BlockSpec((4, GROUP, HD), lambda i, c: (0, 0, 0)),
+                pl.BlockSpec((GROUP, HD), lambda i, c: (0, HEADS)),
+                pl.BlockSpec((GROUP, HD), lambda i, c: (0, 0)),
+                pl.BlockSpec((GROUP, HD), lambda i, c: (0, 0)),
+                pl.BlockSpec((1, HD), lambda i, c: (0, 0)),
+                pl.BlockSpec((GROUP, D), lambda i, c: (0, 0)),
+                pl.BlockSpec(memory_space=pl.ANY),
+            ],
+            out_specs=[
+                pl.BlockSpec((GROUP, HD), lambda i, c: (0, 0)),
+                pl.BlockSpec((1, HD), lambda i, c: (0, 0)),
+                pl.BlockSpec((HD, D), lambda i, c: (HEADS, 0)),
+            ],
+        ),
+        out_shape=[
+            jax.ShapeDtypeStruct((GROUP, HD), bf16),
+            jax.ShapeDtypeStruct((1, HD), f32),
+            jax.ShapeDtypeStruct(((HEADS + 1) * HD, D), bf16),
+        ],
+        input_output_aliases={7: 2},
+        compiler_params=pltpu.CompilerParams(vmem_limit_bytes=60 * 2**20),
+        cost_estimate=pl.CostEstimate(flops=6 * 10**8, bytes_accessed=8 * 2**20, transcendentals=10**3),
+        name="kv_back",
+    )(core, parts, projected, cosine, sine, gain, rows, partial)
+
+
+STEP = 512
 
 
 def forward_kernel(z_ref, q_ref, kv_ref, o_ref, lse_ref, total):
     piece = pl.program_id(0)
     z = z_ref[0]
     total[...] = jnp.zeros_like(total)
-    ones = jnp.ones((PIECE, HD), bf16)
-
-    def step(chunk, masked):
-        row = pl.multiple_of((chunk // 4) * PIECE, PIECE)
-        keys = kv_ref[0, chunk % 4, pl.ds(row, PIECE), :]
-        values = kv_ref[1, chunk % 4, pl.ds(row, PIECE), :]
+    ones = jnp.ones((STEP, HD), bf16)
+
+    def step(group, part, masked):
+        blocks = slice(part * STEP // PIECE, (part + 1) * STEP // PIECE)
+        row = pl.multiple_of(group * PIECE, PIECE)
+        keys = kv_ref[0, blocks, pl.ds(row, PIECE), :].reshape(STEP, HD)
+        values = kv_ref[1, blocks, pl.ds(row, PIECE), :].reshape(STEP, HD)
         wide = jnp.concatenate([values, ones], axis=1)
         for head in range(HEADS):
             lanes = slice(head * HD, (head + 1) * HD)
             scores = lax.dot_general(q_ref[:, lanes], keys, NT, preferred_element_type=f32)
             weights = jnp.exp2(scores * (SCALE * LOG2E))
             if masked:
-                queries_at = lax.broadcasted_iota(jnp.int32, (PIECE, PIECE), 0)
-                keys_at = lax.broadcasted_iota(jnp.int32, (PIECE, PIECE), 1)
+                queries_at = lax.broadcasted_iota(jnp.int32, (PIECE, STEP), 0) + z * PIECE
+                keys_at = lax.broadcasted_iota(jnp.int32, (PIECE, STEP), 1) + part * STEP
                 weights = jnp.where(keys_at <= queries_at, weights, 0.0)
             total[head] += lax.dot_general(weights.astype(bf16), wide, NN, preferred_element_type=f32)
 
-    last = piece * 4 + z
-
-    def body(chunk, carry):
-        step(chunk, False)
+    def body(group, carry):
+        for part in range(GROUP // STEP):
+            step(group, part, False)
         return carry
 
-    lax.fori_loop(0, last, body, 0)
-    step(last, True)
+    lax.fori_loop(0, piece, body, 0)
+    for part in range(GROUP // STEP):
+        step(piece, part, True)
     for head in range(HEADS):
         sums = total[head, :, HD:]
         o_ref[:, head * HD : (head + 1) * HD] = (total[head, :, :HD] / sums).astype(bf16)
@@ -353,7 +404,7 @@
             jax.ShapeDtypeStruct((GROUP, HEADS * HD), bf16),
             jax.ShapeDtypeStruct((HEADS, 4, 8, PIECE), f32),
         ],
-        compiler_params=pltpu.CompilerParams(vmem_limit_bytes=40 * 2**20),
+        compiler_params=pltpu.CompilerParams(vmem_limit_bytes=16 * 2**20),
         cost_estimate=pl.CostEstimate(flops=9 * 10**9, bytes_accessed=8 * 2**20, transcendentals=10**7),
         name="attend_forward",
     )(z, queries, keys_values)
@@ -368,7 +419,9 @@
         dkv[...] = jnp.zeros_like(dkv)
         for block in range(4):
             for part in range(4):
-                kt[block, part] = jnp.transpose(kv_ref[0, block, part * PIECE : (part + 1) * PIECE, :])
+                kt[part, :, block * PIECE : (block + 1) * PIECE] = jnp.transpose(
+                    kv_ref[0, block, part * PIECE : (part + 1) * PIECE, :]
+                )
 
     dqt[...] = jnp.zeros_like(dqt)
     rows = HEADS * PIECE
@@ -382,32 +435,34 @@
     delta = lax.dot_general(jnp.ones((8, HD), f32), product, NT, precision=lax.Precision.HIGHEST, preferred_element_type=f32)[:1]
     sums = jnp.concatenate([lse_ref[head, 0, :1, :] for head in range(HEADS)], axis=1)
 
-    def step(chunk, masked):
-        row = pl.multiple_of((chunk // 4) * PIECE, PIECE)
-        block = chunk % 4
-        keys = kv_ref[0, block, pl.ds(row, PIECE), :]
-        values = kv_ref[1, block, pl.ds(row, PIECE), :]
-        turned = kt[block, chunk // 4]
+    def step(group, part, masked):
+        blocks = slice(part * STEP // PIECE, (part + 1) * STEP // PIECE)
+        row = pl.multiple_of(group * PIECE, PIECE)
+        keys = kv_ref[0, blocks, pl.ds(row, PIECE), :].reshape(STEP, HD)
+        values = kv_ref[1, blocks, pl.ds(row, PIECE), :].reshape(STEP, HD)
+        turned = kt[group, :, part * STEP : (part + 1) * STEP]
         scores = lax.dot_general(keys, queries, NT, preferred_element_type=f32)
         weights = jnp.exp2(scores * (SCALE * LOG2E) - sums)
         if masked:
-            keys_at = lax.broadcasted_iota(jnp.int32, (PIECE, rows), 0)
-            queries_at = lax.broadcasted_iota(jnp.int32, (PIECE, rows), 1) % PIECE
+            keys_at = lax.broadcasted_iota(jnp.int32, (STEP, rows), 0) + part * STEP
+            queries_at = lax.broadcasted_iota(jnp.int32, (STEP, rows), 1) % PIECE + z * PIECE
             weights = jnp.where(keys_at <= queries_at, weights, 0.0)
         back_weights = lax.dot_general(values, backs, NT, preferred_element_type=f32)
         back_scores = (weights * (back_weights - delta)).astype(bf16)
-        dkv[1, block, pl.ds(row, PIECE), :] += lax.dot_general(weights.astype(bf16), backs, NN, preferred_element_type=f32)
-        dkv[0, block, pl.ds(row, PIECE), :] += lax.dot_general(back_scores, queries, NN, preferred_element_type=f32)
+        back_values = lax.dot_general(weights.astype(bf16), backs, NN, preferred_element_type=f32)
+        back_keys = lax.dot_general(back_scores, queries, NN, preferred_element_type=f32)
+        dkv[1, blocks, pl.ds(row, PIECE), :] += back_values.reshape(STEP // PIECE, PIECE, HD)
+        dkv[0, blocks, pl.ds(row, PIECE), :] += back_keys.reshape(STEP // PIECE, PIECE, HD)
         dqt[...] += lax.dot_general(turned, back_scores, NN, preferred_element_type=f32)
 
-    last = piece * 4 + z
-
-    def body(chunk, carry):
-        step(chunk, False)
+    def body(group, carry):
+        for part in range(GROUP // STEP):
+            step(group, part, False)
         return carry
 
-    lax.fori_loop(0, last, body, 0)
-    step(last, True)
+    lax.fori_loop(0, piece, body, 0)
+    for part in range(GROUP // STEP):
+        step(piece, part, True)
     grads = (jnp.transpose(dqt[...]) * SCALE).astype(bf16)
     for head in range(HEADS):
         dq_ref[:, head * HD : (head + 1) * HD] = grads[head * PIECE : (head + 1) * PIECE]
@@ -437,14 +492,14 @@
             scratch_shapes=[
                 pltpu.VMEM((HD, HEADS * PIECE), f32),
                 pltpu.VMEM((2, 4, GROUP, HD), f32),
-                pltpu.VMEM((4, 4, HD, PIECE), bf16),
+                pltpu.VMEM((4, HD, GROUP), bf16),
             ],
         ),
         out_shape=[
             jax.ShapeDtypeStruct((GROUP, HEADS * HD), bf16),
             jax.ShapeDtypeStruct((2, 4, GROUP, HD), bf16),
         ],
-        compiler_params=pltpu.CompilerParams(vmem_limit_bytes=48 * 2**20),
+        compiler_params=pltpu.CompilerParams(vmem_limit_bytes=60 * 2**20),
         cost_estimate=pl.CostEstimate(flops=22 * 10**9, bytes_accessed=8 * 2**20, transcendentals=10**7),
         name="attend_backward",
     )(z, queries, keys_values, backs, outs, lse)
@@ -498,7 +553,7 @@
             jax.ShapeDtypeStruct((LOCAL, D), f32),
             jax.ShapeDtypeStruct((EXPERTS, CAP * CHUNKS + 8, 128), bf16),
         ],
-        compiler_params=pltpu.CompilerParams(vmem_limit_bytes=40 * 2**20),
+        compiler_params=pltpu.CompilerParams(vmem_limit_bytes=12 * 2**20),
         cost_estimate=pl.CostEstimate(flops=10**6, bytes_accessed=6 * 2**20, transcendentals=128),
         name="dispatch",
     )(index, count, moved, tokens, gain)
@@ -509,35 +564,71 @@
         rows_ref[:, lanes_of(k)] = tiles[pl.ds(k, ROWS, stride=CHUNKS), :].astype(bf16)
 
 
-def expert_kernel(x_ref, first_ref, second_ref, rows_ref, mixed_ref, hidden_ref, y_ref, tiles):
-    tiles[...] = x_ref[:, : CAP * CHUNKS, :].reshape(TILES, 128).astype(f32)
-    unpack_rows(tiles, rows_ref)
+HBM = pl.BlockSpec(memory_space=pl.ANY)
+
+
+def expert_kernel(x_hbm, first_hbm, second_hbm, rows_hbm, mixed_hbm, hidden_hbm, y_hbm, x, first, second, rows, mixed, hidden, y, tiles, sems):
+    def copy(source, target, number):
+        return pltpu.make_async_copy(source, target, sems.at[number])
+
+    loads = [copy(x_hbm.at[:, : CAP * CHUNKS, :], x, 0)]
     for j in range(3):
-        gate = jnp.dot(rows_ref[...], first_ref[:, lanes_of(j, 256)], preferred_element_type=f32)
-        up = jnp.dot(rows_ref[...], first_ref[:, lanes_of(j + 3, 256)], preferred_element_type=f32)
-        mixed_ref[:, lanes_of(j, 256)] = gate
-        mixed_ref[:, lanes_of(j + 3, 256)] = up
-        hidden_ref[:, lanes_of(j, 256)] = (gate * jax.nn.sigmoid(gate) * up).astype(bf16)
+        for i in (j, j + 3):
+            loads.append(copy(first_hbm.at[:, lanes_of(i, 256)], first.at[:, lanes_of(i, 256)], 1 + i))
+    loads.append(copy(second_hbm, second, 7))
+    for load in loads:
+        load.start()
+    loads[0].wait()
+    tiles[...] = x[...].reshape(TILES, 128).astype(f32)
+    unpack_rows(tiles, rows)
+    stores = [copy(rows, rows_hbm, 8)]
+    stores[0].start()
+    for j in range(3):
+        loads[1 + 2 * j].wait()
+        loads[2 + 2 * j].wait()
+        gate = jnp.dot(rows[...], first[:, lanes_of(j, 256)], preferred_element_type=f32)
+        up = jnp.dot(rows[...], first[:, lanes_of(j + 3, 256)], preferred_element_type=f32)
+        mixed[:, lanes_of(j, 256)] = gate
+        mixed[:, lanes_of(j + 3, 256)] = up
+        hidden[:, lanes_of(j, 256)] = (gate * jax.nn.sigmoid(gate) * up).astype(bf16)
+    for source, target, number in ((mixed, mixed_hbm, 9), (hidden, hidden_hbm, 10)):
+        stores.append(copy(source, target, number))
+        stores[-1].start()
+    loads[7].wait()
     for j in range(D // 256):
-        part = jnp.dot(hidden_ref[...], second_ref[:, lanes_of(j, 256)], preferred_element_type=f32)
+        part = jnp.dot(hidden[...], second[:, lanes_of(j, 256)], preferred_element_type=f32)
         tiles[pl.ds(2 * j, ROWS, stride=CHUNKS), :] = part[:, :128]
         tiles[pl.ds(2 * j + 1, ROWS, stride=CHUNKS), :] = part[:, 128:]
-    y_ref[...] = tiles[...].astype(bf16)
+    y[...] = tiles[...].astype(bf16)
+    stores.append(copy(y, y_hbm, 11))
+    stores[-1].start()
+    for store in stores:
+        store.wait()
 
 
 def expert_forward(rows, first, second):
     return pl.pallas_call(
         expert_kernel,
-        in_specs=[pl.BlockSpec(memory_space=pltpu.VMEM)] * 3,
-        out_specs=[pl.BlockSpec(memory_space=pltpu.VMEM)] * 4,
-        scratch_shapes=[pltpu.VMEM((TILES, 128), f32)],
+        in_specs=[HBM] * 3,
+        out_specs=[HBM] * 4,
+        scratch_shapes=[
+            pltpu.VMEM((EXPERTS, CAP * CHUNKS, 128), bf16),
+            pltpu.VMEM((D, 2 * FF), bf16),
+            pltpu.VMEM((FF, D), bf16),
+            pltpu.VMEM((ROWS, D), bf16),
+            pltpu.VMEM((ROWS, 2 * FF), f32),
+            pltpu.VMEM((ROWS, FF), bf16),
+            pltpu.VMEM((TILES, 128), bf16),
+            pltpu.VMEM((TILES, 128), f32),
+            pltpu.SemaphoreType.DMA((12,)),
+        ],
         out_shape=[
             jax.ShapeDtypeStruct((ROWS, D), bf16),
             jax.ShapeDtypeStruct((ROWS, 2 * FF), f32),
             jax.ShapeDtypeStruct((ROWS, FF), bf16),
             jax.ShapeDtypeStruct((TILES, 128), bf16),
         ],
-        compiler_params=pltpu.CompilerParams(vmem_limit_bytes=48 * 2**20),
+        compiler_params=pltpu.CompilerParams(vmem_limit_bytes=60 * 2**20),
         cost_estimate=pl.CostEstimate(flops=36 * 10**8, bytes_accessed=17 * 2**20, transcendentals=3 * 10**5),
         name="expert_forward",
     )(rows, first, second)
@@ -584,41 +675,71 @@
             jax.ShapeDtypeStruct((LOCAL, D), f32),
             jax.ShapeDtypeStruct((EXPERTS, CAP * CHUNKS, 128), bf16),
         ],
-        compiler_params=pltpu.CompilerParams(vmem_limit_bytes=40 * 2**20),
+        compiler_params=pltpu.CompilerParams(vmem_limit_bytes=14 * 2**20),
         cost_estimate=pl.CostEstimate(flops=2 * 10**6, bytes_accessed=7 * 2**20, transcendentals=0),
         name="combine",
     )(index, slots, gates, slot_gates, scale, y, x2, target, mask)
 
 
-def expert_back_kernel(g_ref, first_ref, second_ref, mixed_ref, back_out_ref, back_mixed_ref, gh_ref, tiles):
-    tiles[...] = g_ref[...].astype(f32)
-    unpack_rows(tiles, back_out_ref)
+def expert_back_kernel(g_hbm, first_hbm, second_hbm, mixed_hbm, back_out_hbm, back_mixed_hbm, gh_hbm, g, first, second, mixed, back_out, back_mixed, gh, tiles, sems):
+    def copy(source, target, number):
+        return pltpu.make_async_copy(source, target, sems.at[number])
+
+    loads = [copy(g_hbm, g, 0), copy(second_hbm, second, 1), copy(mixed_hbm, mixed, 2)]
+    loads += [copy(first_hbm.at[lanes_of(i, 512), :], first.at[lanes_of(i, 512), :], 3 + i) for i in range(4)]
+    for load in loads:
+        load.start()
+    loads[0].wait()
+    tiles[...] = g[...].astype(f32)
+    unpack_rows(tiles, back_out)
+    stores = [copy(back_out, back_out_hbm, 7)]
+    stores[0].start()
+    loads[1].wait()
+    loads[2].wait()
     for j in range(3):
-        back_hidden = lax.dot_general(back_out_ref[...], second_ref[lanes_of(j, 256), :], NT, preferred_element_type=f32)
-        gate = mixed_ref[:, lanes_of(j, 256)]
-        up = mixed_ref[:, lanes_of(j + 3, 256)]
+        back_hidden = lax.dot_general(back_out[...], second[lanes_of(j, 256), :], NT, preferred_element_type=f32)
+        gate = mixed[:, lanes_of(j, 256)]
+        up = mixed[:, lanes_of(j + 3, 256)]
         sigmoid = jax.nn.sigmoid(gate)
-        back_mixed_ref[:, lanes_of(j, 256)] = (back_hidden * up * (sigmoid * (1.0 + gate * (1.0 - sigmoid)))).astype(bf16)
-        back_mixed_ref[:, lanes_of(j + 3, 256)] = (back_hidden * (gate * sigmoid)).astype(bf16)
+        back_mixed[:, lanes_of(j, 256)] = (back_hidden * up * (sigmoid * (1.0 + gate * (1.0 - sigmoid)))).astype(bf16)
+        back_mixed[:, lanes_of(j + 3, 256)] = (back_hidden * (gate * sigmoid)).astype(bf16)
+    stores.append(copy(back_mixed, back_mixed_hbm, 8))
+    stores[-1].start()
     for j in range(D // 256):
-        part = lax.dot_general(back_mixed_ref[...], first_ref[lanes_of(j, 256), :], NT, preferred_element_type=f32)
+        if j % 2 == 0:
+            loads[3 + j // 2].wait()
+        part = lax.dot_general(back_mixed[...], first[lanes_of(j, 256), :], NT, preferred_element_type=f32)
         tiles[pl.ds(2 * j, ROWS, stride=CHUNKS), :] = part[:, :128]
         tiles[pl.ds(2 * j + 1, ROWS, stride=CHUNKS), :] = part[:, 128:]
-    gh_ref[...] = tiles[...].astype(bf16)
+    gh[...] = tiles[...].astype(bf16)
+    stores.append(copy(gh, gh_hbm, 9))
+    stores[-1].start()
+    for store in stores:
+        store.wait()
 
 
 def expert_backward(rows, first, second, mixed):
     return pl.pallas_call(
         expert_back_kernel,
-        in_specs=[pl.BlockSpec(memory_space=pltpu.VMEM)] * 4,
-        out_specs=[pl.BlockSpec(memory_space=pltpu.VMEM)] * 3,
-        scratch_shapes=[pltpu.VMEM((TILES, 128), f32)],
+        in_specs=[HBM] * 4,
+        out_specs=[HBM] * 3,
+        scratch_shapes=[
+            pltpu.VMEM((TILES, 128), bf16),
+            pltpu.VMEM((D, 2 * FF), bf16),
+            pltpu.VMEM((FF, D), bf16),
+            pltpu.VMEM((ROWS, 2 * FF), f32),
+            pltpu.VMEM((ROWS, D), bf16),
+            pltpu.VMEM((ROWS, 2 * FF), bf16),
+            pltpu.VMEM((TILES, 128), bf16),
+            pltpu.VMEM((TILES, 128), f32),
+            pltpu.SemaphoreType.DMA((10,)),
+        ],
         out_shape=[
             jax.ShapeDtypeStruct((ROWS, D), bf16),
             jax.ShapeDtypeStruct((ROWS, 2 * FF), bf16),
             jax.ShapeDtypeStruct((TILES, 128), bf16),
         ],
-        compiler_params=pltpu.CompilerParams(vmem_limit_bytes=48 * 2**20),
+        compiler_params=pltpu.CompilerParams(vmem_limit_bytes=60 * 2**20),
         cost_estimate=pl.CostEstimate(flops=36 * 10**8, bytes_accessed=17 * 2**20, transcendentals=3 * 10**5),
         name="expert_backward",
     )(rows, first, second, mixed)
@@ -666,7 +787,7 @@
             jax.ShapeDtypeStruct((LOCAL, D), bf16),
             jax.ShapeDtypeStruct((1, D), f32),
         ],
-        compiler_params=pltpu.CompilerParams(vmem_limit_bytes=40 * 2**20),
+        compiler_params=pltpu.CompilerParams(vmem_limit_bytes=12 * 2**20),
         cost_estimate=pl.CostEstimate(flops=2 * 10**6, bytes_accessed=6 * 2**20, transcendentals=128),
         name="collect",
     )(slots, gh, x2, g3, gain)
@@ -718,9 +839,9 @@
     leaving = dot(leave, w_in, NT).astype(bf16)
     arrived = jnp.concatenate([lax.ppermute(leaving[40 * i : 40 * i + 40], ALL, perms[i]) for i in range(3)], axis=0)
     out_slot = lax.ppermute(w_out, ALL, out_perm())
-    arrived, out_slot = lax.optimization_barrier((arrived, out_slot))
+    arrived, out_slot = tie((arrived, out_slot))
     in_slot = dot(arrive, arrived).astype(bf16)
-    in_slot, cosine, sine = lax.optimization_barrier((in_slot, cosine, sine))
+    in_slot, cosine, sine = tie((in_slot, cosine, sine))
     in_some, out_some = ring_gather(in_slot, "y"), ring_gather(out_slot, "z")
     in_some, out_some = tie((in_some, out_some))
     out_mine = ring_gather(out_some, "y").reshape(HEADS * HD, D)
@@ -779,19 +900,15 @@
     there = lax.dynamic_index_in_dim(dkv, 1 - c, 0, keepdims=False)
     chip_kv = (own.astype(f32) + shift(there, "c", 1).astype(f32)).astype(bf16)
 
-    dq, chip_kv = tie((dq, chip_kv))
+    dq, chip_kv, out_moved = tie((dq, chip_kv, out_moved))
+    out_summed = jnp.sum(out_moved.astype(f32), axis=0).astype(bf16)
+    out_gradient = lax.ppermute(out_summed, ALL, [(b, a) for a, b in out_perm()]).astype(f32)
     kv_parts = lax.all_to_all(chip_kv, "z", split_axis=0, concat_axis=0, tiled=True)
 
     gp_q, q_term = project_back(dq, projected, cosine, sine, q_gain_row, 0)
-    in_q = dot(gp_q, h1_group, TN)
-
-    back_kv = jnp.sum(kv_parts.astype(f32), axis=0)
-    back_k, k_term = project_back(back_kv, projected, cosine, sine, k_gain_row, HEADS)
-    gp_kv = jnp.where(c == 0, back_k, back_kv.astype(bf16))
-    k_term = jnp.where(c == 0, k_term, 0.0)
-    in_kv = dot(gp_kv, h1_group, TN)
-    in_partial = jnp.concatenate([in_q.astype(bf16), in_kv.astype(bf16)], axis=0).reshape(16, 40, D)
-    in_partial, gp_q, gp_kv, out_moved = tie((in_partial, gp_q, gp_kv, out_moved))
+    in_q = dot(jnp.pad(gp_q, ((0, 0), (0, HD))), h1_group, TN).astype(bf16)
+    gp_kv, k_term, in_partial = kv_back(c_array, kv_parts, projected, cosine, sine, k_gain_row, h1_group, in_q)
+    in_partial, gp_q, gp_kv, out_gradient = tie((in_partial.reshape(16, 40, D), gp_q, gp_kv, out_gradient))
     in_parts = lax.all_to_all(in_partial, ("z", "y"), split_axis=0, concat_axis=0, tiled=True)
 
     gain1_term = jnp.sum(in_partial.reshape(640, D).astype(f32) * in_mine.astype(f32), axis=0) / gain1
@@ -804,15 +921,12 @@
     gh1 = RingSum(gh1_chip.reshape(4, LOCAL, D), "x").total()
     gn1 = gh1 * gain1
     tokens_gradient = g2 + r1 * (gn1 - n1 * jnp.mean(gn1 * n1, axis=-1, keepdims=True))
-    out_summed = jnp.sum(out_moved.astype(f32), axis=0).astype(bf16)
-
-    in_parts, terms, out_summed = tie((in_parts, terms, out_summed))
     in_summed = jnp.sum(in_parts.astype(f32), axis=0)
-    out_gradient = lax.ppermute(out_summed, ALL, [(b, a) for a, b in out_perm()]).astype(f32)
-    sums = sum_over(sum_over(terms, "y"), "z").reshape(-1)
+    in_summed, terms = tie((in_summed, terms))
 
     going = dot(arrive, in_summed.astype(bf16), TN).astype(bf16)
     home = [lax.ppermute(going[40 * i : 40 * i + 40], ALL, [(b, a) for a, b in perms[i]]) for i in range(3)]
+    sums = jnp.sum(spread(terms, ("y", "z"), 16), axis=0).reshape(-1)
     in_gradient = dot(jnp.concatenate(home, axis=0), leave, TN)
 
     loss = jnp.sum(sums[2 * D + 2 * HD :]) / (2.0 * valid_count * D)

time: 559 us -> 535 us (0.957)
  the two profiles are of different devices: /device:TPU:25 before, /device:TPU:28 now
where the time goes in v4:
time: 535 us; the launch traced here: 525 us
  starting transfers between devices  137 us (26%)
  waiting for transfers between devices  136 us (25%)
  Pallas kernels  96.7 us (18%)
  blocking collectives  60.9 us (11%)
  matrix products  34.9 us (7%)
  local copies, waits for them, and re-layouts  28.9 us (5%)
  other arithmetic  24.6 us (5%)
  between operations  5.86 us (1%)
    ppermute x45, waiting for transfers between devices, shift(): lax.ppermute(value, axis, [(i, (i + step) % size) for i in range(size)])  68.5 us
    all_to_all x2, blocking collectives, exchange(): return lax.all_to_all(rows, ALL, split_axis=0, concat_axis=0, tiled=True)  60.9 us
    ppermute x45, starting transfers between devices, shift(): lax.ppermute(value, axis, [(i, (i + step) % size) for i in range(size)])  51.5 us
    pallas_call x1, Pallas kernels, attend_backward(): pl.pallas_call(backward_kernel, grid_spec=pltpu.PrefetchScalarGridSpec(nu...  35 us
    dot_general x15, matrix products, dot(): return lax.dot_general(a, b, dims, preferred_element_type=f32)  34.9 us
    all_to_all x2, waiting for transfers between devices, exchange(): return lax.all_to_all(rows, ALL, split_axis=0, concat_axis=0, tiled=True)  25.5 us
    all_to_all x1, waiting for transfers between devices, body(): lax.all_to_all(chip_out.astype(bf16).reshape(4, LOCAL, D), 'x', split_axi...  22.8 us
    all_to_all x2, starting transfers between devices, exchange(): return lax.all_to_all(rows, ALL, split_axis=0, concat_axis=0, tiled=True)  19 us
  transfers between devices with their start and end apart: 60, of which 31 were waited for; matrix products, arithmetic and copies ran while one was open for 10% of the time, Pallas kernels for 12%

profile of v4, /device:TPU:28, one launch (start us, length us, event | category | flops | bytes accessed | tf_op | source)
XLA Modules:
  0.0 524.7 jit_solution(6391604725030830899)
XLA Ops:
  8.7 6.9 %collective-permute-start.6 = (bf16[40,2048]{1,0:T(8,128)(2,1)}, bf16[40,2048]{1,0:T(8,128)(2,1)}, u32[]{:S(2)}, u32[]{:S(2)}) collective-permute-start(bf16[40,2048]{1,0:T(8,128)(2,1)} %get-tuple-element.128), channel_id=1, source_target_pairs={{12,1},{13,33},{14,65},{15,97},{16,3},{17,35},{18,67},{19,99},{20,... | collective-permute-start | bytes 491528 | tf_op jit(solution)/shard_map/ppermute | solution.py:840
  25.4 6.7 %collective-permute-done.5 = bf16[40,2048]{1,0:T(8,128)(2,1)} collective-permute-done((bf16[40,2048]{1,0:T(8,128)(2,1)S(1)}, bf16[40,2048]{1,0:T(8,128)(2,1)}, u32[]{:S(2)}, u32[]{:S(2)}) %collective-permute-start.5) | collective-permute-done | bytes 163872 | tf_op jit(solution)/shard_map/ppermute | solution.py:840
  76.7 7.7 %collective-permute-done.20 = bf16[4,40,1024]{2,1,0:T(8,128)(2,1)S(1)} collective-permute-done((bf16[4,40,1024]{2,1,0:T(8,128)(2,1)S(1)}, bf16[4,40,1024]{2,1,0:T(8,128)(2,1)S(1)}, u32[]{:S(2)}, u32[]{:S(2)}) %collective-permute-start.20) | collective-permute-done | bytes 327712 | tf_op jit(solution)/shard_map/ppermute | solution.py:130
  114.5 14.2 %attend_forward.1 = (bf16[1024,512]{1,0:T(8,128)(2,1)S(1)}, f32[4,4,8,256]{3,2,1,0:T(8,128)S(1)}) custom-call(s32[1]{0:T(128)} %bitcast.1.z_ref, bf16[1024,512]{1,0:T(8,128)(2,1)S(1)} %get-tuple-element.68.q_ref, bf16[2,4,1024,128]{3,2,1,0:T(8,128)(2,1)S(1)} %bitcast_dynamic-update-slice_fusion.1.kv_ref), custom_call_target="tpu_custom_call" | custom-call | flops 8999999488 | bytes 8388608 | tf_op jit(solution)/shard_map/attend_forward/pallas_call | solution.py:388
  134.8 8.6 %all-to-all-start = ((bf16[4,128,2048]{2,1,0:T(8,128)(2,1)}), bf16[4,128,2048]{2,1,0:T(8,128)(2,1)}, u32[]{:S(2)}, u32[]{:S(2)}) async-start(bf16[4,128,2048]{2,1,0:T(8,128)(2,1)} %bitcast.208), calls=%async_computation | async-start | bytes 4194304 | tf_op jit(solution)/shard_map/all_to_all | solution.py:859
  144.6 22.8 %all-to-all-done.moved_ref = bf16[4,128,2048]{2,1,0:T(8,128)(2,1)} async-done(((bf16[4,128,2048]{2,1,0:T(8,128)(2,1)}), bf16[4,128,2048]{2,1,0:T(8,128)(2,1)}, u32[]{:S(2)}, u32[]{:S(2)}) %all-to-all-start) | async-done | bytes 2097184 | tf_op jit(solution)/shard_map/all_to_all | solution.py:859
  172.6 31.0 %all_to_all.45.x_hbm = bf16[128,56,128]{2,1,0:T(8,128)(2,1)} all-to-all(bf16[128,56,128]{2,1,0:T(8,128)(2,1)S(1)} %get-tuple-element.72), channel_id=1, replica_groups=mesh['y'=4,'x'=4,'z'=4,'c'=2] {'y','x','z','c'}, dimensions={0} | all-to-all | bytes 3670016 | tf_op jit(solution)/shard_map/all_to_all | solution.py:801
  203.6 9.4 %expert_forward.1 = (bf16[384,2048]{1,0:T(8,128)(2,1)}, f32[384,1536]{1,0:T(8,128)}, bf16[384,768]{1,0:T(8,128)(2,1)}, bf16[6144,128]{1,0:T(8,128)(2,1)}) custom-call(bf16[128,56,128]{2,1,0:T(8,128)(2,1)} %all_to_all.45.x_hbm, bf16[2048,1536]{1,0:T(8,128)(2,1)} %bitcast.220, bf16[768,2048]{1,0:T(8,128)(2,1)} %bitcast.225), custom_call_target="tpu_custom_call" | custom-call | flops 3600000000 | bytes 17825792 | tf_op jit(solution)/shard_map/expert_forward/pallas_call | solution.py:610
  213.0 9.4 %all-to-all-start.2 = ((bf16[128,48,128]{2,1,0:T(8,128)(2,1)}), bf16[128,48,128]{2,1,0:T(8,128)(2,1)}, u32[]{:S(2)}, u32[]{:S(2)}) async-start(bf16[128,48,128]{2,1,0:T(8,128)(2,1)} %bitcast.231), calls=%async_computation.2 | async-start | bytes 3145728 | tf_op jit(solution)/shard_map/all_to_all | solution.py:801
  225.4 17.7 %all-to-all-done.2 = bf16[128,48,128]{2,1,0:T(8,128)(2,1)} async-done(((bf16[128,48,128]{2,1,0:T(8,128)(2,1)}), bf16[128,48,128]{2,1,0:T(8,128)(2,1)}, u32[]{:S(2)}, u32[]{:S(2)}) %all-to-all-start.2) | async-done | bytes 1572896 | tf_op jit(solution)/shard_map/all_to_all | solution.py:801
  250.9 29.9 %all_to_all.46 = bf16[128,48,128]{2,1,0:T(8,128)(2,1)} all-to-all(bf16[128,48,128]{2,1,0:T(8,128)(2,1)S(1)} %get-tuple-element.76), channel_id=1, replica_groups=mesh['y'=4,'x'=4,'z'=4,'c'=2] {'y','x','z','c'}, dimensions={0} | all-to-all | bytes 3145728 | tf_op jit(solution)/shard_map/all_to_all | solution.py:801
  280.8 10.8 %expert_backward.1 = (bf16[384,2048]{1,0:T(8,128)(2,1)}, bf16[384,1536]{1,0:T(8,128)(2,1)}, bf16[6144,128]{1,0:T(8,128)(2,1)}) custom-call(bf16[6144,128]{1,0:T(8,128)(2,1)} %bitcast.222, bf16[2048,1536]{1,0:T(8,128)(2,1)} %bitcast.221, bf16[768,2048]{1,0:T(8,128)(2,1)} %bitcast.226, f32[384,1536]{1,0:T(8,128)} %get-tuple-element.77.mixed_hbm), custom_call_target="tpu_custom_call" | custom-call | flops 3600000000 | bytes 17825792 | tf_op jit(solution)/shard_map/expert_backward/pallas_call | solution.py:722
  291.7 9.6 %all-to-all-start.4 = ((bf16[128,48,128]{2,1,0:T(8,128)(2,1)}), bf16[128,48,128]{2,1,0:T(8,128)(2,1)}, u32[]{:S(2)}, u32[]{:S(2)}) async-start(bf16[128,48,128]{2,1,0:T(8,128)(2,1)} %bitcast.232), calls=%async_computation.4 | async-start | bytes 3145728 | tf_op jit(solution)/shard_map/all_to_all | solution.py:801
  301.3 6.3 %fusion.46 = f32[768,2048]{1,0:T(8,128)} fusion(bf16[384,768]{1,0:T(8,128)(2,1)} %get-tuple-element.81, bf16[384,2048]{1,0:T(8,128)(2,1)} %get-tuple-element.82), kind=kOutput, calls=%fused_computation.149 | convolution fusion | flops 1207959552 | bytes 8454144 | tf_op jit(solution)/shard_map/dot_general | solution.py:797
  307.6 6.6 %fusion.45 = f32[2048,1536]{1,0:T(8,128)} fusion(bf16[384,2048]{1,0:T(8,128)(2,1)S(1)} %copy-done.39, bf16[384,1536]{1,0:T(8,128)(2,1)S(1)} %copy-done.40), kind=kOutput, calls=%fused_computation.148 | convolution fusion | flops 2415919104 | bytes 15335424 | tf_op jit(solution)/shard_map/dot_general | solution.py:797
  314.2 7.7 %all-to-all-done.4 = bf16[128,48,128]{2,1,0:T(8,128)(2,1)} async-done(((bf16[128,48,128]{2,1,0:T(8,128)(2,1)}), bf16[128,48,128]{2,1,0:T(8,128)(2,1)}, u32[]{:S(2)}, u32[]{:S(2)}) %all-to-all-start.4) | async-done | bytes 1572896 | tf_op jit(solution)/shard_map/all_to_all | solution.py:801
  332.1 10.9 %collective-permute-done.33 = bf16[128,2048]{1,0:T(8,128)(2,1)S(1)} collective-permute-done((bf16[128,2048]{1,0:T(8,128)(2,1)S(1)}, bf16[128,2048]{1,0:T(8,128)(2,1)S(1)}, u32[]{:S(2)}, u32[]{:S(2)}) %collective-permute-start.33) | collective-permute-done | bytes 524320 | tf_op jit(solution)/shard_map/ppermute | solution.py:130
  360.9 6.7 %all-to-all-start.5 = ((bf16[16,32,2048]{2,1,0:T(8,128)(2,1)}), bf16[16,32,2048]{2,1,0:T(8,128)(2,1)}, u32[]{:S(2)}, u32[]{:S(2)}) async-start(bf16[16,32,2048]{2,1,0:T(8,128)(2,1)} %bitcast.209), calls=%async_computation.5 | async-start | bytes 4194304 | tf_op jit(solution)/shard_map/all_to_all | solution.py:896
  367.7 35.0 %attend_backward.1 = (bf16[1024,512]{1,0:T(8,128)(2,1)}, bf16[2,4,1024,128]{3,2,1,0:T(8,128)(2,1)}) custom-call(s32[1]{0:T(128)} %bitcast.1.z_ref, bf16[1024,512]{1,0:T(8,128)(2,1)} %copy-done.26, bf16[2,4,1024,128]{3,2,1,0:T(8,128)(2,1)} %copy-done.14, bf16[1024,512]{1,0:T(8,128)(2,1)} %bitcast.233, bf16[1024,512]{1,0:T(8,128)(2,1)} %copy-done.17, ...), custom_call_target="tpu_custom_call" | custom-call | flops 22000001024 | bytes 8388608 | tf_op jit(solution)/shard_map/attend_backward/pallas_call | solution.py:479
  414.9 7.1 %collective-permute-start.39 = (bf16[32,2048]{1,0:T(8,128)(2,1)S(1)}, bf16[32,2048]{1,0:T(8,128)(2,1)S(1)}, u32[]{:S(2)}, u32[]{:S(2)}) collective-permute-start(bf16[32,2048]{1,0:T(8,128)(2,1)S(1)} %reduce_sum.137), channel_id=1, source_target_pairs={{0,0},{2,1},{4,2},{6,3},{32,4},{34,5},{36,6},{38,7},{64,8},{66,9},... | collective-permute-start | bytes 393224 | tf_op jit(solution)/shard_map/ppermute | solution.py:905
  435.0 5.8 %kv_back.1 = (bf16[1024,128]{1,0:T(8,128)(2,1)}, f32[1,128]{1,0:T(1,128)}, bf16[640,2048]{1,0:T(8,128)(2,1)}) custom-call(s32[1]{0:T(128)} %bitcast.2.core_ref, bf16[4,1024,128]{2,1,0:T(8,128)(2,1)} %all-to-all-done.6.parts_ref, f32[1024,640]{1,0:T(8,128)} %copy-done.5, f32[1024,128]{1,0:T(8,128)} %copy-done.7, ...), custom_call_target="tpu_custom_call", output_to_operand_aliasing={{2}: (7, {})} | custom-call | flops 600000000 | bytes 8388608 | tf_op jit(solution)/shard_map/kv_back/pallas_call | solution.py:316
  440.8 7.3 %all-to-all-start.7 = ((bf16[16,40,2048]{2,1,0:T(8,128)(2,1)}), bf16[16,40,2048]{2,1,0:T(8,128)(2,1)}, u32[]{:S(2)}, u32[]{:S(2)}) async-start(bf16[16,40,2048]{2,1,0:T(8,128)(2,1)} %bitcast.202), calls=%async_computation.7 | async-start | bytes 5242880 | tf_op jit(solution)/shard_map/all_to_all | solution.py:912
  475.9 7.4 %collective-permute-done.43 = f32[35,128]{1,0:T(8,128)S(1)} collective-permute-done((f32[35,128]{1,0:T(8,128)S(1)}, f32[35,128]{1,0:T(8,128)S(1)}, u32[]{:S(2)}, u32[]{:S(2)}) %collective-permute-start.43) | collective-permute-done | bytes 17952 | tf_op jit(solution)/shard_map/ppermute | solution.py:130
  488.0 7.2 %all-to-all-start.8 = ((f32[16,35,128]{2,1,0:T(8,128)}), f32[16,35,128]{2,1,0:T(8,128)S(1)}, u32[]{:S(2)}, u32[]{:S(2)}) async-start(f32[16,35,128]{2,1,0:T(8,128)} %broadcast_in_dim.288), calls=%async_computation.8 | async-start | bytes 655360 | tf_op jit(solution)/shard_map/all_to_all | solution.py:195
  (338 shorter events, 226.0 us)
Async XLA Ops:
  4.7 57.8 %collective-permute-start = (bf16[128,2048]{1,0:T(8,128)(2,1)}, bf16[128,2048]{1,0:T(8,128)(2,1)S(1)}, u32[]{:S(2)}, u32[]{:S(2)}) collective-permute-start(bf16[128,2048]{1,0:T(8,128)(2,1)} %get-tuple-element.114), channel_id=1, source_target_pairs={{0,8},{8,16},{16,24},{24,0},{1,9},{9,17},{17,25},{25,1},{2,10},{10... | collective-permute-start | bytes 1572872 | tf_op jit(solution)/shard_map/ppermute | solution.py:130
  5.9 55.0 %collective-permute-start.1 = (bf16[128,2048]{1,0:T(8,128)(2,1)}, bf16[128,2048]{1,0:T(8,128)(2,1)S(1)}, u32[]{:S(2)}, u32[]{:S(2)}) collective-permute-start(bf16[128,2048]{1,0:T(8,128)(2,1)} %get-tuple-element.114), channel_id=1, source_target_pairs={{0,24},{8,0},{16,8},{24,16},{1,25},{9,1},{17,9},{25,17},{2,26},{10... | collective-permute-start | bytes 1572872 | tf_op jit(solution)/shard_map/ppermute | solution.py:130
  8.7 16.7 %collective-permute-start.6 = (bf16[40,2048]{1,0:T(8,128)(2,1)}, bf16[40,2048]{1,0:T(8,128)(2,1)}, u32[]{:S(2)}, u32[]{:S(2)}) collective-permute-start(bf16[40,2048]{1,0:T(8,128)(2,1)} %get-tuple-element.128), channel_id=1, source_target_pairs={{12,1},{13,33},{14,65},{15,97},{16,3},{17,35},{18,67},{19,99},{20,... | collective-permute-start | bytes 491528 | tf_op jit(solution)/shard_map/ppermute | solution.py:840
  15.5 16.5 %collective-permute-start.5 = (bf16[40,2048]{1,0:T(8,128)(2,1)S(1)}, bf16[40,2048]{1,0:T(8,128)(2,1)}, u32[]{:S(2)}, u32[]{:S(2)}) collective-permute-start(bf16[40,2048]{1,0:T(8,128)(2,1)S(1)} %get-tuple-element.126), channel_id=1, source_target_pairs={{0,0},{1,32},{2,64},{3,96},{4,2},{5,34},{6,66},{7,98},{8,4},{9,36}... | collective-permute-start | bytes 491528 | tf_op jit(solution)/shard_map/ppermute | solution.py:840
  54.2 20.2 %collective-permute-start.17 = (bf16[4,40,2048]{2,1,0:T(8,128)(2,1)S(1)}, bf16[4,40,2048]{2,1,0:T(8,128)(2,1)S(1)}, u32[]{:S(2)}, u32[]{:S(2)}) collective-permute-start(bf16[4,40,2048]{2,1,0:T(8,128)(2,1)S(1)} %fusion.30), channel_id=1, source_target_pairs={{0,2},{2,4},{4,6},{6,0},{1,3},{3,5},{5,7},{7,1},{8,10},{10,12},{12... | collective-permute-start | bytes 1966088 | tf_op jit(solution)/shard_map/ppermute | solution.py:130
  55.6 18.6 %collective-permute-start.18 = (bf16[4,40,2048]{2,1,0:T(8,128)(2,1)S(1)}, bf16[4,40,2048]{2,1,0:T(8,128)(2,1)S(1)}, u32[]{:S(2)}, u32[]{:S(2)}) collective-permute-start(bf16[4,40,2048]{2,1,0:T(8,128)(2,1)S(1)} %fusion.30), channel_id=1, source_target_pairs={{0,6},{2,0},{4,2},{6,4},{1,7},{3,1},{5,3},{7,5},{8,14},{10,8},{12,... | collective-permute-start | bytes 1966088 | tf_op jit(solution)/shard_map/ppermute | solution.py:130
  57.5 37.9 %collective-permute-start.26 = (bf16[4,32,2048]{2,1,0:T(8,128)(2,1)S(1)}, bf16[4,32,2048]{2,1,0:T(8,128)(2,1)S(1)}, u32[]{:S(2)}, u32[]{:S(2)}) collective-permute-start(bf16[4,32,2048]{2,1,0:T(8,128)(2,1)S(1)} %fusion.32), channel_id=1, source_target_pairs={{0,32},{32,64},{64,96},{96,0},{1,33},{33,65},{65,97},{97,1},{2,34}... | collective-permute-start | bytes 1572872 | tf_op jit(solution)/shard_map/ppermute | solution.py:130
  68.2 27.0 %collective-permute-start.27 = (bf16[4,32,2048]{2,1,0:T(8,128)(2,1)S(1)}, bf16[4,32,2048]{2,1,0:T(8,128)(2,1)S(1)}, u32[]{:S(2)}, u32[]{:S(2)}) collective-permute-start(bf16[4,32,2048]{2,1,0:T(8,128)(2,1)S(1)} %fusion.32), channel_id=1, source_target_pairs={{0,96},{32,0},{64,32},{96,64},{1,97},{33,1},{65,33},{97,65},{2,98}... | collective-permute-start | bytes 1572872 | tf_op jit(solution)/shard_map/ppermute | solution.py:130
  95.3 16.6 %collective-permute-start.29 = (bf16[4,32,1024]{2,1,0:T(8,128)(2,1)S(1)}, bf16[4,32,1024]{2,1,0:T(8,128)(2,1)S(1)}, u32[]{:S(2)}, u32[]{:S(2)}) collective-permute-start(bf16[4,32,1024]{2,1,0:T(8,128)(2,1)S(1)} %slice.161), channel_id=1, source_target_pairs={{0,96},{32,0},{64,32},{96,64},{1,97},{33,1},{65,33},{97,65},{2,98}... | collective-permute-start | bytes 786440 | tf_op jit(solution)/shard_map/ppermute | solution.py:130
  95.4 16.4 %collective-permute-start.28 = (bf16[4,32,1024]{2,1,0:T(8,128)(2,1)S(1)}, bf16[4,32,1024]{2,1,0:T(8,128)(2,1)S(1)}, u32[]{:S(2)}, u32[]{:S(2)}) collective-permute-start(bf16[4,32,1024]{2,1,0:T(8,128)(2,1)S(1)} %slice.160), channel_id=1, source_target_pairs={{0,32},{32,64},{64,96},{96,0},{1,33},{33,65},{65,97},{97,1},{2,34}... | collective-permute-start | bytes 786440 | tf_op jit(solution)/shard_map/ppermute | solution.py:130
  112.0 17.2 %collective-permute-start.31 = (bf16[512,2048]{1,0:T(8,128)(2,1)S(1)}, bf16[512,2048]{1,0:T(8,128)(2,1)S(1)}, u32[]{:S(2)}, u32[]{:S(2)}) collective-permute-start(bf16[512,2048]{1,0:T(8,128)(2,1)S(1)} %bitcast.213), channel_id=1, source_target_pairs={{0,1},{1,0},{2,3},{3,2},{4,5},{5,4},{6,7},{7,6},{8,9},{9,8},{10,11... | collective-permute-start | bytes 6291464 | tf_op jit(solution)/shard_map/ppermute | solution.py:130
  134.8 32.7 %all-to-all-start = ((bf16[4,128,2048]{2,1,0:T(8,128)(2,1)}), bf16[4,128,2048]{2,1,0:T(8,128)(2,1)}, u32[]{:S(2)}, u32[]{:S(2)}) async-start(bf16[4,128,2048]{2,1,0:T(8,128)(2,1)} %bitcast.208), calls=%async_computation | async-start | bytes 4194304 | tf_op jit(solution)/shard_map/all_to_all | solution.py:859
  213.0 30.1 %all-to-all-start.2 = ((bf16[128,48,128]{2,1,0:T(8,128)(2,1)}), bf16[128,48,128]{2,1,0:T(8,128)(2,1)}, u32[]{:S(2)}, u32[]{:S(2)}) async-start(bf16[128,48,128]{2,1,0:T(8,128)(2,1)} %bitcast.231), calls=%async_computation.2 | async-start | bytes 3145728 | tf_op jit(solution)/shard_map/all_to_all | solution.py:801
  291.7 30.2 %all-to-all-start.4 = ((bf16[128,48,128]{2,1,0:T(8,128)(2,1)}), bf16[128,48,128]{2,1,0:T(8,128)(2,1)}, u32[]{:S(2)}, u32[]{:S(2)}) async-start(bf16[128,48,128]{2,1,0:T(8,128)(2,1)} %bitcast.232), calls=%async_computation.4 | async-start | bytes 3145728 | tf_op jit(solution)/shard_map/all_to_all | solution.py:801
  360.9 41.8 %all-to-all-start.5 = ((bf16[16,32,2048]{2,1,0:T(8,128)(2,1)}), bf16[16,32,2048]{2,1,0:T(8,128)(2,1)}, u32[]{:S(2)}, u32[]{:S(2)}) async-start(bf16[16,32,2048]{2,1,0:T(8,128)(2,1)} %bitcast.209), calls=%async_computation.5 | async-start | bytes 4194304 | tf_op jit(solution)/shard_map/all_to_all | solution.py:896
  404.2 47.2 %collective-permute-start.45 = (bf16[640,2048]{1,0:T(8,128)(2,1)S(1)}, bf16[640,2048]{1,0:T(8,128)(2,1)}, u32[]{:S(2)}, u32[]{:S(2)}) collective-permute-start(bf16[640,2048]{1,0:T(8,128)(2,1)S(1)} %bitcast.189), channel_id=1, source_target_pairs={{0,1},{1,0},{2,3},{3,2},{4,5},{5,4},{6,7},{7,6},{8,9},{9,8},{10,11... | collective-permute-start | bytes 7864328 | tf_op jit(solution)/shard_map/ppermute | solution.py:130
  408.7 26.3 %all-to-all-start.6 = ((bf16[4,1024,128]{2,1,0:T(8,128)(2,1)}), bf16[4,1024,128]{2,1,0:T(8,128)(2,1)}, u32[]{:S(2)}, u32[]{:S(2)}) async-start(bf16[4,1024,128]{2,1,0:T(8,128)(2,1)} %fusion.1), calls=%async_computation.6 | async-start | bytes 2097152 | tf_op jit(solution)/shard_map/all_to_all | solution.py:906
  414.9 19.4 %collective-permute-start.39 = (bf16[32,2048]{1,0:T(8,128)(2,1)S(1)}, bf16[32,2048]{1,0:T(8,128)(2,1)S(1)}, u32[]{:S(2)}, u32[]{:S(2)}) collective-permute-start(bf16[32,2048]{1,0:T(8,128)(2,1)S(1)} %reduce_sum.137), channel_id=1, source_target_pairs={{0,0},{2,1},{4,2},{6,3},{32,4},{34,5},{36,6},{38,7},{64,8},{66,9},... | collective-permute-start | bytes 393224 | tf_op jit(solution)/shard_map/ppermute | solution.py:905
  440.8 44.3 %all-to-all-start.7 = ((bf16[16,40,2048]{2,1,0:T(8,128)(2,1)}), bf16[16,40,2048]{2,1,0:T(8,128)(2,1)}, u32[]{:S(2)}, u32[]{:S(2)}) async-start(bf16[16,40,2048]{2,1,0:T(8,128)(2,1)} %bitcast.202), calls=%async_computation.7 | async-start | bytes 5242880 | tf_op jit(solution)/shard_map/all_to_all | solution.py:912
  466.2 17.2 %collective-permute-start.49 = (bf16[128,2048]{1,0:T(8,128)(2,1)S(1)}, bf16[128,2048]{1,0:T(8,128)(2,1)S(1)}, u32[]{:S(2)}, u32[]{:S(2)}) collective-permute-start(bf16[128,2048]{1,0:T(8,128)(2,1)S(1)} %pad_maximum_fusion.4), channel_id=1, source_target_pairs={{0,24},{8,0},{16,8},{24,16},{1,25},{9,1},{17,9},{25,17},{2,26},{10... | collective-permute-start | bytes 1572872 | tf_op jit(solution)/shard_map/ppermute | solution.py:130
  468.1 15.3 %collective-permute-start.47 = (bf16[128,2048]{1,0:T(8,128)(2,1)S(1)}, bf16[128,2048]{1,0:T(8,128)(2,1)S(1)}, u32[]{:S(2)}, u32[]{:S(2)}) collective-permute-start(bf16[128,2048]{1,0:T(8,128)(2,1)S(1)} %pad_maximum_fusion.3), channel_id=1, source_target_pairs={{0,8},{8,16},{16,24},{24,0},{1,9},{9,17},{17,25},{25,1},{2,10},{10... | collective-permute-start | bytes 1572872 | tf_op jit(solution)/shard_map/ppermute | solution.py:130
  488.0 32.7 %all-to-all-start.8 = ((f32[16,35,128]{2,1,0:T(8,128)}), f32[16,35,128]{2,1,0:T(8,128)S(1)}, u32[]{:S(2)}, u32[]{:S(2)}) async-start(f32[16,35,128]{2,1,0:T(8,128)} %broadcast_in_dim.288), calls=%async_computation.8 | async-start | bytes 655360 | tf_op jit(solution)/shard_map/all_to_all | solution.py:195
  496.4 18.2 %collective-permute-start.51 = (bf16[40,2048]{1,0:T(8,128)(2,1)S(1)}, bf16[40,2048]{1,0:T(8,128)(2,1)S(1)}, u32[]{:S(2)}, u32[]{:S(2)}) collective-permute-start(bf16[40,2048]{1,0:T(8,128)(2,1)S(1)} %get-tuple-element.125), channel_id=1, source_target_pairs={{1,12},{33,13},{65,14},{97,15},{3,16},{35,17},{67,18},{99,19},{5,2... | collective-permute-start | bytes 491528 | tf_op jit(solution)/shard_map/ppermute | solution.py:928
  501.9 17.8 %collective-permute-start.50 = (bf16[40,2048]{1,0:T(8,128)(2,1)S(1)}, bf16[40,2048]{1,0:T(8,128)(2,1)S(1)}, u32[]{:S(2)}, u32[]{:S(2)}) collective-permute-start(bf16[40,2048]{1,0:T(8,128)(2,1)S(1)} %get-tuple-element.123), channel_id=1, source_target_pairs={{0,0},{32,1},{64,2},{96,3},{2,4},{34,5},{66,6},{98,7},{4,8},{36,9}... | collective-permute-start | bytes 491528 | tf_op jit(solution)/shard_map/ppermute | solution.py:928
  (86 other events, 731.7 us)

commit v5 on v4

--- a/solution.py
+++ b/solution.py
@@ -32,6 +32,9 @@
 LOG2E = 1.4426950408889634
 f32 = jnp.float32
 bf16 = jnp.bfloat16
+
+
+HEAD_ORDER = ((0, 1, 2, 3), (1, 2, 3, 0), (2, 3, 1, 0), (3, 2, 0, 1), (3, 0, 1, 2), (0, 1, 2, 3), (1, 2, 3, 0), (2, 3, 1, 0))
 
 
 def device_of(y, x, z, c):
@@ -88,7 +91,7 @@
     for x in range(4):
         for c in range(2):
             group = 2 * x + c
-            wanted = [64 * group + s for s in range(64)]
+            wanted = [64 * group + 16 * head + s for head in HEAD_ORDER[group] for s in range(16)]
             wanted += [512 + 64 * c + 16 * x + s for s in range(16)]
             for s, part in enumerate(wanted):
                 slot, place = s // 5, s % 5
@@ -120,9 +123,13 @@
         for x in range(4):
             for z in range(4):
                 for c in range(2):
-                    slot = device_of(y, x, z, c) % 16
+                    head, quarter = divmod(device_of(y, x, z, c) % 16, 4)
+                    slot = 4 * HEAD_ORDER[2 * y + x // 2].index(head) + quarter
                     perm.append((device_of(y, x, z, c), device_of(slot // 4, y, slot % 4, x // 2)))
     return perm
+
+
+tie = lax.optimization_barrier
 
 
 def shift(value, axis, step):
@@ -130,16 +137,26 @@
     return lax.ppermute(value, axis, [(i, (i + step) % size) for i in range(size)])
 
 
+def ring_gathers(*pairs):
+    near = []
+    for value, axis in pairs:
+        near += [shift(value, axis, 1), shift(value, axis, -1)]
+    if len(pairs) > 1:
+        near = tie(tuple(near))
+    outs = []
+    for (value, axis), before, after in zip(pairs, near[::2], near[1::2]):
+        index = lax.axis_index(axis)
+        half = value.shape[-1] // 2
+        far = jnp.concatenate([shift(before[..., :half], axis, 1), shift(after[..., half:], axis, -1)], axis=-1)
+        out = jnp.zeros((4,) + value.shape, value.dtype)
+        for offset, block in ((0, value), (3, before), (1, after), (2, far)):
+            out = lax.dynamic_update_index_in_dim(out, block, (index + offset) % 4, 0)
+        outs.append(out)
+    return outs
+
+
 def ring_gather(value, axis):
-    index = lax.axis_index(axis)
-    half = value.shape[-1] // 2
-    before = shift(value, axis, 1)
-    after = shift(value, axis, -1)
-    far = jnp.concatenate([shift(before[..., :half], axis, 1), shift(after[..., half:], axis, -1)], axis=-1)
-    out = jnp.zeros((4,) + value.shape, value.dtype)
-    for offset, block in ((0, value), (3, before), (1, after), (2, far)):
-        out = lax.dynamic_update_index_in_dim(out, block, (index + offset) % 4, 0)
-    return out
+    return ring_gathers((value, axis))[0]
 
 
 def core_gather(value):
@@ -158,9 +175,6 @@
 def scatter_sum(value, axes, count):
     moved = lax.all_to_all(value, axes, split_axis=0, concat_axis=0, tiled=True)
     return jnp.sum(moved.astype(f32), axis=0)
-
-
-tie = lax.optimization_barrier
 
 
 class RingSum:
@@ -410,7 +424,7 @@
     )(z, queries, keys_values)
 
 
-def backward_kernel(z_ref, q_ref, kv_ref, go_ref, o_ref, lse_ref, dq_ref, dkv_ref, dqt, dkv, kt):
+def backward_kernel(z_ref, core_ref, q_ref, kv_ref, go_ref, o_ref, lse_ref, dq_ref, own_ref, there_ref, dqt, dkv, kt):
     piece = pl.program_id(0)
     z = z_ref[0]
 
@@ -469,26 +483,28 @@
 
     @pl.when(piece == 3)
     def _():
-        dkv_ref[0] = (dkv[0] * SCALE).astype(bf16)
-        dkv_ref[1] = dkv[1].astype(bf16)
-
-
-def attend_backward(z, queries, keys_values, backs, outs, lse):
-    heads_spec = pl.BlockSpec((PIECE, HEADS * HD), lambda i, z: (i, 0))
-    whole = pl.BlockSpec((2, 4, GROUP, HD), lambda i, z: (0, 0, 0, 0))
+        core = core_ref[0]
+        own_ref[...] = (dkv[core] * jnp.where(core == 0, SCALE, 1.0)).astype(bf16)
+        there_ref[...] = (dkv[1 - core] * jnp.where(core == 0, 1.0, SCALE)).astype(bf16)
+
+
+def attend_backward(z, core, queries, keys_values, backs, outs, lse):
+    heads_spec = pl.BlockSpec((PIECE, HEADS * HD), lambda i, z, c: (i, 0))
+    whole = pl.BlockSpec((2, 4, GROUP, HD), lambda i, z, c: (0, 0, 0, 0))
+    part = pl.BlockSpec((4, GROUP, HD), lambda i, z, c: (0, 0, 0))
     return pl.pallas_call(
         backward_kernel,
         grid_spec=pltpu.PrefetchScalarGridSpec(
-            num_scalar_prefetch=1,
+            num_scalar_prefetch=2,
             grid=(4,),
             in_specs=[
                 heads_spec,
                 whole,
                 heads_spec,
                 heads_spec,
-                pl.BlockSpec((HEADS, 1, 8, PIECE), lambda i, z: (0, i, 0, 0)),
+                pl.BlockSpec((HEADS, 1, 8, PIECE), lambda i, z, c: (0, i, 0, 0)),
             ],
-            out_specs=[heads_spec, whole],
+            out_specs=[heads_spec, part, part],
             scratch_shapes=[
                 pltpu.VMEM((HD, HEADS * PIECE), f32),
                 pltpu.VMEM((2, 4, GROUP, HD), f32),
@@ -497,12 +513,13 @@
         ),
         out_shape=[
             jax.ShapeDtypeStruct((GROUP, HEADS * HD), bf16),
-            jax.ShapeDtypeStruct((2, 4, GROUP, HD), bf16),
+            jax.ShapeDtypeStruct((4, GROUP, HD), bf16),
+            jax.ShapeDtypeStruct((4, GROUP, HD), bf16),
         ],
         compiler_params=pltpu.CompilerParams(vmem_limit_bytes=60 * 2**20),
         cost_estimate=pl.CostEstimate(flops=22 * 10**9, bytes_accessed=8 * 2**20, transcendentals=10**7),
         name="attend_backward",
-    )(z, queries, keys_values, backs, outs, lse)
+    )(z, core, queries, keys_values, backs, outs, lse)
 
 
 ROWS = EXPERTS * CAP
@@ -842,10 +859,12 @@
     arrived, out_slot = tie((arrived, out_slot))
     in_slot = dot(arrive, arrived).astype(bf16)
     in_slot, cosine, sine = tie((in_slot, cosine, sine))
-    in_some, out_some = ring_gather(in_slot, "y"), ring_gather(out_slot, "z")
+    in_some = spread(in_slot, "y", 4)
+    out_some = ring_gather(out_slot, "z")
     in_some, out_some = tie((in_some, out_some))
-    out_mine = ring_gather(out_some, "y").reshape(HEADS * HD, D)
-    in_mine = ring_gather(in_some, "z").reshape(640, D)
+    in_mine, out_mine = ring_gathers((in_some, "z"), (out_some, "y"))
+    in_mine = in_mine.reshape(640, D)
+    out_mine = out_mine.reshape(HEADS * HD, D)
 
     projected, queries, key_or_value = project(c_array, h1_group, in_mine, cosine, sine, q_gain_row, k_gain_row)
     keys_values = core_gather(ring_gather(key_or_value, "z"))
@@ -892,12 +911,9 @@
     gb_other = shift(gb_mine, "c", 1)
     out_partial = (dot(attended_mine, gb_mine, TN) + dot(attended_other, gb_other, TN)).astype(bf16)
     backs, out_partial = lax.optimization_barrier((backs, out_partial))
-    dq, dkv = attend_backward(z_array, queries, keys_values, backs, attended, lse)
+    dq, own, there = attend_backward(z_array, c_array, queries, keys_values, backs, attended, lse)
     out_moved = lax.all_to_all(out_partial.reshape(16, 32, D), ("y", "z"), split_axis=0, concat_axis=0, tiled=True)
-    dkv, out_moved = tie((dkv, out_moved))
-
-    own = lax.dynamic_index_in_dim(dkv, c, 0, keepdims=False)
-    there = lax.dynamic_index_in_dim(dkv, 1 - c, 0, keepdims=False)
+    own, there, out_moved = tie((own, there, out_moved))
     chip_kv = (own.astype(f32) + shift(there, "c", 1).astype(f32)).astype(bf16)
 
     dq, chip_kv, out_moved = tie((dq, chip_kv, out_moved))

time: 535 us -> 532 us (level)
  the two profiles are of different devices: /device:TPU:28 before, /device:TPU:29 now
where the time goes in v5:
time: 532 us; the launch traced here: 523 us
  starting transfers between devices  140 us (26%)
  waiting for transfers between devices  125 us (23%)
  Pallas kernels  96.7 us (18%)
  blocking collectives  61.5 us (12%)
  matrix products  35 us (7%)
  local copies, waits for them, and re-layouts  31.2 us (6%)
  other arithmetic  27.5 us (5%)
  between operations  5.69 us (1%)
    all_to_all x2, blocking collectives, exchange(): return lax.all_to_all(rows, ALL, split_axis=0, concat_axis=0, tiled=True)  61.5 us
    ppermute x41, starting transfers between devices, shift(): lax.ppermute(value, axis, [(i, (i + step) % size) for i in range(size)])  60 us
    ppermute x41, waiting for transfers between devices, shift(): lax.ppermute(value, axis, [(i, (i + step) % size) for i in range(size)])  52.1 us
    pallas_call x1, Pallas kernels, attend_backward(): pl.pallas_call(backward_kernel, grid_spec=pltpu.PrefetchScalarGridSpec(nu...  35 us
    dot_general x15, matrix products, dot(): return lax.dot_general(a, b, dims, preferred_element_type=f32)  35 us
    all_to_all x2, waiting for transfers between devices, exchange(): return lax.all_to_all(rows, ALL, split_axis=0, concat_axis=0, tiled=True)  25.2 us
    all_to_all x1, waiting for transfers between devices, body(): lax.all_to_all(chip_out.astype(bf16).reshape(4, LOCAL, D), 'x', split_axi...  22.4 us
    all_to_all x2, starting transfers between devices, exchange(): return lax.all_to_all(rows, ALL, split_axis=0, concat_axis=0, tiled=True)  19.3 us
  transfers between devices with their start and end apart: 57, of which 26 were waited for; matrix products, arithmetic and copies ran while one was open for 12% of the time, Pallas kernels for 11%

profile of v5, /device:TPU:29, one launch (start us, length us, event | category | flops | bytes accessed | tf_op | source)
XLA Modules:
  0.0 522.5 jit_solution(369101017925455799)
XLA Ops:
  8.1 8.3 %collective-permute-start.6 = (bf16[40,2048]{1,0:T(8,128)(2,1)}, bf16[40,2048]{1,0:T(8,128)(2,1)}, u32[]{:S(2)}, u32[]{:S(2)}) collective-permute-start(bf16[40,2048]{1,0:T(8,128)(2,1)} %get-tuple-element.140), channel_id=1, source_target_pairs={{13,37},{14,69},{15,101},{25,44},{29,74},{30,106},{31,12},{38,75},... | collective-permute-start | bytes 491528 | tf_op jit(solution)/shard_map/ppermute | solution.py:857
  27.6 6.6 %collective-permute-done.8 = bf16[32,2048]{1,0:T(8,128)(2,1)S(1)} collective-permute-done((bf16[32,2048]{1,0:T(8,128)(2,1)S(1)}, bf16[32,2048]{1,0:T(8,128)(2,1)S(1)}, u32[]{:S(2)}, u32[]{:S(2)}) %collective-permute-start.8) | collective-permute-done | bytes 131104 | tf_op jit(solution)/shard_map/ppermute | solution.py:858
  95.4 6.0 %collective-permute-done.22 = bf16[1024,64]{1,0:T(8,128)(2,1)S(1)} collective-permute-done((bf16[1024,64]{1,0:T(8,128)(2,1)S(1)}, bf16[1024,64]{1,0:T(8,128)(2,1)S(1)}, u32[]{:S(2)}, u32[]{:S(2)}) %collective-permute-start.22) | collective-permute-done | bytes 131104 | tf_op jit(solution)/shard_map/ppermute | solution.py:137
  103.1 10.5 %collective-permute-start.23 = (bf16[4,1024,128]{2,1,0:T(8,128)(2,1)S(1)}, bf16[4,1024,128]{2,1,0:T(8,128)(2,1)S(1)}, u32[]{:S(2)}, u32[]{:S(2)}) collective-permute-start(bf16[4,1024,128]{2,1,0:T(8,128)(2,1)S(1)} %fusion.26), channel_id=1, source_target_pairs={{0,1},{1,0},{2,3},{3,2},{4,5},{5,4},{6,7},{7,6},{8,9},{9,8},{10,11... | collective-permute-start | bytes 3145736 | tf_op jit(solution)/shard_map/ppermute | solution.py:137
  116.0 14.2 %attend_forward.1 = (bf16[1024,512]{1,0:T(8,128)(2,1)S(1)}, f32[4,4,8,256]{3,2,1,0:T(8,128)S(1)}) custom-call(s32[1]{0:T(128)} %bitcast.1.z_ref, bf16[1024,512]{1,0:T(8,128)(2,1)S(1)} %get-tuple-element.77.q_ref, bf16[2,4,1024,128]{3,2,1,0:T(8,128)(2,1)S(1)} %bitcast_dynamic-update-slice_fusion.1.kv_ref), custom_call_target="tpu_custom_call" | custom-call | flops 8999999488 | bytes 8388608 | tf_op jit(solution)/shard_map/attend_forward/pallas_call | solution.py:402
  134.9 5.9 %all-to-all-start.1 = ((bf16[4,128,2048]{2,1,0:T(8,128)(2,1)}), bf16[4,128,2048]{2,1,0:T(8,128)(2,1)}, u32[]{:S(2)}, u32[]{:S(2)}) async-start(bf16[4,128,2048]{2,1,0:T(8,128)(2,1)} %bitcast.193), calls=%async_computation.1 | async-start | bytes 4194304 | tf_op jit(solution)/shard_map/all_to_all | solution.py:878
  142.0 22.4 %all-to-all-done.1.moved_ref = bf16[4,128,2048]{2,1,0:T(8,128)(2,1)} async-done(((bf16[4,128,2048]{2,1,0:T(8,128)(2,1)}), bf16[4,128,2048]{2,1,0:T(8,128)(2,1)}, u32[]{:S(2)}, u32[]{:S(2)}) %all-to-all-start.1) | async-done | bytes 2097184 | tf_op jit(solution)/shard_map/all_to_all | solution.py:878
  169.6 31.5 %all_to_all.50.x_hbm = bf16[128,56,128]{2,1,0:T(8,128)(2,1)} all-to-all(bf16[128,56,128]{2,1,0:T(8,128)(2,1)S(1)} %get-tuple-element.82), channel_id=1, replica_groups=mesh['y'=4,'x'=4,'z'=4,'c'=2] {'y','x','z','c'}, dimensions={0} | all-to-all | bytes 3670016 | tf_op jit(solution)/shard_map/all_to_all | solution.py:818
  201.1 9.4 %expert_forward.1 = (bf16[384,2048]{1,0:T(8,128)(2,1)}, f32[384,1536]{1,0:T(8,128)}, bf16[384,768]{1,0:T(8,128)(2,1)}, bf16[6144,128]{1,0:T(8,128)(2,1)}) custom-call(bf16[128,56,128]{2,1,0:T(8,128)(2,1)} %all_to_all.50.x_hbm, bf16[2048,1536]{1,0:T(8,128)(2,1)} %bitcast.205, bf16[768,2048]{1,0:T(8,128)(2,1)} %bitcast.210), custom_call_target="tpu_custom_call" | custom-call | flops 3600000000 | bytes 17825792 | tf_op jit(solution)/shard_map/expert_forward/pallas_call | solution.py:627
  210.6 9.6 %all-to-all-start.3 = ((bf16[128,48,128]{2,1,0:T(8,128)(2,1)}), bf16[128,48,128]{2,1,0:T(8,128)(2,1)}, u32[]{:S(2)}, u32[]{:S(2)}) async-start(bf16[128,48,128]{2,1,0:T(8,128)(2,1)} %bitcast.215), calls=%async_computation.3 | async-start | bytes 3145728 | tf_op jit(solution)/shard_map/all_to_all | solution.py:818
  223.1 17.6 %all-to-all-done.3 = bf16[128,48,128]{2,1,0:T(8,128)(2,1)} async-done(((bf16[128,48,128]{2,1,0:T(8,128)(2,1)}), bf16[128,48,128]{2,1,0:T(8,128)(2,1)}, u32[]{:S(2)}, u32[]{:S(2)}) %all-to-all-start.3) | async-done | bytes 1572896 | tf_op jit(solution)/shard_map/all_to_all | solution.py:818
  248.4 29.9 %all_to_all.51 = bf16[128,48,128]{2,1,0:T(8,128)(2,1)} all-to-all(bf16[128,48,128]{2,1,0:T(8,128)(2,1)S(1)} %get-tuple-element.86), channel_id=1, replica_groups=mesh['y'=4,'x'=4,'z'=4,'c'=2] {'y','x','z','c'}, dimensions={0} | all-to-all | bytes 3145728 | tf_op jit(solution)/shard_map/all_to_all | solution.py:818
  278.4 10.8 %expert_backward.1 = (bf16[384,2048]{1,0:T(8,128)(2,1)}, bf16[384,1536]{1,0:T(8,128)(2,1)}, bf16[6144,128]{1,0:T(8,128)(2,1)}) custom-call(bf16[6144,128]{1,0:T(8,128)(2,1)} %bitcast.207, bf16[2048,1536]{1,0:T(8,128)(2,1)} %bitcast.206, bf16[768,2048]{1,0:T(8,128)(2,1)} %bitcast.211, f32[384,1536]{1,0:T(8,128)} %get-tuple-element.87.mixed_hbm), custom_call_target="tpu_custom_call" | custom-call | flops 3600000000 | bytes 17825792 | tf_op jit(solution)/shard_map/expert_backward/pallas_call | solution.py:739
  289.2 9.7 %all-to-all-start.5 = ((bf16[128,48,128]{2,1,0:T(8,128)(2,1)}), bf16[128,48,128]{2,1,0:T(8,128)(2,1)}, u32[]{:S(2)}, u32[]{:S(2)}) async-start(bf16[128,48,128]{2,1,0:T(8,128)(2,1)} %bitcast.216), calls=%async_computation.5 | async-start | bytes 3145728 | tf_op jit(solution)/shard_map/all_to_all | solution.py:818
  299.0 6.3 %fusion.44 = f32[768,2048]{1,0:T(8,128)} fusion(bf16[384,768]{1,0:T(8,128)(2,1)} %get-tuple-element.91, bf16[384,2048]{1,0:T(8,128)(2,1)} %get-tuple-element.92), kind=kOutput, calls=%fused_computation.142 | convolution fusion | flops 1207959552 | bytes 8454144 | tf_op jit(solution)/shard_map/dot_general | solution.py:814
  305.2 6.6 %fusion.43 = f32[2048,1536]{1,0:T(8,128)} fusion(bf16[384,2048]{1,0:T(8,128)(2,1)S(1)} %copy-done.38, bf16[384,1536]{1,0:T(8,128)(2,1)S(1)} %copy-done.39), kind=kOutput, calls=%fused_computation.141 | convolution fusion | flops 2415919104 | bytes 15335424 | tf_op jit(solution)/shard_map/dot_general | solution.py:814
  311.8 7.6 %all-to-all-done.5 = bf16[128,48,128]{2,1,0:T(8,128)(2,1)} async-done(((bf16[128,48,128]{2,1,0:T(8,128)(2,1)}), bf16[128,48,128]{2,1,0:T(8,128)(2,1)}, u32[]{:S(2)}, u32[]{:S(2)}) %all-to-all-start.5) | async-done | bytes 1572896 | tf_op jit(solution)/shard_map/all_to_all | solution.py:818
  328.8 11.0 %collective-permute-done.29 = bf16[128,2048]{1,0:T(8,128)(2,1)S(1)} collective-permute-done((bf16[128,2048]{1,0:T(8,128)(2,1)S(1)}, bf16[128,2048]{1,0:T(8,128)(2,1)S(1)}, u32[]{:S(2)}, u32[]{:S(2)}) %collective-permute-start.29) | collective-permute-done | bytes 524320 | tf_op jit(solution)/shard_map/ppermute | solution.py:137
  358.6 6.4 %all-to-all-start.6 = ((bf16[16,32,2048]{2,1,0:T(8,128)(2,1)}), bf16[16,32,2048]{2,1,0:T(8,128)(2,1)}, u32[]{:S(2)}, u32[]{:S(2)}) async-start(bf16[16,32,2048]{2,1,0:T(8,128)(2,1)} %bitcast.194), calls=%async_computation.6 | async-start | bytes 4194304 | tf_op jit(solution)/shard_map/all_to_all | solution.py:915
  365.1 35.0 %attend_backward.1 = (bf16[1024,512]{1,0:T(8,128)(2,1)}, bf16[4,1024,128]{2,1,0:T(8,128)(2,1)}, bf16[4,1024,128]{2,1,0:T(8,128)(2,1)}) custom-call(s32[1]{0:T(128)} %bitcast.1.z_ref, s32[1]{0:T(128)} %bitcast.2.core_ref, bf16[1024,512]{1,0:T(8,128)(2,1)} %copy-done.26, bf16[2,4,1024,128]{3,2,1,0:T(8,128)(2,1)} %copy-done.14, bf16[1024,512]{1,0:T(8,128)(2,1)} %bitcast.217, ...), custom_call_target="tpu_custom_call" | custom-call | flops 22000001024 | bytes 8388608 | tf_op jit(solution)/shard_map/attend_backward/pallas_call | solution.py:495
  412.5 7.2 %collective-permute-start.35 = (bf16[32,2048]{1,0:T(8,128)(2,1)S(1)}, bf16[32,2048]{1,0:T(8,128)(2,1)S(1)}, u32[]{:S(2)}, u32[]{:S(2)}) collective-permute-start(bf16[32,2048]{1,0:T(8,128)(2,1)S(1)} %reduce_sum.137), channel_id=1, source_target_pairs={{0,0},{2,1},{4,2},{6,3},{32,4},{34,5},{36,6},{38,7},{64,8},{66,9},... | collective-permute-start | bytes 393224 | tf_op jit(solution)/shard_map/ppermute | solution.py:921
  473.6 5.9 %collective-permute-done.39 = f32[35,128]{1,0:T(8,128)S(1)} collective-permute-done((f32[35,128]{1,0:T(8,128)S(1)}, f32[35,128]{1,0:T(8,128)S(1)}, u32[]{:S(2)}, u32[]{:S(2)}) %collective-permute-start.39) | collective-permute-done | bytes 17952 | tf_op jit(solution)/shard_map/ppermute | solution.py:137
  484.2 6.7 %all-to-all-start.9 = ((f32[16,35,128]{2,1,0:T(8,128)}), f32[16,35,128]{2,1,0:T(8,128)S(1)}, u32[]{:S(2)}, u32[]{:S(2)}) async-start(f32[16,35,128]{2,1,0:T(8,128)} %broadcast_in_dim.274), calls=%async_computation.9 | async-start | bytes 655360 | tf_op jit(solution)/shard_map/all_to_all | solution.py:209
  503.2 14.3 %collective-permute-done.46 = bf16[40,2048]{1,0:T(8,128)(2,1)S(1)} collective-permute-done((bf16[40,2048]{1,0:T(8,128)(2,1)S(1)}, bf16[40,2048]{1,0:T(8,128)(2,1)S(1)}, u32[]{:S(2)}, u32[]{:S(2)}) %collective-permute-start.46) | collective-permute-done | bytes 163872 | tf_op jit(solution)/shard_map/ppermute | solution.py:944
  (323 shorter events, 217.4 us)
Async XLA Ops:
  4.7 49.4 %collective-permute-start = (bf16[128,2048]{1,0:T(8,128)(2,1)}, bf16[128,2048]{1,0:T(8,128)(2,1)S(1)}, u32[]{:S(2)}, u32[]{:S(2)}) collective-permute-start(bf16[128,2048]{1,0:T(8,128)(2,1)} %get-tuple-element.126), channel_id=1, source_target_pairs={{0,8},{8,16},{16,24},{24,0},{1,9},{9,17},{17,25},{25,1},{2,10},{10... | collective-permute-start | bytes 1572872 | tf_op jit(solution)/shard_map/ppermute | solution.py:137
  5.7 45.8 %collective-permute-start.1 = (bf16[128,2048]{1,0:T(8,128)(2,1)}, bf16[128,2048]{1,0:T(8,128)(2,1)S(1)}, u32[]{:S(2)}, u32[]{:S(2)}) collective-permute-start(bf16[128,2048]{1,0:T(8,128)(2,1)} %get-tuple-element.126), channel_id=1, source_target_pairs={{0,24},{8,0},{16,8},{24,16},{1,25},{9,1},{17,9},{25,17},{2,26},{10... | collective-permute-start | bytes 1572872 | tf_op jit(solution)/shard_map/ppermute | solution.py:137
  7.4 14.5 %collective-permute-start.7 = (bf16[40,2048]{1,0:T(8,128)(2,1)}, bf16[40,2048]{1,0:T(8,128)(2,1)S(1)}, u32[]{:S(2)}, u32[]{:S(2)}) collective-permute-start(bf16[40,2048]{1,0:T(8,128)(2,1)} %get-tuple-element.139), channel_id=1, source_target_pairs={{102,6},{105,14},{115,7},{118,15},{121,23},{12,37},{76,60},{28,74}... | collective-permute-start | bytes 491528 | tf_op jit(solution)/shard_map/ppermute | solution.py:857
  8.1 15.8 %collective-permute-start.6 = (bf16[40,2048]{1,0:T(8,128)(2,1)}, bf16[40,2048]{1,0:T(8,128)(2,1)}, u32[]{:S(2)}, u32[]{:S(2)}) collective-permute-start(bf16[40,2048]{1,0:T(8,128)(2,1)} %get-tuple-element.140), channel_id=1, source_target_pairs={{13,37},{14,69},{15,101},{25,44},{29,74},{30,106},{31,12},{38,75},... | collective-permute-start | bytes 491528 | tf_op jit(solution)/shard_map/ppermute | solution.py:857
  38.1 17.8 %all-to-all-start = ((bf16[4,40,2048]{2,1,0:T(8,128)(2,1)}), bf16[4,40,2048]{2,1,0:T(8,128)(2,1)}, u32[]{:S(2)}, u32[]{:S(2)}) async-start(bf16[4,40,2048]{2,1,0:T(8,128)(2,1)} %broadcast_in_dim.239), calls=%async_computation | async-start | bytes 1310720 | tf_op jit(solution)/shard_map/all_to_all | solution.py:209
  55.9 13.9 %collective-permute-start.13 = (bf16[4,40,2048]{2,1,0:T(8,128)(2,1)}, bf16[4,40,2048]{2,1,0:T(8,128)(2,1)S(1)}, u32[]{:S(2)}, u32[]{:S(2)}) collective-permute-start(bf16[4,40,2048]{2,1,0:T(8,128)(2,1)} %all-to-all-done), channel_id=1, source_target_pairs={{0,2},{2,4},{4,6},{6,0},{1,3},{3,5},{5,7},{7,1},{8,10},{10,12},{12... | collective-permute-start | bytes 1966088 | tf_op jit(solution)/shard_map/ppermute | solution.py:137
  56.4 13.3 %collective-permute-start.14 = (bf16[4,40,2048]{2,1,0:T(8,128)(2,1)}, bf16[4,40,2048]{2,1,0:T(8,128)(2,1)S(1)}, u32[]{:S(2)}, u32[]{:S(2)}) collective-permute-start(bf16[4,40,2048]{2,1,0:T(8,128)(2,1)} %all-to-all-done), channel_id=1, source_target_pairs={{0,6},{2,0},{4,2},{6,4},{1,7},{3,1},{5,3},{7,5},{8,14},{10,8},{12,... | collective-permute-start | bytes 1966088 | tf_op jit(solution)/shard_map/ppermute | solution.py:137
  61.6 18.2 %collective-permute-start.4 = (bf16[512,2048]{1,0:T(8,128)(2,1)}, bf16[512,2048]{1,0:T(8,128)(2,1)S(1)}, u32[]{:S(2)}, u32[]{:S(2)}) collective-permute-start(bf16[512,2048]{1,0:T(8,128)(2,1)} %bitcast.8), channel_id=1, source_target_pairs={{0,1},{1,0},{2,3},{3,2},{4,5},{5,4},{6,7},{7,6},{8,9},{9,8},{10,11... | collective-permute-start | bytes 6291464 | tf_op jit(solution)/shard_map/ppermute | solution.py:137
  90.0 23.7 %collective-permute-start.25 = (bf16[4,32,1024]{2,1,0:T(8,128)(2,1)S(1)}, bf16[4,32,1024]{2,1,0:T(8,128)(2,1)S(1)}, u32[]{:S(2)}, u32[]{:S(2)}) collective-permute-start(bf16[4,32,1024]{2,1,0:T(8,128)(2,1)S(1)} %slice.117), channel_id=1, source_target_pairs={{0,96},{32,0},{64,32},{96,64},{1,97},{33,1},{65,33},{97,65},{2,98}... | collective-permute-start | bytes 786440 | tf_op jit(solution)/shard_map/ppermute | solution.py:137
  90.7 23.0 %collective-permute-start.24 = (bf16[4,32,1024]{2,1,0:T(8,128)(2,1)S(1)}, bf16[4,32,1024]{2,1,0:T(8,128)(2,1)S(1)}, u32[]{:S(2)}, u32[]{:S(2)}) collective-permute-start(bf16[4,32,1024]{2,1,0:T(8,128)(2,1)S(1)} %slice.116), channel_id=1, source_target_pairs={{0,32},{32,64},{64,96},{96,0},{1,33},{33,65},{65,97},{97,1},{2,34}... | collective-permute-start | bytes 786440 | tf_op jit(solution)/shard_map/ppermute | solution.py:137
  113.8 18.3 %collective-permute-start.27 = (bf16[512,2048]{1,0:T(8,128)(2,1)S(1)}, bf16[512,2048]{1,0:T(8,128)(2,1)S(1)}, u32[]{:S(2)}, u32[]{:S(2)}) collective-permute-start(bf16[512,2048]{1,0:T(8,128)(2,1)S(1)} %bitcast.196), channel_id=1, source_target_pairs={{0,1},{1,0},{2,3},{3,2},{4,5},{5,4},{6,7},{7,6},{8,9},{9,8},{10,11... | collective-permute-start | bytes 6291464 | tf_op jit(solution)/shard_map/ppermute | solution.py:137
  134.9 29.5 %all-to-all-start.1 = ((bf16[4,128,2048]{2,1,0:T(8,128)(2,1)}), bf16[4,128,2048]{2,1,0:T(8,128)(2,1)}, u32[]{:S(2)}, u32[]{:S(2)}) async-start(bf16[4,128,2048]{2,1,0:T(8,128)(2,1)} %bitcast.193), calls=%async_computation.1 | async-start | bytes 4194304 | tf_op jit(solution)/shard_map/all_to_all | solution.py:878
  210.6 30.1 %all-to-all-start.3 = ((bf16[128,48,128]{2,1,0:T(8,128)(2,1)}), bf16[128,48,128]{2,1,0:T(8,128)(2,1)}, u32[]{:S(2)}, u32[]{:S(2)}) async-start(bf16[128,48,128]{2,1,0:T(8,128)(2,1)} %bitcast.215), calls=%async_computation.3 | async-start | bytes 3145728 | tf_op jit(solution)/shard_map/all_to_all | solution.py:818
  289.2 30.2 %all-to-all-start.5 = ((bf16[128,48,128]{2,1,0:T(8,128)(2,1)}), bf16[128,48,128]{2,1,0:T(8,128)(2,1)}, u32[]{:S(2)}, u32[]{:S(2)}) async-start(bf16[128,48,128]{2,1,0:T(8,128)(2,1)} %bitcast.216), calls=%async_computation.5 | async-start | bytes 3145728 | tf_op jit(solution)/shard_map/all_to_all | solution.py:818
  326.8 13.0 %collective-permute-start.29 = (bf16[128,2048]{1,0:T(8,128)(2,1)S(1)}, bf16[128,2048]{1,0:T(8,128)(2,1)S(1)}, u32[]{:S(2)}, u32[]{:S(2)}) collective-permute-start(bf16[128,2048]{1,0:T(8,128)(2,1)S(1)} %get-tuple-element.95), channel_id=1, source_target_pairs={{0,24},{8,0},{16,8},{24,16},{1,25},{9,1},{17,9},{25,17},{2,26},{10... | collective-permute-start | bytes 1572872 | tf_op jit(solution)/shard_map/ppermute | solution.py:137
  358.6 41.5 %all-to-all-start.6 = ((bf16[16,32,2048]{2,1,0:T(8,128)(2,1)}), bf16[16,32,2048]{2,1,0:T(8,128)(2,1)}, u32[]{:S(2)}, u32[]{:S(2)}) async-start(bf16[16,32,2048]{2,1,0:T(8,128)(2,1)} %bitcast.194), calls=%async_computation.6 | async-start | bytes 4194304 | tf_op jit(solution)/shard_map/all_to_all | solution.py:915
  405.8 26.8 %all-to-all-start.7 = ((bf16[4,1024,128]{2,1,0:T(8,128)(2,1)}), bf16[4,1024,128]{2,1,0:T(8,128)(2,1)}, u32[]{:S(2)}, u32[]{:S(2)}) async-start(bf16[4,1024,128]{2,1,0:T(8,128)(2,1)} %add_convert_fusion.2), calls=%async_computation.7 | async-start | bytes 2097152 | tf_op jit(solution)/shard_map/all_to_all | solution.py:922
  410.1 41.1 %collective-permute-start.41 = (bf16[640,2048]{1,0:T(8,128)(2,1)S(1)}, bf16[640,2048]{1,0:T(8,128)(2,1)}, u32[]{:S(2)}, u32[]{:S(2)}) collective-permute-start(bf16[640,2048]{1,0:T(8,128)(2,1)S(1)} %bitcast.177), channel_id=1, source_target_pairs={{0,1},{1,0},{2,3},{3,2},{4,5},{5,4},{6,7},{7,6},{8,9},{9,8},{10,11... | collective-permute-start | bytes 7864328 | tf_op jit(solution)/shard_map/ppermute | solution.py:137
  412.5 19.4 %collective-permute-start.35 = (bf16[32,2048]{1,0:T(8,128)(2,1)S(1)}, bf16[32,2048]{1,0:T(8,128)(2,1)S(1)}, u32[]{:S(2)}, u32[]{:S(2)}) collective-permute-start(bf16[32,2048]{1,0:T(8,128)(2,1)S(1)} %reduce_sum.137), channel_id=1, source_target_pairs={{0,0},{2,1},{4,2},{6,3},{32,4},{34,5},{36,6},{38,7},{64,8},{66,9},... | collective-permute-start | bytes 393224 | tf_op jit(solution)/shard_map/ppermute | solution.py:921
  438.4 42.7 %all-to-all-start.8 = ((bf16[16,40,2048]{2,1,0:T(8,128)(2,1)}), bf16[16,40,2048]{2,1,0:T(8,128)(2,1)}, u32[]{:S(2)}, u32[]{:S(2)}) async-start(bf16[16,40,2048]{2,1,0:T(8,128)(2,1)} %bitcast.187), calls=%async_computation.8 | async-start | bytes 5242880 | tf_op jit(solution)/shard_map/all_to_all | solution.py:928
  464.0 15.5 %collective-permute-start.45 = (bf16[128,2048]{1,0:T(8,128)(2,1)S(1)}, bf16[128,2048]{1,0:T(8,128)(2,1)S(1)}, u32[]{:S(2)}, u32[]{:S(2)}) collective-permute-start(bf16[128,2048]{1,0:T(8,128)(2,1)S(1)} %pad_maximum_fusion.4), channel_id=1, source_target_pairs={{0,24},{8,0},{16,8},{24,16},{1,25},{9,1},{17,9},{25,17},{2,26},{10... | collective-permute-start | bytes 1572872 | tf_op jit(solution)/shard_map/ppermute | solution.py:137
  464.8 14.7 %collective-permute-start.43 = (bf16[128,2048]{1,0:T(8,128)(2,1)S(1)}, bf16[128,2048]{1,0:T(8,128)(2,1)S(1)}, u32[]{:S(2)}, u32[]{:S(2)}) collective-permute-start(bf16[128,2048]{1,0:T(8,128)(2,1)S(1)} %pad_maximum_fusion.3), channel_id=1, source_target_pairs={{0,8},{8,16},{16,24},{24,0},{1,9},{9,17},{17,25},{25,1},{2,10},{10... | collective-permute-start | bytes 1572872 | tf_op jit(solution)/shard_map/ppermute | solution.py:137
  484.2 34.4 %all-to-all-start.9 = ((f32[16,35,128]{2,1,0:T(8,128)}), f32[16,35,128]{2,1,0:T(8,128)S(1)}, u32[]{:S(2)}, u32[]{:S(2)}) async-start(f32[16,35,128]{2,1,0:T(8,128)} %broadcast_in_dim.274), calls=%async_computation.9 | async-start | bytes 655360 | tf_op jit(solution)/shard_map/all_to_all | solution.py:209
  493.3 24.2 %collective-permute-start.46 = (bf16[40,2048]{1,0:T(8,128)(2,1)S(1)}, bf16[40,2048]{1,0:T(8,128)(2,1)S(1)}, u32[]{:S(2)}, u32[]{:S(2)}) collective-permute-start(bf16[40,2048]{1,0:T(8,128)(2,1)S(1)} %get-tuple-element.135), channel_id=1, source_target_pairs={{0,0},{32,1},{64,2},{96,3},{2,4},{34,5},{66,6},{98,7},{4,8},{36,9}... | collective-permute-start | bytes 491528 | tf_op jit(solution)/shard_map/ppermute | solution.py:944
  (82 other events, 575.9 us)

commit v6 on v5

--- a/solution.py
+++ b/solution.py
@@ -545,10 +545,7 @@
 
 
 def dispatch_kernel(index_ref, count_ref, moved_ref, token_ref, gain_ref, x2_ref, out_ref, tiles):
-    x2 = moved_ref[0].astype(f32)
-    for i in range(1, 4):
-        x2 += moved_ref[i].astype(f32)
-    x2 = token_ref[...].astype(f32) + x2
+    x2 = token_ref[...].astype(f32) + moved_ref[...]
     x2_ref[...] = x2
     h2 = x2 * lax.rsqrt(jnp.mean(x2 * x2, axis=-1, keepdims=True) + epsilon) * gain_ref[...]
     for k in range(CHUNKS):
@@ -651,7 +648,13 @@
     )(rows, first, second)
 
 
-def combine_kernel(index_ref, slot_ref, gate_ref, slot_gate_ref, scale_ref, y_ref, x2_ref, target_ref, mask_ref, output_ref, loss_ref, g3_ref, out_ref, tiles):
+def combine_kernel(index_ref, slot_ref, gate_ref, slot_gate_ref, scale_ref, y_hbm, x2_hbm, target_hbm, mask_ref, output_ref, loss_ref, g3_ref, out_ref, y_ref, x2_ref, target_ref, tiles, sems):
+    pairs = ((y_hbm, y_ref), (x2_hbm, x2_ref), (target_hbm, target_ref))
+    loads = [pltpu.make_async_copy(source, to, sems.at[i]) for i, (source, to) in enumerate(pairs)]
+    for load in loads:
+        load.start()
+    loads[0].wait()
+
     def row_of(number):
         return y_ref[pl.ds(pl.multiple_of(slot_ref[number] * CHUNKS, CHUNKS), CHUNKS), :].astype(f32)
 
@@ -661,6 +664,8 @@
         return carry
 
     lax.fori_loop(0, LOCAL, body, 0, unroll=4)
+    loads[1].wait()
+    loads[2].wait()
     mask = mask_ref[...]
     squares = jnp.zeros((LOCAL, 128), f32)
     for k in range(CHUNKS):
@@ -682,9 +687,15 @@
         combine_kernel,
         grid_spec=pltpu.PrefetchScalarGridSpec(
             num_scalar_prefetch=5,
-            in_specs=[pl.BlockSpec(memory_space=pltpu.VMEM)] * 4,
+            in_specs=[HBM] * 3 + [pl.BlockSpec(memory_space=pltpu.VMEM)],
             out_specs=[pl.BlockSpec(memory_space=pltpu.VMEM)] * 4,
-            scratch_shapes=[pltpu.VMEM((LOCAL * CHUNKS, 128), f32)],
+            scratch_shapes=[
+                pltpu.VMEM((TILES, 128), bf16),
+                pltpu.VMEM((LOCAL, D), f32),
+                pltpu.VMEM((LOCAL, D), bf16),
+                pltpu.VMEM((LOCAL * CHUNKS, 128), f32),
+                pltpu.SemaphoreType.DMA((3,)),
+            ],
         ),
         out_shape=[
             jax.ShapeDtypeStruct((LOCAL, D), bf16),
@@ -692,7 +703,7 @@
             jax.ShapeDtypeStruct((LOCAL, D), f32),
             jax.ShapeDtypeStruct((EXPERTS, CAP * CHUNKS, 128), bf16),
         ],
-        compiler_params=pltpu.CompilerParams(vmem_limit_bytes=14 * 2**20),
+        compiler_params=pltpu.CompilerParams(vmem_limit_bytes=60 * 2**20),
         cost_estimate=pl.CostEstimate(flops=2 * 10**6, bytes_accessed=7 * 2**20, transcendentals=0),
         name="combine",
     )(index, slots, gates, slot_gates, scale, y, x2, target, mask)
@@ -762,7 +773,13 @@
     )(rows, first, second, mixed)
 
 
-def collect_kernel(slot_ref, gh_ref, x2_ref, g3_ref, gain_ref, g2_ref, gb_ref, term_ref, tiles):
+def collect_kernel(slot_ref, gh_hbm, x2_hbm, g3_hbm, gain_ref, g2_ref, gb_ref, term_ref, gh_ref, x2_ref, g3_ref, tiles, sems):
+    pairs = ((gh_hbm, gh_ref), (x2_hbm, x2_ref), (g3_hbm, g3_ref))
+    loads = [pltpu.make_async_copy(source, to, sems.at[i]) for i, (source, to) in enumerate(pairs)]
+    for load in loads:
+        load.start()
+    loads[0].wait()
+
     def row_of(number):
         return gh_ref[pl.ds(pl.multiple_of(slot_ref[number] * CHUNKS, CHUNKS), CHUNKS), :].astype(f32)
 
@@ -771,6 +788,8 @@
         return carry
 
     lax.fori_loop(0, LOCAL, body, 0, unroll=4)
+    loads[1].wait()
+    loads[2].wait()
     x2 = x2_ref[...]
     r2 = lax.rsqrt(jnp.mean(x2 * x2, axis=-1, keepdims=True) + epsilon)
     products = jnp.zeros((LOCAL, 128), f32)
@@ -795,16 +814,22 @@
         collect_kernel,
         grid_spec=pltpu.PrefetchScalarGridSpec(
             num_scalar_prefetch=1,
-            in_specs=[pl.BlockSpec(memory_space=pltpu.VMEM)] * 4,
+            in_specs=[HBM] * 3 + [pl.BlockSpec(memory_space=pltpu.VMEM)],
             out_specs=[pl.BlockSpec(memory_space=pltpu.VMEM)] * 3,
-            scratch_shapes=[pltpu.VMEM((LOCAL * CHUNKS, 128), f32)],
+            scratch_shapes=[
+                pltpu.VMEM((TILES, 128), bf16),
+                pltpu.VMEM((LOCAL, D), f32),
+                pltpu.VMEM((LOCAL, D), f32),
+                pltpu.VMEM((LOCAL * CHUNKS, 128), f32),
+                pltpu.SemaphoreType.DMA((3,)),
+            ],
         ),
         out_shape=[
             jax.ShapeDtypeStruct((LOCAL, D), f32),
             jax.ShapeDtypeStruct((LOCAL, D), bf16),
             jax.ShapeDtypeStruct((1, D), f32),
         ],
-        compiler_params=pltpu.CompilerParams(vmem_limit_bytes=12 * 2**20),
+        compiler_params=pltpu.CompilerParams(vmem_limit_bytes=60 * 2**20),
         cost_estimate=pl.CostEstimate(flops=2 * 10**6, bytes_accessed=6 * 2**20, transcendentals=128),
         name="collect",
     )(slots, gh, x2, g3, gain)
@@ -875,7 +900,7 @@
     attended_mine, attended_other = core_halves(attended, c)
     attended_there = shift(attended_other, "c", 1)
     chip_out = dot(attended_mine, out_mine) + dot(attended_there, out_other)
-    moved = lax.all_to_all(chip_out.astype(bf16).reshape(4, LOCAL, D), "x", split_axis=0, concat_axis=0, tiled=True)
+    moved = RingSum(chip_out.astype(bf16).reshape(4, LOCAL, D), "x").total()
     in_other = shift(in_mine, "c", 1)
 
     route_numbers = routes.reshape(-1)
@@ -916,15 +941,14 @@
     own, there, out_moved = tie((own, there, out_moved))
     chip_kv = (own.astype(f32) + shift(there, "c", 1).astype(f32)).astype(bf16)
 
-    dq, chip_kv, out_moved = tie((dq, chip_kv, out_moved))
-    out_summed = jnp.sum(out_moved.astype(f32), axis=0).astype(bf16)
-    out_gradient = lax.ppermute(out_summed, ALL, [(b, a) for a, b in out_perm()]).astype(f32)
+    dq, chip_kv = tie((dq, chip_kv))
     kv_parts = lax.all_to_all(chip_kv, "z", split_axis=0, concat_axis=0, tiled=True)
 
     gp_q, q_term = project_back(dq, projected, cosine, sine, q_gain_row, 0)
     in_q = dot(jnp.pad(gp_q, ((0, 0), (0, HD))), h1_group, TN).astype(bf16)
     gp_kv, k_term, in_partial = kv_back(c_array, kv_parts, projected, cosine, sine, k_gain_row, h1_group, in_q)
-    in_partial, gp_q, gp_kv, out_gradient = tie((in_partial.reshape(16, 40, D), gp_q, gp_kv, out_gradient))
+    in_partial, gp_q, gp_kv, out_moved = tie((in_partial.reshape(16, 40, D), gp_q, gp_kv, out_moved))
+    out_summed = jnp.sum(out_moved.astype(f32), axis=0).astype(bf16)
     in_parts = lax.all_to_all(in_partial, ("z", "y"), split_axis=0, concat_axis=0, tiled=True)
 
     gain1_term = jnp.sum(in_partial.reshape(640, D).astype(f32) * in_mine.astype(f32), axis=0) / gain1
@@ -934,15 +958,16 @@
     gp = jnp.concatenate([gp_q, gp_kv], axis=1)
     gp_mine, gp_there = core_halves(gp, c)
     gh1_chip = dot(gp_mine, in_mine) + dot(shift(gp_there, "c", 1), in_other)
-    gh1 = RingSum(gh1_chip.reshape(4, LOCAL, D), "x").total()
+    gh1 = RingSum(gh1_chip.astype(bf16).reshape(4, LOCAL, D), "x").total()
     gn1 = gh1 * gain1
     tokens_gradient = g2 + r1 * (gn1 - n1 * jnp.mean(gn1 * n1, axis=-1, keepdims=True))
+    in_parts, out_summed, terms = tie((in_parts, out_summed, terms))
+    sums = jnp.sum(spread(terms, ("y", "z"), 16), axis=0).reshape(-1)
     in_summed = jnp.sum(in_parts.astype(f32), axis=0)
-    in_summed, terms = tie((in_summed, terms))
-
+
+    out_gradient = lax.ppermute(out_summed, ALL, [(b, a) for a, b in out_perm()]).astype(f32)
     going = dot(arrive, in_summed.astype(bf16), TN).astype(bf16)
     home = [lax.ppermute(going[40 * i : 40 * i + 40], ALL, [(b, a) for a, b in perms[i]]) for i in range(3)]
-    sums = jnp.sum(spread(terms, ("y", "z"), 16), axis=0).reshape(-1)
     in_gradient = dot(jnp.concatenate(home, axis=0), leave, TN)
 
     loss = jnp.sum(sums[2 * D + 2 * HD :]) / (2.0 * valid_count * D)

time: 532 us -> 525 us (0.987)
  the two profiles are of different devices: /device:TPU:29 before, /device:TPU:49 now
where the time goes in v6:
time: 525 us; the launch traced here: 515 us
  starting transfers between devices  139 us (26%)
  waiting for transfers between devices  111 us (21%)
  Pallas kernels  98.8 us (19%)
  blocking collectives  63.9 us (12%)
  matrix products  33.6 us (6%)
  other arithmetic  32.8 us (6%)
  local copies, waits for them, and re-layouts  30.7 us (6%)
  between operations  5.52 us (1%)
    ppermute x45, waiting for transfers between devices, shift(): lax.ppermute(value, axis, [(i, (i + step) % size) for i in range(size)])  72.6 us
    all_to_all x2, blocking collectives, exchange(): return lax.all_to_all(rows, ALL, split_axis=0, concat_axis=0, tiled=True)  63.9 us
    ppermute x45, starting transfers between devices, shift(): lax.ppermute(value, axis, [(i, (i + step) % size) for i in range(size)])  58.8 us
    pallas_call x1, Pallas kernels, attend_backward(): pl.pallas_call(backward_kernel, grid_spec=pltpu.PrefetchScalarGridSpec(nu...  35 us
    dot_general x15, matrix products, dot(): return lax.dot_general(a, b, dims, preferred_element_type=f32)  33.6 us
    all_to_all x2, waiting for transfers between devices, exchange(): return lax.all_to_all(rows, ALL, split_axis=0, concat_axis=0, tiled=True)  24.1 us
    all_to_all x2, starting transfers between devices, exchange(): return lax.all_to_all(rows, ALL, split_axis=0, concat_axis=0, tiled=True)  19 us
    ppermute x3, starting transfers between devices, body(): lax.ppermute(going[40 * i:40 * i + 40], ALL, [(b, a) for a, b in perms[i]])  14.9 us
  transfers between devices with their start and end apart: 60, of which 30 were waited for; matrix products, arithmetic and copies ran while one was open for 14% of the time, Pallas kernels for 11%

profile of v6, /device:TPU:49, one launch (start us, length us, event | category | flops | bytes accessed | tf_op | source)
XLA Modules:
  0.0 515.4 jit_solution(17507358013261781120)
XLA Ops:
  10.7 10.6 %collective-permute-start.5 = (bf16[40,2048]{1,0:T(8,128)(2,1)S(1)}, bf16[40,2048]{1,0:T(8,128)(2,1)}, u32[]{:S(2)}, u32[]{:S(2)}) collective-permute-start(bf16[40,2048]{1,0:T(8,128)(2,1)S(1)} %get-tuple-element.144), channel_id=1, source_target_pairs={{0,0},{1,32},{2,64},{3,96},{4,2},{5,34},{6,66},{7,98},{8,4},{9,36}... | collective-permute-start | bytes 491528 | tf_op jit(solution)/shard_map/ppermute | solution.py:882
  28.3 6.9 %collective-permute-done.8 = bf16[32,2048]{1,0:T(8,128)(2,1)S(1)} collective-permute-done((bf16[32,2048]{1,0:T(8,128)(2,1)S(1)}, bf16[32,2048]{1,0:T(8,128)(2,1)S(1)}, u32[]{:S(2)}, u32[]{:S(2)}) %collective-permute-start.8) | collective-permute-done | bytes 131104 | tf_op jit(solution)/shard_map/ppermute | solution.py:883
  101.7 9.3 %collective-permute-start.23 = (bf16[4,1024,128]{2,1,0:T(8,128)(2,1)S(1)}, bf16[4,1024,128]{2,1,0:T(8,128)(2,1)S(1)}, u32[]{:S(2)}, u32[]{:S(2)}) collective-permute-start(bf16[4,1024,128]{2,1,0:T(8,128)(2,1)S(1)} %fusion.24), channel_id=1, source_target_pairs={{0,1},{1,0},{2,3},{3,2},{4,5},{5,4},{6,7},{7,6},{8,9},{9,8},{10,11... | collective-permute-start | bytes 3145736 | tf_op jit(solution)/shard_map/ppermute | solution.py:137
  113.4 14.3 %attend_forward.1 = (bf16[1024,512]{1,0:T(8,128)(2,1)S(1)}, f32[4,4,8,256]{3,2,1,0:T(8,128)S(1)}) custom-call(s32[1]{0:T(128)} %bitcast.1.z_ref, bf16[1024,512]{1,0:T(8,128)(2,1)S(1)} %get-tuple-element.77.q_ref, bf16[2,4,1024,128]{3,2,1,0:T(8,128)(2,1)S(1)} %bitcast_dynamic-update-slice_fusion.1.kv_ref), custom_call_target="tpu_custom_call" | custom-call | flops 8999999488 | bytes 8388608 | tf_op jit(solution)/shard_map/attend_forward/pallas_call | solution.py:402
  147.4 7.7 %collective-permute-done.31 = bf16[128,2048]{1,0:T(8,128)(2,1)S(1)} collective-permute-done((bf16[128,2048]{1,0:T(8,128)(2,1)S(1)}, bf16[128,2048]{1,0:T(8,128)(2,1)S(1)}, u32[]{:S(2)}, u32[]{:S(2)}) %collective-permute-start.31) | collective-permute-done | bytes 524320 | tf_op jit(solution)/shard_map/ppermute | solution.py:137
  164.1 33.2 %all_to_all.45.x_hbm = bf16[128,56,128]{2,1,0:T(8,128)(2,1)} all-to-all(bf16[128,56,128]{2,1,0:T(8,128)(2,1)S(1)} %get-tuple-element.82), channel_id=1, replica_groups=mesh['y'=4,'x'=4,'z'=4,'c'=2] {'y','x','z','c'}, dimensions={0} | all-to-all | bytes 3670016 | tf_op jit(solution)/shard_map/all_to_all | solution.py:843
  197.3 9.5 %expert_forward.1 = (bf16[384,2048]{1,0:T(8,128)(2,1)}, f32[384,1536]{1,0:T(8,128)}, bf16[384,768]{1,0:T(8,128)(2,1)}, bf16[6144,128]{1,0:T(8,128)(2,1)}) custom-call(bf16[128,56,128]{2,1,0:T(8,128)(2,1)} %all_to_all.45.x_hbm, bf16[2048,1536]{1,0:T(8,128)(2,1)} %bitcast.204, bf16[768,2048]{1,0:T(8,128)(2,1)} %bitcast.212), custom_call_target="tpu_custom_call" | custom-call | flops 3600000000 | bytes 17825792 | tf_op jit(solution)/shard_map/expert_forward/pallas_call | solution.py:624
  206.8 9.4 %all-to-all-start.2 = ((bf16[128,48,128]{2,1,0:T(8,128)(2,1)}), bf16[128,48,128]{2,1,0:T(8,128)(2,1)}, u32[]{:S(2)}, u32[]{:S(2)}) async-start(bf16[128,48,128]{2,1,0:T(8,128)(2,1)} %bitcast.217), calls=%async_computation.2 | async-start | bytes 3145728 | tf_op jit(solution)/shard_map/all_to_all | solution.py:843
  220.3 16.5 %all-to-all-done.2 = bf16[128,48,128]{2,1,0:T(8,128)(2,1)} async-done(((bf16[128,48,128]{2,1,0:T(8,128)(2,1)}), bf16[128,48,128]{2,1,0:T(8,128)(2,1)}, u32[]{:S(2)}, u32[]{:S(2)}) %all-to-all-start.2) | async-done | bytes 1572896 | tf_op jit(solution)/shard_map/all_to_all | solution.py:843
  236.8 7.4 %combine.1 = (bf16[128,2048]{1,0:T(8,128)(2,1)}, f32[1,128]{1,0:T(1,128)}, f32[128,2048]{1,0:T(8,128)}, bf16[128,48,128]{2,1,0:T(8,128)(2,1)}) custom-call(s32[384]{0:T(512)} %copy-done.17, s32[256]{0:T(256)} %copy-done.40, f32[256]{0:T(256)} %copy-done.42, f32[384]{0:T(512)} %select_reduce_fusion.slot_gate_ref, f32[1]{0:T(128)} %bitcast.42.scale_ref, ...), custom_call_target="tpu_custom_call" | custom-call | flops 2000000 | bytes 7340032 | tf_op jit(solution)/shard_map/combine/pallas_call | solution.py:686
  244.2 30.6 %all_to_all.46 = bf16[128,48,128]{2,1,0:T(8,128)(2,1)} all-to-all(bf16[128,48,128]{2,1,0:T(8,128)(2,1)} %get-tuple-element.86), channel_id=1, replica_groups=mesh['y'=4,'x'=4,'z'=4,'c'=2] {'y','x','z','c'}, dimensions={0} | all-to-all | bytes 3145728 | tf_op jit(solution)/shard_map/all_to_all | solution.py:843
  274.8 10.9 %expert_backward.1 = (bf16[384,2048]{1,0:T(8,128)(2,1)}, bf16[384,1536]{1,0:T(8,128)(2,1)}, bf16[6144,128]{1,0:T(8,128)(2,1)}) custom-call(bf16[6144,128]{1,0:T(8,128)(2,1)} %bitcast.206, bf16[2048,1536]{1,0:T(8,128)(2,1)} %bitcast.205, bf16[768,2048]{1,0:T(8,128)(2,1)} %bitcast.213, f32[384,1536]{1,0:T(8,128)} %get-tuple-element.87.mixed_hbm), custom_call_target="tpu_custom_call" | custom-call | flops 3600000000 | bytes 17825792 | tf_op jit(solution)/shard_map/expert_backward/pallas_call | solution.py:750
  285.7 9.6 %all-to-all-start.4 = ((bf16[128,48,128]{2,1,0:T(8,128)(2,1)}), bf16[128,48,128]{2,1,0:T(8,128)(2,1)}, u32[]{:S(2)}, u32[]{:S(2)}) async-start(bf16[128,48,128]{2,1,0:T(8,128)(2,1)} %bitcast.218), calls=%async_computation.4 | async-start | bytes 3145728 | tf_op jit(solution)/shard_map/all_to_all | solution.py:843
  295.4 6.3 %fusion.42 = f32[768,2048]{1,0:T(8,128)} fusion(bf16[384,768]{1,0:T(8,128)(2,1)} %get-tuple-element.91, bf16[384,2048]{1,0:T(8,128)(2,1)} %get-tuple-element.92), kind=kOutput, calls=%fused_computation.145 | convolution fusion | flops 1207959552 | bytes 8454144 | tf_op jit(solution)/shard_map/dot_general | solution.py:839
  301.7 6.6 %fusion.41 = f32[2048,1536]{1,0:T(8,128)} fusion(bf16[384,2048]{1,0:T(8,128)(2,1)S(1)} %copy-done.33, bf16[384,1536]{1,0:T(8,128)(2,1)S(1)} %copy-done.34), kind=kOutput, calls=%fused_computation.144 | convolution fusion | flops 2415919104 | bytes 15335424 | tf_op jit(solution)/shard_map/dot_general | solution.py:839
  308.3 7.7 %all-to-all-done.4 = bf16[128,48,128]{2,1,0:T(8,128)(2,1)} async-done(((bf16[128,48,128]{2,1,0:T(8,128)(2,1)}), bf16[128,48,128]{2,1,0:T(8,128)(2,1)}, u32[]{:S(2)}, u32[]{:S(2)}) %all-to-all-start.4) | async-done | bytes 1572896 | tf_op jit(solution)/shard_map/all_to_all | solution.py:843
  323.7 10.7 %collective-permute-done.33 = bf16[128,2048]{1,0:T(8,128)(2,1)S(1)} collective-permute-done((bf16[128,2048]{1,0:T(8,128)(2,1)}, bf16[128,2048]{1,0:T(8,128)(2,1)S(1)}, u32[]{:S(2)}, u32[]{:S(2)}) %collective-permute-start.33) | collective-permute-done | bytes 524320 | tf_op jit(solution)/shard_map/ppermute | solution.py:137
  356.0 7.9 %all-to-all-start.5 = ((bf16[16,32,2048]{2,1,0:T(8,128)(2,1)}), bf16[16,32,2048]{2,1,0:T(8,128)(2,1)}, u32[]{:S(2)}, u32[]{:S(2)}) async-start(bf16[16,32,2048]{2,1,0:T(8,128)(2,1)} %bitcast.193), calls=%async_computation.5 | async-start | bytes 4194304 | tf_op jit(solution)/shard_map/all_to_all | solution.py:940
  363.9 35.0 %attend_backward.1 = (bf16[1024,512]{1,0:T(8,128)(2,1)}, bf16[4,1024,128]{2,1,0:T(8,128)(2,1)}, bf16[4,1024,128]{2,1,0:T(8,128)(2,1)}) custom-call(s32[1]{0:T(128)} %bitcast.1.z_ref, s32[1]{0:T(128)} %bitcast.2.core_ref, bf16[1024,512]{1,0:T(8,128)(2,1)} %copy-done.20, bf16[2,4,1024,128]{3,2,1,0:T(8,128)(2,1)} %copy-done.12, bf16[1024,512]{1,0:T(8,128)(2,1)} %bitcast.219, ...), custom_call_target="tpu_custom_call" | custom-call | flops 22000001024 | bytes 8388608 | tf_op jit(solution)/shard_map/attend_backward/pallas_call | solution.py:495
  429.2 6.2 %all-to-all-start.7 = ((bf16[16,40,2048]{2,1,0:T(8,128)(2,1)}), bf16[16,40,2048]{2,1,0:T(8,128)(2,1)}, u32[]{:S(2)}, u32[]{:S(2)}) async-start(bf16[16,40,2048]{2,1,0:T(8,128)(2,1)} %bitcast.189), calls=%async_computation.7 | async-start | bytes 5242880 | tf_op jit(solution)/shard_map/all_to_all | solution.py:952
  447.3 6.2 %collective-permute-done.47 = bf16[128,1024]{1,0:T(8,128)(2,1)S(1)} collective-permute-done((bf16[128,1024]{1,0:T(8,128)(2,1)S(1)}, bf16[128,1024]{1,0:T(8,128)(2,1)S(1)}, u32[]{:S(2)}, u32[]{:S(2)}) %collective-permute-start.47) | collective-permute-done | bytes 262176 | tf_op jit(solution)/shard_map/ppermute | solution.py:137
  473.3 6.8 %all-to-all-start.8 = ((f32[16,35,128]{2,1,0:T(8,128)}), f32[16,35,128]{2,1,0:T(8,128)}, u32[]{:S(2)}, u32[]{:S(2)}) async-start(f32[16,35,128]{2,1,0:T(8,128)} %broadcast_in_dim.274), calls=%async_computation.8 | async-start | bytes 655360 | tf_op jit(solution)/shard_map/all_to_all | solution.py:209
  484.2 13.6 %collective-permute-start.49 = (bf16[40,2048]{1,0:T(8,128)(2,1)S(1)}, bf16[40,2048]{1,0:T(8,128)(2,1)S(1)}, u32[]{:S(2)}, u32[]{:S(2)}) collective-permute-start(bf16[40,2048]{1,0:T(8,128)(2,1)S(1)} %get-tuple-element.141), channel_id=1, source_target_pairs={{0,0},{32,1},{64,2},{96,3},{2,4},{34,5},{66,6},{98,7},{4,8},{36,9}... | collective-permute-start | bytes 491528 | tf_op jit(solution)/shard_map/ppermute | solution.py:970
  502.4 6.6 %collective-permute-done.52 = bf16[32,2048]{1,0:T(8,128)(2,1)S(1)} collective-permute-done((bf16[32,2048]{1,0:T(8,128)(2,1)S(1)}, bf16[32,2048]{1,0:T(8,128)(2,1)S(1)}, u32[]{:S(2)}, u32[]{:S(2)}) %collective-permute-start.52) | collective-permute-done | bytes 131104 | tf_op jit(solution)/shard_map/ppermute | solution.py:968
  (339 shorter events, 220.4 us)
Async XLA Ops:
  4.7 44.7 %collective-permute-start = (bf16[128,2048]{1,0:T(8,128)(2,1)}, bf16[128,2048]{1,0:T(8,128)(2,1)S(1)}, u32[]{:S(2)}, u32[]{:S(2)}) collective-permute-start(bf16[128,2048]{1,0:T(8,128)(2,1)} %get-tuple-element.126), channel_id=1, source_target_pairs={{0,8},{8,16},{16,24},{24,0},{1,9},{9,17},{17,25},{25,1},{2,10},{10... | collective-permute-start | bytes 1572872 | tf_op jit(solution)/shard_map/ppermute | solution.py:137
  6.0 42.9 %collective-permute-start.1 = (bf16[128,2048]{1,0:T(8,128)(2,1)}, bf16[128,2048]{1,0:T(8,128)(2,1)S(1)}, u32[]{:S(2)}, u32[]{:S(2)}) collective-permute-start(bf16[128,2048]{1,0:T(8,128)(2,1)} %get-tuple-element.126), channel_id=1, source_target_pairs={{0,24},{8,0},{16,8},{24,16},{1,25},{9,1},{17,9},{25,17},{2,26},{10... | collective-permute-start | bytes 1572872 | tf_op jit(solution)/shard_map/ppermute | solution.py:137
  8.7 16.2 %collective-permute-start.7 = (bf16[40,2048]{1,0:T(8,128)(2,1)}, bf16[40,2048]{1,0:T(8,128)(2,1)S(1)}, u32[]{:S(2)}, u32[]{:S(2)}) collective-permute-start(bf16[40,2048]{1,0:T(8,128)(2,1)} %get-tuple-element.145), channel_id=1, source_target_pairs={{102,6},{105,14},{115,7},{118,15},{121,23},{12,37},{76,60},{28,74}... | collective-permute-start | bytes 491528 | tf_op jit(solution)/shard_map/ppermute | solution.py:882
  9.3 17.5 %collective-permute-start.6 = (bf16[40,2048]{1,0:T(8,128)(2,1)}, bf16[40,2048]{1,0:T(8,128)(2,1)}, u32[]{:S(2)}, u32[]{:S(2)}) collective-permute-start(bf16[40,2048]{1,0:T(8,128)(2,1)} %get-tuple-element.146), channel_id=1, source_target_pairs={{13,37},{14,69},{15,101},{25,44},{29,74},{30,106},{31,12},{38,75},... | collective-permute-start | bytes 491528 | tf_op jit(solution)/shard_map/ppermute | solution.py:882
  10.7 16.6 %collective-permute-start.5 = (bf16[40,2048]{1,0:T(8,128)(2,1)S(1)}, bf16[40,2048]{1,0:T(8,128)(2,1)}, u32[]{:S(2)}, u32[]{:S(2)}) collective-permute-start(bf16[40,2048]{1,0:T(8,128)(2,1)S(1)} %get-tuple-element.144), channel_id=1, source_target_pairs={{0,0},{1,32},{2,64},{3,96},{4,2},{5,34},{6,66},{7,98},{8,4},{9,36}... | collective-permute-start | bytes 491528 | tf_op jit(solution)/shard_map/ppermute | solution.py:882
  37.8 18.0 %all-to-all-start = ((bf16[4,40,2048]{2,1,0:T(8,128)(2,1)}), bf16[4,40,2048]{2,1,0:T(8,128)(2,1)}, u32[]{:S(2)}, u32[]{:S(2)}) async-start(bf16[4,40,2048]{2,1,0:T(8,128)(2,1)} %broadcast_in_dim.239), calls=%async_computation | async-start | bytes 1310720 | tf_op jit(solution)/shard_map/all_to_all | solution.py:209
  56.4 13.2 %collective-permute-start.14 = (bf16[4,40,2048]{2,1,0:T(8,128)(2,1)}, bf16[4,40,2048]{2,1,0:T(8,128)(2,1)S(1)}, u32[]{:S(2)}, u32[]{:S(2)}) collective-permute-start(bf16[4,40,2048]{2,1,0:T(8,128)(2,1)} %all-to-all-done), channel_id=1, source_target_pairs={{0,6},{2,0},{4,2},{6,4},{1,7},{3,1},{5,3},{7,5},{8,14},{10,8},{12,... | collective-permute-start | bytes 1966088 | tf_op jit(solution)/shard_map/ppermute | solution.py:137
  60.0 18.5 %collective-permute-start.4 = (bf16[512,2048]{1,0:T(8,128)(2,1)}, bf16[512,2048]{1,0:T(8,128)(2,1)S(1)}, u32[]{:S(2)}, u32[]{:S(2)}) collective-permute-start(bf16[512,2048]{1,0:T(8,128)(2,1)} %bitcast.8), channel_id=1, source_target_pairs={{0,1},{1,0},{2,3},{3,2},{4,5},{5,4},{6,7},{7,6},{8,9},{9,8},{10,11... | collective-permute-start | bytes 6291464 | tf_op jit(solution)/shard_map/ppermute | solution.py:137
  87.8 23.3 %collective-permute-start.25 = (bf16[4,32,1024]{2,1,0:T(8,128)(2,1)S(1)}, bf16[4,32,1024]{2,1,0:T(8,128)(2,1)S(1)}, u32[]{:S(2)}, u32[]{:S(2)}) collective-permute-start(bf16[4,32,1024]{2,1,0:T(8,128)(2,1)S(1)} %slice.149), channel_id=1, source_target_pairs={{0,96},{32,0},{64,32},{96,64},{1,97},{33,1},{65,33},{97,65},{2,98}... | collective-permute-start | bytes 786440 | tf_op jit(solution)/shard_map/ppermute | solution.py:137
  88.9 22.1 %collective-permute-start.24 = (bf16[4,32,1024]{2,1,0:T(8,128)(2,1)S(1)}, bf16[4,32,1024]{2,1,0:T(8,128)(2,1)S(1)}, u32[]{:S(2)}, u32[]{:S(2)}) collective-permute-start(bf16[4,32,1024]{2,1,0:T(8,128)(2,1)S(1)} %slice.148), channel_id=1, source_target_pairs={{0,32},{32,64},{64,96},{96,0},{1,33},{33,65},{65,97},{97,1},{2,34}... | collective-permute-start | bytes 786440 | tf_op jit(solution)/shard_map/ppermute | solution.py:137
  111.2 18.4 %collective-permute-start.27 = (bf16[512,2048]{1,0:T(8,128)(2,1)S(1)}, bf16[512,2048]{1,0:T(8,128)(2,1)S(1)}, u32[]{:S(2)}, u32[]{:S(2)}) collective-permute-start(bf16[512,2048]{1,0:T(8,128)(2,1)S(1)} %bitcast.195), channel_id=1, source_target_pairs={{0,1},{1,0},{2,3},{3,2},{4,5},{5,4},{6,7},{7,6},{8,9},{9,8},{10,11... | collective-permute-start | bytes 6291464 | tf_op jit(solution)/shard_map/ppermute | solution.py:137
  206.8 30.0 %all-to-all-start.2 = ((bf16[128,48,128]{2,1,0:T(8,128)(2,1)}), bf16[128,48,128]{2,1,0:T(8,128)(2,1)}, u32[]{:S(2)}, u32[]{:S(2)}) async-start(bf16[128,48,128]{2,1,0:T(8,128)(2,1)} %bitcast.217), calls=%async_computation.2 | async-start | bytes 3145728 | tf_op jit(solution)/shard_map/all_to_all | solution.py:843
  285.7 30.2 %all-to-all-start.4 = ((bf16[128,48,128]{2,1,0:T(8,128)(2,1)}), bf16[128,48,128]{2,1,0:T(8,128)(2,1)}, u32[]{:S(2)}, u32[]{:S(2)}) async-start(bf16[128,48,128]{2,1,0:T(8,128)(2,1)} %bitcast.218), calls=%async_computation.4 | async-start | bytes 3145728 | tf_op jit(solution)/shard_map/all_to_all | solution.py:843
  323.1 14.0 %collective-permute-start.32 = (bf16[128,2048]{1,0:T(8,128)(2,1)}, bf16[128,2048]{1,0:T(8,128)(2,1)S(1)}, u32[]{:S(2)}, u32[]{:S(2)}) collective-permute-start(bf16[128,2048]{1,0:T(8,128)(2,1)} %get-tuple-element.95), channel_id=1, source_target_pairs={{0,8},{8,16},{16,24},{24,0},{1,9},{9,17},{17,25},{25,1},{2,10},{10... | collective-permute-start | bytes 1572872 | tf_op jit(solution)/shard_map/ppermute | solution.py:137
  356.0 42.9 %all-to-all-start.5 = ((bf16[16,32,2048]{2,1,0:T(8,128)(2,1)}), bf16[16,32,2048]{2,1,0:T(8,128)(2,1)}, u32[]{:S(2)}, u32[]{:S(2)}) async-start(bf16[16,32,2048]{2,1,0:T(8,128)(2,1)} %bitcast.193), calls=%async_computation.5 | async-start | bytes 4194304 | tf_op jit(solution)/shard_map/all_to_all | solution.py:940
  399.7 42.1 %collective-permute-start.44 = (bf16[640,2048]{1,0:T(8,128)(2,1)S(1)}, bf16[640,2048]{1,0:T(8,128)(2,1)}, u32[]{:S(2)}, u32[]{:S(2)}) collective-permute-start(bf16[640,2048]{1,0:T(8,128)(2,1)S(1)} %bitcast.180), channel_id=1, source_target_pairs={{0,1},{1,0},{2,3},{3,2},{4,5},{5,4},{6,7},{7,6},{8,9},{9,8},{10,11... | collective-permute-start | bytes 7864328 | tf_op jit(solution)/shard_map/ppermute | solution.py:137
  405.2 18.2 %all-to-all-start.6 = ((bf16[4,1024,128]{2,1,0:T(8,128)(2,1)}), bf16[4,1024,128]{2,1,0:T(8,128)(2,1)}, u32[]{:S(2)}, u32[]{:S(2)}) async-start(bf16[4,1024,128]{2,1,0:T(8,128)(2,1)} %add_convert_fusion.3), calls=%async_computation.6 | async-start | bytes 2097152 | tf_op jit(solution)/shard_map/all_to_all | solution.py:945
  429.2 43.4 %all-to-all-start.7 = ((bf16[16,40,2048]{2,1,0:T(8,128)(2,1)}), bf16[16,40,2048]{2,1,0:T(8,128)(2,1)}, u32[]{:S(2)}, u32[]{:S(2)}) async-start(bf16[16,40,2048]{2,1,0:T(8,128)(2,1)} %bitcast.189), calls=%async_computation.7 | async-start | bytes 5242880 | tf_op jit(solution)/shard_map/all_to_all | solution.py:952
  454.4 16.6 %collective-permute-start.48 = (bf16[128,2048]{1,0:T(8,128)(2,1)}, bf16[128,2048]{1,0:T(8,128)(2,1)S(1)}, u32[]{:S(2)}, u32[]{:S(2)}) collective-permute-start(bf16[128,2048]{1,0:T(8,128)(2,1)} %pad_maximum_fusion.6), channel_id=1, source_target_pairs={{0,24},{8,0},{16,8},{24,16},{1,25},{9,1},{17,9},{25,17},{2,26},{10... | collective-permute-start | bytes 1572872 | tf_op jit(solution)/shard_map/ppermute | solution.py:137
  456.6 14.5 %collective-permute-start.46 = (bf16[128,2048]{1,0:T(8,128)(2,1)}, bf16[128,2048]{1,0:T(8,128)(2,1)}, u32[]{:S(2)}, u32[]{:S(2)}) collective-permute-start(bf16[128,2048]{1,0:T(8,128)(2,1)} %pad_maximum_fusion.5), channel_id=1, source_target_pairs={{0,8},{8,16},{16,24},{24,0},{1,9},{9,17},{17,25},{25,1},{2,10},{10... | collective-permute-start | bytes 1572872 | tf_op jit(solution)/shard_map/ppermute | solution.py:137
  473.3 37.4 %all-to-all-start.8 = ((f32[16,35,128]{2,1,0:T(8,128)}), f32[16,35,128]{2,1,0:T(8,128)}, u32[]{:S(2)}, u32[]{:S(2)}) async-start(f32[16,35,128]{2,1,0:T(8,128)} %broadcast_in_dim.274), calls=%async_computation.8 | async-start | bytes 655360 | tf_op jit(solution)/shard_map/all_to_all | solution.py:209
  482.9 26.8 %collective-permute-start.51 = (bf16[40,2048]{1,0:T(8,128)(2,1)S(1)}, bf16[40,2048]{1,0:T(8,128)(2,1)S(1)}, u32[]{:S(2)}, u32[]{:S(2)}) collective-permute-start(bf16[40,2048]{1,0:T(8,128)(2,1)S(1)} %get-tuple-element.142), channel_id=1, source_target_pairs={{6,102},{14,105},{7,115},{15,118},{23,121},{37,12},{60,76},{74,28}... | collective-permute-start | bytes 491528 | tf_op jit(solution)/shard_map/ppermute | solution.py:970
  483.6 26.1 %collective-permute-start.50 = (bf16[40,2048]{1,0:T(8,128)(2,1)S(1)}, bf16[40,2048]{1,0:T(8,128)(2,1)S(1)}, u32[]{:S(2)}, u32[]{:S(2)}) collective-permute-start(bf16[40,2048]{1,0:T(8,128)(2,1)S(1)} %get-tuple-element.143), channel_id=1, source_target_pairs={{37,13},{69,14},{101,15},{44,25},{74,29},{106,30},{12,31},{75,38},... | collective-permute-start | bytes 491528 | tf_op jit(solution)/shard_map/ppermute | solution.py:970
  484.2 25.4 %collective-permute-start.49 = (bf16[40,2048]{1,0:T(8,128)(2,1)S(1)}, bf16[40,2048]{1,0:T(8,128)(2,1)S(1)}, u32[]{:S(2)}, u32[]{:S(2)}) collective-permute-start(bf16[40,2048]{1,0:T(8,128)(2,1)S(1)} %get-tuple-element.141), channel_id=1, source_target_pairs={{0,0},{32,1},{64,2},{96,3},{2,4},{34,5},{66,6},{98,7},{4,8},{36,9}... | collective-permute-start | bytes 491528 | tf_op jit(solution)/shard_map/ppermute | solution.py:970
  (86 other events, 687.2 us)

commit v7 on v6

--- a/solution.py
+++ b/solution.py
@@ -544,24 +544,23 @@
     lax.fori_loop(0, EXPERTS, body, 0, unroll=4)
 
 
-def dispatch_kernel(index_ref, count_ref, moved_ref, token_ref, gain_ref, x2_ref, out_ref, tiles):
+def dispatch_kernel(index_ref, moved_ref, token_ref, gain_ref, x2_ref, out_ref, tiles):
     x2 = token_ref[...].astype(f32) + moved_ref[...]
     x2_ref[...] = x2
     h2 = x2 * lax.rsqrt(jnp.mean(x2 * x2, axis=-1, keepdims=True) + epsilon) * gain_ref[...]
     for k in range(CHUNKS):
         tiles[pl.ds(k, LOCAL, stride=CHUNKS), :] = h2[:, lanes_of(k)]
-    out_ref[:, CAP * CHUNKS :, :] = jnp.full((EXPERTS, 8, 128), count_ref[0], f32).astype(bf16)
     place_rows(index_ref, tiles, out_ref)
 
 
-def dispatch(index, count, moved, tokens, gain):
+def dispatch(index, moved, tokens, gain):
     return pl.pallas_call(
         dispatch_kernel,
         grid_spec=pltpu.PrefetchScalarGridSpec(
-            num_scalar_prefetch=2,
+            num_scalar_prefetch=1,
             in_specs=[pl.BlockSpec(memory_space=pltpu.VMEM)] * 3,
             out_specs=[pl.BlockSpec(memory_space=pltpu.VMEM)] * 2,
-            scratch_shapes=[pltpu.VMEM((LOCAL * CHUNKS, 128), f32)],
+            scratch_shapes=[pltpu.VMEM(((LOCAL + 1) * CHUNKS, 128), f32)],
         ),
         out_shape=[
             jax.ShapeDtypeStruct((LOCAL, D), f32),
@@ -570,7 +569,7 @@
         compiler_params=pltpu.CompilerParams(vmem_limit_bytes=12 * 2**20),
         cost_estimate=pl.CostEstimate(flops=10**6, bytes_accessed=6 * 2**20, transcendentals=128),
         name="dispatch",
-    )(index, count, moved, tokens, gain)
+    )(index, moved, tokens, gain)
 
 
 def unpack_rows(tiles, rows_ref):
@@ -593,7 +592,7 @@
     for load in loads:
         load.start()
     loads[0].wait()
-    tiles[...] = x[...].reshape(TILES, 128).astype(f32)
+    tiles[:TILES, :] = x[...].reshape(TILES, 128).astype(f32)
     unpack_rows(tiles, rows)
     stores = [copy(rows, rows_hbm, 8)]
     stores[0].start()
@@ -613,7 +612,7 @@
         part = jnp.dot(hidden[...], second[:, lanes_of(j, 256)], preferred_element_type=f32)
         tiles[pl.ds(2 * j, ROWS, stride=CHUNKS), :] = part[:, :128]
         tiles[pl.ds(2 * j + 1, ROWS, stride=CHUNKS), :] = part[:, 128:]
-    y[...] = tiles[...].astype(bf16)
+    y[...] = tiles[:TILES, :].astype(bf16)
     stores.append(copy(y, y_hbm, 11))
     stores[-1].start()
     for store in stores:
@@ -633,7 +632,7 @@
             pltpu.VMEM((ROWS, 2 * FF), f32),
             pltpu.VMEM((ROWS, FF), bf16),
             pltpu.VMEM((TILES, 128), bf16),
-            pltpu.VMEM((TILES, 128), f32),
+            pltpu.VMEM((TILES + CHUNKS, 128), f32),
             pltpu.SemaphoreType.DMA((12,)),
         ],
         out_shape=[
@@ -693,7 +692,7 @@
                 pltpu.VMEM((TILES, 128), bf16),
                 pltpu.VMEM((LOCAL, D), f32),
                 pltpu.VMEM((LOCAL, D), bf16),
-                pltpu.VMEM((LOCAL * CHUNKS, 128), f32),
+                pltpu.VMEM(((LOCAL + 1) * CHUNKS, 128), f32),
                 pltpu.SemaphoreType.DMA((3,)),
             ],
         ),
@@ -718,7 +717,7 @@
     for load in loads:
         load.start()
     loads[0].wait()
-    tiles[...] = g[...].astype(f32)
+    tiles[:TILES, :] = g[...].astype(f32)
     unpack_rows(tiles, back_out)
     stores = [copy(back_out, back_out_hbm, 7)]
     stores[0].start()
@@ -739,7 +738,7 @@
         part = lax.dot_general(back_mixed[...], first[lanes_of(j, 256), :], NT, preferred_element_type=f32)
         tiles[pl.ds(2 * j, ROWS, stride=CHUNKS), :] = part[:, :128]
         tiles[pl.ds(2 * j + 1, ROWS, stride=CHUNKS), :] = part[:, 128:]
-    gh[...] = tiles[...].astype(bf16)
+    gh[...] = tiles[:TILES, :].astype(bf16)
     stores.append(copy(gh, gh_hbm, 9))
     stores[-1].start()
     for store in stores:
@@ -759,7 +758,7 @@
             pltpu.VMEM((ROWS, D), bf16),
             pltpu.VMEM((ROWS, 2 * FF), bf16),
             pltpu.VMEM((TILES, 128), bf16),
-            pltpu.VMEM((TILES, 128), f32),
+            pltpu.VMEM((TILES + CHUNKS, 128), f32),
             pltpu.SemaphoreType.DMA((10,)),
         ],
         out_shape=[
@@ -820,7 +819,7 @@
                 pltpu.VMEM((TILES, 128), bf16),
                 pltpu.VMEM((LOCAL, D), f32),
                 pltpu.VMEM((LOCAL, D), f32),
-                pltpu.VMEM((LOCAL * CHUNKS, 128), f32),
+                pltpu.VMEM(((LOCAL + 1) * CHUNKS, 128), f32),
                 pltpu.SemaphoreType.DMA((3,)),
             ],
         ),
@@ -913,7 +912,9 @@
     slot_gates = jnp.sum(jnp.where(held, gates.reshape(1, -1), 0.0), axis=1)
 
     gain2_row = gain2[None, :]
-    x2, sent = dispatch(index, jnp.sum(mask)[None], moved, tokens, gain2_row)
+    x2, sent = dispatch(index, moved, tokens, gain2_row)
+    own_count = jnp.broadcast_to(jnp.sum(mask).astype(bf16), (EXPERTS, 8, 128))
+    sent = lax.dynamic_update_slice(sent, own_count, (0, CAP * CHUNKS, 0))
     arrived_rows = exchange(sent)
     valid_count = jnp.sum(arrived_rows[:, CAP * CHUNKS, 0].astype(f32))
     first, second = gate_up[0], down[0]

time: 525 us -> 525 us (level)
  no operation moved by 1% of the time
where the time goes in v7:
time: 525 us; the launch traced here: 515 us
  starting transfers between devices  139 us (26%)
  waiting for transfers between devices  111 us (21%)
  Pallas kernels  98.1 us (19%)
  blocking collectives  63.9 us (12%)
  matrix products  33.6 us (6%)
  other arithmetic  32.8 us (6%)
  local copies, waits for them, and re-layouts  31.4 us (6%)
  between operations  5.53 us (1%)
    ppermute x45, waiting for transfers between devices, shift(): lax.ppermute(value, axis, [(i, (i + step) % size) for i in range(size)])  72.6 us
    all_to_all x2, blocking collectives, exchange(): return lax.all_to_all(rows, ALL, split_axis=0, concat_axis=0, tiled=True)  63.9 us
    ppermute x45, starting transfers between devices, shift(): lax.ppermute(value, axis, [(i, (i + step) % size) for i in range(size)])  58.8 us
    pallas_call x1, Pallas kernels, attend_backward(): pl.pallas_call(backward_kernel, grid_spec=pltpu.PrefetchScalarGridSpec(nu...  35 us
    dot_general x15, matrix products, dot(): return lax.dot_general(a, b, dims, preferred_element_type=f32)  33.6 us
    all_to_all x2, waiting for transfers between devices, exchange(): return lax.all_to_all(rows, ALL, split_axis=0, concat_axis=0, tiled=True)  24.1 us
    all_to_all x2, starting transfers between devices, exchange(): return lax.all_to_all(rows, ALL, split_axis=0, concat_axis=0, tiled=True)  19 us
    ppermute x3, starting transfers between devices, body(): lax.ppermute(going[40 * i:40 * i + 40], ALL, [(b, a) for a, b in perms[i]])  15 us
  transfers between devices with their start and end apart: 60, of which 30 were waited for; matrix products, arithmetic and copies ran while one was open for 14% of the time, Pallas kernels for 11%

profile of v7, /device:TPU:49, one launch (start us, length us, event | category | flops | bytes accessed | tf_op | source)
XLA Modules:
  0.0 515.5 jit_solution(11855075048262283221)
XLA Ops:
  10.7 10.6 %collective-permute-start.5 = (bf16[40,2048]{1,0:T(8,128)(2,1)S(1)}, bf16[40,2048]{1,0:T(8,128)(2,1)}, u32[]{:S(2)}, u32[]{:S(2)}) collective-permute-start(bf16[40,2048]{1,0:T(8,128)(2,1)S(1)} %get-tuple-element.144), channel_id=1, source_target_pairs={{0,0},{1,32},{2,64},{3,96},{4,2},{5,34},{6,66},{7,98},{8,4},{9,36}... | collective-permute-start | bytes 491528 | tf_op jit(solution)/shard_map/ppermute | solution.py:881
  28.3 6.9 %collective-permute-done.8 = bf16[32,2048]{1,0:T(8,128)(2,1)S(1)} collective-permute-done((bf16[32,2048]{1,0:T(8,128)(2,1)S(1)}, bf16[32,2048]{1,0:T(8,128)(2,1)S(1)}, u32[]{:S(2)}, u32[]{:S(2)}) %collective-permute-start.8) | collective-permute-done | bytes 131104 | tf_op jit(solution)/shard_map/ppermute | solution.py:882
  101.7 9.3 %collective-permute-start.23 = (bf16[4,1024,128]{2,1,0:T(8,128)(2,1)S(1)}, bf16[4,1024,128]{2,1,0:T(8,128)(2,1)S(1)}, u32[]{:S(2)}, u32[]{:S(2)}) collective-permute-start(bf16[4,1024,128]{2,1,0:T(8,128)(2,1)S(1)} %fusion.24), channel_id=1, source_target_pairs={{0,1},{1,0},{2,3},{3,2},{4,5},{5,4},{6,7},{7,6},{8,9},{9,8},{10,11... | collective-permute-start | bytes 3145736 | tf_op jit(solution)/shard_map/ppermute | solution.py:137
  113.4 14.3 %attend_forward.1 = (bf16[1024,512]{1,0:T(8,128)(2,1)S(1)}, f32[4,4,8,256]{3,2,1,0:T(8,128)S(1)}) custom-call(s32[1]{0:T(128)} %bitcast.z_ref, bf16[1024,512]{1,0:T(8,128)(2,1)S(1)} %get-tuple-element.77.q_ref, bf16[2,4,1024,128]{3,2,1,0:T(8,128)(2,1)S(1)} %bitcast_dynamic-update-slice_fusion.1.kv_ref), custom_call_target="tpu_custom_call" | custom-call | flops 8999999488 | bytes 8388608 | tf_op jit(solution)/shard_map/attend_forward/pallas_call | solution.py:402
  147.4 7.7 %collective-permute-done.31 = bf16[128,2048]{1,0:T(8,128)(2,1)S(1)} collective-permute-done((bf16[128,2048]{1,0:T(8,128)(2,1)S(1)}, bf16[128,2048]{1,0:T(8,128)(2,1)S(1)}, u32[]{:S(2)}, u32[]{:S(2)}) %collective-permute-start.31) | collective-permute-done | bytes 524320 | tf_op jit(solution)/shard_map/ppermute | solution.py:137
  164.1 33.2 %all_to_all.45.x_hbm = bf16[128,56,128]{2,1,0:T(8,128)(2,1)} all-to-all(bf16[128,56,128]{2,1,0:T(8,128)(2,1)S(1)} %broadcast_dynamic-update-slice_fusion), channel_id=1, replica_groups=mesh['y'=4,'x'=4,'z'=4,'c'=2] {'y','x','z','c'}, dimensions={0} | all-to-all | bytes 3670016 | tf_op jit(solution)/shard_map/all_to_all | solution.py:842
  197.4 9.5 %expert_forward.1 = (bf16[384,2048]{1,0:T(8,128)(2,1)}, f32[384,1536]{1,0:T(8,128)}, bf16[384,768]{1,0:T(8,128)(2,1)}, bf16[6144,128]{1,0:T(8,128)(2,1)}) custom-call(bf16[128,56,128]{2,1,0:T(8,128)(2,1)} %all_to_all.45.x_hbm, bf16[2048,1536]{1,0:T(8,128)(2,1)} %bitcast.203, bf16[768,2048]{1,0:T(8,128)(2,1)} %bitcast.211), custom_call_target="tpu_custom_call" | custom-call | flops 3600000000 | bytes 17825792 | tf_op jit(solution)/shard_map/expert_forward/pallas_call | solution.py:623
  206.9 9.4 %all-to-all-start.2 = ((bf16[128,48,128]{2,1,0:T(8,128)(2,1)}), bf16[128,48,128]{2,1,0:T(8,128)(2,1)}, u32[]{:S(2)}, u32[]{:S(2)}) async-start(bf16[128,48,128]{2,1,0:T(8,128)(2,1)} %bitcast.216), calls=%async_computation.2 | async-start | bytes 3145728 | tf_op jit(solution)/shard_map/all_to_all | solution.py:842
  220.4 16.5 %all-to-all-done.2 = bf16[128,48,128]{2,1,0:T(8,128)(2,1)} async-done(((bf16[128,48,128]{2,1,0:T(8,128)(2,1)}), bf16[128,48,128]{2,1,0:T(8,128)(2,1)}, u32[]{:S(2)}, u32[]{:S(2)}) %all-to-all-start.2) | async-done | bytes 1572896 | tf_op jit(solution)/shard_map/all_to_all | solution.py:842
  236.9 7.4 %combine.1 = (bf16[128,2048]{1,0:T(8,128)(2,1)}, f32[1,128]{1,0:T(1,128)}, f32[128,2048]{1,0:T(8,128)}, bf16[128,48,128]{2,1,0:T(8,128)(2,1)}) custom-call(s32[384]{0:T(512)} %copy-done.17, s32[256]{0:T(256)} %copy-done.40, f32[256]{0:T(256)} %copy-done.42, f32[384]{0:T(512)} %select_reduce_fusion.slot_gate_ref, f32[1]{0:T(128)} %bitcast.41.scale_ref, ...), custom_call_target="tpu_custom_call" | custom-call | flops 2000000 | bytes 7340032 | tf_op jit(solution)/shard_map/combine/pallas_call | solution.py:685
  244.2 30.6 %all_to_all.46 = bf16[128,48,128]{2,1,0:T(8,128)(2,1)} all-to-all(bf16[128,48,128]{2,1,0:T(8,128)(2,1)} %get-tuple-element.86), channel_id=1, replica_groups=mesh['y'=4,'x'=4,'z'=4,'c'=2] {'y','x','z','c'}, dimensions={0} | all-to-all | bytes 3145728 | tf_op jit(solution)/shard_map/all_to_all | solution.py:842
  274.9 10.9 %expert_backward.1 = (bf16[384,2048]{1,0:T(8,128)(2,1)}, bf16[384,1536]{1,0:T(8,128)(2,1)}, bf16[6144,128]{1,0:T(8,128)(2,1)}) custom-call(bf16[6144,128]{1,0:T(8,128)(2,1)} %bitcast.205, bf16[2048,1536]{1,0:T(8,128)(2,1)} %bitcast.204, bf16[768,2048]{1,0:T(8,128)(2,1)} %bitcast.212, f32[384,1536]{1,0:T(8,128)} %get-tuple-element.87.mixed_hbm), custom_call_target="tpu_custom_call" | custom-call | flops 3600000000 | bytes 17825792 | tf_op jit(solution)/shard_map/expert_backward/pallas_call | solution.py:749
  285.7 9.6 %all-to-all-start.4 = ((bf16[128,48,128]{2,1,0:T(8,128)(2,1)}), bf16[128,48,128]{2,1,0:T(8,128)(2,1)}, u32[]{:S(2)}, u32[]{:S(2)}) async-start(bf16[128,48,128]{2,1,0:T(8,128)(2,1)} %bitcast.217), calls=%async_computation.4 | async-start | bytes 3145728 | tf_op jit(solution)/shard_map/all_to_all | solution.py:842
  295.4 6.3 %fusion.42 = f32[768,2048]{1,0:T(8,128)} fusion(bf16[384,768]{1,0:T(8,128)(2,1)} %get-tuple-element.91, bf16[384,2048]{1,0:T(8,128)(2,1)} %get-tuple-element.92), kind=kOutput, calls=%fused_computation.146 | convolution fusion | flops 1207959552 | bytes 8454144 | tf_op jit(solution)/shard_map/dot_general | solution.py:838
  301.7 6.6 %fusion.41 = f32[2048,1536]{1,0:T(8,128)} fusion(bf16[384,2048]{1,0:T(8,128)(2,1)S(1)} %copy-done.33, bf16[384,1536]{1,0:T(8,128)(2,1)S(1)} %copy-done.34), kind=kOutput, calls=%fused_computation.145 | convolution fusion | flops 2415919104 | bytes 15335424 | tf_op jit(solution)/shard_map/dot_general | solution.py:838
  308.3 7.7 %all-to-all-done.4 = bf16[128,48,128]{2,1,0:T(8,128)(2,1)} async-done(((bf16[128,48,128]{2,1,0:T(8,128)(2,1)}), bf16[128,48,128]{2,1,0:T(8,128)(2,1)}, u32[]{:S(2)}, u32[]{:S(2)}) %all-to-all-start.4) | async-done | bytes 1572896 | tf_op jit(solution)/shard_map/all_to_all | solution.py:842
  323.7 10.7 %collective-permute-done.33 = bf16[128,2048]{1,0:T(8,128)(2,1)S(1)} collective-permute-done((bf16[128,2048]{1,0:T(8,128)(2,1)}, bf16[128,2048]{1,0:T(8,128)(2,1)S(1)}, u32[]{:S(2)}, u32[]{:S(2)}) %collective-permute-start.33) | collective-permute-done | bytes 524320 | tf_op jit(solution)/shard_map/ppermute | solution.py:137
  356.0 7.9 %all-to-all-start.5 = ((bf16[16,32,2048]{2,1,0:T(8,128)(2,1)}), bf16[16,32,2048]{2,1,0:T(8,128)(2,1)}, u32[]{:S(2)}, u32[]{:S(2)}) async-start(bf16[16,32,2048]{2,1,0:T(8,128)(2,1)} %bitcast.192), calls=%async_computation.5 | async-start | bytes 4194304 | tf_op jit(solution)/shard_map/all_to_all | solution.py:941
  364.0 35.0 %attend_backward.1 = (bf16[1024,512]{1,0:T(8,128)(2,1)}, bf16[4,1024,128]{2,1,0:T(8,128)(2,1)}, bf16[4,1024,128]{2,1,0:T(8,128)(2,1)}) custom-call(s32[1]{0:T(128)} %bitcast.z_ref, s32[1]{0:T(128)} %bitcast.1.core_ref, bf16[1024,512]{1,0:T(8,128)(2,1)} %copy-done.20, bf16[2,4,1024,128]{3,2,1,0:T(8,128)(2,1)} %copy-done.12, bf16[1024,512]{1,0:T(8,128)(2,1)} %bitcast.218, ...), custom_call_target="tpu_custom_call" | custom-call | flops 22000001024 | bytes 8388608 | tf_op jit(solution)/shard_map/attend_backward/pallas_call | solution.py:495
  429.2 6.2 %all-to-all-start.7 = ((bf16[16,40,2048]{2,1,0:T(8,128)(2,1)}), bf16[16,40,2048]{2,1,0:T(8,128)(2,1)}, u32[]{:S(2)}, u32[]{:S(2)}) async-start(bf16[16,40,2048]{2,1,0:T(8,128)(2,1)} %bitcast.188), calls=%async_computation.7 | async-start | bytes 5242880 | tf_op jit(solution)/shard_map/all_to_all | solution.py:953
  447.3 6.2 %collective-permute-done.47 = bf16[128,1024]{1,0:T(8,128)(2,1)S(1)} collective-permute-done((bf16[128,1024]{1,0:T(8,128)(2,1)S(1)}, bf16[128,1024]{1,0:T(8,128)(2,1)S(1)}, u32[]{:S(2)}, u32[]{:S(2)}) %collective-permute-start.47) | collective-permute-done | bytes 262176 | tf_op jit(solution)/shard_map/ppermute | solution.py:137
  473.3 6.8 %all-to-all-start.8 = ((f32[16,35,128]{2,1,0:T(8,128)}), f32[16,35,128]{2,1,0:T(8,128)}, u32[]{:S(2)}, u32[]{:S(2)}) async-start(f32[16,35,128]{2,1,0:T(8,128)} %broadcast_in_dim.274), calls=%async_computation.8 | async-start | bytes 655360 | tf_op jit(solution)/shard_map/all_to_all | solution.py:209
  484.2 13.6 %collective-permute-start.49 = (bf16[40,2048]{1,0:T(8,128)(2,1)S(1)}, bf16[40,2048]{1,0:T(8,128)(2,1)S(1)}, u32[]{:S(2)}, u32[]{:S(2)}) collective-permute-start(bf16[40,2048]{1,0:T(8,128)(2,1)S(1)} %get-tuple-element.141), channel_id=1, source_target_pairs={{0,0},{32,1},{64,2},{96,3},{2,4},{34,5},{66,6},{98,7},{4,8},{36,9}... | collective-permute-start | bytes 491528 | tf_op jit(solution)/shard_map/ppermute | solution.py:971
  502.4 6.6 %collective-permute-done.52 = bf16[32,2048]{1,0:T(8,128)(2,1)S(1)} collective-permute-done((bf16[32,2048]{1,0:T(8,128)(2,1)S(1)}, bf16[32,2048]{1,0:T(8,128)(2,1)S(1)}, u32[]{:S(2)}, u32[]{:S(2)}) %collective-permute-start.52) | collective-permute-done | bytes 131104 | tf_op jit(solution)/shard_map/ppermute | solution.py:969
  (340 shorter events, 220.4 us)
Async XLA Ops:
  4.7 44.7 %collective-permute-start = (bf16[128,2048]{1,0:T(8,128)(2,1)}, bf16[128,2048]{1,0:T(8,128)(2,1)S(1)}, u32[]{:S(2)}, u32[]{:S(2)}) collective-permute-start(bf16[128,2048]{1,0:T(8,128)(2,1)} %get-tuple-element.126), channel_id=1, source_target_pairs={{0,8},{8,16},{16,24},{24,0},{1,9},{9,17},{17,25},{25,1},{2,10},{10... | collective-permute-start | bytes 1572872 | tf_op jit(solution)/shard_map/ppermute | solution.py:137
  6.0 42.9 %collective-permute-start.1 = (bf16[128,2048]{1,0:T(8,128)(2,1)}, bf16[128,2048]{1,0:T(8,128)(2,1)S(1)}, u32[]{:S(2)}, u32[]{:S(2)}) collective-permute-start(bf16[128,2048]{1,0:T(8,128)(2,1)} %get-tuple-element.126), channel_id=1, source_target_pairs={{0,24},{8,0},{16,8},{24,16},{1,25},{9,1},{17,9},{25,17},{2,26},{10... | collective-permute-start | bytes 1572872 | tf_op jit(solution)/shard_map/ppermute | solution.py:137
  8.7 16.2 %collective-permute-start.7 = (bf16[40,2048]{1,0:T(8,128)(2,1)}, bf16[40,2048]{1,0:T(8,128)(2,1)S(1)}, u32[]{:S(2)}, u32[]{:S(2)}) collective-permute-start(bf16[40,2048]{1,0:T(8,128)(2,1)} %get-tuple-element.145), channel_id=1, source_target_pairs={{102,6},{105,14},{115,7},{118,15},{121,23},{12,37},{76,60},{28,74}... | collective-permute-start | bytes 491528 | tf_op jit(solution)/shard_map/ppermute | solution.py:881
  9.3 17.5 %collective-permute-start.6 = (bf16[40,2048]{1,0:T(8,128)(2,1)}, bf16[40,2048]{1,0:T(8,128)(2,1)}, u32[]{:S(2)}, u32[]{:S(2)}) collective-permute-start(bf16[40,2048]{1,0:T(8,128)(2,1)} %get-tuple-element.146), channel_id=1, source_target_pairs={{13,37},{14,69},{15,101},{25,44},{29,74},{30,106},{31,12},{38,75},... | collective-permute-start | bytes 491528 | tf_op jit(solution)/shard_map/ppermute | solution.py:881
  10.7 16.6 %collective-permute-start.5 = (bf16[40,2048]{1,0:T(8,128)(2,1)S(1)}, bf16[40,2048]{1,0:T(8,128)(2,1)}, u32[]{:S(2)}, u32[]{:S(2)}) collective-permute-start(bf16[40,2048]{1,0:T(8,128)(2,1)S(1)} %get-tuple-element.144), channel_id=1, source_target_pairs={{0,0},{1,32},{2,64},{3,96},{4,2},{5,34},{6,66},{7,98},{8,4},{9,36}... | collective-permute-start | bytes 491528 | tf_op jit(solution)/shard_map/ppermute | solution.py:881
  37.8 18.0 %all-to-all-start = ((bf16[4,40,2048]{2,1,0:T(8,128)(2,1)}), bf16[4,40,2048]{2,1,0:T(8,128)(2,1)}, u32[]{:S(2)}, u32[]{:S(2)}) async-start(bf16[4,40,2048]{2,1,0:T(8,128)(2,1)} %broadcast_in_dim.238), calls=%async_computation | async-start | bytes 1310720 | tf_op jit(solution)/shard_map/all_to_all | solution.py:209
  56.4 13.2 %collective-permute-start.14 = (bf16[4,40,2048]{2,1,0:T(8,128)(2,1)}, bf16[4,40,2048]{2,1,0:T(8,128)(2,1)S(1)}, u32[]{:S(2)}, u32[]{:S(2)}) collective-permute-start(bf16[4,40,2048]{2,1,0:T(8,128)(2,1)} %all-to-all-done), channel_id=1, source_target_pairs={{0,6},{2,0},{4,2},{6,4},{1,7},{3,1},{5,3},{7,5},{8,14},{10,8},{12,... | collective-permute-start | bytes 1966088 | tf_op jit(solution)/shard_map/ppermute | solution.py:137
  60.0 18.5 %collective-permute-start.4 = (bf16[512,2048]{1,0:T(8,128)(2,1)}, bf16[512,2048]{1,0:T(8,128)(2,1)S(1)}, u32[]{:S(2)}, u32[]{:S(2)}) collective-permute-start(bf16[512,2048]{1,0:T(8,128)(2,1)} %bitcast.7), channel_id=1, source_target_pairs={{0,1},{1,0},{2,3},{3,2},{4,5},{5,4},{6,7},{7,6},{8,9},{9,8},{10,11... | collective-permute-start | bytes 6291464 | tf_op jit(solution)/shard_map/ppermute | solution.py:137
  87.8 23.3 %collective-permute-start.25 = (bf16[4,32,1024]{2,1,0:T(8,128)(2,1)S(1)}, bf16[4,32,1024]{2,1,0:T(8,128)(2,1)S(1)}, u32[]{:S(2)}, u32[]{:S(2)}) collective-permute-start(bf16[4,32,1024]{2,1,0:T(8,128)(2,1)S(1)} %slice.149), channel_id=1, source_target_pairs={{0,96},{32,0},{64,32},{96,64},{1,97},{33,1},{65,33},{97,65},{2,98}... | collective-permute-start | bytes 786440 | tf_op jit(solution)/shard_map/ppermute | solution.py:137
  88.9 22.1 %collective-permute-start.24 = (bf16[4,32,1024]{2,1,0:T(8,128)(2,1)S(1)}, bf16[4,32,1024]{2,1,0:T(8,128)(2,1)S(1)}, u32[]{:S(2)}, u32[]{:S(2)}) collective-permute-start(bf16[4,32,1024]{2,1,0:T(8,128)(2,1)S(1)} %slice.148), channel_id=1, source_target_pairs={{0,32},{32,64},{64,96},{96,0},{1,33},{33,65},{65,97},{97,1},{2,34}... | collective-permute-start | bytes 786440 | tf_op jit(solution)/shard_map/ppermute | solution.py:137
  111.2 18.4 %collective-permute-start.27 = (bf16[512,2048]{1,0:T(8,128)(2,1)S(1)}, bf16[512,2048]{1,0:T(8,128)(2,1)S(1)}, u32[]{:S(2)}, u32[]{:S(2)}) collective-permute-start(bf16[512,2048]{1,0:T(8,128)(2,1)S(1)} %bitcast.194), channel_id=1, source_target_pairs={{0,1},{1,0},{2,3},{3,2},{4,5},{5,4},{6,7},{7,6},{8,9},{9,8},{10,11... | collective-permute-start | bytes 6291464 | tf_op jit(solution)/shard_map/ppermute | solution.py:137
  206.9 30.0 %all-to-all-start.2 = ((bf16[128,48,128]{2,1,0:T(8,128)(2,1)}), bf16[128,48,128]{2,1,0:T(8,128)(2,1)}, u32[]{:S(2)}, u32[]{:S(2)}) async-start(bf16[128,48,128]{2,1,0:T(8,128)(2,1)} %bitcast.216), calls=%async_computation.2 | async-start | bytes 3145728 | tf_op jit(solution)/shard_map/all_to_all | solution.py:842
  285.7 30.2 %all-to-all-start.4 = ((bf16[128,48,128]{2,1,0:T(8,128)(2,1)}), bf16[128,48,128]{2,1,0:T(8,128)(2,1)}, u32[]{:S(2)}, u32[]{:S(2)}) async-start(bf16[128,48,128]{2,1,0:T(8,128)(2,1)} %bitcast.217), calls=%async_computation.4 | async-start | bytes 3145728 | tf_op jit(solution)/shard_map/all_to_all | solution.py:842
  323.1 14.0 %collective-permute-start.32 = (bf16[128,2048]{1,0:T(8,128)(2,1)}, bf16[128,2048]{1,0:T(8,128)(2,1)S(1)}, u32[]{:S(2)}, u32[]{:S(2)}) collective-permute-start(bf16[128,2048]{1,0:T(8,128)(2,1)} %get-tuple-element.95), channel_id=1, source_target_pairs={{0,8},{8,16},{16,24},{24,0},{1,9},{9,17},{17,25},{25,1},{2,10},{10... | collective-permute-start | bytes 1572872 | tf_op jit(solution)/shard_map/ppermute | solution.py:137
  356.0 42.9 %all-to-all-start.5 = ((bf16[16,32,2048]{2,1,0:T(8,128)(2,1)}), bf16[16,32,2048]{2,1,0:T(8,128)(2,1)}, u32[]{:S(2)}, u32[]{:S(2)}) async-start(bf16[16,32,2048]{2,1,0:T(8,128)(2,1)} %bitcast.192), calls=%async_computation.5 | async-start | bytes 4194304 | tf_op jit(solution)/shard_map/all_to_all | solution.py:941
  399.7 42.1 %collective-permute-start.44 = (bf16[640,2048]{1,0:T(8,128)(2,1)S(1)}, bf16[640,2048]{1,0:T(8,128)(2,1)}, u32[]{:S(2)}, u32[]{:S(2)}) collective-permute-start(bf16[640,2048]{1,0:T(8,128)(2,1)S(1)} %bitcast.179), channel_id=1, source_target_pairs={{0,1},{1,0},{2,3},{3,2},{4,5},{5,4},{6,7},{7,6},{8,9},{9,8},{10,11... | collective-permute-start | bytes 7864328 | tf_op jit(solution)/shard_map/ppermute | solution.py:137
  405.3 18.2 %all-to-all-start.6 = ((bf16[4,1024,128]{2,1,0:T(8,128)(2,1)}), bf16[4,1024,128]{2,1,0:T(8,128)(2,1)}, u32[]{:S(2)}, u32[]{:S(2)}) async-start(bf16[4,1024,128]{2,1,0:T(8,128)(2,1)} %add_convert_fusion.3), calls=%async_computation.6 | async-start | bytes 2097152 | tf_op jit(solution)/shard_map/all_to_all | solution.py:946
  429.2 43.3 %all-to-all-start.7 = ((bf16[16,40,2048]{2,1,0:T(8,128)(2,1)}), bf16[16,40,2048]{2,1,0:T(8,128)(2,1)}, u32[]{:S(2)}, u32[]{:S(2)}) async-start(bf16[16,40,2048]{2,1,0:T(8,128)(2,1)} %bitcast.188), calls=%async_computation.7 | async-start | bytes 5242880 | tf_op jit(solution)/shard_map/all_to_all | solution.py:953
  454.4 16.6 %collective-permute-start.48 = (bf16[128,2048]{1,0:T(8,128)(2,1)}, bf16[128,2048]{1,0:T(8,128)(2,1)S(1)}, u32[]{:S(2)}, u32[]{:S(2)}) collective-permute-start(bf16[128,2048]{1,0:T(8,128)(2,1)} %pad_maximum_fusion.6), channel_id=1, source_target_pairs={{0,24},{8,0},{16,8},{24,16},{1,25},{9,1},{17,9},{25,17},{2,26},{10... | collective-permute-start | bytes 1572872 | tf_op jit(solution)/shard_map/ppermute | solution.py:137
  456.6 14.5 %collective-permute-start.46 = (bf16[128,2048]{1,0:T(8,128)(2,1)}, bf16[128,2048]{1,0:T(8,128)(2,1)}, u32[]{:S(2)}, u32[]{:S(2)}) collective-permute-start(bf16[128,2048]{1,0:T(8,128)(2,1)} %pad_maximum_fusion.5), channel_id=1, source_target_pairs={{0,8},{8,16},{16,24},{24,0},{1,9},{9,17},{17,25},{25,1},{2,10},{10... | collective-permute-start | bytes 1572872 | tf_op jit(solution)/shard_map/ppermute | solution.py:137
  473.3 37.4 %all-to-all-start.8 = ((f32[16,35,128]{2,1,0:T(8,128)}), f32[16,35,128]{2,1,0:T(8,128)}, u32[]{:S(2)}, u32[]{:S(2)}) async-start(f32[16,35,128]{2,1,0:T(8,128)} %broadcast_in_dim.274), calls=%async_computation.8 | async-start | bytes 655360 | tf_op jit(solution)/shard_map/all_to_all | solution.py:209
  482.9 26.8 %collective-permute-start.51 = (bf16[40,2048]{1,0:T(8,128)(2,1)S(1)}, bf16[40,2048]{1,0:T(8,128)(2,1)S(1)}, u32[]{:S(2)}, u32[]{:S(2)}) collective-permute-start(bf16[40,2048]{1,0:T(8,128)(2,1)S(1)} %get-tuple-element.142), channel_id=1, source_target_pairs={{6,102},{14,105},{7,115},{15,118},{23,121},{37,12},{60,76},{74,28}... | collective-permute-start | bytes 491528 | tf_op jit(solution)/shard_map/ppermute | solution.py:971
  483.6 26.1 %collective-permute-start.50 = (bf16[40,2048]{1,0:T(8,128)(2,1)S(1)}, bf16[40,2048]{1,0:T(8,128)(2,1)S(1)}, u32[]{:S(2)}, u32[]{:S(2)}) collective-permute-start(bf16[40,2048]{1,0:T(8,128)(2,1)S(1)} %get-tuple-element.143), channel_id=1, source_target_pairs={{37,13},{69,14},{101,15},{44,25},{74,29},{106,30},{12,31},{75,38},... | collective-permute-start | bytes 491528 | tf_op jit(solution)/shard_map/ppermute | solution.py:971
  484.2 25.5 %collective-permute-start.49 = (bf16[40,2048]{1,0:T(8,128)(2,1)S(1)}, bf16[40,2048]{1,0:T(8,128)(2,1)S(1)}, u32[]{:S(2)}, u32[]{:S(2)}) collective-permute-start(bf16[40,2048]{1,0:T(8,128)(2,1)S(1)} %get-tuple-element.141), channel_id=1, source_target_pairs={{0,0},{32,1},{64,2},{96,3},{2,4},{34,5},{66,6},{98,7},{4,8},{36,9}... | collective-permute-start | bytes 491528 | tf_op jit(solution)/shard_map/ppermute | solution.py:971
  (86 other events, 686.5 us)

commit v8 on v7

--- a/solution.py
+++ b/solution.py
@@ -157,14 +157,6 @@
 
 def ring_gather(value, axis):
     return ring_gathers((value, axis))[0]
-
-
-def core_gather(value):
-    index = lax.axis_index("c")
-    other = shift(value, "c", 1)
-    out = jnp.zeros((2,) + value.shape, value.dtype)
-    out = lax.dynamic_update_index_in_dim(out, value, index, 0)
-    return lax.dynamic_update_index_in_dim(out, other, 1 - index, 0)
 
 
 def sum_over(value, axis):
@@ -362,9 +354,20 @@
 STEP = 512
 
 
-def forward_kernel(z_ref, q_ref, kv_ref, o_ref, lse_ref, total):
+def place_heads(core_ref, mine_ref, other_ref, kv_ref):
+    core = core_ref[0]
+    kv_ref[core] = mine_ref[...]
+    kv_ref[1 - core] = other_ref[...]
+
+
+def forward_kernel(z_ref, core_ref, q_ref, mine_ref, other_ref, o_ref, lse_ref, total, kv_ref):
     piece = pl.program_id(0)
     z = z_ref[0]
+
+    @pl.when(piece == 0)
+    def _():
+        place_heads(core_ref, mine_ref, other_ref, kv_ref)
+
     total[...] = jnp.zeros_like(total)
     ones = jnp.ones((STEP, HD), bf16)
 
@@ -398,38 +401,40 @@
         lse_ref[head, 0] = jnp.transpose(jnp.log2(sums))[:8, :]
 
 
-def attend_forward(z, queries, keys_values):
+def attend_forward(z, core, queries, mine, other):
     return pl.pallas_call(
         forward_kernel,
         grid_spec=pltpu.PrefetchScalarGridSpec(
-            num_scalar_prefetch=1,
+            num_scalar_prefetch=2,
             grid=(4,),
             in_specs=[
-                pl.BlockSpec((PIECE, HEADS * HD), lambda i, z: (i, 0)),
-                pl.BlockSpec((2, 4, GROUP, HD), lambda i, z: (0, 0, 0, 0)),
+                pl.BlockSpec((PIECE, HEADS * HD), lambda i, z, c: (i, 0)),
+                pl.BlockSpec((4, GROUP, HD), lambda i, z, c: (0, 0, 0)),
+                pl.BlockSpec((4, GROUP, HD), lambda i, z, c: (0, 0, 0)),
             ],
             out_specs=[
-                pl.BlockSpec((PIECE, HEADS * HD), lambda i, z: (i, 0)),
-                pl.BlockSpec((HEADS, 1, 8, PIECE), lambda i, z: (0, i, 0, 0)),
+                pl.BlockSpec((PIECE, HEADS * HD), lambda i, z, c: (i, 0)),
+                pl.BlockSpec((HEADS, 1, 8, PIECE), lambda i, z, c: (0, i, 0, 0)),
             ],
-            scratch_shapes=[pltpu.VMEM((HEADS, PIECE, 2 * HD), f32)],
+            scratch_shapes=[pltpu.VMEM((HEADS, PIECE, 2 * HD), f32), pltpu.VMEM((2, 4, GROUP, HD), bf16)],
         ),
         out_shape=[
             jax.ShapeDtypeStruct((GROUP, HEADS * HD), bf16),
             jax.ShapeDtypeStruct((HEADS, 4, 8, PIECE), f32),
         ],
-        compiler_params=pltpu.CompilerParams(vmem_limit_bytes=16 * 2**20),
+        compiler_params=pltpu.CompilerParams(vmem_limit_bytes=18 * 2**20),
         cost_estimate=pl.CostEstimate(flops=9 * 10**9, bytes_accessed=8 * 2**20, transcendentals=10**7),
         name="attend_forward",
-    )(z, queries, keys_values)
-
-
-def backward_kernel(z_ref, core_ref, q_ref, kv_ref, go_ref, o_ref, lse_ref, dq_ref, own_ref, there_ref, dqt, dkv, kt):
+    )(z, core, queries, mine, other)
+
+
+def backward_kernel(z_ref, core_ref, q_ref, mine_ref, other_ref, go_ref, o_ref, lse_ref, dq_ref, own_ref, there_ref, dqt, dkv, kt, kv_ref):
     piece = pl.program_id(0)
     z = z_ref[0]
 
     @pl.when(piece == 0)
     def _():
+        place_heads(core_ref, mine_ref, other_ref, kv_ref)
         dkv[...] = jnp.zeros_like(dkv)
         for block in range(4):
             for part in range(4):
@@ -488,9 +493,8 @@
         there_ref[...] = (dkv[1 - core] * jnp.where(core == 0, 1.0, SCALE)).astype(bf16)
 
 
-def attend_backward(z, core, queries, keys_values, backs, outs, lse):
+def attend_backward(z, core, queries, mine, other, backs, outs, lse):
     heads_spec = pl.BlockSpec((PIECE, HEADS * HD), lambda i, z, c: (i, 0))
-    whole = pl.BlockSpec((2, 4, GROUP, HD), lambda i, z, c: (0, 0, 0, 0))
     part = pl.BlockSpec((4, GROUP, HD), lambda i, z, c: (0, 0, 0))
     return pl.pallas_call(
         backward_kernel,
@@ -499,7 +503,8 @@
             grid=(4,),
             in_specs=[
                 heads_spec,
-                whole,
+                part,
+                part,
                 heads_spec,
                 heads_spec,
                 pl.BlockSpec((HEADS, 1, 8, PIECE), lambda i, z, c: (0, i, 0, 0)),
@@ -509,6 +514,7 @@
                 pltpu.VMEM((HD, HEADS * PIECE), f32),
                 pltpu.VMEM((2, 4, GROUP, HD), f32),
                 pltpu.VMEM((4, HD, GROUP), bf16),
+                pltpu.VMEM((2, 4, GROUP, HD), bf16),
             ],
         ),
         out_shape=[
@@ -519,7 +525,7 @@
         compiler_params=pltpu.CompilerParams(vmem_limit_bytes=60 * 2**20),
         cost_estimate=pl.CostEstimate(flops=22 * 10**9, bytes_accessed=8 * 2**20, transcendentals=10**7),
         name="attend_backward",
-    )(z, core, queries, keys_values, backs, outs, lse)
+    )(z, core, queries, mine, other, backs, outs, lse)
 
 
 ROWS = EXPERTS * CAP
@@ -891,11 +897,12 @@
     out_mine = out_mine.reshape(HEADS * HD, D)
 
     projected, queries, key_or_value = project(c_array, h1_group, in_mine, cosine, sine, q_gain_row, k_gain_row)
-    keys_values = core_gather(ring_gather(key_or_value, "z"))
+    kv_mine = ring_gather(key_or_value, "z")
+    kv_other = shift(kv_mine, "c", 1)
 
 
     out_other = shift(out_mine, "c", 1)
-    attended, lse = attend_forward(z_array, queries, keys_values)
+    attended, lse = attend_forward(z_array, c_array, queries, kv_mine, kv_other)
     attended_mine, attended_other = core_halves(attended, c)
     attended_there = shift(attended_other, "c", 1)
     chip_out = dot(attended_mine, out_mine) + dot(attended_there, out_other)
@@ -937,7 +944,7 @@
     gb_other = shift(gb_mine, "c", 1)
     out_partial = (dot(attended_mine, gb_mine, TN) + dot(attended_other, gb_other, TN)).astype(bf16)
     backs, out_partial = lax.optimization_barrier((backs, out_partial))
-    dq, own, there = attend_backward(z_array, c_array, queries, keys_values, backs, attended, lse)
+    dq, own, there = attend_backward(z_array, c_array, queries, kv_mine, kv_other, backs, attended, lse)
     out_moved = lax.all_to_all(out_partial.reshape(16, 32, D), ("y", "z"), split_axis=0, concat_axis=0, tiled=True)
     own, there, out_moved = tie((own, there, out_moved))
     chip_kv = (own.astype(f32) + shift(there, "c", 1).astype(f32)).astype(bf16)

time: 525 us -> 528 us (level)
  transfers between devices with their start and end apart: 60 -> 60, of which waited for: 30 -> 27; matrix products, arithmetic and copies ran while one was open for 14% -> 15% of each run, Pallas kernels for 11% -> 12%
where the time goes in v8:
time: 528 us; the launch traced here: 518 us
  starting transfers between devices  136 us (26%)
  waiting for transfers between devices  113 us (21%)
  Pallas kernels  98.1 us (19%)
  blocking collectives  64.6 us (12%)
  other arithmetic  35.4 us (7%)
  matrix products  33.7 us (6%)
  local copies, waits for them, and re-layouts  32 us (6%)
  between operations  5.83 us (1%)
    ppermute x45, waiting for transfers between devices, shift(): lax.ppermute(value, axis, [(i, (i + step) % size) for i in range(size)])  73.9 us
    all_to_all x2, blocking collectives, exchange(): return lax.all_to_all(rows, ALL, split_axis=0, concat_axis=0, tiled=True)  64.6 us
    ppermute x45, starting transfers between devices, shift(): lax.ppermute(value, axis, [(i, (i + step) % size) for i in range(size)])  56.7 us
    pallas_call x1, Pallas kernels, attend_backward(): pl.pallas_call(backward_kernel, grid_spec=pltpu.PrefetchScalarGridSpec(nu...  35 us
    dot_general x15, matrix products, dot(): return lax.dot_general(a, b, dims, preferred_element_type=f32)  33.7 us
    all_to_all x2, waiting for transfers between devices, exchange(): return lax.all_to_all(rows, ALL, split_axis=0, concat_axis=0, tiled=True)  24.1 us
    all_to_all x2, starting transfers between devices, exchange(): return lax.all_to_all(rows, ALL, split_axis=0, concat_axis=0, tiled=True)  19 us
    ppermute x3, starting transfers between devices, body(): lax.ppermute(going[40 * i:40 * i + 40], ALL, [(b, a) for a, b in perms[i]])  14.8 us
  transfers between devices with their start and end apart: 60, of which 27 were waited for; matrix products, arithmetic and copies ran while one was open for 15% of the time, Pallas kernels for 12%

profile of v8, /device:TPU:49, one launch (start us, length us, event | category | flops | bytes accessed | tf_op | source)
XLA Modules:
  0.0 518.3 jit_solution(8497607400909741819)
XLA Ops:
  9.2 10.6 %collective-permute-start.5 = (bf16[40,2048]{1,0:T(8,128)(2,1)S(1)}, bf16[40,2048]{1,0:T(8,128)(2,1)}, u32[]{:S(2)}, u32[]{:S(2)}) collective-permute-start(bf16[40,2048]{1,0:T(8,128)(2,1)S(1)} %get-tuple-element.144), channel_id=1, source_target_pairs={{0,0},{1,32},{2,64},{3,96},{4,2},{5,34},{6,66},{7,98},{8,4},{9,36}... | collective-permute-start | bytes 491528 | tf_op jit(solution)/shard_map/ppermute | solution.py:887
  28.9 7.3 %collective-permute-done.8 = bf16[32,2048]{1,0:T(8,128)(2,1)S(1)} collective-permute-done((bf16[32,2048]{1,0:T(8,128)(2,1)S(1)}, bf16[32,2048]{1,0:T(8,128)(2,1)S(1)}, u32[]{:S(2)}, u32[]{:S(2)}) %collective-permute-start.8) | collective-permute-done | bytes 131104 | tf_op jit(solution)/shard_map/ppermute | solution.py:888
  103.5 9.0 %collective-permute-start.23 = (bf16[4,1024,128]{2,1,0:T(8,128)(2,1)S(1)}, bf16[4,1024,128]{2,1,0:T(8,128)(2,1)S(1)}, u32[]{:S(2)}, u32[]{:S(2)}) collective-permute-start(bf16[4,1024,128]{2,1,0:T(8,128)(2,1)S(1)} %fusion.24.mine_ref), channel_id=1, source_target_pairs={{0,1},{1,0},{2,3},{3,2},{4,5},{5,4},{6,7},{7,6},{8,9},{9,8},{10,11... | collective-permute-start | bytes 3145736 | tf_op jit(solution)/shard_map/ppermute | solution.py:137
  114.8 14.3 %attend_forward.1 = (bf16[1024,512]{1,0:T(8,128)(2,1)S(1)}, f32[4,4,8,256]{3,2,1,0:T(8,128)S(1)}) custom-call(s32[1]{0:T(128)} %bitcast.z_ref, s32[1]{0:T(128)} %bitcast.1.core_ref, bf16[1024,512]{1,0:T(8,128)(2,1)S(1)} %get-tuple-element.77.q_ref, bf16[4,1024,128]{2,1,0:T(8,128)(2,1)S(1)} %fusion.24.mine_ref, ...), custom_call_target="tpu_custom_call" | custom-call | flops 8999999488 | bytes 8388608 | tf_op jit(solution)/shard_map/attend_forward/pallas_call | solution.py:405
  149.0 8.6 %collective-permute-done.31 = bf16[128,2048]{1,0:T(8,128)(2,1)S(1)} collective-permute-done((bf16[128,2048]{1,0:T(8,128)(2,1)S(1)}, bf16[128,2048]{1,0:T(8,128)(2,1)S(1)}, u32[]{:S(2)}, u32[]{:S(2)}) %collective-permute-start.31) | collective-permute-done | bytes 524320 | tf_op jit(solution)/shard_map/ppermute | solution.py:137
  165.8 33.7 %all_to_all.45.x_hbm = bf16[128,56,128]{2,1,0:T(8,128)(2,1)} all-to-all(bf16[128,56,128]{2,1,0:T(8,128)(2,1)S(1)} %broadcast_dynamic-update-slice_fusion), channel_id=1, replica_groups=mesh['y'=4,'x'=4,'z'=4,'c'=2] {'y','x','z','c'}, dimensions={0} | all-to-all | bytes 3670016 | tf_op jit(solution)/shard_map/all_to_all | solution.py:848
  199.5 9.5 %expert_forward.1 = (bf16[384,2048]{1,0:T(8,128)(2,1)}, f32[384,1536]{1,0:T(8,128)}, bf16[384,768]{1,0:T(8,128)(2,1)}, bf16[6144,128]{1,0:T(8,128)(2,1)}) custom-call(bf16[128,56,128]{2,1,0:T(8,128)(2,1)} %all_to_all.45.x_hbm, bf16[2048,1536]{1,0:T(8,128)(2,1)} %bitcast.200, bf16[768,2048]{1,0:T(8,128)(2,1)} %bitcast.208), custom_call_target="tpu_custom_call" | custom-call | flops 3600000000 | bytes 17825792 | tf_op jit(solution)/shard_map/expert_forward/pallas_call | solution.py:629
  209.0 9.4 %all-to-all-start.2 = ((bf16[128,48,128]{2,1,0:T(8,128)(2,1)}), bf16[128,48,128]{2,1,0:T(8,128)(2,1)}, u32[]{:S(2)}, u32[]{:S(2)}) async-start(bf16[128,48,128]{2,1,0:T(8,128)(2,1)} %bitcast.213), calls=%async_computation.2 | async-start | bytes 3145728 | tf_op jit(solution)/shard_map/all_to_all | solution.py:848
  222.6 16.5 %all-to-all-done.2 = bf16[128,48,128]{2,1,0:T(8,128)(2,1)} async-done(((bf16[128,48,128]{2,1,0:T(8,128)(2,1)}), bf16[128,48,128]{2,1,0:T(8,128)(2,1)}, u32[]{:S(2)}, u32[]{:S(2)}) %all-to-all-start.2) | async-done | bytes 1572896 | tf_op jit(solution)/shard_map/all_to_all | solution.py:848
  239.0 7.4 %combine.1 = (bf16[128,2048]{1,0:T(8,128)(2,1)}, f32[1,128]{1,0:T(1,128)}, f32[128,2048]{1,0:T(8,128)}, bf16[128,48,128]{2,1,0:T(8,128)(2,1)}) custom-call(s32[384]{0:T(512)} %copy-done.17, s32[256]{0:T(256)} %copy-done.43, f32[256]{0:T(256)} %copy-done.45, f32[384]{0:T(512)} %select_reduce_fusion.slot_gate_ref, f32[1]{0:T(128)} %bitcast.39.scale_ref, ...), custom_call_target="tpu_custom_call" | custom-call | flops 2000000 | bytes 7340032 | tf_op jit(solution)/shard_map/combine/pallas_call | solution.py:691
  246.4 30.9 %all_to_all.46 = bf16[128,48,128]{2,1,0:T(8,128)(2,1)} all-to-all(bf16[128,48,128]{2,1,0:T(8,128)(2,1)} %get-tuple-element.86), channel_id=1, replica_groups=mesh['y'=4,'x'=4,'z'=4,'c'=2] {'y','x','z','c'}, dimensions={0} | all-to-all | bytes 3145728 | tf_op jit(solution)/shard_map/all_to_all | solution.py:848
  277.3 10.9 %expert_backward.1 = (bf16[384,2048]{1,0:T(8,128)(2,1)}, bf16[384,1536]{1,0:T(8,128)(2,1)}, bf16[6144,128]{1,0:T(8,128)(2,1)}) custom-call(bf16[6144,128]{1,0:T(8,128)(2,1)} %bitcast.202, bf16[2048,1536]{1,0:T(8,128)(2,1)} %bitcast.201, bf16[768,2048]{1,0:T(8,128)(2,1)} %bitcast.209, f32[384,1536]{1,0:T(8,128)} %get-tuple-element.87.mixed_hbm), custom_call_target="tpu_custom_call" | custom-call | flops 3600000000 | bytes 17825792 | tf_op jit(solution)/shard_map/expert_backward/pallas_call | solution.py:755
  288.1 9.6 %all-to-all-start.4 = ((bf16[128,48,128]{2,1,0:T(8,128)(2,1)}), bf16[128,48,128]{2,1,0:T(8,128)(2,1)}, u32[]{:S(2)}, u32[]{:S(2)}) async-start(bf16[128,48,128]{2,1,0:T(8,128)(2,1)} %bitcast.214), calls=%async_computation.4 | async-start | bytes 3145728 | tf_op jit(solution)/shard_map/all_to_all | solution.py:848
  297.8 6.3 %fusion.42 = f32[768,2048]{1,0:T(8,128)} fusion(bf16[384,768]{1,0:T(8,128)(2,1)} %get-tuple-element.91, bf16[384,2048]{1,0:T(8,128)(2,1)} %get-tuple-element.92), kind=kOutput, calls=%fused_computation.144 | convolution fusion | flops 1207959552 | bytes 8454144 | tf_op jit(solution)/shard_map/dot_general | solution.py:844
  304.1 6.6 %fusion.41 = f32[2048,1536]{1,0:T(8,128)} fusion(bf16[384,2048]{1,0:T(8,128)(2,1)S(1)} %copy-done.36, bf16[384,1536]{1,0:T(8,128)(2,1)S(1)} %copy-done.37), kind=kOutput, calls=%fused_computation.143 | convolution fusion | flops 2415919104 | bytes 15335424 | tf_op jit(solution)/shard_map/dot_general | solution.py:844
  310.7 7.7 %all-to-all-done.4 = bf16[128,48,128]{2,1,0:T(8,128)(2,1)} async-done(((bf16[128,48,128]{2,1,0:T(8,128)(2,1)}), bf16[128,48,128]{2,1,0:T(8,128)(2,1)}, u32[]{:S(2)}, u32[]{:S(2)}) %all-to-all-start.4) | async-done | bytes 1572896 | tf_op jit(solution)/shard_map/all_to_all | solution.py:848
  326.1 10.7 %collective-permute-done.33 = bf16[128,2048]{1,0:T(8,128)(2,1)S(1)} collective-permute-done((bf16[128,2048]{1,0:T(8,128)(2,1)}, bf16[128,2048]{1,0:T(8,128)(2,1)S(1)}, u32[]{:S(2)}, u32[]{:S(2)}) %collective-permute-start.33) | collective-permute-done | bytes 524320 | tf_op jit(solution)/shard_map/ppermute | solution.py:137
  358.6 7.7 %all-to-all-start.5 = ((bf16[16,32,2048]{2,1,0:T(8,128)(2,1)}), bf16[16,32,2048]{2,1,0:T(8,128)(2,1)}, u32[]{:S(2)}, u32[]{:S(2)}) async-start(bf16[16,32,2048]{2,1,0:T(8,128)(2,1)} %bitcast.188), calls=%async_computation.5 | async-start | bytes 4194304 | tf_op jit(solution)/shard_map/all_to_all | solution.py:948
  366.3 35.0 %attend_backward.1 = (bf16[1024,512]{1,0:T(8,128)(2,1)}, bf16[4,1024,128]{2,1,0:T(8,128)(2,1)}, bf16[4,1024,128]{2,1,0:T(8,128)(2,1)}) custom-call(s32[1]{0:T(128)} %bitcast.z_ref, s32[1]{0:T(128)} %bitcast.1.core_ref, bf16[1024,512]{1,0:T(8,128)(2,1)} %copy-done.21, bf16[4,1024,128]{2,1,0:T(8,128)(2,1)} %copy-done.14, bf16[4,1024,128]{2,1,0:T(8,128)(2,1)} %copy-done.20, ...), custom_call_target="tpu_custom_call" | custom-call | flops 22000001024 | bytes 8388608 | tf_op jit(solution)/shard_map/attend_backward/pallas_call | solution.py:499
  431.6 6.2 %all-to-all-start.7 = ((bf16[16,40,2048]{2,1,0:T(8,128)(2,1)}), bf16[16,40,2048]{2,1,0:T(8,128)(2,1)}, u32[]{:S(2)}, u32[]{:S(2)}) async-start(bf16[16,40,2048]{2,1,0:T(8,128)(2,1)} %bitcast.184), calls=%async_computation.7 | async-start | bytes 5242880 | tf_op jit(solution)/shard_map/all_to_all | solution.py:960
  449.8 6.3 %collective-permute-done.47 = bf16[128,1024]{1,0:T(8,128)(2,1)S(1)} collective-permute-done((bf16[128,1024]{1,0:T(8,128)(2,1)S(1)}, bf16[128,1024]{1,0:T(8,128)(2,1)S(1)}, u32[]{:S(2)}, u32[]{:S(2)}) %collective-permute-start.47) | collective-permute-done | bytes 262176 | tf_op jit(solution)/shard_map/ppermute | solution.py:137
  476.5 6.5 %all-to-all-start.8 = ((f32[16,35,128]{2,1,0:T(8,128)}), f32[16,35,128]{2,1,0:T(8,128)}, u32[]{:S(2)}, u32[]{:S(2)}) async-start(f32[16,35,128]{2,1,0:T(8,128)} %broadcast_in_dim.261), calls=%async_computation.8 | async-start | bytes 655360 | tf_op jit(solution)/shard_map/all_to_all | solution.py:201
  487.0 13.4 %collective-permute-start.49 = (bf16[40,2048]{1,0:T(8,128)(2,1)S(1)}, bf16[40,2048]{1,0:T(8,128)(2,1)S(1)}, u32[]{:S(2)}, u32[]{:S(2)}) collective-permute-start(bf16[40,2048]{1,0:T(8,128)(2,1)S(1)} %get-tuple-element.141), channel_id=1, source_target_pairs={{0,0},{32,1},{64,2},{96,3},{2,4},{34,5},{66,6},{98,7},{4,8},{36,9}... | collective-permute-start | bytes 491528 | tf_op jit(solution)/shard_map/ppermute | solution.py:978
  505.0 6.6 %collective-permute-done.52 = bf16[32,2048]{1,0:T(8,128)(2,1)S(1)} collective-permute-done((bf16[32,2048]{1,0:T(8,128)(2,1)S(1)}, bf16[32,2048]{1,0:T(8,128)(2,1)S(1)}, u32[]{:S(2)}, u32[]{:S(2)}) %collective-permute-start.52) | collective-permute-done | bytes 131104 | tf_op jit(solution)/shard_map/ppermute | solution.py:976
  (343 shorter events, 221.8 us)
Async XLA Ops:
  3.3 48.4 %collective-permute-start = (bf16[128,2048]{1,0:T(8,128)(2,1)}, bf16[128,2048]{1,0:T(8,128)(2,1)}, u32[]{:S(2)}, u32[]{:S(2)}) collective-permute-start(bf16[128,2048]{1,0:T(8,128)(2,1)} %get-tuple-element.126), channel_id=1, source_target_pairs={{0,8},{8,16},{16,24},{24,0},{1,9},{9,17},{17,25},{25,1},{2,10},{10... | collective-permute-start | bytes 1572872 | tf_op jit(solution)/shard_map/ppermute | solution.py:137
  4.5 44.9 %collective-permute-start.1 = (bf16[128,2048]{1,0:T(8,128)(2,1)}, bf16[128,2048]{1,0:T(8,128)(2,1)}, u32[]{:S(2)}, u32[]{:S(2)}) collective-permute-start(bf16[128,2048]{1,0:T(8,128)(2,1)} %get-tuple-element.126), channel_id=1, source_target_pairs={{0,24},{8,0},{16,8},{24,16},{1,25},{9,1},{17,9},{25,17},{2,26},{10... | collective-permute-start | bytes 1572872 | tf_op jit(solution)/shard_map/ppermute | solution.py:137
  7.2 18.8 %collective-permute-start.7 = (bf16[40,2048]{1,0:T(8,128)(2,1)}, bf16[40,2048]{1,0:T(8,128)(2,1)S(1)}, u32[]{:S(2)}, u32[]{:S(2)}) collective-permute-start(bf16[40,2048]{1,0:T(8,128)(2,1)} %get-tuple-element.145), channel_id=1, source_target_pairs={{102,6},{105,14},{115,7},{118,15},{121,23},{12,37},{76,60},{28,74}... | collective-permute-start | bytes 491528 | tf_op jit(solution)/shard_map/ppermute | solution.py:887
  7.9 20.0 %collective-permute-start.6 = (bf16[40,2048]{1,0:T(8,128)(2,1)}, bf16[40,2048]{1,0:T(8,128)(2,1)}, u32[]{:S(2)}, u32[]{:S(2)}) collective-permute-start(bf16[40,2048]{1,0:T(8,128)(2,1)} %get-tuple-element.146), channel_id=1, source_target_pairs={{13,37},{14,69},{15,101},{25,44},{29,74},{30,106},{31,12},{38,75},... | collective-permute-start | bytes 491528 | tf_op jit(solution)/shard_map/ppermute | solution.py:887
  9.2 18.7 %collective-permute-start.5 = (bf16[40,2048]{1,0:T(8,128)(2,1)S(1)}, bf16[40,2048]{1,0:T(8,128)(2,1)}, u32[]{:S(2)}, u32[]{:S(2)}) collective-permute-start(bf16[40,2048]{1,0:T(8,128)(2,1)S(1)} %get-tuple-element.144), channel_id=1, source_target_pairs={{0,0},{1,32},{2,64},{3,96},{4,2},{5,34},{6,66},{7,98},{8,4},{9,36}... | collective-permute-start | bytes 491528 | tf_op jit(solution)/shard_map/ppermute | solution.py:887
  38.9 19.2 %all-to-all-start = ((bf16[4,40,2048]{2,1,0:T(8,128)(2,1)}), bf16[4,40,2048]{2,1,0:T(8,128)(2,1)}, u32[]{:S(2)}, u32[]{:S(2)}) async-start(bf16[4,40,2048]{2,1,0:T(8,128)(2,1)} %broadcast_in_dim.228), calls=%async_computation | async-start | bytes 1310720 | tf_op jit(solution)/shard_map/all_to_all | solution.py:201
  58.1 13.7 %collective-permute-start.13 = (bf16[4,40,2048]{2,1,0:T(8,128)(2,1)}, bf16[4,40,2048]{2,1,0:T(8,128)(2,1)S(1)}, u32[]{:S(2)}, u32[]{:S(2)}) collective-permute-start(bf16[4,40,2048]{2,1,0:T(8,128)(2,1)} %all-to-all-done), channel_id=1, source_target_pairs={{0,2},{2,4},{4,6},{6,0},{1,3},{3,5},{5,7},{7,1},{8,10},{10,12},{12... | collective-permute-start | bytes 1966088 | tf_op jit(solution)/shard_map/ppermute | solution.py:137
  63.9 16.6 %collective-permute-start.4 = (bf16[512,2048]{1,0:T(8,128)(2,1)S(1)}, bf16[512,2048]{1,0:T(8,128)(2,1)S(1)}, u32[]{:S(2)}, u32[]{:S(2)}) collective-permute-start(bf16[512,2048]{1,0:T(8,128)(2,1)S(1)} %bitcast.190), channel_id=1, source_target_pairs={{0,1},{1,0},{2,3},{3,2},{4,5},{5,4},{6,7},{7,6},{8,9},{9,8},{10,11... | collective-permute-start | bytes 6291464 | tf_op jit(solution)/shard_map/ppermute | solution.py:137
  74.3 38.2 %collective-permute-start.25 = (bf16[4,32,1024]{2,1,0:T(8,128)(2,1)S(1)}, bf16[4,32,1024]{2,1,0:T(8,128)(2,1)S(1)}, u32[]{:S(2)}, u32[]{:S(2)}) collective-permute-start(bf16[4,32,1024]{2,1,0:T(8,128)(2,1)S(1)} %slice.149), channel_id=1, source_target_pairs={{0,96},{32,0},{64,32},{96,64},{1,97},{33,1},{65,33},{97,65},{2,98}... | collective-permute-start | bytes 786440 | tf_op jit(solution)/shard_map/ppermute | solution.py:137
  74.8 37.8 %collective-permute-start.24 = (bf16[4,32,1024]{2,1,0:T(8,128)(2,1)S(1)}, bf16[4,32,1024]{2,1,0:T(8,128)(2,1)S(1)}, u32[]{:S(2)}, u32[]{:S(2)}) collective-permute-start(bf16[4,32,1024]{2,1,0:T(8,128)(2,1)S(1)} %slice.148), channel_id=1, source_target_pairs={{0,32},{32,64},{64,96},{96,0},{1,33},{33,65},{65,97},{97,1},{2,34}... | collective-permute-start | bytes 786440 | tf_op jit(solution)/shard_map/ppermute | solution.py:137
  112.6 18.4 %collective-permute-start.27 = (bf16[512,2048]{1,0:T(8,128)(2,1)S(1)}, bf16[512,2048]{1,0:T(8,128)(2,1)S(1)}, u32[]{:S(2)}, u32[]{:S(2)}) collective-permute-start(bf16[512,2048]{1,0:T(8,128)(2,1)S(1)} %bitcast.191), channel_id=1, source_target_pairs={{0,1},{1,0},{2,3},{3,2},{4,5},{5,4},{6,7},{7,6},{8,9},{9,8},{10,11... | collective-permute-start | bytes 6291464 | tf_op jit(solution)/shard_map/ppermute | solution.py:137
  209.0 30.0 %all-to-all-start.2 = ((bf16[128,48,128]{2,1,0:T(8,128)(2,1)}), bf16[128,48,128]{2,1,0:T(8,128)(2,1)}, u32[]{:S(2)}, u32[]{:S(2)}) async-start(bf16[128,48,128]{2,1,0:T(8,128)(2,1)} %bitcast.213), calls=%async_computation.2 | async-start | bytes 3145728 | tf_op jit(solution)/shard_map/all_to_all | solution.py:848
  288.1 30.2 %all-to-all-start.4 = ((bf16[128,48,128]{2,1,0:T(8,128)(2,1)}), bf16[128,48,128]{2,1,0:T(8,128)(2,1)}, u32[]{:S(2)}, u32[]{:S(2)}) async-start(bf16[128,48,128]{2,1,0:T(8,128)(2,1)} %bitcast.214), calls=%async_computation.4 | async-start | bytes 3145728 | tf_op jit(solution)/shard_map/all_to_all | solution.py:848
  325.6 14.2 %collective-permute-start.32 = (bf16[128,2048]{1,0:T(8,128)(2,1)}, bf16[128,2048]{1,0:T(8,128)(2,1)S(1)}, u32[]{:S(2)}, u32[]{:S(2)}) collective-permute-start(bf16[128,2048]{1,0:T(8,128)(2,1)} %get-tuple-element.95), channel_id=1, source_target_pairs={{0,8},{8,16},{16,24},{24,0},{1,9},{9,17},{17,25},{25,1},{2,10},{10... | collective-permute-start | bytes 1572872 | tf_op jit(solution)/shard_map/ppermute | solution.py:137
  358.6 42.7 %all-to-all-start.5 = ((bf16[16,32,2048]{2,1,0:T(8,128)(2,1)}), bf16[16,32,2048]{2,1,0:T(8,128)(2,1)}, u32[]{:S(2)}, u32[]{:S(2)}) async-start(bf16[16,32,2048]{2,1,0:T(8,128)(2,1)} %bitcast.188), calls=%async_computation.5 | async-start | bytes 4194304 | tf_op jit(solution)/shard_map/all_to_all | solution.py:948
  402.1 42.1 %collective-permute-start.44 = (bf16[640,2048]{1,0:T(8,128)(2,1)S(1)}, bf16[640,2048]{1,0:T(8,128)(2,1)}, u32[]{:S(2)}, u32[]{:S(2)}) collective-permute-start(bf16[640,2048]{1,0:T(8,128)(2,1)S(1)} %bitcast.175), channel_id=1, source_target_pairs={{0,1},{1,0},{2,3},{3,2},{4,5},{5,4},{6,7},{7,6},{8,9},{9,8},{10,11... | collective-permute-start | bytes 7864328 | tf_op jit(solution)/shard_map/ppermute | solution.py:137
  407.6 18.2 %all-to-all-start.6 = ((bf16[4,1024,128]{2,1,0:T(8,128)(2,1)}), bf16[4,1024,128]{2,1,0:T(8,128)(2,1)}, u32[]{:S(2)}, u32[]{:S(2)}) async-start(bf16[4,1024,128]{2,1,0:T(8,128)(2,1)} %add_convert_fusion.3), calls=%async_computation.6 | async-start | bytes 2097152 | tf_op jit(solution)/shard_map/all_to_all | solution.py:953
  431.6 44.1 %all-to-all-start.7 = ((bf16[16,40,2048]{2,1,0:T(8,128)(2,1)}), bf16[16,40,2048]{2,1,0:T(8,128)(2,1)}, u32[]{:S(2)}, u32[]{:S(2)}) async-start(bf16[16,40,2048]{2,1,0:T(8,128)(2,1)} %bitcast.184), calls=%async_computation.7 | async-start | bytes 5242880 | tf_op jit(solution)/shard_map/all_to_all | solution.py:960
  457.0 17.2 %collective-permute-start.48 = (bf16[128,2048]{1,0:T(8,128)(2,1)}, bf16[128,2048]{1,0:T(8,128)(2,1)S(1)}, u32[]{:S(2)}, u32[]{:S(2)}) collective-permute-start(bf16[128,2048]{1,0:T(8,128)(2,1)} %pad_maximum_fusion.6), channel_id=1, source_target_pairs={{0,24},{8,0},{16,8},{24,16},{1,25},{9,1},{17,9},{25,17},{2,26},{10... | collective-permute-start | bytes 1572872 | tf_op jit(solution)/shard_map/ppermute | solution.py:137
  459.3 14.9 %collective-permute-start.46 = (bf16[128,2048]{1,0:T(8,128)(2,1)}, bf16[128,2048]{1,0:T(8,128)(2,1)}, u32[]{:S(2)}, u32[]{:S(2)}) collective-permute-start(bf16[128,2048]{1,0:T(8,128)(2,1)} %pad_maximum_fusion.5), channel_id=1, source_target_pairs={{0,8},{8,16},{16,24},{24,0},{1,9},{9,17},{17,25},{25,1},{2,10},{10... | collective-permute-start | bytes 1572872 | tf_op jit(solution)/shard_map/ppermute | solution.py:137
  476.5 36.9 %all-to-all-start.8 = ((f32[16,35,128]{2,1,0:T(8,128)}), f32[16,35,128]{2,1,0:T(8,128)}, u32[]{:S(2)}, u32[]{:S(2)}) async-start(f32[16,35,128]{2,1,0:T(8,128)} %broadcast_in_dim.261), calls=%async_computation.8 | async-start | bytes 655360 | tf_op jit(solution)/shard_map/all_to_all | solution.py:201
  485.7 26.6 %collective-permute-start.51 = (bf16[40,2048]{1,0:T(8,128)(2,1)S(1)}, bf16[40,2048]{1,0:T(8,128)(2,1)S(1)}, u32[]{:S(2)}, u32[]{:S(2)}) collective-permute-start(bf16[40,2048]{1,0:T(8,128)(2,1)S(1)} %get-tuple-element.142), channel_id=1, source_target_pairs={{6,102},{14,105},{7,115},{15,118},{23,121},{37,12},{60,76},{74,28}... | collective-permute-start | bytes 491528 | tf_op jit(solution)/shard_map/ppermute | solution.py:978
  486.3 25.9 %collective-permute-start.50 = (bf16[40,2048]{1,0:T(8,128)(2,1)S(1)}, bf16[40,2048]{1,0:T(8,128)(2,1)S(1)}, u32[]{:S(2)}, u32[]{:S(2)}) collective-permute-start(bf16[40,2048]{1,0:T(8,128)(2,1)S(1)} %get-tuple-element.143), channel_id=1, source_target_pairs={{37,13},{69,14},{101,15},{44,25},{74,29},{106,30},{12,31},{75,38},... | collective-permute-start | bytes 491528 | tf_op jit(solution)/shard_map/ppermute | solution.py:978
  487.0 25.3 %collective-permute-start.49 = (bf16[40,2048]{1,0:T(8,128)(2,1)S(1)}, bf16[40,2048]{1,0:T(8,128)(2,1)S(1)}, u32[]{:S(2)}, u32[]{:S(2)}) collective-permute-start(bf16[40,2048]{1,0:T(8,128)(2,1)S(1)} %get-tuple-element.141), channel_id=1, source_target_pairs={{0,0},{32,1},{64,2},{96,3},{2,4},{34,5},{66,6},{98,7},{4,8},{36,9}... | collective-permute-start | bytes 491528 | tf_op jit(solution)/shard_map/ppermute | solution.py:978
  (89 other events, 717.1 us)
